TPU v7x, 32 devices: a whole 2x2x4 slice. The times are simulated.
32 devices in a mesh: blk: 4 (over z), sub: 8 (over y, x, core).
Axes of the slice: x: 2, y: 2, z: 4, core: 2. Of those that a mesh axis runs over, the one named last changes fastest.
Arguments:
- right_side: float32 [64, 8192], P(None, ('blk', 'sub')), may hold values from -8 to 8
- conductivity: float32 [8192], P(('blk', 'sub')), may hold values from 1 to 8
- material: int32 [8192], P(('blk', 'sub')), may hold values 0 or 1
- stiffness: float32 [2, 64, 64], replicated, may hold values from -0.0223 to 2.5, as said below
- trace_map: float32 [96, 64], replicated, may hold values from -0.75 to 0.75
- face_neighbour: int32 [6, 8192], P(None, ('blk', 'sub')), may hold values from 0 to 1680
- sub_sends: int32 [32, 128], P(('blk', 'sub')), may hold values from 0 to 1535
- blk_sends: int32 [32, 16], P(('blk', 'sub')), may hold values from 0 to 1535
- group_sizes: int32 [32, 64], P(('blk', 'sub')), may hold values from 1 to 8, 256 in all within a row
- coarse_conductivity: float32 [2048], P(('blk', 'sub')), may hold values from 1 to 8
- coarse_stiffness: float32 [64, 64], replicated, may hold values from -0.0223 to 2.5, as said below
- restriction: float32 [8, 64, 64], replicated, may hold values from -0.5 to 0.5
Outputs:
- solution_field: float32 [64, 8192], P(None, ('blk', 'sub'))
- residual: float32 [64, 8192], P(None, ('blk', 'sub'))
Inputs may be any that keep to these rules, and one draw needn't show every extreme that they name: `group_sizes`: each row sums to 256, and some entry of each row is 8. `stiffness`: symmetric. `coarse_stiffness`: symmetric.
All inputs are finite; a program needn't handle non-finite values. No bound on the sum of `material` on one device may be relied on, other than what follows from the above.
Results may differ from a plain program's by a relative error of at most 0.0003.
Values sent between devices are 32-bit elements; how exact they have to be, the bound alone decides.
No kernel may reach another device: no remote copies, remote signals or barrier semaphores. Data moves between devices by JAX's collectives and lax.ppermute only.
A program may use at most 64 MiB of HBM per device.

v0:
```python
import jax
import jax.numpy as jnp
from jax import lax
from jax.sharding import PartitionSpec as P

HEAD = 8
KF = 3
KC = 4


HIGHEST = lax.Precision.HIGHEST
PENALTY = 0.3
COUPLING = 0.5
LOW_EIG = 0.4
HIGH_EIG = 2.5


def extended(x, sides, width):
    for axis, dim in sides:
        peers, length = (lax.axis_size(axis), x.shape[dim])
        up = [(i, (i + 1) % peers) for i in range(peers - 1)]
        down = [(j, i) for i, j in up]
        last = lax.slice_in_dim(x, length - width, length, axis=dim)
        leading = lax.slice_in_dim(x, 0, width, axis=dim)
        before = lax.ppermute(last, axis, up)
        after = lax.ppermute(leading, axis, down)
        x = jnp.concatenate([before, x, after], axis=dim)
    return x


def from_behind(x, axis, by):
    peers = lax.axis_size(axis)
    pairs = [(i, i + by) for i in range(peers) if 0 <= i + by < peers]
    return lax.ppermute(x, axis, pairs)


def matmul(left, right):
    return jnp.dot(left, right, precision=HIGHEST)


def chebyshev(operator, diagonal, residual, sweeps):
    center_eig = 0.5 * (HIGH_EIG + LOW_EIG)
    half_width = 0.5 * (HIGH_EIG - LOW_EIG)
    sigma_ratio = center_eig / half_width
    recur_now = 1.0 / sigma_ratio
    solution = jnp.zeros_like(residual)
    direction = residual / (diagonal * center_eig)
    for iteration in range(sweeps):
        solution = solution + direction
        residual = residual - operator(direction)
        recur_next = 1.0 / (2.0 * sigma_ratio - recur_now)
        direction = recur_next * recur_now * direction + 2.0 * recur_next / half_width * (
            residual / diagonal
        )
        recur_now = recur_next
    return (solution, residual)


def fine_apply(field, pieces):
    conductivity, material, stiffness, trace_map, face_neighbour, sub_sends, blk_sends = pieces
    count = field.shape[1]
    points = trace_map.shape[0] // 6
    peers = lax.axis_size("sub")
    slots = sub_sends.shape[1] // peers
    rims = blk_sends.shape[1] // 2
    traces = matmul(trace_map, field)
    own_table = traces.reshape(6, points, count).transpose(1, 0, 2).reshape(points, 6 * count)
    outgoing = (
        own_table[:, sub_sends[0]]
        .reshape(points, peers, slots)
        .transpose(1, 2, 0)
        .reshape(peers, slots * points)
    )
    incoming = lax.all_to_all(outgoing, "sub", split_axis=0, concat_axis=0, tiled=True)
    remote = (
        incoming.reshape(peers, slots, points).transpose(2, 0, 1).reshape(points, peers * slots)
    )
    outer = (
        own_table[:, blk_sends[0]]
        .reshape(points, 2, rims)
        .transpose(1, 2, 0)
        .reshape(2, rims * points)
    )
    padded = extended(outer, (("blk", 0),), 1)
    from_lower = padded[0].reshape(rims, points).T
    from_upper = padded[3].reshape(rims, points).T
    boundary = jnp.zeros((points, 1), field.dtype)
    columns = face_neighbour.reshape(-1)
    table = jnp.concatenate([own_table, remote, from_lower, from_upper, boundary], axis=1)
    seen = table[:, columns]
    seen = seen.reshape(points, 6, count).transpose(1, 0, 2).reshape(6 * points, count)
    face_term = matmul(trace_map.T, traces - seen)
    own_term = jnp.where(
        material[None, :] == 1, matmul(stiffness[1], field), matmul(stiffness[0], field)
    )
    return conductivity[None, :] * own_term + PENALTY * face_term


def fine_diagonal(conductivity, material, stiffness, trace_map):
    diagonals = jnp.diagonal(stiffness, axis1=1, axis2=2)
    chosen = jnp.where(material[None, :] == 1, diagonals[1][:, None], diagonals[0][:, None])
    return (
        conductivity[None, :] * chosen + PENALTY * jnp.sum(trace_map * trace_map, axis=0)[:, None]
    )


def parent_layout(sizes, count):
    ends = jnp.cumsum(sizes)
    starts = ends - sizes
    position = jnp.arange(count, dtype=jnp.int32)
    parent = jnp.sum((ends[None, :] <= position[:, None]).astype(jnp.int32), axis=1)
    member_mask = parent[:, None] == jnp.arange(sizes.shape[0], dtype=jnp.int32)[None, :]
    octant = position - jnp.sum(jnp.where(member_mask, starts[None, :], 0), axis=1)
    return (member_mask, octant)


def local(
    right_side,
    conductivity,
    material,
    stiffness,
    trace_map,
    face_neighbour,
    sub_sends,
    blk_sends,
    group_sizes,
    coarse_conductivity,
    coarse_stiffness,
    restriction,
):
    pieces = (conductivity, material, stiffness, trace_map, face_neighbour, sub_sends, blk_sends)

    def operator(field):
        return fine_apply(field, pieces)

    modes = right_side.shape[0]
    count = right_side.shape[1]
    diagonal = fine_diagonal(conductivity, material, stiffness, trace_map)
    pre_field, pre_residual = chebyshev(operator, diagonal, right_side, KF)
    member_mask, octant = parent_layout(group_sizes[0], count)
    member = member_mask.astype(jnp.float32)
    arriving = from_behind(pre_residual[:, :HEAD], ("blk", "sub"), -1)
    frame = jnp.concatenate([pre_residual[:, HEAD:], arriving], axis=1)
    selector = octant[None, None, :] == jnp.arange(8, dtype=jnp.int32)[:, None, None]
    stacked = matmul(restriction.reshape(8 * modes, modes), frame).reshape(8, modes, count)
    children = jnp.sum(jnp.where(selector, stacked, 0.0), axis=0)
    coarse_rhs = matmul(children, member)
    coarse_diag = (
        coarse_conductivity[None, :] * jnp.diagonal(coarse_stiffness)[:, None] + 2.0 * COUPLING
    )

    def coarse_operator(field):
        own_term = coarse_conductivity[None, :] * matmul(coarse_stiffness, field)
        padded = jnp.pad(field, ((0, 0), (1, 1)))
        laplace = 2.0 * field - padded[:, :-2] - padded[:, 2:]
        return own_term + COUPLING * laplace

    coarse_field, unused = chebyshev(coarse_operator, coarse_diag, coarse_rhs, KC)
    spread = matmul(coarse_field, member.T)
    lifted = matmul(
        jnp.transpose(restriction, (0, 2, 1)).reshape(8 * modes, modes), spread
    ).reshape(8, modes, count)
    fine_frame = jnp.sum(jnp.where(selector, lifted, 0.0), axis=0)
    returning = from_behind(fine_frame[:, count - HEAD :], ("blk", "sub"), 1)
    correction = jnp.concatenate([returning, fine_frame[:, : count - HEAD]], axis=1)
    mid_field = pre_field + correction
    mid_residual = right_side - operator(mid_field)
    post_field, residual = chebyshev(operator, diagonal, mid_residual, KF)
    return (mid_field + post_field, residual)


def solution(mesh):
    in_specs = (
        P(None, ("blk", "sub")),
        P(("blk", "sub")),
        P(("blk", "sub")),
        P(),
        P(),
        P(None, ("blk", "sub")),
        P(("blk", "sub"), None),
        P(("blk", "sub"), None),
        P(("blk", "sub"), None),
        P(("blk", "sub")),
        P(),
        P(),
    )
    out_specs = (P(None, ("blk", "sub")), P(None, ("blk", "sub")))
    return jax.shard_map(local, mesh=mesh, in_specs=in_specs, out_specs=out_specs, check_vma=False)
```

profile of v0, /device:TPU:0, one launch (start us, length us, event | category | flops | bytes accessed | tf_op | source)
XLA Modules:
  0.0 161.7 jit_solution(1017144814331230833)
XLA Ops:
  0.7 0.7 broadcast_compare_fusion
  2.8 0.9 multiply_reduce_fusion
  3.6 1.5 copy.104
  5.2 0.9 gather_fusion
  7.5 4.9 %collective-permute-start = (f32[1,128]{1,0:T(1,128)S(1)}, f32[1,128]{1,0:T(1,128)S(1)}, u32[]{:S(2)}, u32[]{:S(2)}) collective-permute-start(f32[1,128]{1,0:T(1,128)S(1)} %slice.143), channel_id=1, source_target_pairs={{0,8},{8,16},{16,24},{1,9},{9,17},{17,25},{2,10},{10,18},{18,26},{... | collective-permute-start | bytes 1544 | tf_op jit(solution)/shard_map/ppermute | solution.py:25
  12.6 1.3 collective-permute-start.1
  15.2 3.7 %all-to-all-start = ((f32[8,1,256]{2,1,0:T(1,128)}), f32[8,1,256]{2,1,0:T(1,128)S(1)}, u32[]{:S(2)}, u32[]{:S(2)}) async-start(f32[8,1,256]{2,1,0:T(1,128)} %all_to_all.42), calls=%async_computation | async-start | bytes 16384 | tf_op jit(solution)/shard_map/all_to_all | solution.py:74
  21.6 0.7 reduce.58
  22.4 1.3 all-to-all-done
  23.8 2.6 %gather_fusion.3 = f32[1536,16]{1,0:T(8,128)S(1)} fusion(f32[16,1681]{0,1:T(8,128)S(1)} %dynamic-update-slice.34, s32[2048]{0:T(1024)S(1)} %pad_clamp_fusion), kind=kCustom, calls=%fused_computation.3 | custom fusion | bytes 202752 | tf_op jit(solution)/shard_map/gather | solution.py:90
  29.1 4.5 %collective-permute-start.2 = (f32[1,128]{1,0:T(1,128)S(1)}, f32[1,128]{1,0:T(1,128)S(1)}, u32[]{:S(2)}, u32[]{:S(2)}) collective-permute-start(f32[1,128]{1,0:T(1,128)S(1)} %slice.147), channel_id=1, source_target_pairs={{0,8},{8,16},{16,24},{1,9},{9,17},{17,25},{2,10},{10,18},{18,26},{... | collective-permute-start | bytes 1544 | tf_op jit(solution)/shard_map/ppermute | solution.py:25
  33.6 1.3 collective-permute-start.3
  35.6 3.3 %all-to-all-start.1 = ((f32[8,1,256]{2,1,0:T(1,128)}), f32[8,1,256]{2,1,0:T(1,128)S(1)}, u32[]{:S(2)}, u32[]{:S(2)}) async-start(f32[8,1,256]{2,1,0:T(1,128)} %all_to_all.44), calls=%async_computation.1 | async-start | bytes 16384 | tf_op jit(solution)/shard_map/all_to_all | solution.py:74
  40.0 0.7 reduce.60
  40.8 2.8 %all-to-all-done.1 = f32[8,1,256]{2,1,0:T(1,128)S(1)} async-done(((f32[8,1,256]{2,1,0:T(1,128)}), f32[8,1,256]{2,1,0:T(1,128)S(1)}, u32[]{:S(2)}, u32[]{:S(2)}) %all-to-all-start.1) | async-done | bytes 8224 | tf_op jit(solution)/shard_map/all_to_all | solution.py:74
  43.8 2.6 %gather_fusion.6 = f32[1536,16]{1,0:T(8,128)S(1)} fusion(f32[16,1681]{0,1:T(8,128)S(1)} %dynamic-update-slice.29, s32[2048]{0:T(1024)S(1)} %pad_clamp_fusion), kind=kCustom, calls=%fused_computation.6 | custom fusion | bytes 202752 | tf_op jit(solution)/shard_map/gather | solution.py:90
  49.1 4.5 %collective-permute-start.4 = (f32[1,128]{1,0:T(1,128)S(1)}, f32[1,128]{1,0:T(1,128)S(1)}, u32[]{:S(2)}, u32[]{:S(2)}) collective-permute-start(f32[1,128]{1,0:T(1,128)S(1)} %slice.151), channel_id=1, source_target_pairs={{0,8},{8,16},{16,24},{1,9},{9,17},{17,25},{2,10},{10,18},{18,26},{... | collective-permute-start | bytes 1544 | tf_op jit(solution)/shard_map/ppermute | solution.py:25
  53.6 1.3 collective-permute-start.5
  55.6 3.3 %all-to-all-start.2 = ((f32[8,1,256]{2,1,0:T(1,128)}), f32[8,1,256]{2,1,0:T(1,128)S(1)}, u32[]{:S(2)}, u32[]{:S(2)}) async-start(f32[8,1,256]{2,1,0:T(1,128)} %all_to_all.46), calls=%async_computation.2 | async-start | bytes 16384 | tf_op jit(solution)/shard_map/all_to_all | solution.py:74
  60.0 0.7 reduce.62
  60.8 2.8 %all-to-all-done.2 = f32[8,1,256]{2,1,0:T(1,128)S(1)} async-done(((f32[8,1,256]{2,1,0:T(1,128)}), f32[8,1,256]{2,1,0:T(1,128)S(1)}, u32[]{:S(2)}, u32[]{:S(2)}) %all-to-all-start.2) | async-done | bytes 8224 | tf_op jit(solution)/shard_map/all_to_all | solution.py:74
  63.8 2.6 %gather_fusion.9 = f32[1536,16]{1,0:T(8,128)S(1)} fusion(f32[16,1681]{0,1:T(8,128)S(1)} %dynamic-update-slice.24, s32[2048]{0:T(1024)S(1)} %pad_clamp_fusion), kind=kCustom, calls=%fused_computation.9 | custom fusion | bytes 202752 | tf_op jit(solution)/shard_map/gather | solution.py:90
  66.9 1.3 collective-permute-start.6
  68.2 0.8 gather_fusion.10
  72.8 3.8 %collective-permute-start.7 = (f32[64,8]{1,0:T(8,128)S(1)}, f32[64,8]{1,0:T(8,128)S(1)}, u32[]{:S(2)}, u32[]{:S(2)}) collective-permute-start(f32[64,8]{1,0:T(8,128)S(1)} %slice.236), channel_id=1, source_target_pairs={{0,1},{1,2},{2,3},{3,4},{4,5},{5,6},{6,7},{7,8},{8,9},{9,10},{10,1... | collective-permute-start | bytes 6152 | tf_op jit(solution)/shard_map/ppermute | solution.py:34
  76.6 0.8 collective-permute-done.7
  79.8 7.3 %collective-permute-start.8 = (f32[1,128]{1,0:T(1,128)S(1)}, f32[1,128]{1,0:T(1,128)S(1)}, u32[]{:S(2)}, u32[]{:S(2)}) collective-permute-start(f32[1,128]{1,0:T(1,128)S(1)} %slice.165), channel_id=1, source_target_pairs={{0,8},{8,16},{16,24},{1,9},{9,17},{17,25},{2,10},{10,18},{18,26},{... | collective-permute-start | bytes 1544 | tf_op jit(solution)/shard_map/ppermute | solution.py:25
  87.1 1.3 collective-permute-start.9
  89.1 3.3 %all-to-all-start.3 = ((f32[8,1,256]{2,1,0:T(1,128)}), f32[8,1,256]{2,1,0:T(1,128)S(1)}, u32[]{:S(2)}, u32[]{:S(2)}) async-start(f32[8,1,256]{2,1,0:T(1,128)} %all_to_all.48), calls=%async_computation.3 | async-start | bytes 16384 | tf_op jit(solution)/shard_map/all_to_all | solution.py:74
  94.2 2.8 %all-to-all-done.3 = f32[8,1,256]{2,1,0:T(1,128)S(1)} async-done(((f32[8,1,256]{2,1,0:T(1,128)}), f32[8,1,256]{2,1,0:T(1,128)S(1)}, u32[]{:S(2)}, u32[]{:S(2)}) %all-to-all-start.3) | async-done | bytes 8224 | tf_op jit(solution)/shard_map/all_to_all | solution.py:74
  97.3 2.6 %gather_fusion.13 = f32[1536,16]{1,0:T(8,128)S(1)} fusion(f32[16,1681]{0,1:T(8,128)S(1)} %dynamic-update-slice.19, s32[2048]{0:T(1024)S(1)} %pad_clamp_fusion), kind=kCustom, calls=%fused_computation.13 | custom fusion | bytes 202752 | tf_op jit(solution)/shard_map/gather | solution.py:90
  102.7 4.5 %collective-permute-start.10 = (f32[1,128]{1,0:T(1,128)S(1)}, f32[1,128]{1,0:T(1,128)S(1)}, u32[]{:S(2)}, u32[]{:S(2)}) collective-permute-start(f32[1,128]{1,0:T(1,128)S(1)} %slice.169), channel_id=1, source_target_pairs={{0,8},{8,16},{16,24},{1,9},{9,17},{17,25},{2,10},{10,18},{18,26},{... | collective-permute-start | bytes 1544 | tf_op jit(solution)/shard_map/ppermute | solution.py:25
  107.2 1.3 collective-permute-start.11
  109.2 3.5 %all-to-all-start.4 = ((f32[8,1,256]{2,1,0:T(1,128)}), f32[8,1,256]{2,1,0:T(1,128)S(1)}, u32[]{:S(2)}, u32[]{:S(2)}) async-start(f32[8,1,256]{2,1,0:T(1,128)} %all_to_all.50), calls=%async_computation.4 | async-start | bytes 16384 | tf_op jit(solution)/shard_map/all_to_all | solution.py:74
  114.6 2.6 %all-to-all-done.4 = f32[8,1,256]{2,1,0:T(1,128)S(1)} async-done(((f32[8,1,256]{2,1,0:T(1,128)}), f32[8,1,256]{2,1,0:T(1,128)S(1)}, u32[]{:S(2)}, u32[]{:S(2)}) %all-to-all-start.4) | async-done | bytes 8224 | tf_op jit(solution)/shard_map/all_to_all | solution.py:74
  117.4 2.6 %gather_fusion.16 = f32[1536,16]{1,0:T(8,128)S(1)} fusion(f32[16,1681]{0,1:T(8,128)S(1)} %dynamic-update-slice.14, s32[2048]{0:T(1024)S(1)} %pad_clamp_fusion), kind=kCustom, calls=%fused_computation.16 | custom fusion | bytes 202752 | tf_op jit(solution)/shard_map/gather | solution.py:90
  122.7 4.5 %collective-permute-start.12 = (f32[1,128]{1,0:T(1,128)S(1)}, f32[1,128]{1,0:T(1,128)S(1)}, u32[]{:S(2)}, u32[]{:S(2)}) collective-permute-start(f32[1,128]{1,0:T(1,128)S(1)} %slice.173), channel_id=1, source_target_pairs={{0,8},{8,16},{16,24},{1,9},{9,17},{17,25},{2,10},{10,18},{18,26},{... | collective-permute-start | bytes 1544 | tf_op jit(solution)/shard_map/ppermute | solution.py:25
  127.2 1.3 collective-permute-start.13
  129.2 3.3 %all-to-all-start.5 = ((f32[8,1,256]{2,1,0:T(1,128)}), f32[8,1,256]{2,1,0:T(1,128)S(1)}, u32[]{:S(2)}, u32[]{:S(2)}) async-start(f32[8,1,256]{2,1,0:T(1,128)} %all_to_all.52), calls=%async_computation.5 | async-start | bytes 16384 | tf_op jit(solution)/shard_map/all_to_all | solution.py:74
  134.4 2.8 %all-to-all-done.5 = f32[8,1,256]{2,1,0:T(1,128)S(1)} async-done(((f32[8,1,256]{2,1,0:T(1,128)}), f32[8,1,256]{2,1,0:T(1,128)S(1)}, u32[]{:S(2)}, u32[]{:S(2)}) %all-to-all-start.5) | async-done | bytes 8224 | tf_op jit(solution)/shard_map/all_to_all | solution.py:74
  137.4 2.6 %gather_fusion.19 = f32[1536,16]{1,0:T(8,128)S(1)} fusion(f32[16,1681]{0,1:T(8,128)S(1)} %dynamic-update-slice.9, s32[2048]{0:T(1024)S(1)} %pad_clamp_fusion), kind=kCustom, calls=%fused_computation.19 | custom fusion | bytes 202752 | tf_op jit(solution)/shard_map/gather | solution.py:90
  140.2 0.9 add_add_fusion
  143.3 4.5 %collective-permute-start.14 = (f32[1,128]{1,0:T(1,128)S(1)}, f32[1,128]{1,0:T(1,128)S(1)}, u32[]{:S(2)}, u32[]{:S(2)}) collective-permute-start(f32[1,128]{1,0:T(1,128)S(1)} %slice.177), channel_id=1, source_target_pairs={{0,8},{8,16},{16,24},{1,9},{9,17},{17,25},{2,10},{10,18},{18,26},{... | collective-permute-start | bytes 1544 | tf_op jit(solution)/shard_map/ppermute | solution.py:25
  147.8 1.3 collective-permute-start.15
  149.8 3.3 %all-to-all-start.6 = ((f32[8,1,256]{2,1,0:T(1,128)}), f32[8,1,256]{2,1,0:T(1,128)S(1)}, u32[]{:S(2)}, u32[]{:S(2)}) async-start(f32[8,1,256]{2,1,0:T(1,128)} %all_to_all.54), calls=%async_computation.6 | async-start | bytes 16384 | tf_op jit(solution)/shard_map/all_to_all | solution.py:74
  155.0 2.8 %all-to-all-done.6 = f32[8,1,256]{2,1,0:T(1,128)S(1)} async-done(((f32[8,1,256]{2,1,0:T(1,128)}), f32[8,1,256]{2,1,0:T(1,128)S(1)}, u32[]{:S(2)}, u32[]{:S(2)}) %all-to-all-start.6) | async-done | bytes 8224 | tf_op jit(solution)/shard_map/all_to_all | solution.py:74
  158.0 2.6 %gather_fusion.22 = f32[1536,16]{1,0:T(8,128)S(1)} fusion(f32[16,1681]{0,1:T(8,128)S(1)} %dynamic-update-slice.4, s32[2048]{0:T(1024)S(1)} %pad_clamp_fusion), kind=kCustom, calls=%fused_computation.22 | custom fusion | bytes 202752 | tf_op jit(solution)/shard_map/gather | solution.py:90
  160.8 0.8 fusion.2
  (232 shorter events, 41.1 us)
Async XLA Ops:
  0.6 67.6 %copy-start = (f32[64,64]{1,0:T(8,128)S(1)}, f32[64,64]{1,0:T(8,128)}, u32[]{:S(2)}) copy-start(f32[64,64]{1,0:T(8,128)} %param.22) | copy-start | bytes 49156
  0.6 5.6 %copy-start.1 = (f32[96,64]{0,1:T(8,128)S(1)}, f32[96,64]{0,1:T(8,128)}, u32[]{:S(2)}) copy-start(f32[96,64]{0,1:T(8,128)} %param.16) | copy-start | bytes 73732
  0.7 18.7 %copy-start.2 = (f32[2,64,64]{2,1,0:T(8,128)S(1)}, f32[2,64,64]{2,1,0:T(8,128)}, u32[]{:S(2)}) copy-start(f32[2,64,64]{2,1,0:T(8,128)} %param.15) | copy-start | bytes 98308
  0.7 5.6 %copy-start.5 = (f32[256]{0:T(256)S(1)}, f32[256]{0:T(256)}, u32[]{:S(2)}) copy-start(f32[256]{0:T(256)} %param.13) | copy-start | bytes 3076
  0.7 5.6 %copy-start.4 = (f32[64,256]{1,0:T(8,128)S(1)}, f32[64,256]{1,0:T(8,128)}, u32[]{:S(2)}) copy-start(f32[64,256]{1,0:T(8,128)} %param.12) | copy-start | bytes 196612
  0.7 18.2 %copy-start.7 = (s32[1,64]{1,0:T(1,128)S(1)}, s32[1,64]{1,0:T(1,128)}, u32[]{:S(2)}) copy-start(s32[1,64]{1,0:T(1,128)} %param.20) | copy-start | bytes 772
  5.2 14.5 %copy-start.6 = (s32[6,256]{1,0:T(8,128)S(1)}, s32[6,256]{1,0:T(8,128)}, u32[]{:S(2)}) copy-start(s32[6,256]{1,0:T(8,128)} %param.17) | copy-start | bytes 18436
  7.5 12.6 %collective-permute-start = (f32[1,128]{1,0:T(1,128)S(1)}, f32[1,128]{1,0:T(1,128)S(1)}, u32[]{:S(2)}, u32[]{:S(2)}) collective-permute-start(f32[1,128]{1,0:T(1,128)S(1)} %slice.143), channel_id=1, source_target_pairs={{0,8},{8,16},{16,24},{1,9},{9,17},{17,25},{2,10},{10,18},{18,26},{... | collective-permute-start | bytes 1544 | tf_op jit(solution)/shard_map/ppermute | solution.py:25
  12.6 9.0 %collective-permute-start.1 = (f32[1,128]{1,0:T(1,128)S(1)}, f32[1,128]{1,0:T(1,128)S(1)}, u32[]{:S(2)}, u32[]{:S(2)}) collective-permute-start(f32[1,128]{1,0:T(1,128)S(1)} %slice.145), channel_id=1, source_target_pairs={{8,0},{16,8},{24,16},{9,1},{17,9},{25,17},{10,2},{18,10},{26,18},{... | collective-permute-start | bytes 1544 | tf_op jit(solution)/shard_map/ppermute | solution.py:26
  15.2 8.4 %all-to-all-start = ((f32[8,1,256]{2,1,0:T(1,128)}), f32[8,1,256]{2,1,0:T(1,128)S(1)}, u32[]{:S(2)}, u32[]{:S(2)}) async-start(f32[8,1,256]{2,1,0:T(1,128)} %all_to_all.42), calls=%async_computation | async-start | bytes 16384 | tf_op jit(solution)/shard_map/all_to_all | solution.py:74
  29.1 10.1 %collective-permute-start.2 = (f32[1,128]{1,0:T(1,128)S(1)}, f32[1,128]{1,0:T(1,128)S(1)}, u32[]{:S(2)}, u32[]{:S(2)}) collective-permute-start(f32[1,128]{1,0:T(1,128)S(1)} %slice.147), channel_id=1, source_target_pairs={{0,8},{8,16},{16,24},{1,9},{9,17},{17,25},{2,10},{10,18},{18,26},{... | collective-permute-start | bytes 1544 | tf_op jit(solution)/shard_map/ppermute | solution.py:25
  33.6 6.3 %collective-permute-start.3 = (f32[1,128]{1,0:T(1,128)S(1)}, f32[1,128]{1,0:T(1,128)S(1)}, u32[]{:S(2)}, u32[]{:S(2)}) collective-permute-start(f32[1,128]{1,0:T(1,128)S(1)} %slice.149), channel_id=1, source_target_pairs={{8,0},{16,8},{24,16},{9,1},{17,9},{25,17},{10,2},{18,10},{26,18},{... | collective-permute-start | bytes 1544 | tf_op jit(solution)/shard_map/ppermute | solution.py:26
  35.6 8.0 %all-to-all-start.1 = ((f32[8,1,256]{2,1,0:T(1,128)}), f32[8,1,256]{2,1,0:T(1,128)S(1)}, u32[]{:S(2)}, u32[]{:S(2)}) async-start(f32[8,1,256]{2,1,0:T(1,128)} %all_to_all.44), calls=%async_computation.1 | async-start | bytes 16384 | tf_op jit(solution)/shard_map/all_to_all | solution.py:74
  48.9 20.1 %copy-start.3 = (f32[8,64,64]{2,1,0:T(8,128)S(1)}, f32[8,64,64]{2,1,0:T(8,128)}, u32[]{:S(2)}) copy-start(f32[8,64,64]{2,1,0:T(8,128)} %param.23) | copy-start | bytes 393220
  49.1 10.1 %collective-permute-start.4 = (f32[1,128]{1,0:T(1,128)S(1)}, f32[1,128]{1,0:T(1,128)S(1)}, u32[]{:S(2)}, u32[]{:S(2)}) collective-permute-start(f32[1,128]{1,0:T(1,128)S(1)} %slice.151), channel_id=1, source_target_pairs={{0,8},{8,16},{16,24},{1,9},{9,17},{17,25},{2,10},{10,18},{18,26},{... | collective-permute-start | bytes 1544 | tf_op jit(solution)/shard_map/ppermute | solution.py:25
  53.6 6.3 %collective-permute-start.5 = (f32[1,128]{1,0:T(1,128)S(1)}, f32[1,128]{1,0:T(1,128)S(1)}, u32[]{:S(2)}, u32[]{:S(2)}) collective-permute-start(f32[1,128]{1,0:T(1,128)S(1)} %slice.153), channel_id=1, source_target_pairs={{8,0},{16,8},{24,16},{9,1},{17,9},{25,17},{10,2},{18,10},{26,18},{... | collective-permute-start | bytes 1544 | tf_op jit(solution)/shard_map/ppermute | solution.py:26
  55.6 8.0 %all-to-all-start.2 = ((f32[8,1,256]{2,1,0:T(1,128)}), f32[8,1,256]{2,1,0:T(1,128)S(1)}, u32[]{:S(2)}, u32[]{:S(2)}) async-start(f32[8,1,256]{2,1,0:T(1,128)} %all_to_all.46), calls=%async_computation.2 | async-start | bytes 16384 | tf_op jit(solution)/shard_map/all_to_all | solution.py:74
  66.9 4.1 %copy-start.8 = (f32[64]{0:T(128)S(1)}, f32[64]{0:T(128)}, u32[]{:S(2)}) copy-start(f32[64]{0:T(128)} %param.21) | copy-start | bytes 772
  66.9 3.1 %collective-permute-start.6 = (f32[64,8]{1,0:T(8,128)S(1)}, f32[64,8]{1,0:T(8,128)S(1)}, u32[]{:S(2)}, u32[]{:S(2)}) collective-permute-start(f32[64,8]{1,0:T(8,128)S(1)} %slice.235), channel_id=1, source_target_pairs={{1,0},{2,1},{3,2},{4,3},{5,4},{6,5},{7,6},{8,7},{9,8},{10,9},{11,1... | collective-permute-start | bytes 6152 | tf_op jit(solution)/shard_map/ppermute | solution.py:34
  72.8 4.7 %collective-permute-start.7 = (f32[64,8]{1,0:T(8,128)S(1)}, f32[64,8]{1,0:T(8,128)S(1)}, u32[]{:S(2)}, u32[]{:S(2)}) collective-permute-start(f32[64,8]{1,0:T(8,128)S(1)} %slice.236), channel_id=1, source_target_pairs={{0,1},{1,2},{2,3},{3,4},{4,5},{5,6},{6,7},{7,8},{8,9},{9,10},{10,1... | collective-permute-start | bytes 6152 | tf_op jit(solution)/shard_map/ppermute | solution.py:34
  79.8 12.9 %collective-permute-start.8 = (f32[1,128]{1,0:T(1,128)S(1)}, f32[1,128]{1,0:T(1,128)S(1)}, u32[]{:S(2)}, u32[]{:S(2)}) collective-permute-start(f32[1,128]{1,0:T(1,128)S(1)} %slice.165), channel_id=1, source_target_pairs={{0,8},{8,16},{16,24},{1,9},{9,17},{17,25},{2,10},{10,18},{18,26},{... | collective-permute-start | bytes 1544 | tf_op jit(solution)/shard_map/ppermute | solution.py:25
  87.1 6.3 %collective-permute-start.9 = (f32[1,128]{1,0:T(1,128)S(1)}, f32[1,128]{1,0:T(1,128)S(1)}, u32[]{:S(2)}, u32[]{:S(2)}) collective-permute-start(f32[1,128]{1,0:T(1,128)S(1)} %slice.167), channel_id=1, source_target_pairs={{8,0},{16,8},{24,16},{9,1},{17,9},{25,17},{10,2},{18,10},{26,18},{... | collective-permute-start | bytes 1544 | tf_op jit(solution)/shard_map/ppermute | solution.py:26
  89.1 8.0 %all-to-all-start.3 = ((f32[8,1,256]{2,1,0:T(1,128)}), f32[8,1,256]{2,1,0:T(1,128)S(1)}, u32[]{:S(2)}, u32[]{:S(2)}) async-start(f32[8,1,256]{2,1,0:T(1,128)} %all_to_all.48), calls=%async_computation.3 | async-start | bytes 16384 | tf_op jit(solution)/shard_map/all_to_all | solution.py:74
  102.7 10.4 %collective-permute-start.10 = (f32[1,128]{1,0:T(1,128)S(1)}, f32[1,128]{1,0:T(1,128)S(1)}, u32[]{:S(2)}, u32[]{:S(2)}) collective-permute-start(f32[1,128]{1,0:T(1,128)S(1)} %slice.169), channel_id=1, source_target_pairs={{0,8},{8,16},{16,24},{1,9},{9,17},{17,25},{2,10},{10,18},{18,26},{... | collective-permute-start | bytes 1544 | tf_op jit(solution)/shard_map/ppermute | solution.py:25
  107.2 6.6 %collective-permute-start.11 = (f32[1,128]{1,0:T(1,128)S(1)}, f32[1,128]{1,0:T(1,128)S(1)}, u32[]{:S(2)}, u32[]{:S(2)}) collective-permute-start(f32[1,128]{1,0:T(1,128)S(1)} %slice.171), channel_id=1, source_target_pairs={{8,0},{16,8},{24,16},{9,1},{17,9},{25,17},{10,2},{18,10},{26,18},{... | collective-permute-start | bytes 1544 | tf_op jit(solution)/shard_map/ppermute | solution.py:26
  109.2 8.0 %all-to-all-start.4 = ((f32[8,1,256]{2,1,0:T(1,128)}), f32[8,1,256]{2,1,0:T(1,128)S(1)}, u32[]{:S(2)}, u32[]{:S(2)}) async-start(f32[8,1,256]{2,1,0:T(1,128)} %all_to_all.50), calls=%async_computation.4 | async-start | bytes 16384 | tf_op jit(solution)/shard_map/all_to_all | solution.py:74
  122.7 10.1 %collective-permute-start.12 = (f32[1,128]{1,0:T(1,128)S(1)}, f32[1,128]{1,0:T(1,128)S(1)}, u32[]{:S(2)}, u32[]{:S(2)}) collective-permute-start(f32[1,128]{1,0:T(1,128)S(1)} %slice.173), channel_id=1, source_target_pairs={{0,8},{8,16},{16,24},{1,9},{9,17},{17,25},{2,10},{10,18},{18,26},{... | collective-permute-start | bytes 1544 | tf_op jit(solution)/shard_map/ppermute | solution.py:25
  127.2 6.3 %collective-permute-start.13 = (f32[1,128]{1,0:T(1,128)S(1)}, f32[1,128]{1,0:T(1,128)S(1)}, u32[]{:S(2)}, u32[]{:S(2)}) collective-permute-start(f32[1,128]{1,0:T(1,128)S(1)} %slice.175), channel_id=1, source_target_pairs={{8,0},{16,8},{24,16},{9,1},{17,9},{25,17},{10,2},{18,10},{26,18},{... | collective-permute-start | bytes 1544 | tf_op jit(solution)/shard_map/ppermute | solution.py:26
  129.2 8.0 %all-to-all-start.5 = ((f32[8,1,256]{2,1,0:T(1,128)}), f32[8,1,256]{2,1,0:T(1,128)S(1)}, u32[]{:S(2)}, u32[]{:S(2)}) async-start(f32[8,1,256]{2,1,0:T(1,128)} %all_to_all.52), calls=%async_computation.5 | async-start | bytes 16384 | tf_op jit(solution)/shard_map/all_to_all | solution.py:74
  143.3 10.1 %collective-permute-start.14 = (f32[1,128]{1,0:T(1,128)S(1)}, f32[1,128]{1,0:T(1,128)S(1)}, u32[]{:S(2)}, u32[]{:S(2)}) collective-permute-start(f32[1,128]{1,0:T(1,128)S(1)} %slice.177), channel_id=1, source_target_pairs={{0,8},{8,16},{16,24},{1,9},{9,17},{17,25},{2,10},{10,18},{18,26},{... | collective-permute-start | bytes 1544 | tf_op jit(solution)/shard_map/ppermute | solution.py:25
  147.8 6.3 %collective-permute-start.15 = (f32[1,128]{1,0:T(1,128)S(1)}, f32[1,128]{1,0:T(1,128)S(1)}, u32[]{:S(2)}, u32[]{:S(2)}) collective-permute-start(f32[1,128]{1,0:T(1,128)S(1)} %slice.179), channel_id=1, source_target_pairs={{8,0},{16,8},{24,16},{9,1},{17,9},{25,17},{10,2},{18,10},{26,18},{... | collective-permute-start | bytes 1544 | tf_op jit(solution)/shard_map/ppermute | solution.py:26
  149.8 8.0 %all-to-all-start.6 = ((f32[8,1,256]{2,1,0:T(1,128)}), f32[8,1,256]{2,1,0:T(1,128)S(1)}, u32[]{:S(2)}, u32[]{:S(2)}) async-start(f32[8,1,256]{2,1,0:T(1,128)} %all_to_all.54), calls=%async_computation.6 | async-start | bytes 16384 | tf_op jit(solution)/shard_map/all_to_all | solution.py:74
where the time goes:
time: 163 us; the launch traced here: 162 us
  starting transfers between devices  73 us (45%)
  local copies, waits for them, and re-layouts  43.4 us (27%)
  waiting for transfers between devices  19.5 us (12%)
  other arithmetic  13.8 us (8%)
  matrix products  10.1 us (6%)
  between operations  1.94 us (1%)
    ppermute x7, starting transfers between devices, extended(): before = lax.ppermute(last, axis, up)  34.9 us
    all_to_all x7, starting transfers between devices, fine_apply(): lax.all_to_all(outgoing, 'sub', split_axis=0, concat_axis=0, tiled=True)  23.9 us
    gather x7, local copies, waits for them, and re-layouts, fine_apply(): seen = table[:, columns]  18.2 us
    all_to_all x7, waiting for transfers between devices, fine_apply(): lax.all_to_all(outgoing, 'sub', split_axis=0, concat_axis=0, tiled=True)  18 us
    dot_general x35, matrix products, matmul(): return jnp.dot(left, right, precision=HIGHEST)  10.1 us
    ppermute x7, starting transfers between devices, extended(): after = lax.ppermute(leading, axis, down)  9.04 us
    ppermute x2, starting transfers between devices, from_behind(): return lax.ppermute(x, axis, pairs)  5.12 us
    ppermute x7, other arithmetic, extended(): after = lax.ppermute(leading, axis, down)  4.99 us
  transfers between devices with their start and end apart: 23, of which 9 were waited for; matrix products, arithmetic and copies ran while one was open for 10% of the time, Pallas kernels for 0%

commit v1 on v0

v1 whole, which is shorter than its diff:
```python
import functools

import jax
import jax.numpy as jnp
from jax import lax
from jax.experimental import pallas as pl
from jax.experimental.pallas import tpu as pltpu
from jax.sharding import PartitionSpec as P

HEAD = 8
KF = 3
KC = 4
FACES = 6
LANES = 128
VMEM = 4 << 20

HIGHEST = lax.Precision.HIGHEST
PENALTY = 0.3
COUPLING = 0.5
LOW_EIG = 0.4
HIGH_EIG = 2.5
CENTER = 0.5 * (HIGH_EIG + LOW_EIG)
HALF = 0.5 * (HIGH_EIG - LOW_EIG)


def steps(sweeps):
    sigma = CENTER / HALF
    rho, pairs = 1.0 / sigma, []
    for _ in range(sweeps):
        rho_next = 1.0 / (2.0 * sigma - rho)
        pairs.append((rho_next * rho, 2.0 * rho_next / HALF))
        rho = rho_next
    return pairs


def dot(left, right):
    return jnp.dot(left, right, precision=HIGHEST, preferred_element_type=jnp.float32)


def dot_t(left, right):
    return lax.dot_general(
        left, right, (((0,), (0,)), ((), ())), precision=HIGHEST, preferred_element_type=jnp.float32
    )


def take(tile, lane):
    index = jnp.broadcast_to(lane, tile.shape)
    return jnp.take_along_axis(tile, index, axis=1, mode="promise_in_bounds")


def pick(tiles, columns):
    lane = jnp.bitwise_and(columns, LANES - 1)
    at = jnp.right_shift(columns, 7)
    out = jnp.zeros(tiles[0].shape, tiles[0].dtype)
    for number, tile in enumerate(tiles):
        out = jnp.where(at == number, take(tile, lane), out)
    return out


def lanes(rows=1):
    return lax.broadcasted_iota(jnp.int32, (rows, LANES), 1)


def trace_tiles(traces):
    points = traces.shape[0] // FACES
    return [
        traces[f * points : (f + 1) * points, h : h + LANES]
        for f in range(FACES)
        for h in range(0, traces.shape[1], LANES)
    ]


def send(traces, sub_ref, blk_ref, sub_out, blk_out):
    tiles = trace_tiles(traces)
    for h in range(0, sub_ref.shape[1], LANES):
        sub_out[:, h : h + LANES] = pick(tiles, sub_ref[:, h : h + LANES])
    blk_out[...] = pick(tiles, blk_ref[...])


def start_kernel(
    b_ref, cond_ref, mat_ref, stiff_ref, map_ref, sub_ref, blk_ref, p_out, ig_out, tr_out, sub_out, blk_out
):
    modes = map_ref.shape[1]
    eye = lax.broadcasted_iota(jnp.int32, (modes, modes), 0) == lax.broadcasted_iota(
        jnp.int32, (modes, modes), 1
    )
    diagonals = [
        jnp.sum(jnp.where(eye, stiff_ref[k], 0.0), axis=1, keepdims=True) for k in range(2)
    ]
    squares = jnp.sum(map_ref[...] * map_ref[...], axis=0, keepdims=True)
    squares = jnp.sum(jnp.where(eye, squares, 0.0), axis=1, keepdims=True)
    chosen = jnp.where(mat_ref[...] == 1, diagonals[1], diagonals[0])
    inverse = 1.0 / (cond_ref[...] * chosen + PENALTY * squares)
    ig_out[...] = inverse
    p = b_ref[...] * inverse * (1.0 / CENTER)
    p_out[...] = p
    traces = dot(map_ref[...], p)
    tr_out[...] = traces
    send(traces, sub_ref, blk_ref, sub_out, blk_out)


def local_kernel(p_ref, tr_ref, x_ref, cond_ref, mat_ref, stiff_ref, map_ref, face_ref, base_out, x_out, seen):
    traces = tr_ref[...]
    tiles = trace_tiles(traces)
    points = tiles[0].shape[0]
    for f in range(FACES):
        for h in range(0, traces.shape[1], LANES):
            seen[f * points : (f + 1) * points, h : h + LANES] = pick(
                tiles, face_ref[f : f + 1, h : h + LANES]
            )
    p = p_ref[...]
    face = dot_t(map_ref[...], traces - seen[...])
    own = jnp.where(mat_ref[...] == 1, dot(stiff_ref[1], p), dot(stiff_ref[0], p))
    base_out[...] = cond_ref[...] * own + PENALTY * face
    x_out[...] = p if x_ref is None else x_ref[...] + p


def remote_residual(r_ref, base_ref, map_ref, face_ref, remote, seen):
    own = FACES * r_ref.shape[1] // LANES
    points = remote[0].shape[0]
    for f in range(FACES):
        for h in range(0, r_ref.shape[1], LANES):
            columns = face_ref[f : f + 1, h : h + LANES] - own * LANES
            seen[f * points : (f + 1) * points, h : h + LANES] = pick(remote, columns)
    return r_ref[...] - base_ref[...] + PENALTY * dot_t(map_ref[...], seen[...])


def remote_tiles(sub_refs, low_ref, high_ref, chips):
    lane = lanes()
    if chips:
        me = lax.axis_index("sub")
        slot = me * 16 + jnp.bitwise_and(lane, 15)
        owner = jnp.right_shift(lane, 4)
        tile = jnp.zeros(low_ref.shape, jnp.float32)
        for k, ref in sub_refs:
            tile = jnp.where(owner == jnp.bitwise_xor(me, k), take(ref(), slot), tile)
        tiles = [tile]
    else:
        tiles = [sub_refs[:, h : h + LANES] for h in range(0, sub_refs.shape[1], LANES)]
    other = jnp.bitwise_xor(lane, 8)
    rim = jnp.where(lane < 8, take(low_ref[...], other), take(high_ref[...], other))
    tiles.append(jnp.where(lane < 16, rim, 0.0))
    return tiles


def finish_kernel(kind, coefficients, chips, *refs):
    refs = list(refs)
    seen = refs.pop()
    r_ref, base_ref, map_ref, face_ref, low_ref, high_ref = refs[:6]
    refs = refs[6:]
    if chips:
        own_ref, two, four, six, swapped = refs[:5]
        refs = refs[5:]
        subs = [(0, lambda: own_ref[...]), (2, lambda: two[...]), (4, lambda: four[...]), (6, lambda: six[...])]
        height = own_ref.shape[0]
        for at, k in enumerate((1, 3, 5, 7)):
            subs.append((k, functools.partial(lambda a: swapped[a * height : (a + 1) * height, :], at)))
    else:
        subs = refs[0]
        refs = refs[1:]
    remote = remote_tiles(subs, low_ref, high_ref, chips)
    residual = remote_residual(r_ref, base_ref, map_ref, face_ref, remote, seen)
    if kind == "last":
        refs[0][...] = residual
        return
    if kind == "frame":
        r_out, head_out = refs
        r_out[...] = residual
        head_out[...] = residual[:, :LANES]
        return
    if kind == "step":
        p_ref = refs.pop(0)
    ig_ref, sub_ref, blk_ref, r_out, p_out, tr_out, sub_out, blk_out = refs
    r_out[...] = residual
    p = coefficients[1] * (residual * ig_ref[...])
    if kind == "step":
        p = p + coefficients[0] * p_ref[...]
    p_out[...] = p
    traces = dot(map_ref[...], p)
    tr_out[...] = traces
    send(traces, sub_ref, blk_ref, sub_out, blk_out)


def layout_kernel(sizes_ref, gather_out, place_out):
    parents = sizes_ref.shape[1]
    row = lax.broadcasted_iota(jnp.int32, (parents, parents), 0)
    col = lax.broadcasted_iota(jnp.int32, (parents, parents), 1)
    sizes = jnp.broadcast_to(sizes_ref[...], (parents, parents))
    size = jnp.sum(jnp.where(row == col, sizes, 0), axis=1, keepdims=True)
    end = jnp.sum(jnp.where(col <= row, sizes, 0), axis=1, keepdims=True)
    lane = lanes(parents)
    parent = jnp.bitwise_and(lane, parents - 1)
    group = lax.broadcasted_iota(jnp.int32, (parents, LANES), 0)
    size_row = jnp.sum(jnp.where(group == parent, size, 0), axis=0, keepdims=True)
    start_row = jnp.sum(jnp.where(group < parent, size, 0), axis=0, keepdims=True)
    half = jnp.right_shift(lanes(), parents.bit_length() - 1)
    for j in range(4):
        octant = 2 * j + half
        gather_out[j : j + 1, :] = jnp.where(octant < size_row, start_row + octant + HEAD, -1)
    for j in range(3):
        position = lane + (j * LANES - HEAD)
        before = end <= position
        place_out[2 * j : 2 * j + 1, :] = jnp.sum(before.astype(jnp.int32), axis=0, keepdims=True)
        place_out[2 * j + 1 : 2 * j + 2, :] = (
            lanes() + (j * LANES - HEAD) - jnp.sum(jnp.where(before, size, 0), axis=0, keepdims=True)
        )


def coarse_kernel(
    r_ref, arriving_ref, gather_ref, place_ref, cond_ref, stiff_ref, down_ref, up_ref, field_out, tail_out, cond
):
    modes = r_ref.shape[0]
    parents = cond_ref.shape[1]
    sources = [r_ref[:, h : h + LANES] for h in range(0, r_ref.shape[1], LANES)] + [arriving_ref[...]]
    first = second = None
    for j in range(4):
        children = pick(sources, gather_ref[j : j + 1, :])
        both = dot(down_ref[2 * j * modes : (2 * j + 2) * modes, :], children)
        one, two = both[:modes], both[modes:]
        first = one if first is None else first + one
        second = two if second is None else second + two
    lane = lanes()
    right = jnp.where(lane < parents, first + pltpu.roll(second, parents, 1), 0.0)
    cond[...] = jnp.ones(cond.shape, jnp.float32)
    cond[:, :parents] = cond_ref[...]
    scale = cond[...]
    eye = lax.broadcasted_iota(jnp.int32, (modes, modes), 0) == lax.broadcasted_iota(
        jnp.int32, (modes, modes), 1
    )
    diagonal = jnp.sum(jnp.where(eye, stiff_ref[...], 0.0), axis=1, keepdims=True)
    inverse = 1.0 / (scale * diagonal + 2.0 * COUPLING)
    p = right * inverse * (1.0 / CENTER)
    field, residual = p, right
    for before, correct in steps(KC - 1):
        left = jnp.where(lane == 0, 0.0, pltpu.roll(p, 1, 1))
        after = jnp.where(lane == parents - 1, 0.0, pltpu.roll(p, LANES - 1, 1))
        residual = residual - (
            scale * dot(stiff_ref[...], p) + COUPLING * (2.0 * p - left - after)
        )
        p = before * p + correct * (residual * inverse)
        field = field + p
    lifted = dot(up_ref[...], field)
    for j in range(3):
        parent, octant = place_ref[2 * j : 2 * j + 1, :], place_ref[2 * j + 1 : 2 * j + 2, :]
        inside = jnp.logical_and(lane + (j * LANES - HEAD) >= 0, lane + (j * LANES - HEAD) < 2 * LANES)
        parent = jnp.where(inside, parent, 0)
        out = jnp.zeros((modes, LANES), jnp.float32)
        for o in range(8):
            out = jnp.where(octant == o, take(lifted[o * modes : (o + 1) * modes], parent), out)
        out = jnp.where(inside, out, 0.0)
        if j < 2:
            field_out[:, j * LANES : (j + 1) * LANES] = out
        else:
            tail_out[...] = out


def middle_kernel(field_ref, arriving_ref, map_ref, sub_ref, blk_ref, p_out, tr_out, sub_out, blk_out):
    p_out[...] = field_ref[...]
    p_out[:, :LANES] = field_ref[:, :LANES] + jnp.where(lanes() < HEAD, arriving_ref[...], 0.0)
    traces = dot(map_ref[...], p_out[...])
    tr_out[...] = traces
    send(traces, sub_ref, blk_ref, sub_out, blk_out)


def call(kernel, outs, *args, scratch=()):
    return pl.pallas_call(
        kernel,
        out_shape=[jax.ShapeDtypeStruct(shape, kind) for shape, kind in outs],
        in_specs=[pl.BlockSpec(memory_space=pltpu.VMEM)] * len(args),
        out_specs=[pl.BlockSpec(memory_space=pltpu.VMEM)] * len(outs),
        scratch_shapes=list(scratch),
        compiler_params=pltpu.CompilerParams(vmem_limit_bytes=VMEM),
    )(*args)


def from_behind(x, axis, by):
    peers = lax.axis_size(axis)
    pairs = [(i, i + by) for i in range(peers) if 0 <= i + by < peers]
    return lax.ppermute(x, axis, pairs)


def local(
    right_side,
    conductivity,
    material,
    stiffness,
    trace_map,
    face_neighbour,
    sub_sends,
    blk_sends,
    group_sizes,
    coarse_conductivity,
    coarse_stiffness,
    restriction,
):
    f32, i32 = jnp.float32, jnp.int32
    modes, count = right_side.shape
    rows = trace_map.shape[0]
    points = rows // FACES
    peers, segments = lax.axis_size("sub"), lax.axis_size("blk")
    chips = peers == 8
    cond = conductivity.reshape(1, count)
    mat = material.reshape(1, count)
    blk_row = jnp.pad(blk_sends, ((0, 0), (0, LANES - blk_sends.shape[1])))
    block = ((modes, count), f32)
    sends = [((rows, count), f32), ((points, sub_sends.shape[1]), f32), ((points, LANES), f32)]
    seen = pltpu.VMEM((rows, count), f32)

    def exchange(sub_out, blk_out):
        ring = [(i, (i + 1) % segments) for i in range(segments)]
        low = lax.ppermute(blk_out, "blk", [(i, j) for i, j in ring if j > 0])
        high = lax.ppermute(blk_out, "blk", [(j, i) for i, j in ring if j > 0])
        if not chips:
            return [low, high, lax.all_to_all(sub_out, "sub", 1, 1, tiled=True)]
        far = [
            lax.ppermute(sub_out, "sub", [(i, i ^ k) for i in range(peers)]) for k in (2, 4, 6)
        ]
        held = jnp.concatenate([sub_out, *far], axis=0)
        swapped = lax.ppermute(held, "sub", [(i, i ^ 1) for i in range(peers)])
        return [low, high, sub_out, *far, swapped]

    def part(p, traces, x):
        args = [p, traces] + ([] if x is None else [x])
        args += [cond, mat, stiffness, trace_map, face_neighbour]
        kernel = local_kernel
        if x is None:
            def kernel(p_ref, tr_ref, *refs):
                return local_kernel(p_ref, tr_ref, None, *refs)
        return call(kernel, [block, block], *args, scratch=[seen])

    def finish(kind, coefficients, r, base, got, p=None):
        args = [r, base, trace_map, face_neighbour, *got]
        if kind == "last":
            outs = [block]
        elif kind == "frame":
            outs = [block, ((modes, LANES), f32)]
        else:
            args += ([p] if kind == "step" else []) + [inverse, sub_sends, blk_row]
            outs = [block, block, *sends]
        kernel = functools.partial(finish_kernel, kind, coefficients, chips)
        return call(kernel, outs, *args, scratch=[seen])

    gather, place = call(layout_kernel, [((4, LANES), i32), ((6, LANES), i32)], group_sizes)
    p, inverse, traces, *out = call(
        start_kernel,
        [block, block, *sends],
        right_side, cond, mat, stiffness, trace_map, sub_sends, blk_row,
    )
    r, x = right_side, None
    pairs = steps(KF)
    for step in range(KF):
        got = exchange(*out)
        base, x = part(p, traces, x)
        if step < KF - 1:
            r, p, traces, *out = finish("step", pairs[step], r, base, got, p)
    r, head = finish("frame", None, r, base, got)

    arriving = from_behind(head, ("blk", "sub"), -1)
    down = restriction.reshape(8 * modes, modes)
    up = jnp.transpose(restriction, (0, 2, 1)).reshape(8 * modes, modes)
    field, tail = call(
        coarse_kernel,
        [block, ((modes, LANES), f32)],
        r, arriving, gather, place, coarse_conductivity.reshape(1, -1), coarse_stiffness, down, up,
        scratch=[pltpu.VMEM((1, LANES), f32)],
    )
    returning = from_behind(tail, ("blk", "sub"), 1)
    p, traces, *out = call(
        middle_kernel, [block, *sends], field, returning, trace_map, sub_sends, blk_row
    )

    got = exchange(*out)
    base, x = part(p, traces, x)
    r, p, traces, *out = finish("first", (0.0, 1.0 / CENTER), r, base, got)
    for step in range(KF):
        got = exchange(*out)
        base, x = part(p, traces, x)
        if step < KF - 1:
            r, p, traces, *out = finish("step", pairs[step], r, base, got, p)
    (residual,) = finish("last", None, r, base, got)
    return x, residual


def solution(mesh):
    in_specs = (
        P(None, ("blk", "sub")),
        P(("blk", "sub")),
        P(("blk", "sub")),
        P(),
        P(),
        P(None, ("blk", "sub")),
        P(("blk", "sub"), None),
        P(("blk", "sub"), None),
        P(("blk", "sub"), None),
        P(("blk", "sub")),
        P(),
        P(),
    )
    out_specs = (P(None, ("blk", "sub")), P(None, ("blk", "sub")))
    return jax.shard_map(local, mesh=mesh, in_specs=in_specs, out_specs=out_specs, check_vma=False)
```

time: 163 us -> 131 us (0.80)
  local copies, waits for them, and re-layouts: 43.4 us -> 3.2 us
  waiting for transfers between devices: 19.5 us -> 49.1 us
  Pallas kernels: 0 us -> 15.8 us
  other arithmetic: 13.8 us -> 0.02 us
  starting transfers between devices: 73 us -> 61.3 us
  matrix products: 10.1 us -> 0 us
    ppermute x14 -> x42, waiting for transfers between devices: 0.04 us -> 46.8 us  [the longest x21 23.7 us: exchange(): lax.ppermute(sub_out, 'sub', [(i, i ^ k) for i in range(peers)])]
    gather x23 -> x0, local copies, waits for them, and re-layouts: 28.3 us -> none  [the longest x7 18.2 us: fine_apply(): seen = table[:, columns]]
    all_to_all x7 -> x0, starting transfers between devices: 23.9 us -> none  [fine_apply(): lax.all_to_all(outgoing, 'sub', split_axis=0, concat_axis=0, tiled=True)]
    all_to_all x7 -> x0, waiting for transfers between devices: 18 us -> none  [fine_apply(): lax.all_to_all(outgoing, 'sub', split_axis=0, concat_axis=0, tiled=True)]
    pallas_call x0 -> x18, Pallas kernels: none -> 15.8 us  [call(): pl.pallas_call(kernel, out_shape=[jax.ShapeDtypeStruct(shape, kind) for s...]
    ppermute x14 -> x42, starting transfers between devices: 44 us -> 56.1 us  [the longest x21 27.2 us: exchange(): lax.ppermute(sub_out, 'sub', [(i, i ^ k) for i in range(peers)])]
    dot_general x35 -> x0, matrix products: 10.1 us -> none  [matmul(): return jnp.dot(left, right, precision=HIGHEST)]
    ppermute x14 -> x0, other arithmetic: 9.94 us -> none  [the longest x7 4.99 us: extended(): after = lax.ppermute(leading, axis, down)]
  transfers between devices with their start and end apart: 23 -> 44, of which waited for: 9 -> 28; matrix products, arithmetic and copies ran while one was open for 10% -> 0% of each run, Pallas kernels for 0% -> 5%
where the time goes in v1:
time: 131 us
  starting transfers between devices  61.3 us (47%)
  waiting for transfers between devices  49.1 us (37%)
  Pallas kernels  15.8 us (12%)
  local copies, waits for them, and re-layouts  3.2 us (2%)
    ppermute x21, starting transfers between devices, exchange(): lax.ppermute(sub_out, 'sub', [(i, i ^ k) for i in range(peers)])  27.2 us
    ppermute x21, waiting for transfers between devices, exchange(): lax.ppermute(sub_out, 'sub', [(i, i ^ k) for i in range(peers)])  23.7 us
    ppermute x7, waiting for transfers between devices, exchange(): high = lax.ppermute(blk_out, 'blk', [(j, i) for i, j in ring if j > 0])  23.1 us
    ppermute x7, starting transfers between devices, exchange(): low = lax.ppermute(blk_out, 'blk', [(i, j) for i, j in ring if j > 0])  19.8 us
    pallas_call x18, Pallas kernels, call(): pl.pallas_call(kernel, out_shape=[jax.ShapeDtypeStruct(shape, kind) for s...  15.8 us
    ppermute x7, starting transfers between devices, exchange(): high = lax.ppermute(blk_out, 'blk', [(j, i) for i, j in ring if j > 0])  9.04 us
    ppermute x2, starting transfers between devices, from_behind(): return lax.ppermute(x, axis, pairs)  5.2 us
    unnamed x25, local copies, waits for them, and re-layouts  3.07 us
  transfers between devices with their start and end apart: 44, of which 28 were waited for; matrix products, arithmetic and copies ran while one was open for 0% of the time, Pallas kernels for 5%

profile of v1, /device:TPU:0, one launch (start us, length us, event | category | flops | bytes accessed | tf_op | source)
XLA Modules:
  0.0 130.6 jit_solution(7905278461013721682)
XLA Ops:
  3.6 3.0 %collective-permute-start.2 = (f32[16,128]{1,0:T(8,128)S(1)}, f32[16,128]{1,0:T(8,128)S(1)}, u32[]{:S(2)}, u32[]{:S(2)}) collective-permute-start(f32[16,128]{1,0:T(8,128)S(1)} %get-tuple-element.60.refs_6_), channel_id=1, source_target_pairs={{0,2},{1,3},{2,0},{3,1},{4,6},{5,7},{6,4},{7,5},{8,10},{9,11},{10,... | collective-permute-start | bytes 24584 | tf_op jit(solution)/shard_map/ppermute | solution.py:316
  6.6 1.5 %collective-permute-start.3 = (f32[16,128]{1,0:T(8,128)S(1)}, f32[16,128]{1,0:T(8,128)S(1)}, u32[]{:S(2)}, u32[]{:S(2)}) collective-permute-start(f32[16,128]{1,0:T(8,128)S(1)} %get-tuple-element.60.refs_6_), channel_id=1, source_target_pairs={{0,4},{1,5},{2,6},{3,7},{4,0},{5,1},{6,2},{7,3},{8,12},{9,13},{10,... | collective-permute-start | bytes 24584 | tf_op jit(solution)/shard_map/ppermute | solution.py:316
  8.2 2.0 %collective-permute-done.3.refs_8_ = f32[16,128]{1,0:T(8,128)S(1)} collective-permute-done((f32[16,128]{1,0:T(8,128)S(1)}, f32[16,128]{1,0:T(8,128)S(1)}, u32[]{:S(2)}, u32[]{:S(2)}) %collective-permute-start.3) | collective-permute-done | bytes 8224 | tf_op jit(solution)/shard_map/ppermute | solution.py:316
  10.2 2.4 %collective-permute-done.4.refs_9_ = f32[16,128]{1,0:T(8,128)S(1)} collective-permute-done((f32[16,128]{1,0:T(8,128)S(1)}, f32[16,128]{1,0:T(8,128)S(1)}, u32[]{:S(2)}, u32[]{:S(2)}) %collective-permute-start.4) | collective-permute-done | bytes 8224 | tf_op jit(solution)/shard_map/ppermute | solution.py:316
  12.6 3.5 %collective-permute-start = (f32[16,128]{1,0:T(8,128)S(1)}, f32[16,128]{1,0:T(8,128)S(1)}, u32[]{:S(2)}, u32[]{:S(2)}) collective-permute-start(f32[16,128]{1,0:T(8,128)S(1)} %get-tuple-element.59), channel_id=1, source_target_pairs={{0,8},{8,16},{16,24},{1,9},{9,17},{17,25},{2,10},{10,18},{18,26},{... | collective-permute-start | bytes 24584 | tf_op jit(solution)/shard_map/ppermute | solution.py:311
  16.1 1.3 collective-permute-start.1
  18.3 3.3 %collective-permute-done.1.refs_5_ = f32[16,128]{1,0:T(8,128)S(1)} collective-permute-done((f32[16,128]{1,0:T(8,128)S(1)}, f32[16,128]{1,0:T(8,128)S(1)}, u32[]{:S(2)}, u32[]{:S(2)}) %collective-permute-start.1) | collective-permute-done | bytes 8224 | tf_op jit(solution)/shard_map/ppermute | solution.py:312
  23.2 1.5 %collective-permute-start.8 = (f32[16,128]{1,0:T(8,128)S(1)}, f32[16,128]{1,0:T(8,128)S(1)}, u32[]{:S(2)}, u32[]{:S(2)}) collective-permute-start(f32[16,128]{1,0:T(8,128)S(1)} %get-tuple-element.68.refs_6_), channel_id=1, source_target_pairs={{0,2},{1,3},{2,0},{3,1},{4,6},{5,7},{6,4},{7,5},{8,10},{9,11},{10,... | collective-permute-start | bytes 24584 | tf_op jit(solution)/shard_map/ppermute | solution.py:316
  24.7 1.5 %collective-permute-start.9 = (f32[16,128]{1,0:T(8,128)S(1)}, f32[16,128]{1,0:T(8,128)S(1)}, u32[]{:S(2)}, u32[]{:S(2)}) collective-permute-start(f32[16,128]{1,0:T(8,128)S(1)} %get-tuple-element.68.refs_6_), channel_id=1, source_target_pairs={{0,4},{1,5},{2,6},{3,7},{4,0},{5,1},{6,2},{7,3},{8,12},{9,13},{10,... | collective-permute-start | bytes 24584 | tf_op jit(solution)/shard_map/ppermute | solution.py:316
  28.3 3.5 %collective-permute-start.6 = (f32[16,128]{1,0:T(8,128)S(1)}, f32[16,128]{1,0:T(8,128)S(1)}, u32[]{:S(2)}, u32[]{:S(2)}) collective-permute-start(f32[16,128]{1,0:T(8,128)S(1)} %get-tuple-element.67), channel_id=1, source_target_pairs={{0,8},{8,16},{16,24},{1,9},{9,17},{17,25},{2,10},{10,18},{18,26},{... | collective-permute-start | bytes 24584 | tf_op jit(solution)/shard_map/ppermute | solution.py:311
  31.8 1.3 collective-permute-start.7
  34.0 3.4 %collective-permute-done.7.refs_5_ = f32[16,128]{1,0:T(8,128)S(1)} collective-permute-done((f32[16,128]{1,0:T(8,128)S(1)}, f32[16,128]{1,0:T(8,128)S(1)}, u32[]{:S(2)}, u32[]{:S(2)}) %collective-permute-start.7) | collective-permute-done | bytes 8224 | tf_op jit(solution)/shard_map/ppermute | solution.py:312
  38.9 1.5 %collective-permute-start.15 = (f32[16,128]{1,0:T(8,128)S(1)}, f32[16,128]{1,0:T(8,128)S(1)}, u32[]{:S(2)}, u32[]{:S(2)}) collective-permute-start(f32[16,128]{1,0:T(8,128)S(1)} %get-tuple-element.75.refs_6_), channel_id=1, source_target_pairs={{0,4},{1,5},{2,6},{3,7},{4,0},{5,1},{6,2},{7,3},{8,12},{9,13},{10,... | collective-permute-start | bytes 24584 | tf_op jit(solution)/shard_map/ppermute | solution.py:316
  40.4 1.4 %collective-permute-start.16 = (f32[16,128]{1,0:T(8,128)S(1)}, f32[16,128]{1,0:T(8,128)S(1)}, u32[]{:S(2)}, u32[]{:S(2)}) collective-permute-start(f32[16,128]{1,0:T(8,128)S(1)} %get-tuple-element.75.refs_6_), channel_id=1, source_target_pairs={{0,6},{1,7},{2,4},{3,5},{4,2},{5,3},{6,0},{7,1},{8,14},{9,15},{10,... | collective-permute-start | bytes 24584 | tf_op jit(solution)/shard_map/ppermute | solution.py:316
  42.6 2.4 %collective-permute-done.16.refs_9_ = f32[16,128]{1,0:T(8,128)S(1)} collective-permute-done((f32[16,128]{1,0:T(8,128)S(1)}, f32[16,128]{1,0:T(8,128)S(1)}, u32[]{:S(2)}, u32[]{:S(2)}) %collective-permute-start.16) | collective-permute-done | bytes 8224 | tf_op jit(solution)/shard_map/ppermute | solution.py:316
  45.0 3.5 %collective-permute-start.12 = (f32[16,128]{1,0:T(8,128)S(1)}, f32[16,128]{1,0:T(8,128)S(1)}, u32[]{:S(2)}, u32[]{:S(2)}) collective-permute-start(f32[16,128]{1,0:T(8,128)S(1)} %get-tuple-element.74), channel_id=1, source_target_pairs={{0,8},{8,16},{16,24},{1,9},{9,17},{17,25},{2,10},{10,18},{18,26},{... | collective-permute-start | bytes 24584 | tf_op jit(solution)/shard_map/ppermute | solution.py:311
  48.4 1.3 collective-permute-start.13
  50.7 3.3 %collective-permute-done.13.refs_5_ = f32[16,128]{1,0:T(8,128)S(1)} collective-permute-done((f32[16,128]{1,0:T(8,128)S(1)}, f32[16,128]{1,0:T(8,128)S(1)}, u32[]{:S(2)}, u32[]{:S(2)}) %collective-permute-start.13) | collective-permute-done | bytes 8224 | tf_op jit(solution)/shard_map/ppermute | solution.py:312
  54.5 1.3 collective-permute-start.18
  56.1 1.5 %collective-permute-done.18.arriving_ref = f32[64,128]{1,0:T(8,128)S(1)} collective-permute-done((f32[64,128]{1,0:T(8,128)S(1)}, f32[64,128]{1,0:T(8,128)S(1)}, u32[]{:S(2)}, u32[]{:S(2)}) %collective-permute-start.18) | collective-permute-done | bytes 32800 | tf_op jit(solution)/shard_map/ppermute | solution.py:279
  58.3 2.1 %shard_map.139 = (f32[64,256]{1,0:T(8,128)S(1)}, f32[64,128]{1,0:T(8,128)S(1)}) custom-call(f32[64,256]{1,0:T(8,128)S(1)} %get-tuple-element.76.r_ref.refs_0_, f32[64,128]{1,0:T(8,128)S(1)} %collective-permute-done.18.arriving_ref, s32[4,128]{1,0:T(4,128)S(1)} %get-tuple-element.78.gather_ref, s32[6,128]{1,0:T(8,128)S(1)} %get-tuple-element.79.place_ref, ...), custom_call_target="tpu_custom_call" | custom-call | tf_op jit(solution)/shard_map/pallas_call | solution.py:266
  60.4 3.9 %collective-permute-start.19 = (f32[64,128]{1,0:T(8,128)S(1)}, f32[64,128]{1,0:T(8,128)S(1)}, u32[]{:S(2)}, u32[]{:S(2)}) collective-permute-start(f32[64,128]{1,0:T(8,128)S(1)} %get-tuple-element.81), channel_id=1, source_target_pairs={{0,1},{1,2},{2,3},{3,4},{4,5},{5,6},{6,7},{7,8},{8,9},{9,10},{10,1... | collective-permute-start | bytes 98312 | tf_op jit(solution)/shard_map/ppermute | solution.py:279
  65.5 2.4 %collective-permute-start.22 = (f32[16,128]{1,0:T(8,128)S(1)}, f32[16,128]{1,0:T(8,128)S(1)}, u32[]{:S(2)}, u32[]{:S(2)}) collective-permute-start(f32[16,128]{1,0:T(8,128)S(1)} %get-tuple-element.87.refs_6_), channel_id=1, source_target_pairs={{0,2},{1,3},{2,0},{3,1},{4,6},{5,7},{6,4},{7,5},{8,10},{9,11},{10,... | collective-permute-start | bytes 24584 | tf_op jit(solution)/shard_map/ppermute | solution.py:316
  69.0 1.4 %collective-permute-start.24 = (f32[16,128]{1,0:T(8,128)S(1)}, f32[16,128]{1,0:T(8,128)S(1)}, u32[]{:S(2)}, u32[]{:S(2)}) collective-permute-start(f32[16,128]{1,0:T(8,128)S(1)} %get-tuple-element.87.refs_6_), channel_id=1, source_target_pairs={{0,6},{1,7},{2,4},{3,5},{4,2},{5,3},{6,0},{7,1},{8,14},{9,15},{10,... | collective-permute-start | bytes 24584 | tf_op jit(solution)/shard_map/ppermute | solution.py:316
  71.6 2.0 %collective-permute-done.24.refs_9_ = f32[16,128]{1,0:T(8,128)S(1)} collective-permute-done((f32[16,128]{1,0:T(8,128)S(1)}, f32[16,128]{1,0:T(8,128)S(1)}, u32[]{:S(2)}, u32[]{:S(2)}) %collective-permute-start.24) | collective-permute-done | bytes 8224 | tf_op jit(solution)/shard_map/ppermute | solution.py:316
  73.6 3.2 %collective-permute-start.20 = (f32[16,128]{1,0:T(8,128)S(1)}, f32[16,128]{1,0:T(8,128)S(1)}, u32[]{:S(2)}, u32[]{:S(2)}) collective-permute-start(f32[16,128]{1,0:T(8,128)S(1)} %get-tuple-element.86), channel_id=1, source_target_pairs={{0,8},{8,16},{16,24},{1,9},{9,17},{17,25},{2,10},{10,18},{18,26},{... | collective-permute-start | bytes 24584 | tf_op jit(solution)/shard_map/ppermute | solution.py:311
  76.8 1.3 collective-permute-start.21
  79.0 3.4 %collective-permute-done.21.refs_5_ = f32[16,128]{1,0:T(8,128)S(1)} collective-permute-done((f32[16,128]{1,0:T(8,128)S(1)}, f32[16,128]{1,0:T(8,128)S(1)}, u32[]{:S(2)}, u32[]{:S(2)}) %collective-permute-start.21) | collective-permute-done | bytes 8224 | tf_op jit(solution)/shard_map/ppermute | solution.py:312
  83.3 1.5 %collective-permute-start.28 = (f32[16,128]{1,0:T(8,128)S(1)}, f32[16,128]{1,0:T(8,128)S(1)}, u32[]{:S(2)}, u32[]{:S(2)}) collective-permute-start(f32[16,128]{1,0:T(8,128)S(1)} %get-tuple-element.94.refs_6_), channel_id=1, source_target_pairs={{0,2},{1,3},{2,0},{3,1},{4,6},{5,7},{6,4},{7,5},{8,10},{9,11},{10,... | collective-permute-start | bytes 24584 | tf_op jit(solution)/shard_map/ppermute | solution.py:316
  84.8 2.0 %collective-permute-start.29 = (f32[16,128]{1,0:T(8,128)S(1)}, f32[16,128]{1,0:T(8,128)S(1)}, u32[]{:S(2)}, u32[]{:S(2)}) collective-permute-start(f32[16,128]{1,0:T(8,128)S(1)} %get-tuple-element.94.refs_6_), channel_id=1, source_target_pairs={{0,4},{1,5},{2,6},{3,7},{4,0},{5,1},{6,2},{7,3},{8,12},{9,13},{10,... | collective-permute-start | bytes 24584 | tf_op jit(solution)/shard_map/ppermute | solution.py:316
  87.0 1.5 %collective-permute-done.29.refs_8_ = f32[16,128]{1,0:T(8,128)S(1)} collective-permute-done((f32[16,128]{1,0:T(8,128)S(1)}, f32[16,128]{1,0:T(8,128)S(1)}, u32[]{:S(2)}, u32[]{:S(2)}) %collective-permute-start.29) | collective-permute-done | bytes 8224 | tf_op jit(solution)/shard_map/ppermute | solution.py:316
  88.5 2.9 %collective-permute-done.30.refs_9_ = f32[16,128]{1,0:T(8,128)S(1)} collective-permute-done((f32[16,128]{1,0:T(8,128)S(1)}, f32[16,128]{1,0:T(8,128)S(1)}, u32[]{:S(2)}, u32[]{:S(2)}) %collective-permute-start.30) | collective-permute-done | bytes 8224 | tf_op jit(solution)/shard_map/ppermute | solution.py:316
  91.4 2.2 %collective-permute-start.26 = (f32[16,128]{1,0:T(8,128)S(1)}, f32[16,128]{1,0:T(8,128)S(1)}, u32[]{:S(2)}, u32[]{:S(2)}) collective-permute-start(f32[16,128]{1,0:T(8,128)S(1)} %get-tuple-element.93), channel_id=1, source_target_pairs={{0,8},{8,16},{16,24},{1,9},{9,17},{17,25},{2,10},{10,18},{18,26},{... | collective-permute-start | bytes 24584 | tf_op jit(solution)/shard_map/ppermute | solution.py:311
  93.6 1.3 collective-permute-start.27
  95.8 3.4 %collective-permute-done.27.refs_5_ = f32[16,128]{1,0:T(8,128)S(1)} collective-permute-done((f32[16,128]{1,0:T(8,128)S(1)}, f32[16,128]{1,0:T(8,128)S(1)}, u32[]{:S(2)}, u32[]{:S(2)}) %collective-permute-start.27) | collective-permute-done | bytes 8224 | tf_op jit(solution)/shard_map/ppermute | solution.py:312
  100.7 2.9 %collective-permute-start.36 = (f32[16,128]{1,0:T(8,128)S(1)}, f32[16,128]{1,0:T(8,128)S(1)}, u32[]{:S(2)}, u32[]{:S(2)}) collective-permute-start(f32[16,128]{1,0:T(8,128)S(1)} %get-tuple-element.101.refs_6_), channel_id=1, source_target_pairs={{0,6},{1,7},{2,4},{3,5},{4,2},{5,3},{6,0},{7,1},{8,14},{9,15},{10,... | collective-permute-start | bytes 24584 | tf_op jit(solution)/shard_map/ppermute | solution.py:316
  103.9 1.4 %collective-permute-done.36.refs_9_ = f32[16,128]{1,0:T(8,128)S(1)} collective-permute-done((f32[16,128]{1,0:T(8,128)S(1)}, f32[16,128]{1,0:T(8,128)S(1)}, u32[]{:S(2)}, u32[]{:S(2)}) %collective-permute-start.36) | collective-permute-done | bytes 8224 | tf_op jit(solution)/shard_map/ppermute | solution.py:316
  105.3 2.1 %collective-permute-start.32 = (f32[16,128]{1,0:T(8,128)S(1)}, f32[16,128]{1,0:T(8,128)S(1)}, u32[]{:S(2)}, u32[]{:S(2)}) collective-permute-start(f32[16,128]{1,0:T(8,128)S(1)} %get-tuple-element.100), channel_id=1, source_target_pairs={{0,8},{8,16},{16,24},{1,9},{9,17},{17,25},{2,10},{10,18},{18,26},{... | collective-permute-start | bytes 24584 | tf_op jit(solution)/shard_map/ppermute | solution.py:311
  107.4 1.3 collective-permute-start.33
  109.6 3.4 %collective-permute-done.33.refs_5_ = f32[16,128]{1,0:T(8,128)S(1)} collective-permute-done((f32[16,128]{1,0:T(8,128)S(1)}, f32[16,128]{1,0:T(8,128)S(1)}, u32[]{:S(2)}, u32[]{:S(2)}) %collective-permute-start.33) | collective-permute-done | bytes 8224 | tf_op jit(solution)/shard_map/ppermute | solution.py:312
  113.9 1.5 %collective-permute-start.40 = (f32[16,128]{1,0:T(8,128)S(1)}, f32[16,128]{1,0:T(8,128)S(1)}, u32[]{:S(2)}, u32[]{:S(2)}) collective-permute-start(f32[16,128]{1,0:T(8,128)S(1)} %get-tuple-element.109.refs_6_), channel_id=1, source_target_pairs={{0,2},{1,3},{2,0},{3,1},{4,6},{5,7},{6,4},{7,5},{8,10},{9,11},{10,... | collective-permute-start | bytes 24584 | tf_op jit(solution)/shard_map/ppermute | solution.py:316
  115.4 2.0 %collective-permute-start.41 = (f32[16,128]{1,0:T(8,128)S(1)}, f32[16,128]{1,0:T(8,128)S(1)}, u32[]{:S(2)}, u32[]{:S(2)}) collective-permute-start(f32[16,128]{1,0:T(8,128)S(1)} %get-tuple-element.109.refs_6_), channel_id=1, source_target_pairs={{0,4},{1,5},{2,6},{3,7},{4,0},{5,1},{6,2},{7,3},{8,12},{9,13},{10,... | collective-permute-start | bytes 24584 | tf_op jit(solution)/shard_map/ppermute | solution.py:316
  117.6 1.5 %collective-permute-done.41.refs_8_ = f32[16,128]{1,0:T(8,128)S(1)} collective-permute-done((f32[16,128]{1,0:T(8,128)S(1)}, f32[16,128]{1,0:T(8,128)S(1)}, u32[]{:S(2)}, u32[]{:S(2)}) %collective-permute-start.41) | collective-permute-done | bytes 8224 | tf_op jit(solution)/shard_map/ppermute | solution.py:316
  119.1 2.9 %collective-permute-done.42.refs_9_ = f32[16,128]{1,0:T(8,128)S(1)} collective-permute-done((f32[16,128]{1,0:T(8,128)S(1)}, f32[16,128]{1,0:T(8,128)S(1)}, u32[]{:S(2)}, u32[]{:S(2)}) %collective-permute-start.42) | collective-permute-done | bytes 8224 | tf_op jit(solution)/shard_map/ppermute | solution.py:316
  122.0 1.9 %collective-permute-start.38 = (f32[16,128]{1,0:T(8,128)S(1)}, f32[16,128]{1,0:T(8,128)S(1)}, u32[]{:S(2)}, u32[]{:S(2)}) collective-permute-start(f32[16,128]{1,0:T(8,128)S(1)} %get-tuple-element.108), channel_id=1, source_target_pairs={{0,8},{8,16},{16,24},{1,9},{9,17},{17,25},{2,10},{10,18},{18,26},{... | collective-permute-start | bytes 24584 | tf_op jit(solution)/shard_map/ppermute | solution.py:311
  123.9 1.3 collective-permute-start.39
  125.2 1.2 shard_map.147
  126.4 3.0 %collective-permute-done.39.refs_5_ = f32[16,128]{1,0:T(8,128)S(1)} collective-permute-done((f32[16,128]{1,0:T(8,128)S(1)}, f32[16,128]{1,0:T(8,128)S(1)}, u32[]{:S(2)}, u32[]{:S(2)}) %collective-permute-start.39) | collective-permute-done | bytes 8224 | tf_op jit(solution)/shard_map/ppermute | solution.py:312
  (92 shorter events, 24.2 us)
Async XLA Ops:
  3.6 4.6 %collective-permute-start.2 = (f32[16,128]{1,0:T(8,128)S(1)}, f32[16,128]{1,0:T(8,128)S(1)}, u32[]{:S(2)}, u32[]{:S(2)}) collective-permute-start(f32[16,128]{1,0:T(8,128)S(1)} %get-tuple-element.60.refs_6_), channel_id=1, source_target_pairs={{0,2},{1,3},{2,0},{3,1},{4,6},{5,7},{6,4},{7,5},{8,10},{9,11},{10,... | collective-permute-start | bytes 24584 | tf_op jit(solution)/shard_map/ppermute | solution.py:316
  6.6 3.7 %collective-permute-start.3 = (f32[16,128]{1,0:T(8,128)S(1)}, f32[16,128]{1,0:T(8,128)S(1)}, u32[]{:S(2)}, u32[]{:S(2)}) collective-permute-start(f32[16,128]{1,0:T(8,128)S(1)} %get-tuple-element.60.refs_6_), channel_id=1, source_target_pairs={{0,4},{1,5},{2,6},{3,7},{4,0},{5,1},{6,2},{7,3},{8,12},{9,13},{10,... | collective-permute-start | bytes 24584 | tf_op jit(solution)/shard_map/ppermute | solution.py:316
  8.1 4.5 %collective-permute-start.4 = (f32[16,128]{1,0:T(8,128)S(1)}, f32[16,128]{1,0:T(8,128)S(1)}, u32[]{:S(2)}, u32[]{:S(2)}) collective-permute-start(f32[16,128]{1,0:T(8,128)S(1)} %get-tuple-element.60.refs_6_), channel_id=1, source_target_pairs={{0,6},{1,7},{2,4},{3,5},{4,2},{5,3},{6,0},{7,1},{8,14},{9,15},{10,... | collective-permute-start | bytes 24584 | tf_op jit(solution)/shard_map/ppermute | solution.py:316
  12.6 4.8 %copy-start.1 = (s32[6,256]{1,0:T(8,128)S(1)}, s32[6,256]{1,0:T(8,128)}, u32[]{:S(2)}) copy-start(s32[6,256]{1,0:T(8,128)} %refs_3_.14) | copy-start | bytes 18436
  12.6 9.0 %collective-permute-start.5 = (f32[64,128]{1,0:T(8,128)S(1)}, f32[64,128]{1,0:T(8,128)S(1)}, u32[]{:S(2)}, u32[]{:S(2)}) collective-permute-start(f32[64,128]{1,0:T(8,128)S(1)} %pad_maximum_fusion), channel_id=1, source_target_pairs={{0,1},{1,0},{2,3},{3,2},{4,5},{5,4},{6,7},{7,6},{8,9},{9,8},{10,11... | collective-permute-start | bytes 98312 | tf_op jit(solution)/shard_map/ppermute | solution.py:319
  12.6 5.7 %collective-permute-start = (f32[16,128]{1,0:T(8,128)S(1)}, f32[16,128]{1,0:T(8,128)S(1)}, u32[]{:S(2)}, u32[]{:S(2)}) collective-permute-start(f32[16,128]{1,0:T(8,128)S(1)} %get-tuple-element.59), channel_id=1, source_target_pairs={{0,8},{8,16},{16,24},{1,9},{9,17},{17,25},{2,10},{10,18},{18,26},{... | collective-permute-start | bytes 24584 | tf_op jit(solution)/shard_map/ppermute | solution.py:311
  16.1 5.5 %collective-permute-start.1 = (f32[16,128]{1,0:T(8,128)S(1)}, f32[16,128]{1,0:T(8,128)S(1)}, u32[]{:S(2)}, u32[]{:S(2)}) collective-permute-start(f32[16,128]{1,0:T(8,128)S(1)} %get-tuple-element.59), channel_id=1, source_target_pairs={{8,0},{16,8},{24,16},{9,1},{17,9},{25,17},{10,2},{18,10},{26,18},{... | collective-permute-start | bytes 24584 | tf_op jit(solution)/shard_map/ppermute | solution.py:312
  17.4 4.2 %copy-start.4 = (f32[64,256]{1,0:T(8,128)S(1)}, f32[64,256]{1,0:T(8,128)}, u32[]{:S(2)}) copy-start(f32[64,256]{1,0:T(8,128)} %refs_0_.1) | copy-start | bytes 196612
  22.6 4.6 %collective-permute-start.10 = (f32[16,128]{1,0:T(8,128)S(1)}, f32[16,128]{1,0:T(8,128)S(1)}, u32[]{:S(2)}, u32[]{:S(2)}) collective-permute-start(f32[16,128]{1,0:T(8,128)S(1)} %get-tuple-element.68.refs_6_), channel_id=1, source_target_pairs={{0,6},{1,7},{2,4},{3,5},{4,2},{5,3},{6,0},{7,1},{8,14},{9,15},{10,... | collective-permute-start | bytes 24584 | tf_op jit(solution)/shard_map/ppermute | solution.py:316
  23.2 4.1 %collective-permute-start.8 = (f32[16,128]{1,0:T(8,128)S(1)}, f32[16,128]{1,0:T(8,128)S(1)}, u32[]{:S(2)}, u32[]{:S(2)}) collective-permute-start(f32[16,128]{1,0:T(8,128)S(1)} %get-tuple-element.68.refs_6_), channel_id=1, source_target_pairs={{0,2},{1,3},{2,0},{3,1},{4,6},{5,7},{6,4},{7,5},{8,10},{9,11},{10,... | collective-permute-start | bytes 24584 | tf_op jit(solution)/shard_map/ppermute | solution.py:316
  24.7 3.7 %collective-permute-start.9 = (f32[16,128]{1,0:T(8,128)S(1)}, f32[16,128]{1,0:T(8,128)S(1)}, u32[]{:S(2)}, u32[]{:S(2)}) collective-permute-start(f32[16,128]{1,0:T(8,128)S(1)} %get-tuple-element.68.refs_6_), channel_id=1, source_target_pairs={{0,4},{1,5},{2,6},{3,7},{4,0},{5,1},{6,2},{7,3},{8,12},{9,13},{10,... | collective-permute-start | bytes 24584 | tf_op jit(solution)/shard_map/ppermute | solution.py:316
  28.3 9.0 %collective-permute-start.11 = (f32[64,128]{1,0:T(8,128)S(1)}, f32[64,128]{1,0:T(8,128)S(1)}, u32[]{:S(2)}, u32[]{:S(2)}) collective-permute-start(f32[64,128]{1,0:T(8,128)S(1)} %pad_maximum_fusion.1), channel_id=1, source_target_pairs={{0,1},{1,0},{2,3},{3,2},{4,5},{5,4},{6,7},{7,6},{8,9},{9,8},{10,11... | collective-permute-start | bytes 98312 | tf_op jit(solution)/shard_map/ppermute | solution.py:319
  28.3 5.7 %collective-permute-start.6 = (f32[16,128]{1,0:T(8,128)S(1)}, f32[16,128]{1,0:T(8,128)S(1)}, u32[]{:S(2)}, u32[]{:S(2)}) collective-permute-start(f32[16,128]{1,0:T(8,128)S(1)} %get-tuple-element.67), channel_id=1, source_target_pairs={{0,8},{8,16},{16,24},{1,9},{9,17},{17,25},{2,10},{10,18},{18,26},{... | collective-permute-start | bytes 24584 | tf_op jit(solution)/shard_map/ppermute | solution.py:311
  31.8 5.5 %collective-permute-start.7 = (f32[16,128]{1,0:T(8,128)S(1)}, f32[16,128]{1,0:T(8,128)S(1)}, u32[]{:S(2)}, u32[]{:S(2)}) collective-permute-start(f32[16,128]{1,0:T(8,128)S(1)} %get-tuple-element.67), channel_id=1, source_target_pairs={{8,0},{16,8},{24,16},{9,1},{17,9},{25,17},{10,2},{18,10},{26,18},{... | collective-permute-start | bytes 24584 | tf_op jit(solution)/shard_map/ppermute | solution.py:312
  38.3 3.7 %collective-permute-start.14 = (f32[16,128]{1,0:T(8,128)S(1)}, f32[16,128]{1,0:T(8,128)S(1)}, u32[]{:S(2)}, u32[]{:S(2)}) collective-permute-start(f32[16,128]{1,0:T(8,128)S(1)} %get-tuple-element.75.refs_6_), channel_id=1, source_target_pairs={{0,2},{1,3},{2,0},{3,1},{4,6},{5,7},{6,4},{7,5},{8,10},{9,11},{10,... | collective-permute-start | bytes 24584 | tf_op jit(solution)/shard_map/ppermute | solution.py:316
  38.9 3.7 %collective-permute-start.15 = (f32[16,128]{1,0:T(8,128)S(1)}, f32[16,128]{1,0:T(8,128)S(1)}, u32[]{:S(2)}, u32[]{:S(2)}) collective-permute-start(f32[16,128]{1,0:T(8,128)S(1)} %get-tuple-element.75.refs_6_), channel_id=1, source_target_pairs={{0,4},{1,5},{2,6},{3,7},{4,0},{5,1},{6,2},{7,3},{8,12},{9,13},{10,... | collective-permute-start | bytes 24584 | tf_op jit(solution)/shard_map/ppermute | solution.py:316
  40.4 4.5 %collective-permute-start.16 = (f32[16,128]{1,0:T(8,128)S(1)}, f32[16,128]{1,0:T(8,128)S(1)}, u32[]{:S(2)}, u32[]{:S(2)}) collective-permute-start(f32[16,128]{1,0:T(8,128)S(1)} %get-tuple-element.75.refs_6_), channel_id=1, source_target_pairs={{0,6},{1,7},{2,4},{3,5},{4,2},{5,3},{6,0},{7,1},{8,14},{9,15},{10,... | collective-permute-start | bytes 24584 | tf_op jit(solution)/shard_map/ppermute | solution.py:316
  45.0 9.0 %collective-permute-start.17 = (f32[64,128]{1,0:T(8,128)S(1)}, f32[64,128]{1,0:T(8,128)S(1)}, u32[]{:S(2)}, u32[]{:S(2)}) collective-permute-start(f32[64,128]{1,0:T(8,128)S(1)} %pad_maximum_fusion.2), channel_id=1, source_target_pairs={{0,1},{1,0},{2,3},{3,2},{4,5},{5,4},{6,7},{7,6},{8,9},{9,8},{10,11... | collective-permute-start | bytes 98312 | tf_op jit(solution)/shard_map/ppermute | solution.py:319
  45.0 5.7 %collective-permute-start.12 = (f32[16,128]{1,0:T(8,128)S(1)}, f32[16,128]{1,0:T(8,128)S(1)}, u32[]{:S(2)}, u32[]{:S(2)}) collective-permute-start(f32[16,128]{1,0:T(8,128)S(1)} %get-tuple-element.74), channel_id=1, source_target_pairs={{0,8},{8,16},{16,24},{1,9},{9,17},{17,25},{2,10},{10,18},{18,26},{... | collective-permute-start | bytes 24584 | tf_op jit(solution)/shard_map/ppermute | solution.py:311
  48.4 5.5 %collective-permute-start.13 = (f32[16,128]{1,0:T(8,128)S(1)}, f32[16,128]{1,0:T(8,128)S(1)}, u32[]{:S(2)}, u32[]{:S(2)}) collective-permute-start(f32[16,128]{1,0:T(8,128)S(1)} %get-tuple-element.74), channel_id=1, source_target_pairs={{8,0},{16,8},{24,16},{9,1},{17,9},{25,17},{10,2},{18,10},{26,18},{... | collective-permute-start | bytes 24584 | tf_op jit(solution)/shard_map/ppermute | solution.py:312
  49.7 6.2 %copy-start.2 = (f32[8,64,64]{2,1,0:T(8,128)S(1)}, f32[8,64,64]{2,1,0:T(8,128)}, u32[]{:S(2)}) copy-start(f32[8,64,64]{2,1,0:T(8,128)} %param.23) | copy-start | bytes 393220
  54.5 3.1 %collective-permute-start.18 = (f32[64,128]{1,0:T(8,128)S(1)}, f32[64,128]{1,0:T(8,128)S(1)}, u32[]{:S(2)}, u32[]{:S(2)}) collective-permute-start(f32[64,128]{1,0:T(8,128)S(1)} %get-tuple-element.77), channel_id=1, source_target_pairs={{1,0},{2,1},{3,2},{4,3},{5,4},{6,5},{7,6},{8,7},{9,8},{10,9},{11,1... | collective-permute-start | bytes 98312 | tf_op jit(solution)/shard_map/ppermute | solution.py:279
  56.0 1.6 %copy-start.7 = (f32[64,64]{1,0:T(8,128)S(1)}, f32[64,64]{1,0:T(8,128)}, u32[]{:S(2)}) copy-start(f32[64,64]{1,0:T(8,128)} %stiff_ref.11) | copy-start | bytes 49156
  60.4 4.8 %collective-permute-start.19 = (f32[64,128]{1,0:T(8,128)S(1)}, f32[64,128]{1,0:T(8,128)S(1)}, u32[]{:S(2)}, u32[]{:S(2)}) collective-permute-start(f32[64,128]{1,0:T(8,128)S(1)} %get-tuple-element.81), channel_id=1, source_target_pairs={{0,1},{1,2},{2,3},{3,4},{4,5},{5,6},{6,7},{7,8},{8,9},{9,10},{10,1... | collective-permute-start | bytes 98312 | tf_op jit(solution)/shard_map/ppermute | solution.py:279
  65.5 4.9 %collective-permute-start.22 = (f32[16,128]{1,0:T(8,128)S(1)}, f32[16,128]{1,0:T(8,128)S(1)}, u32[]{:S(2)}, u32[]{:S(2)}) collective-permute-start(f32[16,128]{1,0:T(8,128)S(1)} %get-tuple-element.87.refs_6_), channel_id=1, source_target_pairs={{0,2},{1,3},{2,0},{3,1},{4,6},{5,7},{6,4},{7,5},{8,10},{9,11},{10,... | collective-permute-start | bytes 24584 | tf_op jit(solution)/shard_map/ppermute | solution.py:316
  67.9 3.7 %collective-permute-start.23 = (f32[16,128]{1,0:T(8,128)S(1)}, f32[16,128]{1,0:T(8,128)S(1)}, u32[]{:S(2)}, u32[]{:S(2)}) collective-permute-start(f32[16,128]{1,0:T(8,128)S(1)} %get-tuple-element.87.refs_6_), channel_id=1, source_target_pairs={{0,4},{1,5},{2,6},{3,7},{4,0},{5,1},{6,2},{7,3},{8,12},{9,13},{10,... | collective-permute-start | bytes 24584 | tf_op jit(solution)/shard_map/ppermute | solution.py:316
  69.0 4.5 %collective-permute-start.24 = (f32[16,128]{1,0:T(8,128)S(1)}, f32[16,128]{1,0:T(8,128)S(1)}, u32[]{:S(2)}, u32[]{:S(2)}) collective-permute-start(f32[16,128]{1,0:T(8,128)S(1)} %get-tuple-element.87.refs_6_), channel_id=1, source_target_pairs={{0,6},{1,7},{2,4},{3,5},{4,2},{5,3},{6,0},{7,1},{8,14},{9,15},{10,... | collective-permute-start | bytes 24584 | tf_op jit(solution)/shard_map/ppermute | solution.py:316
  73.6 8.8 %collective-permute-start.25 = (f32[64,128]{1,0:T(8,128)S(1)}, f32[64,128]{1,0:T(8,128)S(1)}, u32[]{:S(2)}, u32[]{:S(2)}) collective-permute-start(f32[64,128]{1,0:T(8,128)S(1)} %pad_maximum_fusion.3), channel_id=1, source_target_pairs={{0,1},{1,0},{2,3},{3,2},{4,5},{5,4},{6,7},{7,6},{8,9},{9,8},{10,11... | collective-permute-start | bytes 98312 | tf_op jit(solution)/shard_map/ppermute | solution.py:319
  73.6 5.4 %collective-permute-start.20 = (f32[16,128]{1,0:T(8,128)S(1)}, f32[16,128]{1,0:T(8,128)S(1)}, u32[]{:S(2)}, u32[]{:S(2)}) collective-permute-start(f32[16,128]{1,0:T(8,128)S(1)} %get-tuple-element.86), channel_id=1, source_target_pairs={{0,8},{8,16},{16,24},{1,9},{9,17},{17,25},{2,10},{10,18},{18,26},{... | collective-permute-start | bytes 24584 | tf_op jit(solution)/shard_map/ppermute | solution.py:311
  76.8 5.5 %collective-permute-start.21 = (f32[16,128]{1,0:T(8,128)S(1)}, f32[16,128]{1,0:T(8,128)S(1)}, u32[]{:S(2)}, u32[]{:S(2)}) collective-permute-start(f32[16,128]{1,0:T(8,128)S(1)} %get-tuple-element.86), channel_id=1, source_target_pairs={{8,0},{16,8},{24,16},{9,1},{17,9},{25,17},{10,2},{18,10},{26,18},{... | collective-permute-start | bytes 24584 | tf_op jit(solution)/shard_map/ppermute | solution.py:312
  83.3 3.7 %collective-permute-start.28 = (f32[16,128]{1,0:T(8,128)S(1)}, f32[16,128]{1,0:T(8,128)S(1)}, u32[]{:S(2)}, u32[]{:S(2)}) collective-permute-start(f32[16,128]{1,0:T(8,128)S(1)} %get-tuple-element.94.refs_6_), channel_id=1, source_target_pairs={{0,2},{1,3},{2,0},{3,1},{4,6},{5,7},{6,4},{7,5},{8,10},{9,11},{10,... | collective-permute-start | bytes 24584 | tf_op jit(solution)/shard_map/ppermute | solution.py:316
  84.8 3.7 %collective-permute-start.29 = (f32[16,128]{1,0:T(8,128)S(1)}, f32[16,128]{1,0:T(8,128)S(1)}, u32[]{:S(2)}, u32[]{:S(2)}) collective-permute-start(f32[16,128]{1,0:T(8,128)S(1)} %get-tuple-element.94.refs_6_), channel_id=1, source_target_pairs={{0,4},{1,5},{2,6},{3,7},{4,0},{5,1},{6,2},{7,3},{8,12},{9,13},{10,... | collective-permute-start | bytes 24584 | tf_op jit(solution)/shard_map/ppermute | solution.py:316
  86.8 4.5 %collective-permute-start.30 = (f32[16,128]{1,0:T(8,128)S(1)}, f32[16,128]{1,0:T(8,128)S(1)}, u32[]{:S(2)}, u32[]{:S(2)}) collective-permute-start(f32[16,128]{1,0:T(8,128)S(1)} %get-tuple-element.94.refs_6_), channel_id=1, source_target_pairs={{0,6},{1,7},{2,4},{3,5},{4,2},{5,3},{6,0},{7,1},{8,14},{9,15},{10,... | collective-permute-start | bytes 24584 | tf_op jit(solution)/shard_map/ppermute | solution.py:316
  91.4 7.8 %collective-permute-start.31 = (f32[64,128]{1,0:T(8,128)S(1)}, f32[64,128]{1,0:T(8,128)S(1)}, u32[]{:S(2)}, u32[]{:S(2)}) collective-permute-start(f32[64,128]{1,0:T(8,128)S(1)} %pad_maximum_fusion.4), channel_id=1, source_target_pairs={{0,1},{1,0},{2,3},{3,2},{4,5},{5,4},{6,7},{7,6},{8,9},{9,8},{10,11... | collective-permute-start | bytes 98312 | tf_op jit(solution)/shard_map/ppermute | solution.py:319
  91.4 4.4 %collective-permute-start.26 = (f32[16,128]{1,0:T(8,128)S(1)}, f32[16,128]{1,0:T(8,128)S(1)}, u32[]{:S(2)}, u32[]{:S(2)}) collective-permute-start(f32[16,128]{1,0:T(8,128)S(1)} %get-tuple-element.93), channel_id=1, source_target_pairs={{0,8},{8,16},{16,24},{1,9},{9,17},{17,25},{2,10},{10,18},{18,26},{... | collective-permute-start | bytes 24584 | tf_op jit(solution)/shard_map/ppermute | solution.py:311
  93.6 5.5 %collective-permute-start.27 = (f32[16,128]{1,0:T(8,128)S(1)}, f32[16,128]{1,0:T(8,128)S(1)}, u32[]{:S(2)}, u32[]{:S(2)}) collective-permute-start(f32[16,128]{1,0:T(8,128)S(1)} %get-tuple-element.93), channel_id=1, source_target_pairs={{8,0},{16,8},{24,16},{9,1},{17,9},{25,17},{10,2},{18,10},{26,18},{... | collective-permute-start | bytes 24584 | tf_op jit(solution)/shard_map/ppermute | solution.py:312
  100.1 3.7 %collective-permute-start.34 = (f32[16,128]{1,0:T(8,128)S(1)}, f32[16,128]{1,0:T(8,128)S(1)}, u32[]{:S(2)}, u32[]{:S(2)}) collective-permute-start(f32[16,128]{1,0:T(8,128)S(1)} %get-tuple-element.101.refs_6_), channel_id=1, source_target_pairs={{0,2},{1,3},{2,0},{3,1},{4,6},{5,7},{6,4},{7,5},{8,10},{9,11},{10,... | collective-permute-start | bytes 24584 | tf_op jit(solution)/shard_map/ppermute | solution.py:316
  100.2 3.7 %collective-permute-start.35 = (f32[16,128]{1,0:T(8,128)S(1)}, f32[16,128]{1,0:T(8,128)S(1)}, u32[]{:S(2)}, u32[]{:S(2)}) collective-permute-start(f32[16,128]{1,0:T(8,128)S(1)} %get-tuple-element.101.refs_6_), channel_id=1, source_target_pairs={{0,4},{1,5},{2,6},{3,7},{4,0},{5,1},{6,2},{7,3},{8,12},{9,13},{10,... | collective-permute-start | bytes 24584 | tf_op jit(solution)/shard_map/ppermute | solution.py:316
  100.7 4.5 %collective-permute-start.36 = (f32[16,128]{1,0:T(8,128)S(1)}, f32[16,128]{1,0:T(8,128)S(1)}, u32[]{:S(2)}, u32[]{:S(2)}) collective-permute-start(f32[16,128]{1,0:T(8,128)S(1)} %get-tuple-element.101.refs_6_), channel_id=1, source_target_pairs={{0,6},{1,7},{2,4},{3,5},{4,2},{5,3},{6,0},{7,1},{8,14},{9,15},{10,... | collective-permute-start | bytes 24584 | tf_op jit(solution)/shard_map/ppermute | solution.py:316
  105.3 7.6 %collective-permute-start.37 = (f32[64,128]{1,0:T(8,128)S(1)}, f32[64,128]{1,0:T(8,128)S(1)}, u32[]{:S(2)}, u32[]{:S(2)}) collective-permute-start(f32[64,128]{1,0:T(8,128)S(1)} %pad_maximum_fusion.5), channel_id=1, source_target_pairs={{0,1},{1,0},{2,3},{3,2},{4,5},{5,4},{6,7},{7,6},{8,9},{9,8},{10,11... | collective-permute-start | bytes 98312 | tf_op jit(solution)/shard_map/ppermute | solution.py:319
  105.3 4.3 %collective-permute-start.32 = (f32[16,128]{1,0:T(8,128)S(1)}, f32[16,128]{1,0:T(8,128)S(1)}, u32[]{:S(2)}, u32[]{:S(2)}) collective-permute-start(f32[16,128]{1,0:T(8,128)S(1)} %get-tuple-element.100), channel_id=1, source_target_pairs={{0,8},{8,16},{16,24},{1,9},{9,17},{17,25},{2,10},{10,18},{18,26},{... | collective-permute-start | bytes 24584 | tf_op jit(solution)/shard_map/ppermute | solution.py:311
  107.4 5.5 %collective-permute-start.33 = (f32[16,128]{1,0:T(8,128)S(1)}, f32[16,128]{1,0:T(8,128)S(1)}, u32[]{:S(2)}, u32[]{:S(2)}) collective-permute-start(f32[16,128]{1,0:T(8,128)S(1)} %get-tuple-element.100), channel_id=1, source_target_pairs={{8,0},{16,8},{24,16},{9,1},{17,9},{25,17},{10,2},{18,10},{26,18},{... | collective-permute-start | bytes 24584 | tf_op jit(solution)/shard_map/ppermute | solution.py:312
  113.9 3.7 %collective-permute-start.40 = (f32[16,128]{1,0:T(8,128)S(1)}, f32[16,128]{1,0:T(8,128)S(1)}, u32[]{:S(2)}, u32[]{:S(2)}) collective-permute-start(f32[16,128]{1,0:T(8,128)S(1)} %get-tuple-element.109.refs_6_), channel_id=1, source_target_pairs={{0,2},{1,3},{2,0},{3,1},{4,6},{5,7},{6,4},{7,5},{8,10},{9,11},{10,... | collective-permute-start | bytes 24584 | tf_op jit(solution)/shard_map/ppermute | solution.py:316
  115.4 3.7 %collective-permute-start.41 = (f32[16,128]{1,0:T(8,128)S(1)}, f32[16,128]{1,0:T(8,128)S(1)}, u32[]{:S(2)}, u32[]{:S(2)}) collective-permute-start(f32[16,128]{1,0:T(8,128)S(1)} %get-tuple-element.109.refs_6_), channel_id=1, source_target_pairs={{0,4},{1,5},{2,6},{3,7},{4,0},{5,1},{6,2},{7,3},{8,12},{9,13},{10,... | collective-permute-start | bytes 24584 | tf_op jit(solution)/shard_map/ppermute | solution.py:316
  117.4 4.5 %collective-permute-start.42 = (f32[16,128]{1,0:T(8,128)S(1)}, f32[16,128]{1,0:T(8,128)S(1)}, u32[]{:S(2)}, u32[]{:S(2)}) collective-permute-start(f32[16,128]{1,0:T(8,128)S(1)} %get-tuple-element.109.refs_6_), channel_id=1, source_target_pairs={{0,6},{1,7},{2,4},{3,5},{4,2},{5,3},{6,0},{7,1},{8,14},{9,15},{10,... | collective-permute-start | bytes 24584 | tf_op jit(solution)/shard_map/ppermute | solution.py:316
  122.0 7.5 %collective-permute-start.43 = (f32[64,128]{1,0:T(8,128)S(1)}, f32[64,128]{1,0:T(8,128)S(1)}, u32[]{:S(2)}, u32[]{:S(2)}) collective-permute-start(f32[64,128]{1,0:T(8,128)S(1)} %pad_maximum_fusion.6), channel_id=1, source_target_pairs={{0,1},{1,0},{2,3},{3,2},{4,5},{5,4},{6,7},{7,6},{8,9},{9,8},{10,11... | collective-permute-start | bytes 98312 | tf_op jit(solution)/shard_map/ppermute | solution.py:319
  122.0 4.4 %collective-permute-start.38 = (f32[16,128]{1,0:T(8,128)S(1)}, f32[16,128]{1,0:T(8,128)S(1)}, u32[]{:S(2)}, u32[]{:S(2)}) collective-permute-start(f32[16,128]{1,0:T(8,128)S(1)} %get-tuple-element.108), channel_id=1, source_target_pairs={{0,8},{8,16},{16,24},{1,9},{9,17},{17,25},{2,10},{10,18},{18,26},{... | collective-permute-start | bytes 24584 | tf_op jit(solution)/shard_map/ppermute | solution.py:311
  123.9 5.5 %collective-permute-start.39 = (f32[16,128]{1,0:T(8,128)S(1)}, f32[16,128]{1,0:T(8,128)S(1)}, u32[]{:S(2)}, u32[]{:S(2)}) collective-permute-start(f32[16,128]{1,0:T(8,128)S(1)} %get-tuple-element.108), channel_id=1, source_target_pairs={{8,0},{16,8},{24,16},{9,1},{17,9},{25,17},{10,2},{18,10},{26,18},{... | collective-permute-start | bytes 24584 | tf_op jit(solution)/shard_map/ppermute | solution.py:312
  (8 other events, 6.7 us)

commit v2 on v0

v2 whole, which is shorter than its diff:
```python
import functools

import jax
import jax.numpy as jnp
from jax import lax
from jax.experimental import pallas as pl
from jax.experimental.pallas import tpu as pltpu
from jax.sharding import PartitionSpec as P

HEAD = 8
KF = 3
KC = 4
FACES = 6
OCTANTS = 8
LANES = 128
CORES = 2

PENALTY = 0.3
COUPLING = 0.5
LOW_EIG = 0.4
HIGH_EIG = 2.5
CENTER = 0.5 * (HIGH_EIG + LOW_EIG)
HALF = 0.5 * (HIGH_EIG - LOW_EIG)


def steps(sweeps):
    sigma = CENTER / HALF
    rho, pairs = 1.0 / sigma, []
    for _ in range(sweeps):
        rho_next = 1.0 / (2.0 * sigma - rho)
        pairs.append((rho_next * rho, 2.0 * rho_next / HALF))
        rho = rho_next
    return pairs


def halves(x):
    high = x.astype(jnp.bfloat16)
    return high, (x - high.astype(jnp.float32)).astype(jnp.bfloat16)


def product(left, x):
    high, low = halves(x)
    right = jnp.concatenate([high, low, high], axis=0)
    return jnp.dot(left, right, preferred_element_type=jnp.float32)


def store_left(out, rows, x):
    high, low = halves(x)
    width = x.shape[1]
    for place, piece in enumerate((high, high, low)):
        out[rows, place * width : (place + 1) * width] = piece


def take(tile, lane):
    index = jnp.broadcast_to(lane, tile.shape)
    return jnp.take_along_axis(tile, index, axis=1, mode="promise_in_bounds")


def pick(tiles, at, lane):
    out = jnp.zeros(tiles[0].shape, tiles[0].dtype)
    for number, tile in enumerate(tiles):
        out = jnp.where(at == number, take(tile, lane), out)
    return out


def lanes(rows=1):
    return lax.broadcasted_iota(jnp.int32, (rows, LANES), 1)


def cols(j, width, base=None):
    size, start = (width, j * width) if base is None else (LANES, j * width + base)
    return pl.ds(start if isinstance(j, int) else pl.multiple_of(start, LANES), size)


def over(blocks, body):
    if blocks <= 4:
        for j in range(blocks):
            body(j)
    else:
        lax.fori_loop(0, blocks, lambda j, carry: (body(j), carry)[1], 0)


def own_place():
    me = lax.axis_index("sub")
    return jnp.right_shift(me, 1), jnp.bitwise_and(me, 1)


def trace_tiles(traces):
    points = traces.shape[0] // FACES
    return [
        traces[f * points : (f + 1) * points, h : h + LANES]
        for f in range(FACES)
        for h in range(0, traces.shape[1], LANES)
    ]


def faces(tiles_of, shape):
    return jnp.concatenate(
        [
            jnp.concatenate([tiles_of(f, h) for h in range(0, shape, LANES)], axis=1)
            for f in range(FACES)
        ],
        axis=0,
    )


def send(j, traces, sub_ref, rim_ref, sub_out, rim_out, width, rims):
    tiles = trace_tiles(traces)
    for h in range(0, width, LANES):
        columns = sub_ref[:, cols(j, width, h)]
        sub_out[:, cols(j, width, h)] = pick(
            tiles, jnp.right_shift(columns, 7), jnp.bitwise_and(columns, LANES - 1)
        )
    group = LANES // rims
    tile = cols(j // group, LANES)
    columns = rim_ref[:, tile]
    rim = pick(tiles, jnp.right_shift(columns, 7), jnp.bitwise_and(columns, LANES - 1))
    mine = lanes() // rims == j % group
    rim_out[:, tile] = jnp.where(mine, rim, rim_out[:, tile])


def prep_kernel(map_ref, stiff_ref, t_out, tt_out, k_out):
    modes, rows = map_ref.shape
    transposed = map_ref[...]
    store_left(tt_out, slice(0, modes), transposed)
    store_left(t_out, slice(0, rows), transposed.T)
    for k in range(2):
        store_left(k_out, slice(k * modes, (k + 1) * modes), stiff_ref[k])


def prep_coarse_kernel(restriction_ref, stiff_ref, down_out, up_out, c_out):
    modes = stiff_ref.shape[0]
    store_left(c_out, slice(0, modes), stiff_ref[...])
    for o in range(OCTANTS):
        rows = slice(o * modes, (o + 1) * modes)
        store_left(down_out, rows, restriction_ref[o])
        store_left(up_out, rows, restriction_ref[o].T)


def pack_kernel(b_ref, cond_ref, mat_ref, face_ref, sub_ref, rim_ref, size_ref, coarse_ref, out):
    modes, count = b_ref.shape
    out[modes:, :] = jnp.zeros((out.shape[0] - modes, count), jnp.float32)
    out[:modes, :] = b_ref[...]
    out[modes : modes + 1, :] = cond_ref[...]
    out[modes + 1 : modes + 2, :] = mat_ref[...].astype(jnp.float32)
    out[modes + 2 : modes + 8, :] = face_ref[...].astype(jnp.float32)
    out[modes + 8 : modes + 9, : rim_ref.shape[1]] = rim_ref[...].astype(jnp.float32)
    out[modes + 9 : modes + 10, : size_ref.shape[1]] = size_ref[...].astype(jnp.float32)
    out[modes + 10 : modes + 11, : coarse_ref.shape[1]] = coarse_ref[...]
    width = sub_ref.shape[1]
    for at, h in enumerate(range(0, width, count)):
        piece = sub_ref[:, h : min(h + count, width)].astype(jnp.float32)
        out[modes + 11 + at : modes + 12 + at, : piece.shape[1]] = piece


def start_kernel(blocks, width, rims, *refs):
    gathered, refs = refs[:blocks], refs[blocks:]
    stiff_ref, map_ref, t_ref = refs[:3]
    b_out, ig_out, meta_out, lane_out, at_out, far_out, sub_out, rim_out, size_out, coarse_out = refs[3:13]
    p_out, tr_out, subs_out, rims_out, held = refs[13:]
    modes, count = map_ref.shape[0], gathered[0].shape[1]
    chip, core = own_place()
    for k, ref in enumerate(gathered):
        held[jnp.bitwise_xor(chip, k)] = ref[...]
    eye = lax.broadcasted_iota(jnp.int32, (modes, modes), 0) == lax.broadcasted_iota(
        jnp.int32, (modes, modes), 1
    )
    diagonals = [
        jnp.sum(jnp.where(eye, stiff_ref[k], 0.0), axis=1, keepdims=True) for k in range(2)
    ]
    squares = PENALTY * jnp.sum(map_ref[...] * map_ref[...], axis=1, keepdims=True)
    own_tiles = FACES * count // LANES
    sub_tiles = width // LANES
    rim_out[...] = jnp.zeros(rim_out.shape, jnp.int32)
    rims_out[...] = jnp.zeros(rims_out.shape, jnp.float32)
    peers = blocks * CORES
    slots = width // peers
    group = LANES // rims

    def body(j):
        b = held[j, :modes, :]
        cond = held[j, modes : modes + 1, :]
        mat = held[j, modes + 1 : modes + 2, :]
        b_out[:, cols(j, count)] = b
        meta_out[0:1, cols(j, count)] = cond
        meta_out[1:2, cols(j, count)] = mat
        column = held[j, modes + 2 : modes + 8, :].astype(jnp.int32)
        lane = jnp.bitwise_and(column, LANES - 1)
        at = jnp.right_shift(column, 7)
        lane_out[0:FACES, cols(j, count)] = lane
        at_out[0:FACES, cols(j, count)] = at
        remote = column - own_tiles * LANES
        other = jnp.bitwise_and(lax.div(lane, jnp.int32(slots)), 1) != core
        sub = jnp.logical_and(jnp.logical_and(at >= own_tiles, at < own_tiles + sub_tiles), other)
        rim = jnp.logical_and(at == own_tiles + sub_tiles, lane < rims)
        nothing = slots * (core + CORES)
        far_out[0:FACES, cols(j, count)] = jnp.where(
            sub, remote, jnp.where(rim, lane + slots * core, nothing)
        )
        for h in range(0, width, LANES):
            row = modes + 11 + h // count
            piece = held[j, row : row + 1, h % count : h % count + LANES]
            sub_out[:, cols(j, width, h)] = piece.astype(jnp.int32)
        row = jnp.broadcast_to(held[j, modes + 8 : modes + 9, :LANES], (8, LANES))
        row = pltpu.roll(row, (j % group) * rims, 1)[0:1].astype(jnp.int32)
        tile = cols(j // group, LANES)
        rim_out[:, tile] = jnp.where(lanes() // rims == j % group, row, rim_out[:, tile])
        size_out[pl.ds(j, 1), :] = held[j, modes + 9 : modes + 10, :LANES].astype(jnp.int32)
        coarse_out[pl.ds(j, 1), :] = held[j, modes + 10 : modes + 11, :LANES]
        inverse = 1.0 / (cond * jnp.where(mat == 1.0, diagonals[1], diagonals[0]) + squares)
        ig_out[:, cols(j, count)] = inverse
        p = b * inverse * (1.0 / CENTER)
        p_out[:, cols(j, count)] = p
        traces = product(t_ref[...], p)
        tr_out[:, cols(j, count)] = traces
        send(j, traces, sub_out, rim_out, subs_out, rims_out, width, rims)

    over(blocks, body)


def sub_tiles_of(j, sends_ref, core, width, blocks):
    slots = width // (blocks * CORES)
    pairs = LANES // slots // CORES
    lane = lanes()
    mine = lax.axis_index("sub") % CORES
    source = (CORES * (j % pairs) + mine) * slots + lane % slots
    tiles = []
    for t in range(width // LANES):
        tile = None
        for i in range(pairs):
            sent = sends_ref[:, cols(j // pairs, LANES, (pairs * t + i) * width)]
            there = take(sent, source)
            there = jnp.where(lane // slots == CORES * i + core, there, 0.0)
            tile = there if tile is None else tile + there
        tiles.append(tile)
    return tiles


def local_kernel(only_own, blocks, width, first, *refs):
    p_ref, tr_ref, subs_ref, meta_ref, lane_ref, at_ref, tt_ref, k_ref = refs[:8]
    refs = refs[8:]
    if not first:
        x_ref, refs = refs[0], refs[1:]
    base_out, x_out = refs
    modes = p_ref.shape[0]
    chip, core = own_place()
    count = x_out.shape[1]

    def body(j, out):
        traces = tr_ref[:, cols(j, count)]
        tiles = trace_tiles(traces) + sub_tiles_of(j, subs_ref, core, width, blocks)

        def tile(f, h):
            return pick(tiles, at_rows[f : f + 1, h : h + LANES], lane_rows[f : f + 1, h : h + LANES])

        at_rows, lane_rows = at_ref[:, cols(j, count)], lane_ref[:, cols(j, count)]
        seen = faces(tile, count)
        p = p_ref[:, cols(j, count)]
        both = product(k_ref[...], p)
        meta = meta_ref[:, cols(j, count)]
        own = meta[0:1] * jnp.where(meta[1:2] == 1.0, both[modes:], both[:modes])
        base_out[:, out] = own + PENALTY * product(tt_ref[...], traces - seen)

    if only_own:
        body(chip, slice(0, count))
    else:
        over(blocks, lambda j: body(j, cols(j, count)))
    p = p_ref[:, cols(chip, count)]
    x_out[...] = p if first else x_ref[...] + p


def rim_tiles(one_ref, two_ref, rims):
    segment, segments = lax.axis_index("blk"), lax.axis_size("blk")
    odd = segment % 2 == 1
    lane = lanes()
    tiles = []
    for h in range(0, one_ref.shape[1], LANES):
        one = take(one_ref[:, h : h + LANES], jnp.bitwise_xor(lane, rims // 2))
        two = take(two_ref[:, h : h + LANES], jnp.bitwise_xor(lane, rims // 2))
        low = jnp.where(segment == 0, 0.0, jnp.where(odd, one, two))
        high = jnp.where(segment == segments - 1, 0.0, jnp.where(odd, two, one))
        tiles.append(jnp.where(lane % rims < rims // 2, low, high))
    return tiles


def finish_kernel(kind, coefficients, blocks, width, rims, *refs):
    r_ref, base_ref, swapped_ref, one_ref, two_ref, far_ref, tt_ref = refs[:7]
    refs = list(refs[7:])
    modes = r_ref.shape[0]
    chip, core = own_place()
    slots = width // (blocks * CORES)
    group = LANES // rims
    lane = lanes()
    rim = rim_tiles(one_ref, two_ref, rims)
    if kind == "step":
        p_ref = refs.pop(0)
    if kind in ("step", "first"):
        ig_ref, t_ref, sub_ref, rim_ref, r_out, p_out, tr_out, subs_out, rims_out = refs
        rims_out[...] = jnp.zeros(rims_out.shape, jnp.float32)
    elif kind == "frame":
        r_out, head_out = refs
        head_out[...] = jnp.zeros(head_out.shape, jnp.float32)
    else:
        r_out = refs[0]
    count = r_out.shape[1] if kind == "last" else r_out.shape[1] // blocks

    def body(j):
        tiles = sub_tiles_of(j, swapped_ref, 1 - core, width, blocks)
        if len(rim) == 1:
            mine = rim[0]
        else:
            mine = rim[0]
            for t in range(1, len(rim)):
                mine = jnp.where(j // group == t, rim[t], mine)
        mine = pltpu.roll(mine, (slots * core - (j % group) * rims) % LANES, 1)
        tiles[0] = jnp.where(lane // slots == core, mine, tiles[0])
        far = far_ref[:, cols(j, count)]

        def tile(f, h):
            column = far[f : f + 1, h : h + LANES]
            if len(tiles) == 1:
                return take(tiles[0], column)
            return pick(tiles, jnp.right_shift(column, 7), jnp.bitwise_and(column, LANES - 1))

        here = cols(j, count)
        base = base_ref[...] if kind == "last" else base_ref[:, here]
        residual = r_ref[:, here] - base + PENALTY * product(tt_ref[...], faces(tile, count))
        if kind == "last":
            r_out[...] = residual
            return
        r_out[:, here] = residual
        if kind == "frame":
            heads = LANES // HEAD
            spot = cols(j // heads, LANES)
            moved = pltpu.roll(residual[:, :LANES], (j % heads) * HEAD, 1)
            head_out[:, spot] = jnp.where(lane // HEAD == j % heads, moved, head_out[:, spot])
            return
        p = coefficients[1] * (residual * ig_ref[:, here])
        if kind == "step":
            p = p + coefficients[0] * p_ref[:, here]
        p_out[:, here] = p
        traces = product(t_ref[...], p)
        tr_out[:, here] = traces
        send(j, traces, sub_ref, rim_ref, subs_out, rims_out, width, rims)

    if kind == "last":
        body(chip)
    else:
        over(blocks, body)


def layout_kernel(blocks, parents, size_ref, gather_out, parent_out, octant_out):
    row = lax.broadcasted_iota(jnp.int32, (parents, LANES), 0)
    lane = lanes(parents)
    pairs = LANES // parents
    group = jnp.bitwise_and(lane, parents - 1)
    half = jnp.right_shift(lanes(), parents.bit_length() - 1)
    count = parent_out.shape[1] // blocks

    def body(j):
        sizes = jnp.broadcast_to(size_ref[pl.ds(j, 1), :], (parents, LANES))
        size = jnp.sum(jnp.where(row == lane, sizes, 0), axis=1, keepdims=True)
        end = jnp.sum(jnp.where(lane <= row, sizes, 0), axis=1, keepdims=True)
        size_row = jnp.sum(jnp.where(row == group, size, 0), axis=0, keepdims=True)
        start_row = jnp.sum(jnp.where(row < group, size, 0), axis=0, keepdims=True)
        for i in range(OCTANTS // pairs):
            octant = pairs * i + half
            place = jnp.bitwise_and(start_row + octant + HEAD, count - 1)
            gather_out[i : i + 1, cols(j, LANES)] = jnp.where(octant < size_row, place, -1)
        for h in range(0, count, LANES):
            position = jnp.bitwise_and(lane + (h - HEAD), count - 1)
            before = end <= position
            parent = jnp.sum(before.astype(jnp.int32), axis=0, keepdims=True)
            start = jnp.sum(jnp.where(before, size, 0), axis=0, keepdims=True)
            parent_out[:, cols(j, count, h)] = parent + parents * (j % pairs)
            octant_out[:, cols(j, count, h)] = position[0:1] - start

    over(blocks, body)


def heads_of(j, swapped_ref, cross_ref, by, blocks):
    chip, core = own_place()
    heads = LANES // HEAD
    lane = lanes()
    apart = core if by == 1 else 1 - core
    source = j + by * apart
    inside = jnp.logical_and(source >= 0, source < blocks)
    at = jnp.clip(source, 0, blocks - 1)
    edge = 0 if by == 1 else blocks - 1
    tile = pl.ds(pl.multiple_of((at // heads) * LANES, LANES), LANES)
    near = pltpu.roll(swapped_ref[:, tile], (LANES - (at % heads) * HEAD) % LANES, 1)
    cross = cross_ref[:, (edge // heads) * LANES : (edge // heads + 1) * LANES]
    if edge % heads:
        cross = pltpu.roll(cross, LANES - (edge % heads) * HEAD, 1)
    segment, segments = lax.axis_index("blk"), lax.axis_size("blk")
    outside = segment == (segments - 1 if by == 1 else 0)
    cross = jnp.where(outside, 0.0, cross)
    return jnp.where(lane < HEAD, jnp.where(inside, near, cross), 0.0)


def coarse_kernel(
    blocks, parents, r_ref, swapped_ref, cross_ref, gather_ref, parent_ref, octant_ref, cond_ref, stiff_ref,
    down_ref, up_ref, c_ref, field_out, tail_out, right, field_ref, lifted,
):
    modes = r_ref.shape[0]
    count = r_ref.shape[1] // blocks
    lane = lanes()
    pairs = LANES // parents

    def restrict(j):
        arriving = heads_of(j, swapped_ref, cross_ref, 1, blocks)
        sources = [r_ref[:, cols(j, count, h)] for h in range(0, count, LANES)]
        sources[0] = jnp.where(lane < HEAD, arriving, sources[0])
        sums = [None] * pairs
        for i in range(OCTANTS // pairs):
            place = gather_ref[i : i + 1, cols(j, LANES)]
            children = pick(sources, jnp.right_shift(place, 7), jnp.bitwise_and(place, LANES - 1))
            both = product(down_ref[pairs * i * modes : pairs * (i + 1) * modes, :], children)
            for k in range(pairs):
                one = both[k * modes : (k + 1) * modes]
                sums[k] = one if sums[k] is None else sums[k] + one
        total = sums[0]
        for k in range(1, pairs):
            total = total + pltpu.roll(sums[k], LANES - k * parents, 1)
        tile = cols(j // pairs, LANES)
        moved = pltpu.roll(total, (j % pairs) * parents, 1)
        right[:, tile] = jnp.where(lane // parents == j % pairs, moved, right[:, tile])

    right[...] = jnp.zeros(right.shape, jnp.float32)
    over(blocks, restrict)
    eye = lax.broadcasted_iota(jnp.int32, (modes, modes), 0) == lax.broadcasted_iota(
        jnp.int32, (modes, modes), 1
    )
    diagonal = jnp.sum(jnp.where(eye, stiff_ref[...], 0.0), axis=1, keepdims=True)

    def solve(t):
        scale = jnp.zeros((1, LANES), jnp.float32)
        for k in range(pairs):
            row = jnp.broadcast_to(cond_ref[pl.ds(pairs * t + k, 1), :], (8, LANES))
            row = pltpu.roll(row, k * parents, 1)[0:1] if k else row[0:1]
            scale = jnp.where(lane // parents == k, row, scale)
        inverse = 1.0 / (scale * diagonal + 2.0 * COUPLING)
        residual = right[:, cols(t, LANES)]
        p = residual * inverse * (1.0 / CENTER)
        field = p
        for before, correct in steps(KC - 1):
            left = jnp.where(lane % parents == 0, 0.0, pltpu.roll(p, 1, 1))
            after = jnp.where(lane % parents == parents - 1, 0.0, pltpu.roll(p, LANES - 1, 1))
            residual = residual - (
                scale * product(c_ref[...], p) + COUPLING * (2.0 * p - left - after)
            )
            p = before * p + correct * (residual * inverse)
            field = field + p
        lifted[:, cols(t, LANES)] = product(up_ref[...], field)

    over(blocks // pairs, solve)
    tail_out[...] = jnp.zeros(tail_out.shape, jnp.float32)
    heads = LANES // HEAD

    def prolong(j):
        sources = [lifted[o * modes : (o + 1) * modes, cols(j // pairs, LANES)] for o in range(OCTANTS)]
        for h in range(0, count, LANES):
            parent, octant = parent_ref[:, cols(j, count, h)], octant_ref[:, cols(j, count, h)]
            out = pick(sources, octant, parent)
            field_out[:, cols(j, count, h)] = out
            if h == 0:
                spot = cols(j // heads, LANES)
                moved = pltpu.roll(out, (j % heads) * HEAD, 1)
                tail_out[:, spot] = jnp.where(lane // HEAD == j % heads, moved, tail_out[:, spot])

    over(blocks, prolong)


def middle_kernel(
    blocks, width, rims, field_ref, swapped_ref, cross_ref, t_ref, sub_ref, rim_ref, p_out, tr_out, subs_out, rims_out
):
    count = field_ref.shape[1] // blocks
    lane = lanes()
    rims_out[...] = jnp.zeros(rims_out.shape, jnp.float32)

    def body(j):
        arriving = heads_of(j, swapped_ref, cross_ref, -1, blocks)
        field = field_ref[:, cols(j, count)]
        first = jnp.where(lane < HEAD, arriving, field[:, :LANES])
        field = jnp.concatenate([first, field[:, LANES:]], axis=1)
        p_out[:, cols(j, count)] = field
        traces = product(t_ref[...], field)
        tr_out[:, cols(j, count)] = traces
        send(j, traces, sub_ref, rim_ref, subs_out, rims_out, width, rims)

    over(blocks, body)


def call(limit, kernel, outs, *args, scratch=()):
    return pl.pallas_call(
        kernel,
        out_shape=[jax.ShapeDtypeStruct(shape, kind) for shape, kind in outs],
        in_specs=[pl.BlockSpec(memory_space=pltpu.VMEM)] * len(args),
        out_specs=[pl.BlockSpec(memory_space=pltpu.VMEM)] * len(outs),
        scratch_shapes=list(scratch),
        compiler_params=pltpu.CompilerParams(vmem_limit_bytes=limit),
    )(*args)


def local(
    right_side,
    conductivity,
    material,
    stiffness,
    trace_map,
    face_neighbour,
    sub_sends,
    blk_sends,
    group_sizes,
    coarse_conductivity,
    coarse_stiffness,
    restriction,
):
    f32, i32, bf16 = jnp.float32, jnp.int32, jnp.bfloat16
    modes, count = right_side.shape
    rows = trace_map.shape[0]
    points = rows // FACES
    peers, segments = lax.axis_size("sub"), lax.axis_size("blk")
    blocks = peers // CORES
    width, rims = sub_sends.shape[1], blk_sends.shape[1]
    parents = group_sizes.shape[1]
    total = blocks * count
    limit = (4 << 20) if blocks <= 4 else (40 << 20)
    run = functools.partial(call, limit)

    def pad(size, to):
        return -(-size // to) * to

    rim_width = pad(blocks * rims, LANES)
    head_width = pad(blocks * HEAD, LANES)
    field = ((modes, total), f32)
    block = ((modes, count), f32)
    sends = [((rows, total), f32), ((points, blocks * width), f32), ((points, rim_width), f32)]

    def everywhere(partner):
        pairs = []
        for b in range(segments):
            for s in range(peers):
                other_b, other_s = partner(b, s)
                pairs.append((b * peers + s, other_b * peers + other_s))
        return pairs

    def above_or_below(first):
        def partner(b, s):
            other = b + 1 if b % 2 == first else b - 1
            return (other, s) if 0 <= other < segments else (b, s ^ 2)

        return everywhere(partner)

    def crossing(b, s):
        other = b - 1 if s % 2 == 0 else b + 1
        return (other, s ^ 1) if 0 <= other < segments else (b, s ^ 2)

    both = ("blk", "sub")
    cores = [(s, s ^ 1) for s in range(peers)]
    ones, twos, crossings = above_or_below(0), above_or_below(1), everywhere(crossing)

    def exchange(subs, rim):
        one = lax.ppermute(rim, both, ones)
        two = lax.ppermute(rim, both, twos)
        return [lax.ppermute(subs, "sub", cores), one, two]

    def shift(heads):
        return lax.ppermute(heads, "sub", cores), lax.ppermute(heads, both, crossings)

    map_t = trace_map.T
    t3, tt3, k3 = run(
        prep_kernel,
        [((rows, 3 * modes), bf16), ((modes, 3 * rows), bf16), ((2 * modes, 3 * modes), bf16)],
        map_t, stiffness,
    )
    height = pad(modes + 11 + pad(width, count) // count, 8)
    (packed,) = run(
        pack_kernel,
        [((height, count), f32)],
        right_side, conductivity.reshape(1, count), material.reshape(1, count), face_neighbour, sub_sends, blk_sends,
        group_sizes, coarse_conductivity.reshape(1, -1),
    )
    gathered = [packed] + [
        lax.ppermute(packed, "sub", [(s, s ^ (CORES * k)) for s in range(peers)]) for k in range(1, blocks)
    ]
    b, inverse, meta, lane, at, far, subs, rim, sizes, coarse_cond, p, traces, *out = run(
        functools.partial(start_kernel, blocks, width, rims),
        [
            field, field, ((8, total), f32), ((8, total), i32), ((8, total), i32), ((8, total), i32),
            ((1, blocks * width), i32), ((1, rim_width), i32), ((blocks, LANES), i32), ((blocks, LANES), f32),
            field, *sends,
        ],
        *gathered, stiffness, map_t, t3,
        scratch=[pltpu.VMEM((blocks, height, count), f32)],
    )

    def part(p, traces, subs_sent, x, only_own=False):
        args = [p, traces, subs_sent, meta, lane, at, tt3, k3] + ([] if x is None else [x])
        kernel = functools.partial(local_kernel, only_own, blocks, width, x is None)
        return run(kernel, [block if only_own else field, block], *args)

    def finish(kind, coefficients, r, base, got, p=None):
        args = [r, base, *got, far, tt3]
        if kind == "last":
            outs = [block]
        elif kind == "frame":
            outs = [field, ((modes, head_width), f32)]
        else:
            args += ([p] if kind == "step" else []) + [inverse, t3, subs, rim]
            outs = [field, field, *sends]
        return run(functools.partial(finish_kernel, kind, coefficients, blocks, width, rims), outs, *args)

    gather, parent, octant = run(
        functools.partial(layout_kernel, blocks, parents),
        [((OCTANTS * parents // LANES, blocks * LANES), i32), ((1, total), i32), ((1, total), i32)],
        sizes,
    )
    down3, up3, c3 = run(
        prep_coarse_kernel,
        [((OCTANTS * modes, 3 * modes), bf16), ((OCTANTS * modes, 3 * modes), bf16), ((modes, 3 * modes), bf16)],
        restriction, coarse_stiffness,
    )

    r, x = b, None
    pairs = steps(KF)
    for step in range(KF):
        got = exchange(*out)
        base, x = part(p, traces, out[0], x)
        if step < KF - 1:
            r, p, traces, *out = finish("step", pairs[step], r, base, got, p)
    r, heads = finish("frame", None, r, base, got)

    correction, tails = run(
        functools.partial(coarse_kernel, blocks, parents),
        [field, ((modes, head_width), f32)],
        r, *shift(heads), gather, parent, octant, coarse_cond, coarse_stiffness, down3, up3, c3,
        scratch=[
            pltpu.VMEM((modes, blocks * parents), f32),
            pltpu.VMEM((8, LANES), f32),
            pltpu.VMEM((OCTANTS * modes, blocks * parents), f32),
        ],
    )
    p, traces, *out = run(
        functools.partial(middle_kernel, blocks, width, rims), [field, *sends], correction, *shift(tails), t3, subs, rim
    )

    got = exchange(*out)
    base, x = part(p, traces, out[0], x)
    r, p, traces, *out = finish("first", (0.0, 1.0 / CENTER), r, base, got)
    for step in range(KF):
        got = exchange(*out)
        base, x = part(p, traces, out[0], x, step == KF - 1)
        if step < KF - 1:
            r, p, traces, *out = finish("step", pairs[step], r, base, got, p)
    (residual,) = finish("last", None, r, base, got)
    return x, residual


def solution(mesh):
    in_specs = (
        P(None, ("blk", "sub")),
        P(("blk", "sub")),
        P(("blk", "sub")),
        P(),
        P(),
        P(None, ("blk", "sub")),
        P(("blk", "sub"), None),
        P(("blk", "sub"), None),
        P(("blk", "sub"), None),
        P(("blk", "sub")),
        P(),
        P(),
    )
    out_specs = (P(None, ("blk", "sub")), P(None, ("blk", "sub")))
    return jax.shard_map(local, mesh=mesh, in_specs=in_specs, out_specs=out_specs, check_vma=False)
```

time: 163 us -> 68.1 us (0.42)
  starting transfers between devices: 73 us -> 18.4 us
  local copies, waits for them, and re-layouts: 43.4 us -> 2.25 us
  Pallas kernels: 0 us -> 26.6 us
  other arithmetic: 13.8 us -> 0 us
  matrix products: 10.1 us -> 0 us
    ppermute x16 -> x28, starting transfers between devices: 49.1 us -> 18.4 us  [the longest x7 8.05 us: exchange(): one = lax.ppermute(rim, both, ones)]
    gather x23 -> x0, local copies, waits for them, and re-layouts: 28.3 us -> none  [the longest x7 18.2 us: fine_apply(): seen = table[:, columns]]
    pallas_call x0 -> x21, Pallas kernels: none -> 26.6 us  [call(): pl.pallas_call(kernel, out_shape=[jax.ShapeDtypeStruct(shape, kind) for s...]
    all_to_all x7 -> x0, starting transfers between devices: 23.9 us -> none  [fine_apply(): lax.all_to_all(outgoing, 'sub', split_axis=0, concat_axis=0, tiled=True)]
    ppermute x16 -> x28, waiting for transfers between devices: 1.49 us -> 19.6 us  [the longest x7 6.59 us: exchange(): two = lax.ppermute(rim, both, twos)]
    all_to_all x7 -> x0, waiting for transfers between devices: 18 us -> none  [fine_apply(): lax.all_to_all(outgoing, 'sub', split_axis=0, concat_axis=0, tiled=True)]
    dot_general x35 -> x0, matrix products: 10.1 us -> none  [matmul(): return jnp.dot(left, right, precision=HIGHEST)]
    ppermute x14 -> x0, other arithmetic: 9.94 us -> none  [the longest x7 4.99 us: extended(): after = lax.ppermute(leading, axis, down)]
  transfers between devices with their start and end apart: 23 -> 28, of which waited for: 9 -> 17; matrix products, arithmetic and copies ran while one was open for 10% -> 0% of each run, Pallas kernels for 0% -> 21%
where the time goes in v2:
time: 68.1 us; the launch traced here: 67.9 us
  Pallas kernels  26.6 us (39%)
  waiting for transfers between devices  19.6 us (29%)
  starting transfers between devices  18.4 us (27%)
  local copies, waits for them, and re-layouts  2.25 us (3%)
  between operations  0.89 us (1%)
    pallas_call x21, Pallas kernels, call(): pl.pallas_call(kernel, out_shape=[jax.ShapeDtypeStruct(shape, kind) for s...  26.6 us
    ppermute x7, starting transfers between devices, exchange(): one = lax.ppermute(rim, both, ones)  8.05 us
    ppermute x7, waiting for transfers between devices, exchange(): two = lax.ppermute(rim, both, twos)  6.59 us
    ppermute x2, waiting for transfers between devices, shift(): lax.ppermute(heads, both, crossings)  5.61 us
    ppermute x3, waiting for transfers between devices, local(): lax.ppermute(packed, 'sub', [(s, s ^ CORES * k) for s in range(peers)])  5.15 us
    ppermute x3, starting transfers between devices, local(): lax.ppermute(packed, 'sub', [(s, s ^ CORES * k) for s in range(peers)])  4.54 us
    ppermute x7, starting transfers between devices, exchange(): two = lax.ppermute(rim, both, twos)  3.86 us
    unnamed x24, local copies, waits for them, and re-layouts  2.25 us
  transfers between devices with their start and end apart: 28, of which 17 were waited for; matrix products, arithmetic and copies ran while one was open for 0% of the time, Pallas kernels for 21%

profile of v2, /device:TPU:0, one launch (start us, length us, event | category | flops | bytes accessed | tf_op | source)
XLA Modules:
  0.0 67.9 jit_solution(16174565471842864361)
XLA Ops:
  0.7 0.6 copy-done.11
  1.4 0.8 %copy-done.4 = f32[64,256]{1,0:T(8,128)S(1)} copy-done((f32[64,256]{1,0:T(8,128)S(1)}, f32[64,256]{1,0:T(8,128)}, u32[]{:S(2)}) %copy-start.4) | copy-done | bytes 65560
  2.2 0.7 %copy-done.5 = s32[6,256]{1,0:T(8,128)S(1)} copy-done((s32[6,256]{1,0:T(8,128)S(1)}, s32[6,256]{1,0:T(8,128)}, u32[]{:S(2)}) %copy-start.5) | copy-done | bytes 6168
  2.9 3.0 %collective-permute-start = (f32[80,256]{1,0:T(8,128)S(1)}, f32[80,256]{1,0:T(8,128)S(1)}, u32[]{:S(2)}, u32[]{:S(2)}) collective-permute-start(f32[80,256]{1,0:T(8,128)S(1)} %shard_map.131.refs_0_), channel_id=1, source_target_pairs={{0,2},{1,3},{2,0},{3,1},{4,6},{5,7},{6,4},{7,5},{8,10},{9,11},{10,... | collective-permute-start | bytes 245768 | tf_op jit(solution)/shard_map/ppermute | solution.py:585
  5.9 1.5 %collective-permute-start.1 = (f32[80,256]{1,0:T(8,128)S(1)}, f32[80,256]{1,0:T(8,128)S(1)}, u32[]{:S(2)}, u32[]{:S(2)}) collective-permute-start(f32[80,256]{1,0:T(8,128)S(1)} %shard_map.131.refs_0_), channel_id=1, source_target_pairs={{0,4},{1,5},{2,6},{3,7},{4,0},{5,1},{6,2},{7,3},{8,12},{9,13},{10,... | collective-permute-start | bytes 245768 | tf_op jit(solution)/shard_map/ppermute | solution.py:585
  7.6 1.0 %collective-permute-done.refs_1_ = f32[80,256]{1,0:T(8,128)S(1)} collective-permute-done((f32[80,256]{1,0:T(8,128)S(1)}, f32[80,256]{1,0:T(8,128)S(1)}, u32[]{:S(2)}, u32[]{:S(2)}) %collective-permute-start) | collective-permute-done | bytes 81952 | tf_op jit(solution)/shard_map/ppermute | solution.py:585
  8.6 2.6 %collective-permute-done.1.refs_2_ = f32[80,256]{1,0:T(8,128)S(1)} collective-permute-done((f32[80,256]{1,0:T(8,128)S(1)}, f32[80,256]{1,0:T(8,128)S(1)}, u32[]{:S(2)}, u32[]{:S(2)}) %collective-permute-start.1) | collective-permute-done | bytes 81952 | tf_op jit(solution)/shard_map/ppermute | solution.py:585
  11.3 1.5 %collective-permute-done.2.refs_3_ = f32[80,256]{1,0:T(8,128)S(1)} collective-permute-done((f32[80,256]{1,0:T(8,128)S(1)}, f32[80,256]{1,0:T(8,128)S(1)}, u32[]{:S(2)}, u32[]{:S(2)}) %collective-permute-start.2) | collective-permute-done | bytes 81952 | tf_op jit(solution)/shard_map/ppermute | solution.py:585
  12.8 0.8 %shard_map.133 = (f32[64,1024]{1,0:T(8,128)S(1)}, f32[64,1024]{1,0:T(8,128)S(1)}, f32[8,1024]{1,0:T(8,128)S(1)}, s32[8,1024]{1,0:T(8,128)S(1)}, s32[8,1024]{1,0:...) custom-call(f32[80,256]{1,0:T(8,128)S(1)} %shard_map.131.refs_0_, ...), custom_call_target="tpu_custom_call" | custom-call | tf_op jit(solution)/shard_map/pallas_call | solution.py:495
  13.7 1.6 %collective-permute-start.4 = (f32[16,128]{1,0:T(8,128)S(1)}, f32[16,128]{1,0:T(8,128)S(1)}, u32[]{:S(2)}, u32[]{:S(2)}) collective-permute-start(f32[16,128]{1,0:T(8,128)S(1)} %get-tuple-element.83), channel_id=1, source_target_pairs={{0,8},{1,9},{2,10},{3,11},{4,12},{5,13},{6,14},{7,15},{8,0},{9,1},... | collective-permute-start | bytes 24584 | tf_op jit(solution)/shard_map/ppermute | solution.py:564
  15.9 2.0 %shard_map.134 = (f32[64,1024]{1,0:T(8,128)S(1)}, f32[64,256]{1,0:T(8,128)S(1)}) custom-call(f32[64,1024]{1,0:T(8,128)S(1)} %get-tuple-element.74.refs_0_.refs_7_, f32[96,1024]{1,0:T(8,128)S(1)} %get-tuple-element.75.refs_1_, f32[16,512]{1,0:T(8,128)S(1)} %get-tuple-element.76.refs_2_, f32[8,1024]{1,0:T(8,128)S(1)} %get-tuple-element.77.refs_3_, ...), custom_call_target="tpu_custom_call" | custom-call | tf_op jit(solution)/shard_map/pallas_call | solution.py:495
  17.9 1.1 %collective-permute-done.5.refs_4_ = f32[16,128]{1,0:T(8,128)S(1)} collective-permute-done((f32[16,128]{1,0:T(8,128)S(1)}, f32[16,128]{1,0:T(8,128)S(1)}, u32[]{:S(2)}, u32[]{:S(2)}) %collective-permute-start.5) | collective-permute-done | bytes 8224 | tf_op jit(solution)/shard_map/ppermute | solution.py:565
  19.0 1.3 %shard_map.135 = (f32[64,1024]{1,0:T(8,128)S(1)}, f32[64,1024]{1,0:T(8,128)S(1)}, f32[96,1024]{1,0:T(8,128)S(1)}, f32[16,512]{1,0:T(8,128)S(1)}, f32[16,128]{1,0:T(8,128)S(1)}) custom-call(f32[64,1024]{1,0:T(8,128)S(1)} %get-tuple-element.73.refs_0_, f32[64,1024]{1,0:T(8,128)S(1)} %get-tuple-element.82.refs_1_, ...), custom_call_target="tpu_custom_call" | custom-call | tf_op jit(solution)/shard_map/pallas_call | solution.py:495
  20.4 1.6 %collective-permute-start.7 = (f32[16,128]{1,0:T(8,128)S(1)}, f32[16,128]{1,0:T(8,128)S(1)}, u32[]{:S(2)}, u32[]{:S(2)}) collective-permute-start(f32[16,128]{1,0:T(8,128)S(1)} %get-tuple-element.94), channel_id=1, source_target_pairs={{0,8},{1,9},{2,10},{3,11},{4,12},{5,13},{6,14},{7,15},{8,0},{9,1},... | collective-permute-start | bytes 24584 | tf_op jit(solution)/shard_map/ppermute | solution.py:564
  22.0 0.5 collective-permute-start.8
  22.5 2.0 %shard_map.136 = (f32[64,1024]{1,0:T(8,128)S(1)}, f32[64,256]{1,0:T(8,128)S(1)}) custom-call(f32[64,1024]{1,0:T(8,128)S(1)} %get-tuple-element.89.refs_0_.refs_7_, f32[96,1024]{1,0:T(8,128)S(1)} %get-tuple-element.90.refs_1_, f32[16,512]{1,0:T(8,128)S(1)} %get-tuple-element.91.refs_2_, f32[8,1024]{1,0:T(8,128)S(1)} %get-tuple-element.77.refs_3_, ...), custom_call_target="tpu_custom_call" | custom-call | tf_op jit(solution)/shard_map/pallas_call | solution.py:495
  24.5 1.1 %collective-permute-done.8.refs_4_ = f32[16,128]{1,0:T(8,128)S(1)} collective-permute-done((f32[16,128]{1,0:T(8,128)S(1)}, f32[16,128]{1,0:T(8,128)S(1)}, u32[]{:S(2)}, u32[]{:S(2)}) %collective-permute-start.8) | collective-permute-done | bytes 8224 | tf_op jit(solution)/shard_map/ppermute | solution.py:565
  25.6 1.3 %shard_map.137 = (f32[64,1024]{1,0:T(8,128)S(1)}, f32[64,1024]{1,0:T(8,128)S(1)}, f32[96,1024]{1,0:T(8,128)S(1)}, f32[16,512]{1,0:T(8,128)S(1)}, f32[16,128]{1,0:T(8,128)S(1)}) custom-call(f32[64,1024]{1,0:T(8,128)S(1)} %get-tuple-element.88.refs_0_, f32[64,1024]{1,0:T(8,128)S(1)} %get-tuple-element.93.refs_1_, ...), custom_call_target="tpu_custom_call" | custom-call | tf_op jit(solution)/shard_map/pallas_call | solution.py:495
  27.1 0.6 collective-permute-start.10
  28.2 2.0 %shard_map.138 = (f32[64,1024]{1,0:T(8,128)S(1)}, f32[64,256]{1,0:T(8,128)S(1)}) custom-call(f32[64,1024]{1,0:T(8,128)S(1)} %get-tuple-element.96.refs_0_, f32[96,1024]{1,0:T(8,128)S(1)} %get-tuple-element.97.refs_1_, f32[16,512]{1,0:T(8,128)S(1)} %get-tuple-element.98.refs_2_, f32[8,1024]{1,0:T(8,128)S(1)} %get-tuple-element.77.refs_3_, ...), custom_call_target="tpu_custom_call" | custom-call | tf_op jit(solution)/shard_map/pallas_call | solution.py:495
  30.2 0.6 collective-permute-done.10.refs_3_
  31.3 0.7 %shard_map.139 = (f32[64,1024]{1,0:T(8,128)S(1)}, f32[64,128]{1,0:T(8,128)S(1)}) custom-call(f32[64,1024]{1,0:T(8,128)S(1)} %get-tuple-element.95.refs_0_, f32[64,1024]{1,0:T(8,128)S(1)} %get-tuple-element.100.refs_1_, f32[16,512]{1,0:T(8,128)S(1)} %collective-permute-done.9.refs_2_, f32[16,128]{1,0:T(8,128)S(1)} %collective-permute-done.10.refs_3_, ...), custom_call_target="tpu_custom_call" | custom-call | tf_op jit(solution)/shard_map/pallas_call | solution.py:495
  32.1 0.6 collective-permute-start.13
  33.3 2.8 %collective-permute-done.13.cross_ref = f32[64,128]{1,0:T(8,128)S(1)} collective-permute-done((f32[64,128]{1,0:T(8,128)S(1)}, f32[64,128]{1,0:T(8,128)S(1)}, u32[]{:S(2)}, u32[]{:S(2)}) %collective-permute-start.13) | collective-permute-done | bytes 32800 | tf_op jit(solution)/shard_map/ppermute | solution.py:569
  36.1 2.6 %shard_map.142 = (f32[64,1024]{1,0:T(8,128)S(1)}, f32[64,128]{1,0:T(8,128)S(1)}) custom-call(f32[64,1024]{1,0:T(8,128)S(1)} %get-tuple-element.102.r_ref.refs_0_, f32[64,128]{1,0:T(8,128)S(1)} %collective-permute-done.12.swapped_ref, f32[64,128]{1,0:T(8,128)S(1)} %collective-permute-done.13.cross_ref, s32[4,512]{1,0:T(4,128)S(1)} %get-tuple-element.105.gather_ref, ...), custom_call_target="tpu_custom_call" | custom-call | tf_op jit(solution)/shard_map/pallas_call | solution.py:495
  38.9 0.5 collective-permute-start.15
  39.4 0.6 collective-permute-done.14.swapped_ref
  39.9 2.8 %collective-permute-done.15.cross_ref = f32[64,128]{1,0:T(8,128)S(1)} collective-permute-done((f32[64,128]{1,0:T(8,128)S(1)}, f32[64,128]{1,0:T(8,128)S(1)}, u32[]{:S(2)}, u32[]{:S(2)}) %collective-permute-start.15) | collective-permute-done | bytes 32800 | tf_op jit(solution)/shard_map/ppermute | solution.py:569
  42.8 0.7 %shard_map.143 = (f32[64,1024]{1,0:T(8,128)S(1)}, f32[96,1024]{1,0:T(8,128)S(1)}, f32[16,512]{1,0:T(8,128)S(1)}, f32[16,128]{1,0:T(8,128)S(1)}) custom-call(f32[64,1024]{1,0:T(8,128)S(1)} %get-tuple-element.112.field_ref, f32[64,128]{1,0:T(8,128)S(1)} %collective-permute-done.14.swapped_ref, f32[64,128]{1,0:T(8,128)S(1)} %collective-permute-done.15.cross_ref, ...), custom_call_target="tpu_custom_call" | custom-call | tf_op jit(solution)/shard_map/pallas_call | solution.py:495
  43.7 0.7 %collective-permute-start.17 = (f32[16,128]{1,0:T(8,128)S(1)}, f32[16,128]{1,0:T(8,128)S(1)}, u32[]{:S(2)}, u32[]{:S(2)}) collective-permute-start(f32[16,128]{1,0:T(8,128)S(1)} %get-tuple-element.119), channel_id=1, source_target_pairs={{0,8},{1,9},{2,10},{3,11},{4,12},{5,13},{6,14},{7,15},{8,0},{9,1},... | collective-permute-start | bytes 24584 | tf_op jit(solution)/shard_map/ppermute | solution.py:564
  45.0 2.2 %shard_map.144 = (f32[64,1024]{1,0:T(8,128)S(1)}, f32[64,256]{1,0:T(8,128)S(1)}) custom-call(f32[64,1024]{1,0:T(8,128)S(1)} %get-tuple-element.114.refs_0_, f32[96,1024]{1,0:T(8,128)S(1)} %get-tuple-element.115.refs_1_, f32[16,512]{1,0:T(8,128)S(1)} %get-tuple-element.116.refs_2_, f32[8,1024]{1,0:T(8,128)S(1)} %get-tuple-element.77.refs_3_, ...), custom_call_target="tpu_custom_call" | custom-call | tf_op jit(solution)/shard_map/pallas_call | solution.py:495
  47.3 0.7 %collective-permute-done.18.refs_4_ = f32[16,128]{1,0:T(8,128)S(1)} collective-permute-done((f32[16,128]{1,0:T(8,128)S(1)}, f32[16,128]{1,0:T(8,128)S(1)}, u32[]{:S(2)}, u32[]{:S(2)}) %collective-permute-start.18) | collective-permute-done | bytes 8224 | tf_op jit(solution)/shard_map/ppermute | solution.py:565
  48.1 1.3 %shard_map.145 = (f32[64,1024]{1,0:T(8,128)S(1)}, f32[64,1024]{1,0:T(8,128)S(1)}, f32[96,1024]{1,0:T(8,128)S(1)}, f32[16,512]{1,0:T(8,128)S(1)}, f32[16,128]{1,0:T(8,128)S(1)}) custom-call(f32[64,1024]{1,0:T(8,128)S(1)} %get-tuple-element.102.r_ref.refs_0_, f32[64,1024]{1,0:T(8,128)S(1)} %get-tuple-element.118.refs_1_, ...), custom_call_target="tpu_custom_call" | custom-call | tf_op jit(solution)/shard_map/pallas_call | solution.py:495
  49.5 1.3 %collective-permute-start.20 = (f32[16,128]{1,0:T(8,128)S(1)}, f32[16,128]{1,0:T(8,128)S(1)}, u32[]{:S(2)}, u32[]{:S(2)}) collective-permute-start(f32[16,128]{1,0:T(8,128)S(1)} %get-tuple-element.126), channel_id=1, source_target_pairs={{0,8},{1,9},{2,10},{3,11},{4,12},{5,13},{6,14},{7,15},{8,0},{9,1},... | collective-permute-start | bytes 24584 | tf_op jit(solution)/shard_map/ppermute | solution.py:564
  50.8 0.6 collective-permute-start.21
  51.4 2.0 %shard_map.146 = (f32[64,1024]{1,0:T(8,128)S(1)}, f32[64,256]{1,0:T(8,128)S(1)}) custom-call(f32[64,1024]{1,0:T(8,128)S(1)} %get-tuple-element.121.refs_0_.refs_7_, f32[96,1024]{1,0:T(8,128)S(1)} %get-tuple-element.122.refs_1_, f32[16,512]{1,0:T(8,128)S(1)} %get-tuple-element.123.refs_2_, f32[8,1024]{1,0:T(8,128)S(1)} %get-tuple-element.77.refs_3_, ...), custom_call_target="tpu_custom_call" | custom-call | tf_op jit(solution)/shard_map/pallas_call | solution.py:495
  53.4 1.1 %collective-permute-done.21.refs_4_ = f32[16,128]{1,0:T(8,128)S(1)} collective-permute-done((f32[16,128]{1,0:T(8,128)S(1)}, f32[16,128]{1,0:T(8,128)S(1)}, u32[]{:S(2)}, u32[]{:S(2)}) %collective-permute-start.21) | collective-permute-done | bytes 8224 | tf_op jit(solution)/shard_map/ppermute | solution.py:565
  54.5 1.3 %shard_map.147 = (f32[64,1024]{1,0:T(8,128)S(1)}, f32[64,1024]{1,0:T(8,128)S(1)}, f32[96,1024]{1,0:T(8,128)S(1)}, f32[16,512]{1,0:T(8,128)S(1)}, f32[16,128]{1,0:T(8,128)S(1)}) custom-call(f32[64,1024]{1,0:T(8,128)S(1)} %get-tuple-element.120.refs_0_, f32[64,1024]{1,0:T(8,128)S(1)} %get-tuple-element.125.refs_1_, ...), custom_call_target="tpu_custom_call" | custom-call | tf_op jit(solution)/shard_map/pallas_call | solution.py:495
  55.9 0.8 %collective-permute-start.23 = (f32[16,128]{1,0:T(8,128)S(1)}, f32[16,128]{1,0:T(8,128)S(1)}, u32[]{:S(2)}, u32[]{:S(2)}) collective-permute-start(f32[16,128]{1,0:T(8,128)S(1)} %get-tuple-element.133), channel_id=1, source_target_pairs={{0,8},{1,9},{2,10},{3,11},{4,12},{5,13},{6,14},{7,15},{8,0},{9,1},... | collective-permute-start | bytes 24584 | tf_op jit(solution)/shard_map/ppermute | solution.py:564
  56.7 0.6 collective-permute-start.24
  57.3 2.0 %shard_map.148 = (f32[64,1024]{1,0:T(8,128)S(1)}, f32[64,256]{1,0:T(8,128)S(1)}) custom-call(f32[64,1024]{1,0:T(8,128)S(1)} %get-tuple-element.128.refs_0_.refs_7_, f32[96,1024]{1,0:T(8,128)S(1)} %get-tuple-element.129.refs_1_, f32[16,512]{1,0:T(8,128)S(1)} %get-tuple-element.130.refs_2_, f32[8,1024]{1,0:T(8,128)S(1)} %get-tuple-element.77.refs_3_, ...), custom_call_target="tpu_custom_call" | custom-call | tf_op jit(solution)/shard_map/pallas_call | solution.py:495
  59.6 0.7 %collective-permute-done.24.refs_4_ = f32[16,128]{1,0:T(8,128)S(1)} collective-permute-done((f32[16,128]{1,0:T(8,128)S(1)}, f32[16,128]{1,0:T(8,128)S(1)}, u32[]{:S(2)}, u32[]{:S(2)}) %collective-permute-start.24) | collective-permute-done | bytes 8224 | tf_op jit(solution)/shard_map/ppermute | solution.py:565
  60.4 1.3 %shard_map.149 = (f32[64,1024]{1,0:T(8,128)S(1)}, f32[64,1024]{1,0:T(8,128)S(1)}, f32[96,1024]{1,0:T(8,128)S(1)}, f32[16,512]{1,0:T(8,128)S(1)}, f32[16,128]{1,0:T(8,128)S(1)}) custom-call(f32[64,1024]{1,0:T(8,128)S(1)} %get-tuple-element.127.refs_0_, f32[64,1024]{1,0:T(8,128)S(1)} %get-tuple-element.132.refs_1_, ...), custom_call_target="tpu_custom_call" | custom-call | tf_op jit(solution)/shard_map/pallas_call | solution.py:495
  61.8 1.3 %collective-permute-start.26 = (f32[16,128]{1,0:T(8,128)S(1)}, f32[16,128]{1,0:T(8,128)S(1)}, u32[]{:S(2)}, u32[]{:S(2)}) collective-permute-start(f32[16,128]{1,0:T(8,128)S(1)} %get-tuple-element.141), channel_id=1, source_target_pairs={{0,8},{1,9},{2,10},{3,11},{4,12},{5,13},{6,14},{7,15},{8,0},{9,1},... | collective-permute-start | bytes 24584 | tf_op jit(solution)/shard_map/ppermute | solution.py:564
  63.1 0.6 collective-permute-start.27
  63.7 1.3 %shard_map.150 = (f32[64,256]{1,0:T(8,128)S(1)}, f32[64,256]{1,0:T(8,128)}) custom-call(f32[64,1024]{1,0:T(8,128)S(1)} %get-tuple-element.134.refs_0_, f32[96,1024]{1,0:T(8,128)S(1)} %get-tuple-element.135.refs_1_, f32[16,512]{1,0:T(8,128)S(1)} %get-tuple-element.136.refs_2_, f32[8,1024]{1,0:T(8,128)S(1)} %get-tuple-element.77.refs_3_, ...), custom_call_target="tpu_custom_call" | custom-call | tf_op jit(solution)/shard_map/pallas_call | solution.py:495
  65.5 1.3 %collective-permute-done.27.refs_4_ = f32[16,128]{1,0:T(8,128)S(1)} collective-permute-done((f32[16,128]{1,0:T(8,128)S(1)}, f32[16,128]{1,0:T(8,128)S(1)}, u32[]{:S(2)}, u32[]{:S(2)}) %collective-permute-start.27) | collective-permute-done | bytes 8224 | tf_op jit(solution)/shard_map/ppermute | solution.py:565
  66.8 1.1 %shard_map.151 = f32[64,256]{1,0:T(8,128)} custom-call(f32[64,1024]{1,0:T(8,128)S(1)} %get-tuple-element.139.refs_0_, f32[64,256]{1,0:T(8,128)S(1)} %get-tuple-element.140.refs_1_, f32[16,512]{1,0:T(8,128)S(1)} %collective-permute-done.25.refs_2_, f32[16,128]{1,0:T(8,128)S(1)} %collective-permute-done.26.refs_3_, ...), custom_call_target="tpu_custom_call" | custom-call | tf_op jit(solution)/shard_map/pallas_call | solution.py:495
  (53 shorter events, 4.9 us)
Async XLA Ops:
  0.6 0.7 copy-start.11
  0.6 0.7 %copy-start.7 = (s32[256]{0:T(256)S(1)}, s32[256]{0:T(256)}, u32[]{:S(2)}) copy-start(s32[256]{0:T(256)} %param.14) | copy-start | bytes 3076
  0.7 0.7 copy-start.9
  0.7 0.7 copy-start.10
  0.7 0.7 %copy-start.6 = (f32[256]{0:T(256)S(1)}, f32[256]{0:T(256)}, u32[]{:S(2)}) copy-start(f32[256]{0:T(256)} %param.13) | copy-start | bytes 3076
  0.7 0.7 %copy-start.8 = (s32[1,128]{1,0:T(1,128)S(1)}, s32[1,128]{1,0:T(1,128)}, u32[]{:S(2)}) copy-start(s32[1,128]{1,0:T(1,128)} %sub_ref.1) | copy-start | bytes 1540
  1.4 0.8 %copy-start.4 = (f32[64,256]{1,0:T(8,128)S(1)}, f32[64,256]{1,0:T(8,128)}, u32[]{:S(2)}) copy-start(f32[64,256]{1,0:T(8,128)} %b_ref.1) | copy-start | bytes 196612
  2.2 0.7 %copy-start.5 = (s32[6,256]{1,0:T(8,128)S(1)}, s32[6,256]{1,0:T(8,128)}, u32[]{:S(2)}) copy-start(s32[6,256]{1,0:T(8,128)} %face_ref.1) | copy-start | bytes 18436
  2.9 4.6 %copy-start.1 = (f32[2,64,64]{2,1,0:T(8,128)S(1)}, f32[2,64,64]{2,1,0:T(8,128)}, u32[]{:S(2)}) copy-start(f32[2,64,64]{2,1,0:T(8,128)} %refs_4_.1) | copy-start | bytes 98308
  2.9 4.6 %copy-start.3 = (f32[96,64]{0,1:T(8,128)S(1)}, f32[96,64]{0,1:T(8,128)}, u32[]{:S(2)}) copy-start(f32[96,64]{0,1:T(8,128)} %param.16) | copy-start | bytes 73732
  2.9 5.7 %collective-permute-start = (f32[80,256]{1,0:T(8,128)S(1)}, f32[80,256]{1,0:T(8,128)S(1)}, u32[]{:S(2)}, u32[]{:S(2)}) collective-permute-start(f32[80,256]{1,0:T(8,128)S(1)} %shard_map.131.refs_0_), channel_id=1, source_target_pairs={{0,2},{1,3},{2,0},{3,1},{4,6},{5,7},{6,4},{7,5},{8,10},{9,11},{10,... | collective-permute-start | bytes 245768 | tf_op jit(solution)/shard_map/ppermute | solution.py:585
  5.9 5.3 %collective-permute-start.1 = (f32[80,256]{1,0:T(8,128)S(1)}, f32[80,256]{1,0:T(8,128)S(1)}, u32[]{:S(2)}, u32[]{:S(2)}) collective-permute-start(f32[80,256]{1,0:T(8,128)S(1)} %shard_map.131.refs_0_), channel_id=1, source_target_pairs={{0,4},{1,5},{2,6},{3,7},{4,0},{5,1},{6,2},{7,3},{8,12},{9,13},{10,... | collective-permute-start | bytes 245768 | tf_op jit(solution)/shard_map/ppermute | solution.py:585
  7.5 5.3 %collective-permute-start.2 = (f32[80,256]{1,0:T(8,128)S(1)}, f32[80,256]{1,0:T(8,128)S(1)}, u32[]{:S(2)}, u32[]{:S(2)}) collective-permute-start(f32[80,256]{1,0:T(8,128)S(1)} %shard_map.131.refs_0_), channel_id=1, source_target_pairs={{0,6},{1,7},{2,4},{3,5},{4,2},{5,3},{6,0},{7,1},{8,14},{9,15},{10,... | collective-permute-start | bytes 245768 | tf_op jit(solution)/shard_map/ppermute | solution.py:585
  13.6 5.4 %collective-permute-start.3 = (f32[16,512]{1,0:T(8,128)S(1)}, f32[16,512]{1,0:T(8,128)S(1)}, u32[]{:S(2)}, u32[]{:S(2)}) collective-permute-start(f32[16,512]{1,0:T(8,128)S(1)} %get-tuple-element.76.refs_2_), channel_id=1, source_target_pairs={{0,1},{1,0},{2,3},{3,2},{4,5},{5,4},{6,7},{7,6},{8,9},{9,8},{10,11... | collective-permute-start | bytes 98312 | tf_op jit(solution)/shard_map/ppermute | solution.py:566
  13.7 4.2 %collective-permute-start.4 = (f32[16,128]{1,0:T(8,128)S(1)}, f32[16,128]{1,0:T(8,128)S(1)}, u32[]{:S(2)}, u32[]{:S(2)}) collective-permute-start(f32[16,128]{1,0:T(8,128)S(1)} %get-tuple-element.83), channel_id=1, source_target_pairs={{0,8},{1,9},{2,10},{3,11},{4,12},{5,13},{6,14},{7,15},{8,0},{9,1},... | collective-permute-start | bytes 24584 | tf_op jit(solution)/shard_map/ppermute | solution.py:564
  15.3 3.7 %collective-permute-start.5 = (f32[16,128]{1,0:T(8,128)S(1)}, f32[16,128]{1,0:T(8,128)S(1)}, u32[]{:S(2)}, u32[]{:S(2)}) collective-permute-start(f32[16,128]{1,0:T(8,128)S(1)} %get-tuple-element.83), channel_id=1, source_target_pairs={{0,2},{1,3},{2,0},{3,1},{4,6},{5,7},{6,4},{7,5},{8,16},{9,17},{10,... | collective-permute-start | bytes 24584 | tf_op jit(solution)/shard_map/ppermute | solution.py:565
  20.3 5.3 %collective-permute-start.6 = (f32[16,512]{1,0:T(8,128)S(1)}, f32[16,512]{1,0:T(8,128)S(1)}, u32[]{:S(2)}, u32[]{:S(2)}) collective-permute-start(f32[16,512]{1,0:T(8,128)S(1)} %get-tuple-element.91.refs_2_), channel_id=1, source_target_pairs={{0,1},{1,0},{2,3},{3,2},{4,5},{5,4},{6,7},{7,6},{8,9},{9,8},{10,11... | collective-permute-start | bytes 98312 | tf_op jit(solution)/shard_map/ppermute | solution.py:566
  20.4 4.1 %collective-permute-start.7 = (f32[16,128]{1,0:T(8,128)S(1)}, f32[16,128]{1,0:T(8,128)S(1)}, u32[]{:S(2)}, u32[]{:S(2)}) collective-permute-start(f32[16,128]{1,0:T(8,128)S(1)} %get-tuple-element.94), channel_id=1, source_target_pairs={{0,8},{1,9},{2,10},{3,11},{4,12},{5,13},{6,14},{7,15},{8,0},{9,1},... | collective-permute-start | bytes 24584 | tf_op jit(solution)/shard_map/ppermute | solution.py:564
  22.0 3.7 %collective-permute-start.8 = (f32[16,128]{1,0:T(8,128)S(1)}, f32[16,128]{1,0:T(8,128)S(1)}, u32[]{:S(2)}, u32[]{:S(2)}) collective-permute-start(f32[16,128]{1,0:T(8,128)S(1)} %get-tuple-element.94), channel_id=1, source_target_pairs={{0,2},{1,3},{2,0},{3,1},{4,6},{5,7},{6,4},{7,5},{8,16},{9,17},{10,... | collective-permute-start | bytes 24584 | tf_op jit(solution)/shard_map/ppermute | solution.py:565
  27.0 4.3 %collective-permute-start.9 = (f32[16,512]{1,0:T(8,128)S(1)}, f32[16,512]{1,0:T(8,128)S(1)}, u32[]{:S(2)}, u32[]{:S(2)}) collective-permute-start(f32[16,512]{1,0:T(8,128)S(1)} %get-tuple-element.98.refs_2_), channel_id=1, source_target_pairs={{0,1},{1,0},{2,3},{3,2},{4,5},{5,4},{6,7},{7,6},{8,9},{9,8},{10,11... | collective-permute-start | bytes 98312 | tf_op jit(solution)/shard_map/ppermute | solution.py:566
  27.1 3.7 %collective-permute-start.10 = (f32[16,128]{1,0:T(8,128)S(1)}, f32[16,128]{1,0:T(8,128)S(1)}, u32[]{:S(2)}, u32[]{:S(2)}) collective-permute-start(f32[16,128]{1,0:T(8,128)S(1)} %get-tuple-element.101), channel_id=1, source_target_pairs={{0,8},{1,9},{2,10},{3,11},{4,12},{5,13},{6,14},{7,15},{8,0},{9,1},... | collective-permute-start | bytes 24584 | tf_op jit(solution)/shard_map/ppermute | solution.py:564
  27.6 3.7 %collective-permute-start.11 = (f32[16,128]{1,0:T(8,128)S(1)}, f32[16,128]{1,0:T(8,128)S(1)}, u32[]{:S(2)}, u32[]{:S(2)}) collective-permute-start(f32[16,128]{1,0:T(8,128)S(1)} %get-tuple-element.101), channel_id=1, source_target_pairs={{0,2},{1,3},{2,0},{3,1},{4,6},{5,7},{6,4},{7,5},{8,16},{9,17},{10,... | collective-permute-start | bytes 24584 | tf_op jit(solution)/shard_map/ppermute | solution.py:565
  31.3 1.4 %copy-start = (f32[8,64,64]{2,1,0:T(8,128)S(1)}, f32[8,64,64]{2,1,0:T(8,128)}, u32[]{:S(2)}) copy-start(f32[8,64,64]{2,1,0:T(8,128)} %restriction_ref.1) | copy-start | bytes 393220
  31.3 1.4 %copy-start.2 = (f32[64,64]{1,0:T(8,128)S(1)}, f32[64,64]{1,0:T(8,128)}, u32[]{:S(2)}) copy-start(f32[64,64]{1,0:T(8,128)} %stiff_ref.5) | copy-start | bytes 49156
  32.0 1.3 %collective-permute-start.12 = (f32[64,128]{1,0:T(8,128)S(1)}, f32[64,128]{1,0:T(8,128)S(1)}, u32[]{:S(2)}, u32[]{:S(2)}) collective-permute-start(f32[64,128]{1,0:T(8,128)S(1)} %get-tuple-element.103), channel_id=1, source_target_pairs={{0,1},{1,0},{2,3},{3,2},{4,5},{5,4},{6,7},{7,6},{8,9},{9,8},{10,11... | collective-permute-start | bytes 98312 | tf_op jit(solution)/shard_map/ppermute | solution.py:569
  32.1 4.0 %collective-permute-start.13 = (f32[64,128]{1,0:T(8,128)S(1)}, f32[64,128]{1,0:T(8,128)S(1)}, u32[]{:S(2)}, u32[]{:S(2)}) collective-permute-start(f32[64,128]{1,0:T(8,128)S(1)} %get-tuple-element.103), channel_id=1, source_target_pairs={{0,2},{1,8},{2,0},{3,10},{4,6},{5,12},{6,4},{7,14},{8,1},{9,16},{1... | collective-permute-start | bytes 98312 | tf_op jit(solution)/shard_map/ppermute | solution.py:569
  38.7 1.3 %collective-permute-start.14 = (f32[64,128]{1,0:T(8,128)S(1)}, f32[64,128]{1,0:T(8,128)S(1)}, u32[]{:S(2)}, u32[]{:S(2)}) collective-permute-start(f32[64,128]{1,0:T(8,128)S(1)} %get-tuple-element.113), channel_id=1, source_target_pairs={{0,1},{1,0},{2,3},{3,2},{4,5},{5,4},{6,7},{7,6},{8,9},{9,8},{10,11... | collective-permute-start | bytes 98312 | tf_op jit(solution)/shard_map/ppermute | solution.py:569
  38.9 3.9 %collective-permute-start.15 = (f32[64,128]{1,0:T(8,128)S(1)}, f32[64,128]{1,0:T(8,128)S(1)}, u32[]{:S(2)}, u32[]{:S(2)}) collective-permute-start(f32[64,128]{1,0:T(8,128)S(1)} %get-tuple-element.113), channel_id=1, source_target_pairs={{0,2},{1,8},{2,0},{3,10},{4,6},{5,12},{6,4},{7,14},{8,1},{9,16},{1... | collective-permute-start | bytes 98312 | tf_op jit(solution)/shard_map/ppermute | solution.py:569
  43.5 4.6 %collective-permute-start.16 = (f32[16,512]{1,0:T(8,128)S(1)}, f32[16,512]{1,0:T(8,128)S(1)}, u32[]{:S(2)}, u32[]{:S(2)}) collective-permute-start(f32[16,512]{1,0:T(8,128)S(1)} %get-tuple-element.116.refs_2_), channel_id=1, source_target_pairs={{0,1},{1,0},{2,3},{3,2},{4,5},{5,4},{6,7},{7,6},{8,9},{9,8},{10,11... | collective-permute-start | bytes 98312 | tf_op jit(solution)/shard_map/ppermute | solution.py:566
  43.7 3.7 %collective-permute-start.17 = (f32[16,128]{1,0:T(8,128)S(1)}, f32[16,128]{1,0:T(8,128)S(1)}, u32[]{:S(2)}, u32[]{:S(2)}) collective-permute-start(f32[16,128]{1,0:T(8,128)S(1)} %get-tuple-element.119), channel_id=1, source_target_pairs={{0,8},{1,9},{2,10},{3,11},{4,12},{5,13},{6,14},{7,15},{8,0},{9,1},... | collective-permute-start | bytes 24584 | tf_op jit(solution)/shard_map/ppermute | solution.py:564
  44.4 3.7 %collective-permute-start.18 = (f32[16,128]{1,0:T(8,128)S(1)}, f32[16,128]{1,0:T(8,128)S(1)}, u32[]{:S(2)}, u32[]{:S(2)}) collective-permute-start(f32[16,128]{1,0:T(8,128)S(1)} %get-tuple-element.119), channel_id=1, source_target_pairs={{0,2},{1,3},{2,0},{3,1},{4,6},{5,7},{6,4},{7,5},{8,16},{9,17},{10,... | collective-permute-start | bytes 24584 | tf_op jit(solution)/shard_map/ppermute | solution.py:565
  49.4 5.1 %collective-permute-start.19 = (f32[16,512]{1,0:T(8,128)S(1)}, f32[16,512]{1,0:T(8,128)S(1)}, u32[]{:S(2)}, u32[]{:S(2)}) collective-permute-start(f32[16,512]{1,0:T(8,128)S(1)} %get-tuple-element.123.refs_2_), channel_id=1, source_target_pairs={{0,1},{1,0},{2,3},{3,2},{4,5},{5,4},{6,7},{7,6},{8,9},{9,8},{10,11... | collective-permute-start | bytes 98312 | tf_op jit(solution)/shard_map/ppermute | solution.py:566
  49.5 3.9 %collective-permute-start.20 = (f32[16,128]{1,0:T(8,128)S(1)}, f32[16,128]{1,0:T(8,128)S(1)}, u32[]{:S(2)}, u32[]{:S(2)}) collective-permute-start(f32[16,128]{1,0:T(8,128)S(1)} %get-tuple-element.126), channel_id=1, source_target_pairs={{0,8},{1,9},{2,10},{3,11},{4,12},{5,13},{6,14},{7,15},{8,0},{9,1},... | collective-permute-start | bytes 24584 | tf_op jit(solution)/shard_map/ppermute | solution.py:564
  50.8 3.7 %collective-permute-start.21 = (f32[16,128]{1,0:T(8,128)S(1)}, f32[16,128]{1,0:T(8,128)S(1)}, u32[]{:S(2)}, u32[]{:S(2)}) collective-permute-start(f32[16,128]{1,0:T(8,128)S(1)} %get-tuple-element.126), channel_id=1, source_target_pairs={{0,2},{1,3},{2,0},{3,1},{4,6},{5,7},{6,4},{7,5},{8,16},{9,17},{10,... | collective-permute-start | bytes 24584 | tf_op jit(solution)/shard_map/ppermute | solution.py:565
  55.8 4.5 %collective-permute-start.22 = (f32[16,512]{1,0:T(8,128)S(1)}, f32[16,512]{1,0:T(8,128)S(1)}, u32[]{:S(2)}, u32[]{:S(2)}) collective-permute-start(f32[16,512]{1,0:T(8,128)S(1)} %get-tuple-element.130.refs_2_), channel_id=1, source_target_pairs={{0,1},{1,0},{2,3},{3,2},{4,5},{5,4},{6,7},{7,6},{8,9},{9,8},{10,11... | collective-permute-start | bytes 98312 | tf_op jit(solution)/shard_map/ppermute | solution.py:566
  55.9 3.7 %collective-permute-start.23 = (f32[16,128]{1,0:T(8,128)S(1)}, f32[16,128]{1,0:T(8,128)S(1)}, u32[]{:S(2)}, u32[]{:S(2)}) collective-permute-start(f32[16,128]{1,0:T(8,128)S(1)} %get-tuple-element.133), channel_id=1, source_target_pairs={{0,8},{1,9},{2,10},{3,11},{4,12},{5,13},{6,14},{7,15},{8,0},{9,1},... | collective-permute-start | bytes 24584 | tf_op jit(solution)/shard_map/ppermute | solution.py:564
  56.7 3.7 %collective-permute-start.24 = (f32[16,128]{1,0:T(8,128)S(1)}, f32[16,128]{1,0:T(8,128)S(1)}, u32[]{:S(2)}, u32[]{:S(2)}) collective-permute-start(f32[16,128]{1,0:T(8,128)S(1)} %get-tuple-element.133), channel_id=1, source_target_pairs={{0,2},{1,3},{2,0},{3,1},{4,6},{5,7},{6,4},{7,5},{8,16},{9,17},{10,... | collective-permute-start | bytes 24584 | tf_op jit(solution)/shard_map/ppermute | solution.py:565
  61.7 5.1 %collective-permute-start.25 = (f32[16,512]{1,0:T(8,128)S(1)}, f32[16,512]{1,0:T(8,128)S(1)}, u32[]{:S(2)}, u32[]{:S(2)}) collective-permute-start(f32[16,512]{1,0:T(8,128)S(1)} %get-tuple-element.136.refs_2_), channel_id=1, source_target_pairs={{0,1},{1,0},{2,3},{3,2},{4,5},{5,4},{6,7},{7,6},{8,9},{9,8},{10,11... | collective-permute-start | bytes 98312 | tf_op jit(solution)/shard_map/ppermute | solution.py:566
  61.8 3.7 %collective-permute-start.26 = (f32[16,128]{1,0:T(8,128)S(1)}, f32[16,128]{1,0:T(8,128)S(1)}, u32[]{:S(2)}, u32[]{:S(2)}) collective-permute-start(f32[16,128]{1,0:T(8,128)S(1)} %get-tuple-element.141), channel_id=1, source_target_pairs={{0,8},{1,9},{2,10},{3,11},{4,12},{5,13},{6,14},{7,15},{8,0},{9,1},... | collective-permute-start | bytes 24584 | tf_op jit(solution)/shard_map/ppermute | solution.py:564
  63.1 3.7 %collective-permute-start.27 = (f32[16,128]{1,0:T(8,128)S(1)}, f32[16,128]{1,0:T(8,128)S(1)}, u32[]{:S(2)}, u32[]{:S(2)}) collective-permute-start(f32[16,128]{1,0:T(8,128)S(1)} %get-tuple-element.141), channel_id=1, source_target_pairs={{0,2},{1,3},{2,0},{3,1},{4,6},{5,7},{6,4},{7,5},{8,16},{9,17},{10,... | collective-permute-start | bytes 24584 | tf_op jit(solution)/shard_map/ppermute | solution.py:565

commit v3 on v2

--- a/solution.py
+++ b/solution.py
@@ -80,6 +80,11 @@
         lax.fori_loop(0, blocks, lambda j, carry: (body(j), carry)[1], 0)
 
 
+def over_groups(blocks, body):
+    size = min(blocks, 4)
+    over(blocks // size, lambda g: body([g * size + i for i in range(size)], g))
+
+
 def own_place():
     me = lax.axis_index("sub")
     return jnp.right_shift(me, 1), jnp.bitwise_and(me, 1)
@@ -94,23 +99,29 @@
     ]
 
 
-def faces(tiles_of, shape):
+def faces(tile_of, js, count):
     return jnp.concatenate(
         [
-            jnp.concatenate([tiles_of(f, h) for h in range(0, shape, LANES)], axis=1)
+            jnp.concatenate([tile_of(j, f, h) for j in js for h in range(0, count, LANES)], axis=1)
             for f in range(FACES)
         ],
         axis=0,
     )
 
 
-def send(j, traces, sub_ref, rim_ref, sub_out, rim_out, width, rims):
-    tiles = trace_tiles(traces)
+def of_block(x, i, count):
+    return x[:, i * count : (i + 1) * count]
+
+
+def send_sub(j, tiles, sub_ref, sub_out, width):
     for h in range(0, width, LANES):
         columns = sub_ref[:, cols(j, width, h)]
         sub_out[:, cols(j, width, h)] = pick(
             tiles, jnp.right_shift(columns, 7), jnp.bitwise_and(columns, LANES - 1)
         )
+
+
+def send_rim(j, tiles, rim_ref, rim_out, rims):
     group = LANES // rims
     tile = cols(j // group, LANES)
     columns = rim_ref[:, tile]
@@ -137,27 +148,40 @@
         store_left(up_out, rows, restriction_ref[o].T)
 
 
-def pack_kernel(b_ref, cond_ref, mat_ref, face_ref, sub_ref, rim_ref, size_ref, coarse_ref, out):
-    modes, count = b_ref.shape
+def pack_kernel(
+    b_ref, cond_ref, mat_ref, face_ref, sub_ref, rim_ref, size_ref, coarse_ref, out,
+    b_in, cond_in, mat_in, face_in, sub_in, rim_in, size_in, coarse_in, done,
+):
+    sources = (b_ref, cond_ref, mat_ref, face_ref, sub_ref, rim_ref, size_ref, coarse_ref)
+    places = (b_in, cond_in, mat_in, face_in, sub_in, rim_in, size_in, coarse_in)
+    copies = [
+        pltpu.make_async_copy(source, place, done.at[at])
+        for at, (source, place) in enumerate(zip(sources, places))
+    ]
+    for copy in copies:
+        copy.start()
+    modes, count = b_in.shape
     out[modes:, :] = jnp.zeros((out.shape[0] - modes, count), jnp.float32)
-    out[:modes, :] = b_ref[...]
-    out[modes : modes + 1, :] = cond_ref[...]
-    out[modes + 1 : modes + 2, :] = mat_ref[...].astype(jnp.float32)
-    out[modes + 2 : modes + 8, :] = face_ref[...].astype(jnp.float32)
-    out[modes + 8 : modes + 9, : rim_ref.shape[1]] = rim_ref[...].astype(jnp.float32)
-    out[modes + 9 : modes + 10, : size_ref.shape[1]] = size_ref[...].astype(jnp.float32)
-    out[modes + 10 : modes + 11, : coarse_ref.shape[1]] = coarse_ref[...]
-    width = sub_ref.shape[1]
+    for copy in copies:
+        copy.wait()
+    out[:modes, :] = b_in[...]
+    out[modes : modes + 1, :] = cond_in[...]
+    out[modes + 1 : modes + 2, :] = mat_in[...].astype(jnp.float32)
+    out[modes + 2 : modes + 8, :] = face_in[...].astype(jnp.float32)
+    out[modes + 8 : modes + 9, : rim_in.shape[1]] = rim_in[...].astype(jnp.float32)
+    out[modes + 9 : modes + 10, : size_in.shape[1]] = size_in[...].astype(jnp.float32)
+    out[modes + 10 : modes + 11, : coarse_in.shape[1]] = coarse_in[...]
+    width = sub_in.shape[1]
     for at, h in enumerate(range(0, width, count)):
-        piece = sub_ref[:, h : min(h + count, width)].astype(jnp.float32)
+        piece = sub_in[:, h : min(h + count, width)].astype(jnp.float32)
         out[modes + 11 + at : modes + 12 + at, : piece.shape[1]] = piece
 
 
 def start_kernel(blocks, width, rims, *refs):
     gathered, refs = refs[:blocks], refs[blocks:]
     stiff_ref, map_ref, t_ref = refs[:3]
-    b_out, ig_out, meta_out, lane_out, at_out, far_out, sub_out, rim_out, size_out, coarse_out = refs[3:13]
-    p_out, tr_out, subs_out, rims_out, held = refs[13:]
+    b_out, ig_out, meta_out, lane_out, at_out, far_out, edge_out, sub_out, rim_out, size_out, coarse_out = refs[3:14]
+    p_out, tr_out, subs_out, rims_out, held = refs[14:]
     modes, count = map_ref.shape[0], gathered[0].shape[1]
     chip, core = own_place()
     for k, ref in enumerate(gathered):
@@ -189,13 +213,12 @@
         at = jnp.right_shift(column, 7)
         lane_out[0:FACES, cols(j, count)] = lane
         at_out[0:FACES, cols(j, count)] = at
-        remote = column - own_tiles * LANES
         other = jnp.bitwise_and(lax.div(lane, jnp.int32(slots)), 1) != core
         sub = jnp.logical_and(jnp.logical_and(at >= own_tiles, at < own_tiles + sub_tiles), other)
         rim = jnp.logical_and(at == own_tiles + sub_tiles, lane < rims)
-        nothing = slots * (core + CORES)
-        far_out[0:FACES, cols(j, count)] = jnp.where(
-            sub, remote, jnp.where(rim, lane + slots * core, nothing)
+        far_out[0:FACES, cols(j, count)] = jnp.where(sub, column - own_tiles * LANES, slots * core)
+        edge_out[0:FACES, cols(j, count)] = jnp.where(
+            rim, jnp.bitwise_xor(lane, rims // 2) + (j % group) * rims, -1
         )
         for h in range(0, width, LANES):
             row = modes + 11 + h // count
@@ -209,13 +232,19 @@
         coarse_out[pl.ds(j, 1), :] = held[j, modes + 10 : modes + 11, :LANES]
         inverse = 1.0 / (cond * jnp.where(mat == 1.0, diagonals[1], diagonals[0]) + squares)
         ig_out[:, cols(j, count)] = inverse
-        p = b * inverse * (1.0 / CENTER)
-        p_out[:, cols(j, count)] = p
-        traces = product(t_ref[...], p)
-        tr_out[:, cols(j, count)] = traces
-        send(j, traces, sub_out, rim_out, subs_out, rims_out, width, rims)
+        p_out[:, cols(j, count)] = b * inverse * (1.0 / CENTER)
+
+    def first(js, g):
+        span = cols(g, len(js) * count)
+        traces = product(t_ref[...], p_out[:, span])
+        tr_out[:, span] = traces
+        for i, j in enumerate(js):
+            tiles = trace_tiles(of_block(traces, i, count))
+            send_sub(j, tiles, sub_out, subs_out, width)
+            send_rim(j, tiles, rim_out, rims_out, rims)
 
     over(blocks, body)
+    over_groups(blocks, first)
 
 
 def sub_tiles_of(j, sends_ref, core, width, blocks):
@@ -236,117 +265,185 @@
     return tiles
 
 
+def rim_kernel(blocks, rims, rim_ref, edge_ref, ig_ref, edges_out, igs_out):
+    group = LANES // rims
+    lane = lanes()
+    edges_out[...] = jnp.full(edges_out.shape, -1, jnp.int32)
+    igs_out[...] = jnp.zeros(igs_out.shape, jnp.float32)
+    count = ig_ref.shape[1] // blocks
+
+    def body(j):
+        tile = cols(j // group, LANES)
+        mine = lane // rims == j % group
+        at, there = rim_element(rim_ref[:, tile], count)
+        edges = pick([edge_ref[:, cols(j, count, h)] for h in range(0, count, LANES)], at, there)
+        igs = pick([ig_ref[:, cols(j, count, h)] for h in range(0, count, LANES)], at, there)
+        edges_out[:, tile] = jnp.where(mine, edges, edges_out[:, tile])
+        igs_out[:, tile] = jnp.where(mine, igs, igs_out[:, tile])
+
+    over(blocks, body)
+
+
+def rim_element(columns, count):
+    return jnp.bitwise_and(jnp.right_shift(columns, 7), count // LANES - 1), jnp.bitwise_and(columns, LANES - 1)
+
+
 def local_kernel(only_own, blocks, width, first, *refs):
-    p_ref, tr_ref, subs_ref, meta_ref, lane_ref, at_ref, tt_ref, k_ref = refs[:8]
-    refs = refs[8:]
+    p_ref, tr_ref, subs_ref, meta_ref, lane_ref, at_ref, k_ref = refs[:7]
+    refs = refs[7:]
     if not first:
         x_ref, refs = refs[0], refs[1:]
-    base_out, x_out = refs
+    jump_out, own_out, x_out = refs
     modes = p_ref.shape[0]
     chip, core = own_place()
     count = x_out.shape[1]
 
-    def body(j, out):
-        traces = tr_ref[:, cols(j, count)]
-        tiles = trace_tiles(traces) + sub_tiles_of(j, subs_ref, core, width, blocks)
-
-        def tile(f, h):
-            return pick(tiles, at_rows[f : f + 1, h : h + LANES], lane_rows[f : f + 1, h : h + LANES])
-
-        at_rows, lane_rows = at_ref[:, cols(j, count)], lane_ref[:, cols(j, count)]
-        seen = faces(tile, count)
-        p = p_ref[:, cols(j, count)]
-        both = product(k_ref[...], p)
-        meta = meta_ref[:, cols(j, count)]
-        own = meta[0:1] * jnp.where(meta[1:2] == 1.0, both[modes:], both[:modes])
-        base_out[:, out] = own + PENALTY * product(tt_ref[...], traces - seen)
+    def body(js, span, out):
+        traces = tr_ref[:, span]
+        at_rows, lane_rows = at_ref[:, span], lane_ref[:, span]
+        both = product(k_ref[...], p_ref[:, span])
+        meta = meta_ref[:, span]
+        own_out[:, out] = meta[0:1] * jnp.where(meta[1:2] == 1.0, both[modes:], both[:modes])
+        tiles = [
+            trace_tiles(of_block(traces, i, count)) + sub_tiles_of(j, subs_ref, core, width, blocks)
+            for i, j in enumerate(js)
+        ]
+
+        def tile(i, f, h):
+            row, place = slice(f, f + 1), slice(i * count + h, i * count + h + LANES)
+            return pick(tiles[i], at_rows[row, place], lane_rows[row, place])
+
+        jump_out[:, out] = traces - faces(tile, range(len(js)), count)
 
     if only_own:
-        body(chip, slice(0, count))
+        body([chip], cols(chip, count), slice(0, count))
     else:
-        over(blocks, lambda j: body(j, cols(j, count)))
+        over_groups(blocks, lambda js, g: body(js, cols(g, len(js) * count), cols(g, len(js) * count)))
     p = p_ref[:, cols(chip, count)]
     x_out[...] = p if first else x_ref[...] + p
 
 
-def rim_tiles(one_ref, two_ref, rims):
+def ahead_kernel(kind, coefficients, blocks, width, rims, *refs):
+    r_ref, jump_ref, own_ref, swapped_ref, far_ref, tt_ref = refs[:6]
+    refs = list(refs[6:])
+    chip, core = own_place()
+    count = own_ref.shape[1] // (1 if kind == "last" else blocks)
+    group = LANES // rims
+    lane = lanes()
+    p_ref = refs.pop(0) if kind == "step" else None
+    if kind in ("step", "first"):
+        ig_ref, rim_ref, r_out, p_out, edge_out = refs
+        edge_out[...] = jnp.zeros(edge_out.shape, jnp.float32)
+    else:
+        r_out = refs[0]
+
+    def body(js, span, here):
+        tiles = [sub_tiles_of(j, swapped_ref, 1 - core, width, blocks) for j in js]
+        far = far_ref[:, span]
+
+        def tile(i, f, h):
+            column = far[f : f + 1, i * count + h : i * count + h + LANES]
+            if len(tiles[i]) == 1:
+                return take(tiles[i][0], column)
+            return pick(tiles[i], jnp.right_shift(column, 7), jnp.bitwise_and(column, LANES - 1))
+
+        jump = product(tt_ref[...], jump_ref[:, here] - faces(tile, range(len(js)), count))
+        residual = r_ref[:, span] - own_ref[:, here] - PENALTY * jump
+        r_out[:, here] = residual
+        if kind in ("frame", "last"):
+            return
+        p = coefficients[1] * (residual * ig_ref[:, here])
+        if kind == "step":
+            p = p + coefficients[0] * p_ref[:, here]
+        p_out[:, here] = p
+        for i, j in enumerate(js):
+            spot = cols(j // group, LANES)
+            at, there = rim_element(rim_ref[:, spot], count)
+            mine = of_block(p, i, count)
+            edge = pick([mine[:, h : h + LANES] for h in range(0, count, LANES)], at, there)
+            edge_out[:, spot] = jnp.where(lane // rims == j % group, edge, edge_out[:, spot])
+
+    if kind == "last":
+        body([chip], cols(chip, count), slice(0, count))
+    else:
+        over_groups(blocks, lambda js, g: body(js, cols(g, len(js) * count), cols(g, len(js) * count)))
+
+
+def rim_tile(one_ref, two_ref, spot, rims):
     segment, segments = lax.axis_index("blk"), lax.axis_size("blk")
     odd = segment % 2 == 1
-    lane = lanes()
-    tiles = []
-    for h in range(0, one_ref.shape[1], LANES):
-        one = take(one_ref[:, h : h + LANES], jnp.bitwise_xor(lane, rims // 2))
-        two = take(two_ref[:, h : h + LANES], jnp.bitwise_xor(lane, rims // 2))
-        low = jnp.where(segment == 0, 0.0, jnp.where(odd, one, two))
-        high = jnp.where(segment == segments - 1, 0.0, jnp.where(odd, two, one))
-        tiles.append(jnp.where(lane % rims < rims // 2, low, high))
-    return tiles
-
-
-def finish_kernel(kind, coefficients, blocks, width, rims, *refs):
-    r_ref, base_ref, swapped_ref, one_ref, two_ref, far_ref, tt_ref = refs[:7]
-    refs = list(refs[7:])
-    modes = r_ref.shape[0]
+    low = jnp.where(odd, one_ref[:, spot], two_ref[:, spot])
+    high = jnp.where(odd, two_ref[:, spot], one_ref[:, spot])
+    low = jnp.where(segment == 0, 0.0, low)
+    high = jnp.where(segment == segments - 1, 0.0, high)
+    return jnp.where(lanes() % rims < rims // 2, high, low)
+
+
+def rim_seen(rim, edge, f, h):
+    place = edge[f : f + 1, h : h + LANES]
+    return jnp.where(place >= 0, take(rim, jnp.bitwise_and(place, LANES - 1)), 0.0)
+
+
+def edge_kernel(rate, rims, one_ref, two_ref, edges_ref, igs_ref, p_ref, tt_ref, t_ref, rim_ref, rims_out):
+    points = one_ref.shape[0]
+    for t in range(one_ref.shape[1] // LANES):
+        spot = slice(t * LANES, (t + 1) * LANES)
+        rim = rim_tile(one_ref, two_ref, spot, rims)
+        edge = edges_ref[:, spot]
+        added = product(tt_ref[...], faces(lambda _, f, h: rim_seen(rim, edge, f, h), [0], LANES))
+        p = p_ref[:, spot] + (rate * PENALTY) * (igs_ref[:, spot] * added)
+        traces = product(t_ref[...], p)
+        face = rim_ref[:, spot]
+        out = jnp.zeros((points, LANES), jnp.float32)
+        for f in range(FACES):
+            out = jnp.where(face == f, traces[f * points : (f + 1) * points], out)
+        rims_out[:, spot] = out
+
+
+def finish_kernel(kind, rate, blocks, width, rims, *refs):
+    r_ref, one_ref, two_ref, edge_ref, tt_ref = refs[:5]
+    refs = list(refs[5:])
     chip, core = own_place()
-    slots = width // (blocks * CORES)
     group = LANES // rims
     lane = lanes()
-    rim = rim_tiles(one_ref, two_ref, rims)
-    if kind == "step":
-        p_ref = refs.pop(0)
     if kind in ("step", "first"):
-        ig_ref, t_ref, sub_ref, rim_ref, r_out, p_out, tr_out, subs_out, rims_out = refs
-        rims_out[...] = jnp.zeros(rims_out.shape, jnp.float32)
+        p_ref, ig_ref, t_ref, sub_ref, _, r_out, p_out, tr_out, subs_out = refs
     elif kind == "frame":
         r_out, head_out = refs
         head_out[...] = jnp.zeros(head_out.shape, jnp.float32)
     else:
         r_out = refs[0]
-    count = r_out.shape[1] if kind == "last" else r_out.shape[1] // blocks
-
-    def body(j):
-        tiles = sub_tiles_of(j, swapped_ref, 1 - core, width, blocks)
-        if len(rim) == 1:
-            mine = rim[0]
-        else:
-            mine = rim[0]
-            for t in range(1, len(rim)):
-                mine = jnp.where(j // group == t, rim[t], mine)
-        mine = pltpu.roll(mine, (slots * core - (j % group) * rims) % LANES, 1)
-        tiles[0] = jnp.where(lane // slots == core, mine, tiles[0])
-        far = far_ref[:, cols(j, count)]
-
-        def tile(f, h):
-            column = far[f : f + 1, h : h + LANES]
-            if len(tiles) == 1:
-                return take(tiles[0], column)
-            return pick(tiles, jnp.right_shift(column, 7), jnp.bitwise_and(column, LANES - 1))
-
-        here = cols(j, count)
-        base = base_ref[...] if kind == "last" else base_ref[:, here]
-        residual = r_ref[:, here] - base + PENALTY * product(tt_ref[...], faces(tile, count))
-        if kind == "last":
-            r_out[...] = residual
-            return
+    count = r_out.shape[1] // (1 if kind == "last" else blocks)
+
+    def body(js, span, here):
+        rim = [rim_tile(one_ref, two_ref, cols(j // group, LANES), rims) for j in js]
+        edge = edge_ref[:, span]
+
+        def tile(i, f, h):
+            return rim_seen(rim[i], edge, f, i * count + h)
+
+        added = PENALTY * product(tt_ref[...], faces(tile, range(len(js)), count))
+        residual = r_ref[:, here] + added
         r_out[:, here] = residual
         if kind == "frame":
             heads = LANES // HEAD
-            spot = cols(j // heads, LANES)
-            moved = pltpu.roll(residual[:, :LANES], (j % heads) * HEAD, 1)
-            head_out[:, spot] = jnp.where(lane // HEAD == j % heads, moved, head_out[:, spot])
+            for i, j in enumerate(js):
+                spot = cols(j // heads, LANES)
+                moved = pltpu.roll(of_block(residual, i, count)[:, :LANES], (j % heads) * HEAD, 1)
+                head_out[:, spot] = jnp.where(lane // HEAD == j % heads, moved, head_out[:, spot])
+        if kind in ("frame", "last"):
             return
-        p = coefficients[1] * (residual * ig_ref[:, here])
-        if kind == "step":
-            p = p + coefficients[0] * p_ref[:, here]
+        p = p_ref[:, here] + rate * (ig_ref[:, here] * added)
         p_out[:, here] = p
         traces = product(t_ref[...], p)
         tr_out[:, here] = traces
-        send(j, traces, sub_ref, rim_ref, subs_out, rims_out, width, rims)
+        for i, j in enumerate(js):
+            send_sub(j, trace_tiles(of_block(traces, i, count)), sub_ref, subs_out, width)
 
     if kind == "last":
-        body(chip)
+        body([chip], cols(chip, count), slice(0, count))
     else:
-        over(blocks, body)
+        over_groups(blocks, lambda js, g: body(js, cols(g, len(js) * count), cols(g, len(js) * count)))
 
 
 def layout_kernel(blocks, parents, size_ref, gather_out, parent_out, octant_out):
@@ -478,27 +575,32 @@
     lane = lanes()
     rims_out[...] = jnp.zeros(rims_out.shape, jnp.float32)
 
-    def body(j):
-        arriving = heads_of(j, swapped_ref, cross_ref, -1, blocks)
-        field = field_ref[:, cols(j, count)]
-        first = jnp.where(lane < HEAD, arriving, field[:, :LANES])
-        field = jnp.concatenate([first, field[:, LANES:]], axis=1)
-        p_out[:, cols(j, count)] = field
-        traces = product(t_ref[...], field)
-        tr_out[:, cols(j, count)] = traces
-        send(j, traces, sub_ref, rim_ref, subs_out, rims_out, width, rims)
-
-    over(blocks, body)
-
-
-def call(limit, kernel, outs, *args, scratch=()):
+    def body(js, g):
+        span = cols(g, len(js) * count)
+        for j in js:
+            arriving = heads_of(j, swapped_ref, cross_ref, -1, blocks)
+            p_out[:, cols(j, count)] = field_ref[:, cols(j, count)]
+            first = cols(j, count, 0)
+            p_out[:, first] = jnp.where(lane < HEAD, arriving, field_ref[:, first])
+        traces = product(t_ref[...], p_out[:, span])
+        tr_out[:, span] = traces
+        for i, j in enumerate(js):
+            tiles = trace_tiles(of_block(traces, i, count))
+            send_sub(j, tiles, sub_ref, subs_out, width)
+            send_rim(j, tiles, rim_ref, rims_out, rims)
+
+    over_groups(blocks, body)
+
+
+def call(limit, kernel, outs, *args, scratch=(), hbm=False):
     return pl.pallas_call(
         kernel,
         out_shape=[jax.ShapeDtypeStruct(shape, kind) for shape, kind in outs],
-        in_specs=[pl.BlockSpec(memory_space=pltpu.VMEM)] * len(args),
+        in_specs=[pl.BlockSpec(memory_space=pltpu.HBM if hbm else pltpu.VMEM)] * len(args),
         out_specs=[pl.BlockSpec(memory_space=pltpu.VMEM)] * len(outs),
         scratch_shapes=list(scratch),
         compiler_params=pltpu.CompilerParams(vmem_limit_bytes=limit),
+        cost_estimate=pl.CostEstimate(flops=10**9, bytes_accessed=1, transcendentals=0),
     )(*args)
 
 
@@ -560,10 +662,8 @@
     cores = [(s, s ^ 1) for s in range(peers)]
     ones, twos, crossings = above_or_below(0), above_or_below(1), everywhere(crossing)
 
-    def exchange(subs, rim):
-        one = lax.ppermute(rim, both, ones)
-        two = lax.ppermute(rim, both, twos)
-        return [lax.ppermute(subs, "sub", cores), one, two]
+    def over_segments(rim):
+        return lax.ppermute(rim, both, ones), lax.ppermute(rim, both, twos)
 
     def shift(heads):
         return lax.ppermute(heads, "sub", cores), lax.ppermute(heads, both, crossings)
@@ -575,19 +675,24 @@
         map_t, stiffness,
     )
     height = pad(modes + 11 + pad(width, count) // count, 8)
+    inputs = [
+        right_side, conductivity.reshape(1, count), material.reshape(1, count), face_neighbour, sub_sends, blk_sends,
+        group_sizes, coarse_conductivity.reshape(1, -1),
+    ]
     (packed,) = run(
         pack_kernel,
         [((height, count), f32)],
-        right_side, conductivity.reshape(1, count), material.reshape(1, count), face_neighbour, sub_sends, blk_sends,
-        group_sizes, coarse_conductivity.reshape(1, -1),
+        *inputs,
+        scratch=[pltpu.VMEM(x.shape, x.dtype) for x in inputs] + [pltpu.SemaphoreType.DMA((len(inputs),))],
+        hbm=True,
     )
     gathered = [packed] + [
         lax.ppermute(packed, "sub", [(s, s ^ (CORES * k)) for s in range(peers)]) for k in range(1, blocks)
     ]
-    b, inverse, meta, lane, at, far, subs, rim, sizes, coarse_cond, p, traces, *out = run(
+    b, inverse, meta, lane, at, far, edge, subs, rim, sizes, coarse_cond, p, traces, sub_out, rim_out = run(
         functools.partial(start_kernel, blocks, width, rims),
         [
-            field, field, ((8, total), f32), ((8, total), i32), ((8, total), i32), ((8, total), i32),
+            field, field, ((8, total), f32), *[((8, total), i32)] * 4,
             ((1, blocks * width), i32), ((1, rim_width), i32), ((blocks, LANES), i32), ((blocks, LANES), f32),
             field, *sends,
         ],
@@ -595,21 +700,43 @@
         scratch=[pltpu.VMEM((blocks, height, count), f32)],
     )
 
-    def part(p, traces, subs_sent, x, only_own=False):
-        args = [p, traces, subs_sent, meta, lane, at, tt3, k3] + ([] if x is None else [x])
-        kernel = functools.partial(local_kernel, only_own, blocks, width, x is None)
-        return run(kernel, [block if only_own else field, block], *args)
-
-    def finish(kind, coefficients, r, base, got, p=None):
-        args = [r, base, *got, far, tt3]
-        if kind == "last":
-            outs = [block]
-        elif kind == "frame":
-            outs = [field, ((modes, head_width), f32)]
-        else:
-            args += ([p] if kind == "step" else []) + [inverse, t3, subs, rim]
-            outs = [field, field, *sends]
-        return run(functools.partial(finish_kernel, kind, coefficients, blocks, width, rims), outs, *args)
+    edges, igs = run(
+        functools.partial(rim_kernel, blocks, rims), [((8, rim_width), i32), ((modes, rim_width), f32)], rim, edge, inverse
+    )
+    spot = jnp.arange(rim_width, dtype=i32)[None, :]
+    rim_face = jnp.where(spot < blocks * rims, lax.div(rim, jnp.int32(count)), -1)
+
+    def apply(kind, coefficients, r, p, traces, sub_out, rim_out, x):
+        one, two = over_segments(rim_out)
+        swapped = lax.ppermute(sub_out, "sub", cores)
+        only_own = kind == "last"
+        size = count if only_own else total
+        part, col = ((modes, size), f32), ((rows, size), f32)
+        jump, own, x = run(
+            functools.partial(local_kernel, only_own, blocks, width, x is None),
+            [col, part, block],
+            p, traces, sub_out, meta, lane, at, k3, *([] if x is None else [x]),
+        )
+        goes_on = kind in ("step", "first")
+        kernel = functools.partial(ahead_kernel, kind, coefficients, blocks, width, rims)
+        args = [r, jump, own, swapped, far, tt3] + ([p] if kind == "step" else [])
+        if not goes_on:
+            (r,) = run(kernel, [part], *args)
+            outs = [block] if only_own else [field, ((modes, head_width), f32)]
+            kernel = functools.partial(finish_kernel, kind, None, blocks, width, rims)
+            return *run(kernel, outs, r, one, two, edge, tt3), x
+        r, p, p_edge = run(kernel, [field, field, ((modes, rim_width), f32)], *args, inverse, rim)
+        rate = coefficients[1]
+        (rim_out,) = run(
+            functools.partial(edge_kernel, rate, rims), [((points, rim_width), f32)],
+            one, two, edges, igs, p_edge, tt3, t3, rim_face,
+        )
+        r, p, traces, sub_out = run(
+            functools.partial(finish_kernel, kind, rate, blocks, width, rims),
+            [field, field, ((rows, total), f32), ((points, blocks * width), f32)],
+            r, one, two, edge, tt3, p, inverse, t3, subs, rim_out,
+        )
+        return r, p, traces, sub_out, rim_out, x
 
     gather, parent, octant = run(
         functools.partial(layout_kernel, blocks, parents),
@@ -622,14 +749,12 @@
         restriction, coarse_stiffness,
     )
 
-    r, x = b, None
+    x = None
+    r = b
     pairs = steps(KF)
-    for step in range(KF):
-        got = exchange(*out)
-        base, x = part(p, traces, out[0], x)
-        if step < KF - 1:
-            r, p, traces, *out = finish("step", pairs[step], r, base, got, p)
-    r, heads = finish("frame", None, r, base, got)
+    for step in range(KF - 1):
+        r, p, traces, sub_out, rim_out, x = apply("step", pairs[step], r, p, traces, sub_out, rim_out, x)
+    r, heads, x = apply("frame", None, r, p, traces, sub_out, rim_out, x)
 
     correction, tails = run(
         functools.partial(coarse_kernel, blocks, parents),
@@ -641,19 +766,13 @@
             pltpu.VMEM((OCTANTS * modes, blocks * parents), f32),
         ],
     )
-    p, traces, *out = run(
+    p, traces, sub_out, rim_out = run(
         functools.partial(middle_kernel, blocks, width, rims), [field, *sends], correction, *shift(tails), t3, subs, rim
     )
-
-    got = exchange(*out)
-    base, x = part(p, traces, out[0], x)
-    r, p, traces, *out = finish("first", (0.0, 1.0 / CENTER), r, base, got)
-    for step in range(KF):
-        got = exchange(*out)
-        base, x = part(p, traces, out[0], x, step == KF - 1)
-        if step < KF - 1:
-            r, p, traces, *out = finish("step", pairs[step], r, base, got, p)
-    (residual,) = finish("last", None, r, base, got)
+    r, p, traces, sub_out, rim_out, x = apply("first", (0.0, 1.0 / CENTER), r, p, traces, sub_out, rim_out, x)
+    for step in range(KF - 1):
+        r, p, traces, sub_out, rim_out, x = apply("step", pairs[step], r, p, traces, sub_out, rim_out, x)
+    residual, x = apply("last", None, r, p, traces, sub_out, rim_out, x)
     return x, residual
 
 

time: 68.1 us -> 66 us (0.969)
  waiting for transfers between devices: 19.6 us -> 10.4 us
  starting transfers between devices: 18.4 us -> 23 us
  Pallas kernels: 26.6 us -> 28.2 us
  local copies, waits for them, and re-layouts: 2.25 us -> 3.02 us
    ppermute x21, waiting for transfers between devices: 8.29 us -> 0.99 us  [the longest x14 0.84 us: over_segments(): return (lax.ppermute(rim, both, ones), lax.ppermute(rim, both, twos))]
    ppermute x21, starting transfers between devices: 12.5 us -> 15.6 us  [the longest x14 15.2 us: over_segments(): return (lax.ppermute(rim, both, ones), lax.ppermute(rim, both, twos))]
    pallas_call x21 -> x34, Pallas kernels: 26.6 us -> 28.2 us  [call(): pl.pallas_call(kernel, out_shape=[jax.ShapeDtypeStruct(shape, kind) for s...]
    ppermute x2, starting transfers between devices: 1.14 us -> 2.24 us  [shift(): lax.ppermute(heads, both, crossings)]
    ppermute x3, waiting for transfers between devices: 5.15 us -> 4.05 us  [local(): lax.ppermute(packed, 'sub', [(s, s ^ CORES * k) for s in range(peers)])]
    unnamed x24, local copies, waits for them, and re-layouts: 2.25 us -> 3.02 us
  transfers between devices with their start and end apart: 28 -> 28, of which waited for: 17 -> 7; matrix products, arithmetic and copies ran while one was open for 0% -> 0% of each run, Pallas kernels for 21% -> 31%
where the time goes in v3:
time: 66 us; the launch traced here: 65.7 us
  Pallas kernels  28.2 us (43%)
  starting transfers between devices  23 us (35%)
  waiting for transfers between devices  10.4 us (16%)
  local copies, waits for them, and re-layouts  3.02 us (5%)
  between operations  1.05 us (2%)
    pallas_call x34, Pallas kernels, call(): pl.pallas_call(kernel, out_shape=[jax.ShapeDtypeStruct(shape, kind) for s...  28.2 us
    ppermute x14, starting transfers between devices, over_segments(): return (lax.ppermute(rim, both, ones), lax.ppermute(rim, both, twos))  15.2 us
    ppermute x2, waiting for transfers between devices, shift(): lax.ppermute(heads, both, crossings)  5.36 us
    ppermute x3, starting transfers between devices, local(): lax.ppermute(packed, 'sub', [(s, s ^ CORES * k) for s in range(peers)])  4.54 us
    ppermute x3, waiting for transfers between devices, local(): lax.ppermute(packed, 'sub', [(s, s ^ CORES * k) for s in range(peers)])  4.05 us
    unnamed x24, local copies, waits for them, and re-layouts  3.02 us
    ppermute x2, starting transfers between devices, shift(): lax.ppermute(heads, both, crossings)  2.24 us
  transfers between devices with their start and end apart: 28, of which 7 were waited for; matrix products, arithmetic and copies ran while one was open for 0% of the time, Pallas kernels for 31%

profile of v3, /device:TPU:0, one launch (start us, length us, event | category | flops | bytes accessed | tf_op | source)
XLA Modules:
  0.0 65.7 jit_solution(3955253133357019414)
XLA Ops:
  0.7 0.6 copy-done.11
  1.4 0.8 %copy-done.1 = f32[64,256]{1,0:T(8,128)S(1)} copy-done((f32[64,256]{1,0:T(8,128)S(1)}, f32[64,256]{1,0:T(8,128)}, u32[]{:S(2)}) %copy-start.1) | copy-done | bytes 65560
  2.2 0.7 %copy-done.5 = s32[6,256]{1,0:T(8,128)S(1)} copy-done((s32[6,256]{1,0:T(8,128)S(1)}, s32[6,256]{1,0:T(8,128)}, u32[]{:S(2)}) %copy-start.5) | copy-done | bytes 6168
  3.1 3.0 %collective-permute-start = (f32[80,256]{1,0:T(8,128)S(1)}, f32[80,256]{1,0:T(8,128)S(1)}, u32[]{:S(2)}, u32[]{:S(2)}) collective-permute-start(f32[80,256]{1,0:T(8,128)S(1)} %shard_map.131.refs_0_), channel_id=1, source_target_pairs={{0,2},{1,3},{2,0},{3,1},{4,6},{5,7},{6,4},{7,5},{8,10},{9,11},{10,... | collective-permute-start | bytes 245768 | tf_op jit(solution)/shard_map/ppermute | solution.py:690
  6.1 1.5 %collective-permute-start.1 = (f32[80,256]{1,0:T(8,128)S(1)}, f32[80,256]{1,0:T(8,128)S(1)}, u32[]{:S(2)}, u32[]{:S(2)}) collective-permute-start(f32[80,256]{1,0:T(8,128)S(1)} %shard_map.131.refs_0_), channel_id=1, source_target_pairs={{0,4},{1,5},{2,6},{3,7},{4,0},{5,1},{6,2},{7,3},{8,12},{9,13},{10,... | collective-permute-start | bytes 245768 | tf_op jit(solution)/shard_map/ppermute | solution.py:690
  7.8 0.8 %copy-done = f32[8,64,64]{2,1,0:T(8,128)S(1)} copy-done((f32[8,64,64]{2,1,0:T(8,128)S(1)}, f32[8,64,64]{2,1,0:T(8,128)}, u32[]{:S(2)}) %copy-start) | copy-done | bytes 131096
  8.9 2.5 %collective-permute-done.1.refs_2_ = f32[80,256]{1,0:T(8,128)S(1)} collective-permute-done((f32[80,256]{1,0:T(8,128)S(1)}, f32[80,256]{1,0:T(8,128)S(1)}, u32[]{:S(2)}, u32[]{:S(2)}) %collective-permute-start.1) | collective-permute-done | bytes 81952 | tf_op jit(solution)/shard_map/ppermute | solution.py:690
  11.4 1.5 %collective-permute-done.2.refs_3_ = f32[80,256]{1,0:T(8,128)S(1)} collective-permute-done((f32[80,256]{1,0:T(8,128)S(1)}, f32[80,256]{1,0:T(8,128)S(1)}, u32[]{:S(2)}, u32[]{:S(2)}) %collective-permute-start.2) | collective-permute-done | bytes 81952 | tf_op jit(solution)/shard_map/ppermute | solution.py:690
  13.0 0.8 %shard_map.133 = (f32[64,1024]{1,0:T(8,128)S(1)}, f32[64,1024]{1,0:T(8,128)S(1)}, f32[8,1024]{1,0:T(8,128)S(1)}, s32[8,1024]{1,0:T(8,128)S(1)}, s32[8,1024]{1,0:...) custom-call(f32[80,256]{1,0:T(8,128)S(1)} %shard_map.131.refs_0_, ...), custom_call_target="tpu_custom_call" | custom-call | flops 1000000000 | bytes 1 | tf_op jit(solution)/shard_map/pallas_call | solution.py:596
  13.8 1.6 %collective-permute-start.4 = (f32[16,128]{1,0:T(8,128)S(1)}, f32[16,128]{1,0:T(8,128)S(1)}, u32[]{:S(2)}, u32[]{:S(2)}) collective-permute-start(f32[16,128]{1,0:T(8,128)S(1)} %get-tuple-element.108), channel_id=1, source_target_pairs={{0,8},{1,9},{2,10},{3,11},{4,12},{5,13},{6,14},{7,15},{8,0},{9,1},... | collective-permute-start | bytes 24584 | tf_op jit(solution)/shard_map/ppermute | solution.py:666
  16.1 1.7 %shard_map.134 = (f32[96,1024]{1,0:T(8,128)S(1)}, f32[64,1024]{1,0:T(8,128)S(1)}, f32[64,256]{1,0:T(8,128)S(1)}) custom-call(f32[64,1024]{1,0:T(8,128)S(1)} %get-tuple-element.94.refs_0_.refs_6_, f32[96,1024]{1,0:T(8,128)S(1)} %get-tuple-element.95.refs_1_, f32[16,512]{1,0:T(8,128)S(1)} %get-tuple-element.96.refs_2_, ...), custom_call_target="tpu_custom_call" | custom-call | flops 1000000000 | bytes 1 | tf_op jit(solution)/shard_map/pallas_call | solution.py:596
  17.8 0.7 %shard_map.135 = (f32[64,1024]{1,0:T(8,128)S(1)}, f32[64,1024]{1,0:T(8,128)S(1)}, f32[64,128]{1,0:T(8,128)S(1)}) custom-call(f32[64,1024]{1,0:T(8,128)S(1)} %get-tuple-element.93.refs_0_, f32[96,1024]{1,0:T(8,128)S(1)} %get-tuple-element.101.refs_1_, f32[64,1024]{1,0:T(8,128)S(1)} %get-tuple-element.102.refs_2_, ...), custom_call_target="tpu_custom_call" | custom-call | flops 1000000000 | bytes 1 | tf_op jit(solution)/shard_map/pallas_call | solution.py:596
  18.5 0.6 collective-permute-done.5.two_ref.refs_2_
  19.5 2.1 %collective-permute-start.7 = (f32[16,128]{1,0:T(8,128)S(1)}, f32[16,128]{1,0:T(8,128)S(1)}, u32[]{:S(2)}, u32[]{:S(2)}) collective-permute-start(f32[16,128]{1,0:T(8,128)S(1)} %shard_map.137.refs_9_), channel_id=1, source_target_pairs={{0,8},{1,9},{2,10},{3,11},{4,12},{5,13},{6,14},{7,15},{8,0},{9,1},... | collective-permute-start | bytes 24584 | tf_op jit(solution)/shard_map/ppermute | solution.py:666
  21.6 0.5 collective-permute-start.8
  22.2 0.8 %shard_map.138 = (f32[64,1024]{1,0:T(8,128)S(1)}, f32[64,1024]{1,0:T(8,128)S(1)}, f32[96,1024]{1,0:T(8,128)S(1)}, f32[16,512]{1,0:T(8,128)S(1)}) custom-call(f32[64,1024]{1,0:T(8,128)S(1)} %get-tuple-element.107.refs_0_, f32[16,128]{1,0:T(8,128)S(1)} %collective-permute-done.4.one_ref.refs_1_, f32[16,128]{1,0:T(8,128)S(1)} %collective-permute-done.5.two_ref.refs_2_, ...), custom_call_target="tpu_custom_call" | custom-call | flops 1000000000 | bytes 1 | tf_op jit(solution)/shard_map/pallas_call | solution.py:596
  23.1 1.7 %shard_map.139 = (f32[96,1024]{1,0:T(8,128)S(1)}, f32[64,1024]{1,0:T(8,128)S(1)}, f32[64,256]{1,0:T(8,128)S(1)}) custom-call(f32[64,1024]{1,0:T(8,128)S(1)} %get-tuple-element.116.refs_0_.refs_6_, f32[96,1024]{1,0:T(8,128)S(1)} %get-tuple-element.117.refs_1_, f32[16,512]{1,0:T(8,128)S(1)} %get-tuple-element.118.refs_2_, ...), custom_call_target="tpu_custom_call" | custom-call | flops 1000000000 | bytes 1 | tf_op jit(solution)/shard_map/pallas_call | solution.py:596
  24.7 0.7 %shard_map.140 = (f32[64,1024]{1,0:T(8,128)S(1)}, f32[64,1024]{1,0:T(8,128)S(1)}, f32[64,128]{1,0:T(8,128)S(1)}) custom-call(f32[64,1024]{1,0:T(8,128)S(1)} %get-tuple-element.115.refs_0_, f32[96,1024]{1,0:T(8,128)S(1)} %get-tuple-element.120.refs_1_, f32[64,1024]{1,0:T(8,128)S(1)} %get-tuple-element.121.refs_2_, ...), custom_call_target="tpu_custom_call" | custom-call | flops 1000000000 | bytes 1 | tf_op jit(solution)/shard_map/pallas_call | solution.py:596
  25.9 1.1 %collective-permute-start.10 = (f32[16,128]{1,0:T(8,128)S(1)}, f32[16,128]{1,0:T(8,128)S(1)}, u32[]{:S(2)}, u32[]{:S(2)}) collective-permute-start(f32[16,128]{1,0:T(8,128)S(1)} %shard_map.141.refs_9_), channel_id=1, source_target_pairs={{0,8},{1,9},{2,10},{3,11},{4,12},{5,13},{6,14},{7,15},{8,0},{9,1},... | collective-permute-start | bytes 24584 | tf_op jit(solution)/shard_map/ppermute | solution.py:666
  26.9 0.9 %collective-permute-start.11 = (f32[16,128]{1,0:T(8,128)S(1)}, f32[16,128]{1,0:T(8,128)S(1)}, u32[]{:S(2)}, u32[]{:S(2)}) collective-permute-start(f32[16,128]{1,0:T(8,128)S(1)} %shard_map.141.refs_9_), channel_id=1, source_target_pairs={{0,2},{1,3},{2,0},{3,1},{4,6},{5,7},{6,4},{7,5},{8,16},{9,17},{10,... | collective-permute-start | bytes 24584 | tf_op jit(solution)/shard_map/ppermute | solution.py:666
  27.9 0.8 %shard_map.142 = (f32[64,1024]{1,0:T(8,128)S(1)}, f32[64,1024]{1,0:T(8,128)S(1)}, f32[96,1024]{1,0:T(8,128)S(1)}, f32[16,512]{1,0:T(8,128)S(1)}) custom-call(f32[64,1024]{1,0:T(8,128)S(1)} %get-tuple-element.122.refs_0_, f32[16,128]{1,0:T(8,128)S(1)} %collective-permute-done.7.one_ref.refs_1_, f32[16,128]{1,0:T(8,128)S(1)} %collective-permute-done.8.two_ref.refs_2_, ...), custom_call_target="tpu_custom_call" | custom-call | flops 1000000000 | bytes 1 | tf_op jit(solution)/shard_map/pallas_call | solution.py:596
  28.8 1.6 %shard_map.143 = (f32[96,1024]{1,0:T(8,128)S(1)}, f32[64,1024]{1,0:T(8,128)S(1)}, f32[64,256]{1,0:T(8,128)S(1)}) custom-call(f32[64,1024]{1,0:T(8,128)S(1)} %get-tuple-element.126.refs_0_, f32[96,1024]{1,0:T(8,128)S(1)} %get-tuple-element.127.refs_1_, f32[16,512]{1,0:T(8,128)S(1)} %get-tuple-element.128.refs_2_, f32[8,1024]{1,0:T(8,128)S(1)} %get-tuple-element.97.refs_3_, ...), custom_call_target="tpu_custom_call" | custom-call | flops 1000000000 | bytes 1 | tf_op jit(solution)/shard_map/pallas_call | solution.py:596
  30.4 0.7 %shard_map.144.refs_0_ = f32[64,1024]{1,0:T(8,128)S(1)} custom-call(f32[64,1024]{1,0:T(8,128)S(1)} %get-tuple-element.125.refs_0_, f32[96,1024]{1,0:T(8,128)S(1)} %get-tuple-element.130.refs_1_, f32[64,1024]{1,0:T(8,128)S(1)} %get-tuple-element.131.refs_2_, f32[16,512]{1,0:T(8,128)S(1)} %collective-permute-done.9.refs_3_, ...), custom_call_target="tpu_custom_call" | custom-call | flops 1000000000 | bytes 1 | tf_op jit(solution)/shard_map/pallas_call | solution.py:596
  31.1 0.6 shard_map.145
  31.7 0.6 collective-permute-start.12
  32.2 1.1 %collective-permute-start.13 = (f32[64,128]{1,0:T(8,128)S(1)}, f32[64,128]{1,0:T(8,128)S(1)}, u32[]{:S(2)}, u32[]{:S(2)}) collective-permute-start(f32[64,128]{1,0:T(8,128)S(1)} %get-tuple-element.133), channel_id=1, source_target_pairs={{0,2},{1,8},{2,0},{3,10},{4,6},{5,12},{6,4},{7,14},{8,1},{9,16},{1... | collective-permute-start | bytes 98312 | tf_op jit(solution)/shard_map/ppermute | solution.py:669
  33.6 2.6 %collective-permute-done.13.cross_ref = f32[64,128]{1,0:T(8,128)S(1)} collective-permute-done((f32[64,128]{1,0:T(8,128)S(1)}, f32[64,128]{1,0:T(8,128)S(1)}, u32[]{:S(2)}, u32[]{:S(2)}) %collective-permute-start.13) | collective-permute-done | bytes 32800 | tf_op jit(solution)/shard_map/ppermute | solution.py:669
  36.2 2.6 %shard_map.148 = (f32[64,1024]{1,0:T(8,128)S(1)}, f32[64,128]{1,0:T(8,128)S(1)}) custom-call(f32[64,1024]{1,0:T(8,128)S(1)} %get-tuple-element.132.r_ref.refs_0_, f32[64,128]{1,0:T(8,128)S(1)} %collective-permute-done.12.swapped_ref, f32[64,128]{1,0:T(8,128)S(1)} %collective-permute-done.13.cross_ref, s32[4,512]{1,0:T(4,128)S(1)} %get-tuple-element.135.gather_ref, ...), custom_call_target="tpu_custom_call" | custom-call | flops 1000000000 | bytes 1 | tf_op jit(solution)/shard_map/pallas_call | solution.py:596
  38.8 1.2 %collective-permute-start.15 = (f32[64,128]{1,0:T(8,128)S(1)}, f32[64,128]{1,0:T(8,128)S(1)}, u32[]{:S(2)}, u32[]{:S(2)}) collective-permute-start(f32[64,128]{1,0:T(8,128)S(1)} %get-tuple-element.143), channel_id=1, source_target_pairs={{0,2},{1,8},{2,0},{3,10},{4,6},{5,12},{6,4},{7,14},{8,1},{9,16},{1... | collective-permute-start | bytes 98312 | tf_op jit(solution)/shard_map/ppermute | solution.py:669
  40.0 2.8 %collective-permute-done.15.cross_ref = f32[64,128]{1,0:T(8,128)S(1)} collective-permute-done((f32[64,128]{1,0:T(8,128)S(1)}, f32[64,128]{1,0:T(8,128)S(1)}, u32[]{:S(2)}, u32[]{:S(2)}) %collective-permute-start.15) | collective-permute-done | bytes 32800 | tf_op jit(solution)/shard_map/ppermute | solution.py:669
  42.8 0.7 %shard_map.149 = (f32[64,1024]{1,0:T(8,128)S(1)}, f32[96,1024]{1,0:T(8,128)S(1)}, f32[16,512]{1,0:T(8,128)S(1)}, f32[16,128]{1,0:T(8,128)S(1)}) custom-call(f32[64,1024]{1,0:T(8,128)S(1)} %get-tuple-element.142.field_ref, f32[64,128]{1,0:T(8,128)S(1)} %collective-permute-done.14.swapped_ref, f32[64,128]{1,0:T(8,128)S(1)} %collective-permute-done.15.cross_ref, ...), custom_call_target="tpu_custom_call" | custom-call | flops 1000000000 | bytes 1 | tf_op jit(solution)/shard_map/pallas_call | solution.py:596
  43.7 1.5 %collective-permute-start.18 = (f32[16,128]{1,0:T(8,128)S(1)}, f32[16,128]{1,0:T(8,128)S(1)}, u32[]{:S(2)}, u32[]{:S(2)}) collective-permute-start(f32[16,128]{1,0:T(8,128)S(1)} %get-tuple-element.151), channel_id=1, source_target_pairs={{0,2},{1,3},{2,0},{3,1},{4,6},{5,7},{6,4},{7,5},{8,16},{9,17},{10,... | collective-permute-start | bytes 24584 | tf_op jit(solution)/shard_map/ppermute | solution.py:666
  45.2 1.7 %shard_map.150 = (f32[96,1024]{1,0:T(8,128)S(1)}, f32[64,1024]{1,0:T(8,128)S(1)}, f32[64,256]{1,0:T(8,128)S(1)}) custom-call(f32[64,1024]{1,0:T(8,128)S(1)} %get-tuple-element.144.refs_0_, f32[96,1024]{1,0:T(8,128)S(1)} %get-tuple-element.145.refs_1_, f32[16,512]{1,0:T(8,128)S(1)} %get-tuple-element.146.refs_2_, f32[8,1024]{1,0:T(8,128)S(1)} %get-tuple-element.97.refs_3_, ...), custom_call_target="tpu_custom_call" | custom-call | flops 1000000000 | bytes 1 | tf_op jit(solution)/shard_map/pallas_call | solution.py:596
  46.9 0.7 %shard_map.151 = (f32[64,1024]{1,0:T(8,128)S(1)}, f32[64,1024]{1,0:T(8,128)S(1)}, f32[64,128]{1,0:T(8,128)S(1)}) custom-call(f32[64,1024]{1,0:T(8,128)S(1)} %get-tuple-element.132.r_ref.refs_0_, f32[96,1024]{1,0:T(8,128)S(1)} %get-tuple-element.148.refs_1_, f32[64,1024]{1,0:T(8,128)S(1)} %get-tuple-element.149.refs_2_, ...), custom_call_target="tpu_custom_call" | custom-call | flops 1000000000 | bytes 1 | tf_op jit(solution)/shard_map/pallas_call | solution.py:596
  48.0 1.8 %collective-permute-start.20 = (f32[16,128]{1,0:T(8,128)S(1)}, f32[16,128]{1,0:T(8,128)S(1)}, u32[]{:S(2)}, u32[]{:S(2)}) collective-permute-start(f32[16,128]{1,0:T(8,128)S(1)} %shard_map.152.refs_9_), channel_id=1, source_target_pairs={{0,8},{1,9},{2,10},{3,11},{4,12},{5,13},{6,14},{7,15},{8,0},{9,1},... | collective-permute-start | bytes 24584 | tf_op jit(solution)/shard_map/ppermute | solution.py:666
  49.8 1.1 %collective-permute-start.21 = (f32[16,128]{1,0:T(8,128)S(1)}, f32[16,128]{1,0:T(8,128)S(1)}, u32[]{:S(2)}, u32[]{:S(2)}) collective-permute-start(f32[16,128]{1,0:T(8,128)S(1)} %shard_map.152.refs_9_), channel_id=1, source_target_pairs={{0,2},{1,3},{2,0},{3,1},{4,6},{5,7},{6,4},{7,5},{8,16},{9,17},{10,... | collective-permute-start | bytes 24584 | tf_op jit(solution)/shard_map/ppermute | solution.py:666
  50.9 0.8 %shard_map.153 = (f32[64,1024]{1,0:T(8,128)S(1)}, f32[64,1024]{1,0:T(8,128)S(1)}, f32[96,1024]{1,0:T(8,128)S(1)}, f32[16,512]{1,0:T(8,128)S(1)}) custom-call(f32[64,1024]{1,0:T(8,128)S(1)} %get-tuple-element.150.refs_0_, f32[16,128]{1,0:T(8,128)S(1)} %collective-permute-done.17.one_ref.refs_1_, f32[16,128]{1,0:T(8,128)S(1)} %collective-permute-done.18.two_ref.refs_2_, ...), custom_call_target="tpu_custom_call" | custom-call | flops 1000000000 | bytes 1 | tf_op jit(solution)/shard_map/pallas_call | solution.py:596
  51.8 1.7 %shard_map.154 = (f32[96,1024]{1,0:T(8,128)S(1)}, f32[64,1024]{1,0:T(8,128)S(1)}, f32[64,256]{1,0:T(8,128)S(1)}) custom-call(f32[64,1024]{1,0:T(8,128)S(1)} %get-tuple-element.155.refs_0_.refs_6_, f32[96,1024]{1,0:T(8,128)S(1)} %get-tuple-element.156.refs_1_, f32[16,512]{1,0:T(8,128)S(1)} %get-tuple-element.157.refs_2_, ...), custom_call_target="tpu_custom_call" | custom-call | flops 1000000000 | bytes 1 | tf_op jit(solution)/shard_map/pallas_call | solution.py:596
  53.4 0.7 %shard_map.155 = (f32[64,1024]{1,0:T(8,128)S(1)}, f32[64,1024]{1,0:T(8,128)S(1)}, f32[64,128]{1,0:T(8,128)S(1)}) custom-call(f32[64,1024]{1,0:T(8,128)S(1)} %get-tuple-element.154.refs_0_, f32[96,1024]{1,0:T(8,128)S(1)} %get-tuple-element.159.refs_1_, f32[64,1024]{1,0:T(8,128)S(1)} %get-tuple-element.160.refs_2_, ...), custom_call_target="tpu_custom_call" | custom-call | flops 1000000000 | bytes 1 | tf_op jit(solution)/shard_map/pallas_call | solution.py:596
  54.8 1.3 %collective-permute-start.24 = (f32[16,128]{1,0:T(8,128)S(1)}, f32[16,128]{1,0:T(8,128)S(1)}, u32[]{:S(2)}, u32[]{:S(2)}) collective-permute-start(f32[16,128]{1,0:T(8,128)S(1)} %shard_map.156.refs_9_), channel_id=1, source_target_pairs={{0,2},{1,3},{2,0},{3,1},{4,6},{5,7},{6,4},{7,5},{8,16},{9,17},{10,... | collective-permute-start | bytes 24584 | tf_op jit(solution)/shard_map/ppermute | solution.py:666
  56.0 0.8 %shard_map.157 = (f32[64,1024]{1,0:T(8,128)S(1)}, f32[64,1024]{1,0:T(8,128)S(1)}, f32[96,1024]{1,0:T(8,128)S(1)}, f32[16,512]{1,0:T(8,128)S(1)}) custom-call(f32[64,1024]{1,0:T(8,128)S(1)} %get-tuple-element.161.refs_0_, f32[16,128]{1,0:T(8,128)S(1)} %collective-permute-done.20.one_ref.refs_1_, f32[16,128]{1,0:T(8,128)S(1)} %collective-permute-done.21.two_ref.refs_2_, ...), custom_call_target="tpu_custom_call" | custom-call | flops 1000000000 | bytes 1 | tf_op jit(solution)/shard_map/pallas_call | solution.py:596
  56.9 1.7 %shard_map.158 = (f32[96,1024]{1,0:T(8,128)S(1)}, f32[64,1024]{1,0:T(8,128)S(1)}, f32[64,256]{1,0:T(8,128)S(1)}) custom-call(f32[64,1024]{1,0:T(8,128)S(1)} %get-tuple-element.165.refs_0_.refs_6_, f32[96,1024]{1,0:T(8,128)S(1)} %get-tuple-element.166.refs_1_, f32[16,512]{1,0:T(8,128)S(1)} %get-tuple-element.167.refs_2_, ...), custom_call_target="tpu_custom_call" | custom-call | flops 1000000000 | bytes 1 | tf_op jit(solution)/shard_map/pallas_call | solution.py:596
  58.6 0.7 %shard_map.159 = (f32[64,1024]{1,0:T(8,128)S(1)}, f32[64,1024]{1,0:T(8,128)S(1)}, f32[64,128]{1,0:T(8,128)S(1)}) custom-call(f32[64,1024]{1,0:T(8,128)S(1)} %get-tuple-element.164.refs_0_, f32[96,1024]{1,0:T(8,128)S(1)} %get-tuple-element.169.refs_1_, f32[64,1024]{1,0:T(8,128)S(1)} %get-tuple-element.170.refs_2_, ...), custom_call_target="tpu_custom_call" | custom-call | flops 1000000000 | bytes 1 | tf_op jit(solution)/shard_map/pallas_call | solution.py:596
  59.7 1.4 %collective-permute-start.26 = (f32[16,128]{1,0:T(8,128)S(1)}, f32[16,128]{1,0:T(8,128)S(1)}, u32[]{:S(2)}, u32[]{:S(2)}) collective-permute-start(f32[16,128]{1,0:T(8,128)S(1)} %shard_map.160.refs_9_), channel_id=1, source_target_pairs={{0,8},{1,9},{2,10},{3,11},{4,12},{5,13},{6,14},{7,15},{8,0},{9,1},... | collective-permute-start | bytes 24584 | tf_op jit(solution)/shard_map/ppermute | solution.py:666
  61.2 0.9 %collective-permute-start.27 = (f32[16,128]{1,0:T(8,128)S(1)}, f32[16,128]{1,0:T(8,128)S(1)}, u32[]{:S(2)}, u32[]{:S(2)}) collective-permute-start(f32[16,128]{1,0:T(8,128)S(1)} %shard_map.160.refs_9_), channel_id=1, source_target_pairs={{0,2},{1,3},{2,0},{3,1},{4,6},{5,7},{6,4},{7,5},{8,16},{9,17},{10,... | collective-permute-start | bytes 24584 | tf_op jit(solution)/shard_map/ppermute | solution.py:666
  62.1 0.8 %shard_map.161 = (f32[64,1024]{1,0:T(8,128)S(1)}, f32[64,1024]{1,0:T(8,128)S(1)}, f32[96,1024]{1,0:T(8,128)S(1)}, f32[16,512]{1,0:T(8,128)S(1)}) custom-call(f32[64,1024]{1,0:T(8,128)S(1)} %get-tuple-element.171.refs_0_, f32[16,128]{1,0:T(8,128)S(1)} %collective-permute-done.23.one_ref.refs_1_, f32[16,128]{1,0:T(8,128)S(1)} %collective-permute-done.24.two_ref.refs_2_, ...), custom_call_target="tpu_custom_call" | custom-call | flops 1000000000 | bytes 1 | tf_op jit(solution)/shard_map/pallas_call | solution.py:596
  63.0 1.1 %shard_map.162 = (f32[96,256]{1,0:T(8,128)S(1)}, f32[64,256]{1,0:T(8,128)S(1)}, f32[64,256]{1,0:T(8,128)}) custom-call(f32[64,1024]{1,0:T(8,128)S(1)} %get-tuple-element.174.refs_0_, f32[96,1024]{1,0:T(8,128)S(1)} %get-tuple-element.175.refs_1_, f32[16,512]{1,0:T(8,128)S(1)} %get-tuple-element.176.refs_2_, f32[8,1024]{1,0:T(8,128)S(1)} %get-tuple-element.97.refs_3_, ...), custom_call_target="tpu_custom_call" | custom-call | flops 1000000000 | bytes 1 | tf_op jit(solution)/shard_map/pallas_call | solution.py:596
  64.8 0.9 %shard_map.164 = f32[64,256]{1,0:T(8,128)} custom-call(f32[64,256]{1,0:T(8,128)S(1)} %shard_map.163.refs_0_, f32[16,128]{1,0:T(8,128)S(1)} %collective-permute-done.26.refs_1_, f32[16,128]{1,0:T(8,128)S(1)} %collective-permute-done.27.refs_2_, s32[8,1024]{1,0:T(8,128)S(1)} %get-tuple-element.109.edge_ref.refs_3_, ...), custom_call_target="tpu_custom_call" | custom-call | flops 1000000000 | bytes 1 | tf_op jit(solution)/shard_map/pallas_call | solution.py:596
  (67 shorter events, 5.4 us)
Async XLA Ops:
  0.6 0.7 copy-start.11
  0.6 0.7 %copy-start.7 = (s32[256]{0:T(256)S(1)}, s32[256]{0:T(256)}, u32[]{:S(2)}) copy-start(s32[256]{0:T(256)} %param.14) | copy-start | bytes 3076
  0.7 0.7 %copy-start.9 = (s32[1,16]{1,0:T(1,128)S(1)}, s32[1,16]{1,0:T(1,128)}, u32[]{:S(2)}) copy-start(s32[1,16]{1,0:T(1,128)} %rim_ref.1) | copy-start | bytes 196
  0.7 0.7 %copy-start.10 = (s32[1,64]{1,0:T(1,128)S(1)}, s32[1,64]{1,0:T(1,128)}, u32[]{:S(2)}) copy-start(s32[1,64]{1,0:T(1,128)} %size_ref.1) | copy-start | bytes 772
  0.7 0.7 %copy-start.6 = (f32[256]{0:T(256)S(1)}, f32[256]{0:T(256)}, u32[]{:S(2)}) copy-start(f32[256]{0:T(256)} %param.13) | copy-start | bytes 3076
  0.7 0.7 %copy-start.8 = (s32[1,128]{1,0:T(1,128)S(1)}, s32[1,128]{1,0:T(1,128)}, u32[]{:S(2)}) copy-start(s32[1,128]{1,0:T(1,128)} %sub_ref.1) | copy-start | bytes 1540
  1.4 0.8 %copy-start.1 = (f32[64,256]{1,0:T(8,128)S(1)}, f32[64,256]{1,0:T(8,128)}, u32[]{:S(2)}) copy-start(f32[64,256]{1,0:T(8,128)} %b_ref.1) | copy-start | bytes 196612
  2.2 0.7 %copy-start.5 = (s32[6,256]{1,0:T(8,128)S(1)}, s32[6,256]{1,0:T(8,128)}, u32[]{:S(2)}) copy-start(s32[6,256]{1,0:T(8,128)} %face_ref.1) | copy-start | bytes 18436
  2.9 4.7 %copy-start.2 = (f32[2,64,64]{2,1,0:T(8,128)S(1)}, f32[2,64,64]{2,1,0:T(8,128)}, u32[]{:S(2)}) copy-start(f32[2,64,64]{2,1,0:T(8,128)} %refs_4_.1) | copy-start | bytes 98308
  2.9 4.7 %copy-start.3 = (f32[96,64]{0,1:T(8,128)S(1)}, f32[96,64]{0,1:T(8,128)}, u32[]{:S(2)}) copy-start(f32[96,64]{0,1:T(8,128)} %param.16) | copy-start | bytes 73732
  3.1 5.8 %collective-permute-start = (f32[80,256]{1,0:T(8,128)S(1)}, f32[80,256]{1,0:T(8,128)S(1)}, u32[]{:S(2)}, u32[]{:S(2)}) collective-permute-start(f32[80,256]{1,0:T(8,128)S(1)} %shard_map.131.refs_0_), channel_id=1, source_target_pairs={{0,2},{1,3},{2,0},{3,1},{4,6},{5,7},{6,4},{7,5},{8,10},{9,11},{10,... | collective-permute-start | bytes 245768 | tf_op jit(solution)/shard_map/ppermute | solution.py:690
  6.1 5.3 %collective-permute-start.1 = (f32[80,256]{1,0:T(8,128)S(1)}, f32[80,256]{1,0:T(8,128)S(1)}, u32[]{:S(2)}, u32[]{:S(2)}) collective-permute-start(f32[80,256]{1,0:T(8,128)S(1)} %shard_map.131.refs_0_), channel_id=1, source_target_pairs={{0,4},{1,5},{2,6},{3,7},{4,0},{5,1},{6,2},{7,3},{8,12},{9,13},{10,... | collective-permute-start | bytes 245768 | tf_op jit(solution)/shard_map/ppermute | solution.py:690
  7.6 5.3 %collective-permute-start.2 = (f32[80,256]{1,0:T(8,128)S(1)}, f32[80,256]{1,0:T(8,128)S(1)}, u32[]{:S(2)}, u32[]{:S(2)}) collective-permute-start(f32[80,256]{1,0:T(8,128)S(1)} %shard_map.131.refs_0_), channel_id=1, source_target_pairs={{0,6},{1,7},{2,4},{3,5},{4,2},{5,3},{6,0},{7,1},{8,14},{9,15},{10,... | collective-permute-start | bytes 245768 | tf_op jit(solution)/shard_map/ppermute | solution.py:690
  7.7 1.0 %copy-start = (f32[8,64,64]{2,1,0:T(8,128)S(1)}, f32[8,64,64]{2,1,0:T(8,128)}, u32[]{:S(2)}) copy-start(f32[8,64,64]{2,1,0:T(8,128)} %restriction_ref.1) | copy-start | bytes 393220
  7.7 1.0 %copy-start.4 = (f32[64,64]{1,0:T(8,128)S(1)}, f32[64,64]{1,0:T(8,128)}, u32[]{:S(2)}) copy-start(f32[64,64]{1,0:T(8,128)} %stiff_ref.5) | copy-start | bytes 49156
  13.8 4.7 %collective-permute-start.4 = (f32[16,128]{1,0:T(8,128)S(1)}, f32[16,128]{1,0:T(8,128)S(1)}, u32[]{:S(2)}, u32[]{:S(2)}) collective-permute-start(f32[16,128]{1,0:T(8,128)S(1)} %get-tuple-element.108), channel_id=1, source_target_pairs={{0,8},{1,9},{2,10},{3,11},{4,12},{5,13},{6,14},{7,15},{8,0},{9,1},... | collective-permute-start | bytes 24584 | tf_op jit(solution)/shard_map/ppermute | solution.py:666
  15.4 3.7 %collective-permute-start.5 = (f32[16,128]{1,0:T(8,128)S(1)}, f32[16,128]{1,0:T(8,128)S(1)}, u32[]{:S(2)}, u32[]{:S(2)}) collective-permute-start(f32[16,128]{1,0:T(8,128)S(1)} %get-tuple-element.108), channel_id=1, source_target_pairs={{0,2},{1,3},{2,0},{3,1},{4,6},{5,7},{6,4},{7,5},{8,16},{9,17},{10,... | collective-permute-start | bytes 24584 | tf_op jit(solution)/shard_map/ppermute | solution.py:666
  16.0 1.8 %collective-permute-start.3 = (f32[16,512]{1,0:T(8,128)S(1)}, f32[16,512]{1,0:T(8,128)S(1)}, u32[]{:S(2)}, u32[]{:S(2)}) collective-permute-start(f32[16,512]{1,0:T(8,128)S(1)} %get-tuple-element.96.refs_2_), channel_id=1, source_target_pairs={{0,1},{1,0},{2,3},{3,2},{4,5},{5,4},{6,7},{7,6},{8,9},{9,8},{10,11... | collective-permute-start | bytes 98312 | tf_op jit(solution)/shard_map/ppermute | solution.py:711
  19.5 5.9 %collective-permute-start.7 = (f32[16,128]{1,0:T(8,128)S(1)}, f32[16,128]{1,0:T(8,128)S(1)}, u32[]{:S(2)}, u32[]{:S(2)}) collective-permute-start(f32[16,128]{1,0:T(8,128)S(1)} %shard_map.137.refs_9_), channel_id=1, source_target_pairs={{0,8},{1,9},{2,10},{3,11},{4,12},{5,13},{6,14},{7,15},{8,0},{9,1},... | collective-permute-start | bytes 24584 | tf_op jit(solution)/shard_map/ppermute | solution.py:666
  21.6 3.8 %collective-permute-start.8 = (f32[16,128]{1,0:T(8,128)S(1)}, f32[16,128]{1,0:T(8,128)S(1)}, u32[]{:S(2)}, u32[]{:S(2)}) collective-permute-start(f32[16,128]{1,0:T(8,128)S(1)} %shard_map.137.refs_9_), channel_id=1, source_target_pairs={{0,2},{1,3},{2,0},{3,1},{4,6},{5,7},{6,4},{7,5},{8,16},{9,17},{10,... | collective-permute-start | bytes 24584 | tf_op jit(solution)/shard_map/ppermute | solution.py:666
  23.0 1.7 %collective-permute-start.6 = (f32[16,512]{1,0:T(8,128)S(1)}, f32[16,512]{1,0:T(8,128)S(1)}, u32[]{:S(2)}, u32[]{:S(2)}) collective-permute-start(f32[16,512]{1,0:T(8,128)S(1)} %get-tuple-element.118.refs_2_), channel_id=1, source_target_pairs={{0,1},{1,0},{2,3},{3,2},{4,5},{5,4},{6,7},{7,6},{8,9},{9,8},{10,11... | collective-permute-start | bytes 98312 | tf_op jit(solution)/shard_map/ppermute | solution.py:711
  25.9 5.2 %collective-permute-start.10 = (f32[16,128]{1,0:T(8,128)S(1)}, f32[16,128]{1,0:T(8,128)S(1)}, u32[]{:S(2)}, u32[]{:S(2)}) collective-permute-start(f32[16,128]{1,0:T(8,128)S(1)} %shard_map.141.refs_9_), channel_id=1, source_target_pairs={{0,8},{1,9},{2,10},{3,11},{4,12},{5,13},{6,14},{7,15},{8,0},{9,1},... | collective-permute-start | bytes 24584 | tf_op jit(solution)/shard_map/ppermute | solution.py:666
  26.9 4.2 %collective-permute-start.11 = (f32[16,128]{1,0:T(8,128)S(1)}, f32[16,128]{1,0:T(8,128)S(1)}, u32[]{:S(2)}, u32[]{:S(2)}) collective-permute-start(f32[16,128]{1,0:T(8,128)S(1)} %shard_map.141.refs_9_), channel_id=1, source_target_pairs={{0,2},{1,3},{2,0},{3,1},{4,6},{5,7},{6,4},{7,5},{8,16},{9,17},{10,... | collective-permute-start | bytes 24584 | tf_op jit(solution)/shard_map/ppermute | solution.py:666
  28.7 1.7 %collective-permute-start.9 = (f32[16,512]{1,0:T(8,128)S(1)}, f32[16,512]{1,0:T(8,128)S(1)}, u32[]{:S(2)}, u32[]{:S(2)}) collective-permute-start(f32[16,512]{1,0:T(8,128)S(1)} %get-tuple-element.128.refs_2_), channel_id=1, source_target_pairs={{0,1},{1,0},{2,3},{3,2},{4,5},{5,4},{6,7},{7,6},{8,9},{9,8},{10,11... | collective-permute-start | bytes 98312 | tf_op jit(solution)/shard_map/ppermute | solution.py:711
  31.7 1.9 %collective-permute-start.12 = (f32[64,128]{1,0:T(8,128)S(1)}, f32[64,128]{1,0:T(8,128)S(1)}, u32[]{:S(2)}, u32[]{:S(2)}) collective-permute-start(f32[64,128]{1,0:T(8,128)S(1)} %get-tuple-element.133), channel_id=1, source_target_pairs={{0,1},{1,0},{2,3},{3,2},{4,5},{5,4},{6,7},{7,6},{8,9},{9,8},{10,11... | collective-permute-start | bytes 98312 | tf_op jit(solution)/shard_map/ppermute | solution.py:669
  32.2 3.9 %collective-permute-start.13 = (f32[64,128]{1,0:T(8,128)S(1)}, f32[64,128]{1,0:T(8,128)S(1)}, u32[]{:S(2)}, u32[]{:S(2)}) collective-permute-start(f32[64,128]{1,0:T(8,128)S(1)} %get-tuple-element.133), channel_id=1, source_target_pairs={{0,2},{1,8},{2,0},{3,10},{4,6},{5,12},{6,4},{7,14},{8,1},{9,16},{1... | collective-permute-start | bytes 98312 | tf_op jit(solution)/shard_map/ppermute | solution.py:669
  38.8 1.3 %collective-permute-start.14 = (f32[64,128]{1,0:T(8,128)S(1)}, f32[64,128]{1,0:T(8,128)S(1)}, u32[]{:S(2)}, u32[]{:S(2)}) collective-permute-start(f32[64,128]{1,0:T(8,128)S(1)} %get-tuple-element.143), channel_id=1, source_target_pairs={{0,1},{1,0},{2,3},{3,2},{4,5},{5,4},{6,7},{7,6},{8,9},{9,8},{10,11... | collective-permute-start | bytes 98312 | tf_op jit(solution)/shard_map/ppermute | solution.py:669
  38.8 4.0 %collective-permute-start.15 = (f32[64,128]{1,0:T(8,128)S(1)}, f32[64,128]{1,0:T(8,128)S(1)}, u32[]{:S(2)}, u32[]{:S(2)}) collective-permute-start(f32[64,128]{1,0:T(8,128)S(1)} %get-tuple-element.143), channel_id=1, source_target_pairs={{0,2},{1,8},{2,0},{3,10},{4,6},{5,12},{6,4},{7,14},{8,1},{9,16},{1... | collective-permute-start | bytes 98312 | tf_op jit(solution)/shard_map/ppermute | solution.py:669
  43.5 4.0 %collective-permute-start.17 = (f32[16,128]{1,0:T(8,128)S(1)}, f32[16,128]{1,0:T(8,128)S(1)}, u32[]{:S(2)}, u32[]{:S(2)}) collective-permute-start(f32[16,128]{1,0:T(8,128)S(1)} %get-tuple-element.151), channel_id=1, source_target_pairs={{0,8},{1,9},{2,10},{3,11},{4,12},{5,13},{6,14},{7,15},{8,0},{9,1},... | collective-permute-start | bytes 24584 | tf_op jit(solution)/shard_map/ppermute | solution.py:666
  43.7 3.9 %collective-permute-start.18 = (f32[16,128]{1,0:T(8,128)S(1)}, f32[16,128]{1,0:T(8,128)S(1)}, u32[]{:S(2)}, u32[]{:S(2)}) collective-permute-start(f32[16,128]{1,0:T(8,128)S(1)} %get-tuple-element.151), channel_id=1, source_target_pairs={{0,2},{1,3},{2,0},{3,1},{4,6},{5,7},{6,4},{7,5},{8,16},{9,17},{10,... | collective-permute-start | bytes 24584 | tf_op jit(solution)/shard_map/ppermute | solution.py:666
  45.2 1.7 %collective-permute-start.16 = (f32[16,512]{1,0:T(8,128)S(1)}, f32[16,512]{1,0:T(8,128)S(1)}, u32[]{:S(2)}, u32[]{:S(2)}) collective-permute-start(f32[16,512]{1,0:T(8,128)S(1)} %get-tuple-element.146.refs_2_), channel_id=1, source_target_pairs={{0,1},{1,0},{2,3},{3,2},{4,5},{5,4},{6,7},{7,6},{8,9},{9,8},{10,11... | collective-permute-start | bytes 98312 | tf_op jit(solution)/shard_map/ppermute | solution.py:711
  48.0 6.1 %collective-permute-start.20 = (f32[16,128]{1,0:T(8,128)S(1)}, f32[16,128]{1,0:T(8,128)S(1)}, u32[]{:S(2)}, u32[]{:S(2)}) collective-permute-start(f32[16,128]{1,0:T(8,128)S(1)} %shard_map.152.refs_9_), channel_id=1, source_target_pairs={{0,8},{1,9},{2,10},{3,11},{4,12},{5,13},{6,14},{7,15},{8,0},{9,1},... | collective-permute-start | bytes 24584 | tf_op jit(solution)/shard_map/ppermute | solution.py:666
  49.8 4.4 %collective-permute-start.21 = (f32[16,128]{1,0:T(8,128)S(1)}, f32[16,128]{1,0:T(8,128)S(1)}, u32[]{:S(2)}, u32[]{:S(2)}) collective-permute-start(f32[16,128]{1,0:T(8,128)S(1)} %shard_map.152.refs_9_), channel_id=1, source_target_pairs={{0,2},{1,3},{2,0},{3,1},{4,6},{5,7},{6,4},{7,5},{8,16},{9,17},{10,... | collective-permute-start | bytes 24584 | tf_op jit(solution)/shard_map/ppermute | solution.py:666
  51.7 1.7 %collective-permute-start.19 = (f32[16,512]{1,0:T(8,128)S(1)}, f32[16,512]{1,0:T(8,128)S(1)}, u32[]{:S(2)}, u32[]{:S(2)}) collective-permute-start(f32[16,512]{1,0:T(8,128)S(1)} %get-tuple-element.157.refs_2_), channel_id=1, source_target_pairs={{0,1},{1,0},{2,3},{3,2},{4,5},{5,4},{6,7},{7,6},{8,9},{9,8},{10,11... | collective-permute-start | bytes 98312 | tf_op jit(solution)/shard_map/ppermute | solution.py:711
  54.6 4.7 %collective-permute-start.23 = (f32[16,128]{1,0:T(8,128)S(1)}, f32[16,128]{1,0:T(8,128)S(1)}, u32[]{:S(2)}, u32[]{:S(2)}) collective-permute-start(f32[16,128]{1,0:T(8,128)S(1)} %shard_map.156.refs_9_), channel_id=1, source_target_pairs={{0,8},{1,9},{2,10},{3,11},{4,12},{5,13},{6,14},{7,15},{8,0},{9,1},... | collective-permute-start | bytes 24584 | tf_op jit(solution)/shard_map/ppermute | solution.py:666
  54.8 4.5 %collective-permute-start.24 = (f32[16,128]{1,0:T(8,128)S(1)}, f32[16,128]{1,0:T(8,128)S(1)}, u32[]{:S(2)}, u32[]{:S(2)}) collective-permute-start(f32[16,128]{1,0:T(8,128)S(1)} %shard_map.156.refs_9_), channel_id=1, source_target_pairs={{0,2},{1,3},{2,0},{3,1},{4,6},{5,7},{6,4},{7,5},{8,16},{9,17},{10,... | collective-permute-start | bytes 24584 | tf_op jit(solution)/shard_map/ppermute | solution.py:666
  56.9 1.7 %collective-permute-start.22 = (f32[16,512]{1,0:T(8,128)S(1)}, f32[16,512]{1,0:T(8,128)S(1)}, u32[]{:S(2)}, u32[]{:S(2)}) collective-permute-start(f32[16,512]{1,0:T(8,128)S(1)} %get-tuple-element.167.refs_2_), channel_id=1, source_target_pairs={{0,1},{1,0},{2,3},{3,2},{4,5},{5,4},{6,7},{7,6},{8,9},{9,8},{10,11... | collective-permute-start | bytes 98312 | tf_op jit(solution)/shard_map/ppermute | solution.py:711
  59.7 4.8 %collective-permute-start.26 = (f32[16,128]{1,0:T(8,128)S(1)}, f32[16,128]{1,0:T(8,128)S(1)}, u32[]{:S(2)}, u32[]{:S(2)}) collective-permute-start(f32[16,128]{1,0:T(8,128)S(1)} %shard_map.160.refs_9_), channel_id=1, source_target_pairs={{0,8},{1,9},{2,10},{3,11},{4,12},{5,13},{6,14},{7,15},{8,0},{9,1},... | collective-permute-start | bytes 24584 | tf_op jit(solution)/shard_map/ppermute | solution.py:666
  61.2 3.7 %collective-permute-start.27 = (f32[16,128]{1,0:T(8,128)S(1)}, f32[16,128]{1,0:T(8,128)S(1)}, u32[]{:S(2)}, u32[]{:S(2)}) collective-permute-start(f32[16,128]{1,0:T(8,128)S(1)} %shard_map.160.refs_9_), channel_id=1, source_target_pairs={{0,2},{1,3},{2,0},{3,1},{4,6},{5,7},{6,4},{7,5},{8,16},{9,17},{10,... | collective-permute-start | bytes 24584 | tf_op jit(solution)/shard_map/ppermute | solution.py:666
  62.9 1.3 %collective-permute-start.25 = (f32[16,512]{1,0:T(8,128)S(1)}, f32[16,512]{1,0:T(8,128)S(1)}, u32[]{:S(2)}, u32[]{:S(2)}) collective-permute-start(f32[16,512]{1,0:T(8,128)S(1)} %get-tuple-element.176.refs_2_), channel_id=1, source_target_pairs={{0,1},{1,0},{2,3},{3,2},{4,5},{5,4},{6,7},{7,6},{8,9},{9,8},{10,11... | collective-permute-start | bytes 98312 | tf_op jit(solution)/shard_map/ppermute | solution.py:711

commit v4 on v3

--- a/solution.py
+++ b/solution.py
@@ -44,11 +44,11 @@
     return jnp.dot(left, right, preferred_element_type=jnp.float32)
 
 
-def store_left(out, rows, x):
+def store_left(out, rows, x, base=0):
     high, low = halves(x)
     width = x.shape[1]
     for place, piece in enumerate((high, high, low)):
-        out[rows, place * width : (place + 1) * width] = piece
+        out[rows, base + place * width : base + (place + 1) * width] = piece
 
 
 def take(tile, lane):
@@ -142,10 +142,11 @@
 def prep_coarse_kernel(restriction_ref, stiff_ref, down_out, up_out, c_out):
     modes = stiff_ref.shape[0]
     store_left(c_out, slice(0, modes), stiff_ref[...])
+    pairs = down_out.shape[0] // modes
     for o in range(OCTANTS):
-        rows = slice(o * modes, (o + 1) * modes)
-        store_left(down_out, rows, restriction_ref[o])
-        store_left(up_out, rows, restriction_ref[o].T)
+        rows = slice(o % pairs * modes, (o % pairs + 1) * modes)
+        store_left(down_out, rows, restriction_ref[o], o // pairs * 3 * modes)
+        store_left(up_out, slice(0, modes), restriction_ref[o].T, o * 3 * modes)
 
 
 def pack_kernel(
@@ -179,9 +180,9 @@
 
 def start_kernel(blocks, width, rims, *refs):
     gathered, refs = refs[:blocks], refs[blocks:]
-    stiff_ref, map_ref, t_ref = refs[:3]
-    b_out, ig_out, meta_out, lane_out, at_out, far_out, edge_out, sub_out, rim_out, size_out, coarse_out = refs[3:14]
-    p_out, tr_out, subs_out, rims_out, held = refs[14:]
+    stiff_ref, map_ref, t_ref, _ = refs[:4]
+    b_out, ig_out, meta_out, lane_out, at_out, far_out, edge_out, sub_out, rim_out, size_out, coarse_out = refs[4:15]
+    p_out, tr_out, subs_out, rims_out, held = refs[15:]
     modes, count = map_ref.shape[0], gathered[0].shape[1]
     chip, core = own_place()
     for k, ref in enumerate(gathered):
@@ -265,25 +266,6 @@
     return tiles
 
 
-def rim_kernel(blocks, rims, rim_ref, edge_ref, ig_ref, edges_out, igs_out):
-    group = LANES // rims
-    lane = lanes()
-    edges_out[...] = jnp.full(edges_out.shape, -1, jnp.int32)
-    igs_out[...] = jnp.zeros(igs_out.shape, jnp.float32)
-    count = ig_ref.shape[1] // blocks
-
-    def body(j):
-        tile = cols(j // group, LANES)
-        mine = lane // rims == j % group
-        at, there = rim_element(rim_ref[:, tile], count)
-        edges = pick([edge_ref[:, cols(j, count, h)] for h in range(0, count, LANES)], at, there)
-        igs = pick([ig_ref[:, cols(j, count, h)] for h in range(0, count, LANES)], at, there)
-        edges_out[:, tile] = jnp.where(mine, edges, edges_out[:, tile])
-        igs_out[:, tile] = jnp.where(mine, igs, igs_out[:, tile])
-
-    over(blocks, body)
-
-
 def rim_element(columns, count):
     return jnp.bitwise_and(jnp.right_shift(columns, 7), count // LANES - 1), jnp.bitwise_and(columns, LANES - 1)
 
@@ -357,11 +339,7 @@
             p = p + coefficients[0] * p_ref[:, here]
         p_out[:, here] = p
         for i, j in enumerate(js):
-            spot = cols(j // group, LANES)
-            at, there = rim_element(rim_ref[:, spot], count)
-            mine = of_block(p, i, count)
-            edge = pick([mine[:, h : h + LANES] for h in range(0, count, LANES)], at, there)
-            edge_out[:, spot] = jnp.where(lane // rims == j % group, edge, edge_out[:, spot])
+            keep_edge(j, of_block(p, i, count), rim_ref, edge_out, rims)
 
     if kind == "last":
         body([chip], cols(chip, count), slice(0, count))
@@ -384,20 +362,53 @@
     return jnp.where(place >= 0, take(rim, jnp.bitwise_and(place, LANES - 1)), 0.0)
 
 
-def edge_kernel(rate, rims, one_ref, two_ref, edges_ref, igs_ref, p_ref, tt_ref, t_ref, rim_ref, rims_out):
-    points = one_ref.shape[0]
+def keep_edge(j, p, rim_ref, edge_out, rims):
+    group = LANES // rims
+    spot = cols(j // group, LANES)
+    count = p.shape[1]
+    at, there = rim_element(rim_ref[:, spot], count)
+    edge = pick([p[:, h : h + LANES] for h in range(0, count, LANES)], at, there)
+    edge_out[:, spot] = jnp.where(lanes() // rims == j % group, edge, edge_out[:, spot])
+
+
+def rim_traces(t_ref, p, face):
+    traces = product(t_ref[...], p)
+    points = traces.shape[0] // FACES
+    out = jnp.zeros((points, p.shape[1]), jnp.float32)
+    for f in range(FACES):
+        out = jnp.where(face == f, traces[f * points : (f + 1) * points], out)
+    return out
+
+
+def edge_kernel(rate, rims, one_ref, two_ref, edges_ref, igs_ref, p_ref, tt_ref, t_ref, face_ref, rims_out):
     for t in range(one_ref.shape[1] // LANES):
         spot = slice(t * LANES, (t + 1) * LANES)
         rim = rim_tile(one_ref, two_ref, spot, rims)
         edge = edges_ref[:, spot]
         added = product(tt_ref[...], faces(lambda _, f, h: rim_seen(rim, edge, f, h), [0], LANES))
         p = p_ref[:, spot] + (rate * PENALTY) * (igs_ref[:, spot] * added)
-        traces = product(t_ref[...], p)
-        face = rim_ref[:, spot]
-        out = jnp.zeros((points, LANES), jnp.float32)
-        for f in range(FACES):
-            out = jnp.where(face == f, traces[f * points : (f + 1) * points], out)
-        rims_out[:, spot] = out
+        rims_out[:, spot] = rim_traces(t_ref, p, face_ref[:, spot])
+
+
+def cross_kernel(blocks, rims, r_ref, one_ref, two_ref, edge_ref, tt_ref, size_ref, cond_ref, cross_out):
+    modes = r_ref.shape[0]
+    count = r_ref.shape[1] // blocks
+    group = LANES // rims
+    chip, core = own_place()
+    last = blocks - 1
+    first_tile, last_tile = cols(0, count, 0), cols(last, count, count - LANES)
+    rim = jnp.where(
+        core == 0,
+        rim_tile(one_ref, two_ref, cols(0, LANES), rims),
+        rim_tile(one_ref, two_ref, cols(last // group, LANES), rims),
+    )
+    edge = jnp.where(core == 0, edge_ref[:, first_tile], edge_ref[:, last_tile])
+    seen = faces(lambda _, f, h: rim_seen(rim, edge, f, h), [0], LANES)
+    residual = jnp.where(core == 0, r_ref[:, first_tile], r_ref[:, last_tile])
+    cross_out[modes:, :] = jnp.zeros((cross_out.shape[0] - modes, LANES), jnp.float32)
+    cross_out[:modes, :] = residual + PENALTY * product(tt_ref[...], seen)
+    cross_out[modes : modes + 1, :] = size_ref[last : last + 1, :].astype(jnp.float32)
+    cross_out[modes + 1 : modes + 2, :] = cond_ref[last : last + 1, :]
 
 
 def finish_kernel(kind, rate, blocks, width, rims, *refs):
@@ -409,11 +420,12 @@
     if kind in ("step", "first"):
         p_ref, ig_ref, t_ref, sub_ref, _, r_out, p_out, tr_out, subs_out = refs
     elif kind == "frame":
-        r_out, head_out = refs
-        head_out[...] = jnp.zeros(head_out.shape, jnp.float32)
+        size_ref, cond_ref, _, r_out, near_out = refs
+        near_out[...] = jnp.zeros(near_out.shape, jnp.float32)
     else:
         r_out = refs[0]
     count = r_out.shape[1] // (1 if kind == "last" else blocks)
+    modes = r_ref.shape[0]
 
     def body(js, span, here):
         rim = [rim_tile(one_ref, two_ref, cols(j // group, LANES), rims) for j in js]
@@ -429,8 +441,13 @@
             heads = LANES // HEAD
             for i, j in enumerate(js):
                 spot = cols(j // heads, LANES)
-                moved = pltpu.roll(of_block(residual, i, count)[:, :LANES], (j % heads) * HEAD, 1)
-                head_out[:, spot] = jnp.where(lane // HEAD == j % heads, moved, head_out[:, spot])
+                mine = of_block(residual, i, count)
+                moved = pltpu.roll(mine[:, :LANES], (j % heads) * HEAD, 1)
+                near_out[:modes, spot] = jnp.where(lane // HEAD == j % heads, moved, near_out[:modes, spot])
+                tail = cols(j, LANES, near_out.shape[1] - blocks * LANES)
+                near_out[:modes, tail] = mine[:, count - LANES :]
+                near_out[modes : modes + 1, tail] = size_ref[pl.ds(j, 1), :].astype(jnp.float32)
+                near_out[modes + 1 : modes + 2, tail] = cond_ref[pl.ds(j, 1), :]
         if kind in ("frame", "last"):
             return
         p = p_ref[:, here] + rate * (ig_ref[:, here] * added)
@@ -447,152 +464,279 @@
 
 
 def layout_kernel(blocks, parents, size_ref, gather_out, parent_out, octant_out):
+    lane = lanes()
+    pairs = LANES // parents
+    half = jnp.right_shift(lane, parents.bit_length() - 1)
+    count = parent_out.shape[1] // blocks
+
+    def body(j):
+        each, end, size, start = children(size_ref[pl.ds(j, 1), :], parents, jnp.bitwise_and(lanes(parents), parents - 1))
+        for i in range(OCTANTS // pairs):
+            octant = pairs * i + half
+            place = jnp.bitwise_and(start + octant + HEAD, count - 1)
+            gather_out[i : i + 1, cols(j, LANES)] = jnp.where(octant < size, place, -1)
+        for h in range(0, count, LANES):
+            position = jnp.bitwise_and(lanes(parents) + (h - HEAD), count - 1)
+            parent, octant = owner(each, end, position)
+            parent_out[:, cols(j, count, h)] = parent + parents * (j % pairs)
+            octant_out[:, cols(j, count, h)] = octant
+
+    over(blocks, body)
+
+
+def rim_kernel(blocks, rims, rim_ref, edge_ref, ig_ref, edges_out, igs_out):
+    group = LANES // rims
+    edges_out[...] = jnp.full(edges_out.shape, -1, jnp.int32)
+    igs_out[...] = jnp.zeros(igs_out.shape, jnp.float32)
+    count = ig_ref.shape[1] // blocks
+
+    def body(j):
+        tile = cols(j // group, LANES)
+        mine = lanes() // rims == j % group
+        at, there = rim_element(rim_ref[:, tile], count)
+        edges = pick([edge_ref[:, cols(j, count, h)] for h in range(0, count, LANES)], at, there)
+        igs = pick([ig_ref[:, cols(j, count, h)] for h in range(0, count, LANES)], at, there)
+        edges_out[:, tile] = jnp.where(mine, edges, edges_out[:, tile])
+        igs_out[:, tile] = jnp.where(mine, igs, igs_out[:, tile])
+
+    over(blocks, body)
+
+
+def children(sizes, parents, wanted):
     row = lax.broadcasted_iota(jnp.int32, (parents, LANES), 0)
     lane = lanes(parents)
-    pairs = LANES // parents
-    group = jnp.bitwise_and(lane, parents - 1)
-    half = jnp.right_shift(lanes(), parents.bit_length() - 1)
-    count = parent_out.shape[1] // blocks
-
-    def body(j):
-        sizes = jnp.broadcast_to(size_ref[pl.ds(j, 1), :], (parents, LANES))
-        size = jnp.sum(jnp.where(row == lane, sizes, 0), axis=1, keepdims=True)
-        end = jnp.sum(jnp.where(lane <= row, sizes, 0), axis=1, keepdims=True)
-        size_row = jnp.sum(jnp.where(row == group, size, 0), axis=0, keepdims=True)
-        start_row = jnp.sum(jnp.where(row < group, size, 0), axis=0, keepdims=True)
-        for i in range(OCTANTS // pairs):
-            octant = pairs * i + half
-            place = jnp.bitwise_and(start_row + octant + HEAD, count - 1)
-            gather_out[i : i + 1, cols(j, LANES)] = jnp.where(octant < size_row, place, -1)
-        for h in range(0, count, LANES):
-            position = jnp.bitwise_and(lane + (h - HEAD), count - 1)
-            before = end <= position
-            parent = jnp.sum(before.astype(jnp.int32), axis=0, keepdims=True)
-            start = jnp.sum(jnp.where(before, size, 0), axis=0, keepdims=True)
-            parent_out[:, cols(j, count, h)] = parent + parents * (j % pairs)
-            octant_out[:, cols(j, count, h)] = position[0:1] - start
-
-    over(blocks, body)
-
-
-def heads_of(j, swapped_ref, cross_ref, by, blocks):
-    chip, core = own_place()
-    heads = LANES // HEAD
-    lane = lanes()
-    apart = core if by == 1 else 1 - core
-    source = j + by * apart
-    inside = jnp.logical_and(source >= 0, source < blocks)
-    at = jnp.clip(source, 0, blocks - 1)
-    edge = 0 if by == 1 else blocks - 1
-    tile = pl.ds(pl.multiple_of((at // heads) * LANES, LANES), LANES)
-    near = pltpu.roll(swapped_ref[:, tile], (LANES - (at % heads) * HEAD) % LANES, 1)
-    cross = cross_ref[:, (edge // heads) * LANES : (edge // heads + 1) * LANES]
-    if edge % heads:
-        cross = pltpu.roll(cross, LANES - (edge % heads) * HEAD, 1)
-    segment, segments = lax.axis_index("blk"), lax.axis_size("blk")
-    outside = segment == (segments - 1 if by == 1 else 0)
-    cross = jnp.where(outside, 0.0, cross)
-    return jnp.where(lane < HEAD, jnp.where(inside, near, cross), 0.0)
-
-
-def coarse_kernel(
-    blocks, parents, r_ref, swapped_ref, cross_ref, gather_ref, parent_ref, octant_ref, cond_ref, stiff_ref,
-    down_ref, up_ref, c_ref, field_out, tail_out, right, field_ref, lifted,
+    sizes = jnp.broadcast_to(sizes, (parents, LANES))
+    each = jnp.sum(jnp.where(row == lane, sizes, 0), axis=1, keepdims=True)
+    end = jnp.sum(jnp.where(lane <= row, sizes, 0), axis=1, keepdims=True)
+    size = jnp.sum(jnp.where(row == wanted, each, 0), axis=0, keepdims=True)
+    start = jnp.sum(jnp.where(row < wanted, each, 0), axis=0, keepdims=True)
+    return each, end, size, start
+
+
+def owner(each, end, position):
+    passed = end <= position
+    parent = jnp.sum(passed.astype(jnp.int32), axis=0, keepdims=True)
+    return parent, position[0:1] - jnp.sum(jnp.where(passed, each, 0), axis=0, keepdims=True)
+
+
+def restrict(sources, at, lane_of, down_ref):
+    parts = []
+    for i in range(len(at[0])):
+        picked = [pick(*one) for one in zip(sources, [row[i] for row in at], [row[i] for row in lane_of])]
+        high, low = halves(jnp.concatenate(picked, axis=1))
+        parts += [high, low, high]
+    both = jnp.dot(down_ref[...], jnp.concatenate(parts, axis=0), preferred_element_type=jnp.float32)
+    modes = sources[0][0].shape[0]
+    pairs = both.shape[0] // modes
+    width = LANES // pairs
+    totals = []
+    for b in range(len(sources)):
+        mine = both[:, b * LANES : (b + 1) * LANES]
+        total = mine[:modes]
+        for k in range(1, pairs):
+            total = total + pltpu.roll(mine[k * modes : (k + 1) * modes], LANES - k * width, 1)
+        totals.append(jnp.where(lanes() < width, total, 0.0))
+    return totals
+
+
+def last_parents(tail, modes, parents, extra):
+    wanted = parents - extra + jnp.bitwise_and(lanes(parents), extra - 1)
+    each, end, size, start = children(tail[modes : modes + 1].astype(jnp.int32), parents, wanted)
+    rows = jnp.broadcast_to(tail[modes + 1 : modes + 2], (8, LANES))
+    conds = take(rows, wanted[0:1])[0:1]
+    total = jnp.sum(each, axis=0, keepdims=True)
+    position = total - HEAD + jnp.bitwise_and(lanes(parents), HEAD - 1)
+    parent, octant = owner(each, end, position)
+    return size, start, conds, parent - (parents - extra), octant
+
+
+def restrict_kernel(
+    blocks, parents, r_ref, near_ref, gather_ref, cond_ref, down_ref, right_out, scale_out, front_out
 ):
     modes = r_ref.shape[0]
     count = r_ref.shape[1] // blocks
     lane = lanes()
     pairs = LANES // parents
-
-    def restrict(j):
-        arriving = heads_of(j, swapped_ref, cross_ref, 1, blocks)
-        sources = [r_ref[:, cols(j, count, h)] for h in range(0, count, LANES)]
-        sources[0] = jnp.where(lane < HEAD, arriving, sources[0])
-        sums = [None] * pairs
-        for i in range(OCTANTS // pairs):
-            place = gather_ref[i : i + 1, cols(j, LANES)]
-            children = pick(sources, jnp.right_shift(place, 7), jnp.bitwise_and(place, LANES - 1))
-            both = product(down_ref[pairs * i * modes : pairs * (i + 1) * modes, :], children)
-            for k in range(pairs):
-                one = both[k * modes : (k + 1) * modes]
-                sums[k] = one if sums[k] is None else sums[k] + one
-        total = sums[0]
-        for k in range(1, pairs):
-            total = total + pltpu.roll(sums[k], LANES - k * parents, 1)
-        tile = cols(j // pairs, LANES)
-        moved = pltpu.roll(total, (j % pairs) * parents, 1)
-        right[:, tile] = jnp.where(lane // parents == j % pairs, moved, right[:, tile])
-
-    right[...] = jnp.zeros(right.shape, jnp.float32)
-    over(blocks, restrict)
+    heads = LANES // HEAD
+    extra = LANES // OCTANTS
+    packed = parents // extra
+    chip, core = own_place()
+    own_tiles = blocks // pairs
+    tails = near_ref.shape[1] - blocks * LANES
+    right_out[...] = jnp.zeros(right_out.shape, jnp.float32)
+    scale_out[...] = jnp.ones(scale_out.shape, jnp.float32)
+
+    def body(js, g):
+        sources, at, there = [], [], []
+        for j in js:
+            source = j + core
+            tile = pl.ds(pl.multiple_of((jnp.minimum(source, blocks - 1) // heads) * LANES, LANES), LANES)
+            arriving = pltpu.roll(near_ref[:modes, tile], (LANES - (source % heads) * HEAD) % LANES, 1)
+            arriving = jnp.where(source < blocks, arriving, 0.0)
+            own = [r_ref[:, cols(j, count, h)] for h in range(0, count, LANES)]
+            sources.append([jnp.where(lane < HEAD, arriving, own[0])] + own[1:])
+            places = [gather_ref[i : i + 1, cols(j, LANES)] for i in range(OCTANTS // pairs)]
+            at.append([jnp.right_shift(place, 7) for place in places])
+            there.append([jnp.bitwise_and(place, LANES - 1) for place in places])
+            mine = jnp.broadcast_to(cond_ref[pl.ds(j, 1), :], (8, LANES))
+            mine = pltpu.roll(mine, (j % pairs) * parents, 1)[0:1]
+            spot = cols(j // pairs, LANES)
+            scale_out[:, spot] = jnp.where(lane // parents == j % pairs, mine, scale_out[:, spot])
+        before(js[0] // packed, sources, at, there)
+        totals = restrict(sources, at, there, down_ref)
+        for j, total in zip(js, totals):
+            spot = cols(j // pairs, LANES)
+            right_out[:, spot] = right_out[:, spot] + pltpu.roll(total, (j % pairs) * parents, 1)
+        v = js[0] // packed
+        spot = cols(v // pairs, LANES, own_tiles * LANES)
+        right_out[:, spot] = right_out[:, spot] + pltpu.roll(totals[-1], (v % pairs) * parents, 1)
+
+    def before(v, all_sources, all_at, all_there):
+        group = jnp.bitwise_and(lane // extra, packed - 1)
+        sources = []
+        start = size = head_parent = head_octant = jnp.zeros((1, LANES), jnp.int32)
+        conds = jnp.ones((1, LANES), jnp.float32)
+        for i in range(packed):
+            j = packed * v + i
+            at = j - (1 - core)
+            tail = near_ref[:, pl.ds(pl.multiple_of(tails + jnp.maximum(at, 0) * LANES, LANES), LANES)]
+            sources.append(jnp.where(lane < HEAD, r_ref[:, cols(j, count, 0)], tail[:modes]))
+            one_size, one_start, one_cond, parent, octant = last_parents(tail, modes, parents, extra)
+            mine = group == i
+            size = jnp.where(jnp.logical_and(mine, at >= 0), one_size, size)
+            start = jnp.where(mine, one_start, start)
+            conds = jnp.where(jnp.logical_and(mine, lane < parents), one_cond, conds)
+            here = lane // HEAD == j % heads
+            head_parent = jnp.where(here, parent + (v % pairs) * parents + i * extra, head_parent)
+            head_octant = jnp.where(here, octant, head_octant)
+        octants = [pairs * i + lane // parents for i in range(OCTANTS // pairs)]
+        all_sources.append(sources)
+        all_at.append([jnp.where(octant < size, group, -1) for octant in octants])
+        all_there.append([jnp.bitwise_and(start + octant + HEAD, LANES - 1) for octant in octants])
+        spot = cols(v // pairs, LANES, own_tiles * LANES)
+        conds = pltpu.roll(jnp.broadcast_to(conds, (8, LANES)), (v % pairs) * parents, 1)[0:1]
+        scale_out[:, spot] = jnp.where(lane // parents == v % pairs, conds, scale_out[:, spot])
+        front_out[v, 0:1, :LANES] = head_parent
+        front_out[v, 0:1, LANES:] = head_octant
+
+    over_groups(blocks, body)
+
+
+def coarse_kernel(
+    blocks, parents, rims, right_ref, scale_ref, front_ref, r_ref, cross_ref, gather_ref, parent_ref, octant_ref,
+    stiff_ref, down_ref, up_ref, c_ref, t_ref, rim_ref, face_ref, p_out, rims_out, right, scale, front, edge,
+):
+    modes = r_ref.shape[0]
+    count = r_ref.shape[1] // blocks
+    lane = lanes()
+    pairs = LANES // parents
+    heads = LANES // HEAD
+    extra = LANES // OCTANTS
+    packed = parents // extra
+    chip, core = own_place()
+    segment, segments = lax.axis_index("blk"), lax.axis_size("blk")
+    own_tiles = blocks // pairs
+    edge[...] = jnp.zeros(edge.shape, jnp.float32)
+    right[...] = right_ref[...]
+    scale[...] = scale_ref[...]
+    front[...] = front_ref[...]
+
+    cross = cross_ref[...]
+    size, start, conds, parent, octant = last_parents(cross, modes, parents, extra)
+    above = jnp.where(jnp.logical_and(lane < HEAD, segment < segments - 1), cross[:modes], 0.0)
+    below = jnp.where(lane < HEAD, r_ref[:, :LANES], cross[:modes])
+    below = jnp.where(segment == 0, 0.0, below)
+    at, there = [], []
+    for i in range(OCTANTS // pairs):
+        place = gather_ref[i : i + 1, cols(blocks - 1, LANES)]
+        one = pairs * i + lane // parents
+        inside = jnp.logical_and(place >= 0, place < HEAD)
+        mine = jnp.logical_and(jnp.bitwise_and(lane, parents - 1) < extra, one < size)
+        at.append(jnp.where(core == 1, jnp.where(inside, 0, -1), jnp.where(mine, 0, -1)))
+        there.append(jnp.bitwise_and(jnp.where(core == 1, place, start + one + HEAD), LANES - 1))
+    (added,) = restrict([[jnp.where(core == 1, above, below)]], [at], [there], down_ref)
+    spot = cols((blocks - 1) // pairs, LANES)
+    moved = pltpu.roll(added, ((blocks - 1) % pairs) * parents, 1)
+    right[:, spot] = right[:, spot] + jnp.where(core == 1, moved, 0.0)
+    spot = cols(0, LANES, own_tiles * LANES)
+    right[:, spot] = right[:, spot] + jnp.where(core == 0, added, 0.0)
+    scale[:, spot] = jnp.where(jnp.logical_and(core == 0, lane < extra), conds, scale[:, spot])
+    first = jnp.logical_and(core == 0, lane < HEAD)
+    front[0, 0:1, :LANES] = jnp.where(first, parent, front[0, 0:1, :LANES])
+    front[0, 0:1, LANES:] = jnp.where(first, octant, front[0, 0:1, LANES:])
+
     eye = lax.broadcasted_iota(jnp.int32, (modes, modes), 0) == lax.broadcasted_iota(
         jnp.int32, (modes, modes), 1
     )
     diagonal = jnp.sum(jnp.where(eye, stiff_ref[...], 0.0), axis=1, keepdims=True)
-
-    def solve(t):
-        scale = jnp.zeros((1, LANES), jnp.float32)
-        for k in range(pairs):
-            row = jnp.broadcast_to(cond_ref[pl.ds(pairs * t + k, 1), :], (8, LANES))
-            row = pltpu.roll(row, k * parents, 1)[0:1] if k else row[0:1]
-            scale = jnp.where(lane // parents == k, row, scale)
-        inverse = 1.0 / (scale * diagonal + 2.0 * COUPLING)
-        residual = right[:, cols(t, LANES)]
-        p = residual * inverse * (1.0 / CENTER)
-        field = p
-        for before, correct in steps(KC - 1):
-            left = jnp.where(lane % parents == 0, 0.0, pltpu.roll(p, 1, 1))
-            after = jnp.where(lane % parents == parents - 1, 0.0, pltpu.roll(p, LANES - 1, 1))
-            residual = residual - (
-                scale * product(c_ref[...], p) + COUPLING * (2.0 * p - left - after)
-            )
-            p = before * p + correct * (residual * inverse)
-            field = field + p
-        lifted[:, cols(t, LANES)] = product(up_ref[...], field)
-
-    over(blocks // pairs, solve)
-    tail_out[...] = jnp.zeros(tail_out.shape, jnp.float32)
-    heads = LANES // HEAD
-
-    def prolong(j):
-        sources = [lifted[o * modes : (o + 1) * modes, cols(j // pairs, LANES)] for o in range(OCTANTS)]
-        for h in range(0, count, LANES):
-            parent, octant = parent_ref[:, cols(j, count, h)], octant_ref[:, cols(j, count, h)]
-            out = pick(sources, octant, parent)
-            field_out[:, cols(j, count, h)] = out
-            if h == 0:
-                spot = cols(j // heads, LANES)
-                moved = pltpu.roll(out, (j % heads) * HEAD, 1)
-                tail_out[:, spot] = jnp.where(lane // HEAD == j % heads, moved, tail_out[:, spot])
-
-    over(blocks, prolong)
-
-
-def middle_kernel(
-    blocks, width, rims, field_ref, swapped_ref, cross_ref, t_ref, sub_ref, rim_ref, p_out, tr_out, subs_out, rims_out
-):
-    count = field_ref.shape[1] // blocks
-    lane = lanes()
-    rims_out[...] = jnp.zeros(rims_out.shape, jnp.float32)
+    tiles = right.shape[1] // LANES
+    inverse = 1.0 / (scale[...] * diagonal + 2.0 * COUPLING)
+    residual = right[...]
+    p = residual * inverse * (1.0 / CENTER)
+    field = p
+    for ahead, correct in steps(KC - 1):
+        pieces = []
+        for t in range(tiles):
+            here = p[:, t * LANES : (t + 1) * LANES]
+            last = (parents if t < own_tiles else extra) - 1
+            left = jnp.where(jnp.bitwise_and(lane, last) == 0, 0.0, pltpu.roll(here, 1, 1))
+            after = jnp.where(jnp.bitwise_and(lane, last) == last, 0.0, pltpu.roll(here, LANES - 1, 1))
+            pieces.append(left + after)
+        sides = jnp.concatenate(pieces, axis=1)
+        residual = residual - (scale[...] * product(c_ref[...], p) + COUPLING * (2.0 * p - sides))
+        p = ahead * p + correct * (residual * inverse)
+        field = field + p
+    right[...] = field
+
+    def prolong(js, g):
+        span = cols(g, len(js) * count)
+        v = js[0] // packed
+        leading = take(right[:, cols(own_tiles + v // pairs, LANES)], front[v, 0:1, :LANES])
+        leading_octant = jnp.broadcast_to(front[v, 0:1, LANES:], (8, LANES))
+        spread, octants = [], []
+        for j in js:
+            parent = right[:, cols(j // pairs, LANES)]
+            back = (LANES - (j % heads) * HEAD) % LANES
+            for h in range(0, count, LANES):
+                spot = cols(j, count, h)
+                one, octant = take(parent, parent_ref[:, spot]), octant_ref[:, spot]
+                if h == 0:
+                    one = jnp.where(lane < HEAD, pltpu.roll(leading, back, 1), one)
+                    octant = jnp.where(lane < HEAD, pltpu.roll(leading_octant, back, 1)[0:1], octant)
+                spread.append(one)
+                octants.append(octant)
+        high, low = halves(jnp.concatenate(spread, axis=1))
+        octant = jnp.concatenate(octants, axis=1)
+        parts = []
+        for o in range(OCTANTS):
+            mine = (octant == o).astype(jnp.float32).astype(jnp.bfloat16)
+            parts += [high * mine, low * mine, high * mine]
+        p = jnp.dot(up_ref[...], jnp.concatenate(parts, axis=0), preferred_element_type=jnp.float32)
+        p_out[:, span] = p
+        for i, j in enumerate(js):
+            keep_edge(j, of_block(p, i, count), rim_ref, edge, rims)
+
+    over_groups(blocks, prolong)
+    for t in range(edge.shape[1] // LANES):
+        spot = slice(t * LANES, (t + 1) * LANES)
+        rims_out[:, spot] = rim_traces(t_ref, edge[:, spot], face_ref[:, spot])
+
+
+def spread_kernel(blocks, width, p_ref, t_ref, sub_ref, _, tr_out, subs_out):
+    count = p_ref.shape[1] // blocks
 
     def body(js, g):
         span = cols(g, len(js) * count)
-        for j in js:
-            arriving = heads_of(j, swapped_ref, cross_ref, -1, blocks)
-            p_out[:, cols(j, count)] = field_ref[:, cols(j, count)]
-            first = cols(j, count, 0)
-            p_out[:, first] = jnp.where(lane < HEAD, arriving, field_ref[:, first])
-        traces = product(t_ref[...], p_out[:, span])
+        traces = product(t_ref[...], p_ref[:, span])
         tr_out[:, span] = traces
         for i, j in enumerate(js):
-            tiles = trace_tiles(of_block(traces, i, count))
-            send_sub(j, tiles, sub_ref, subs_out, width)
-            send_rim(j, tiles, rim_ref, rims_out, rims)
+            send_sub(j, trace_tiles(of_block(traces, i, count)), sub_ref, subs_out, width)
 
     over_groups(blocks, body)
 
 
-def call(limit, kernel, outs, *args, scratch=(), hbm=False):
+def call(limit, kernel, outs, *args, scratch=(), hbm=False, flops=3 * 10**9):
+    limit = (60 << 20) if hbm else limit
     return pl.pallas_call(
         kernel,
         out_shape=[jax.ShapeDtypeStruct(shape, kind) for shape, kind in outs],
@@ -600,7 +744,7 @@
         out_specs=[pl.BlockSpec(memory_space=pltpu.VMEM)] * len(outs),
         scratch_shapes=list(scratch),
         compiler_params=pltpu.CompilerParams(vmem_limit_bytes=limit),
-        cost_estimate=pl.CostEstimate(flops=10**9, bytes_accessed=1, transcendentals=0),
+        cost_estimate=pl.CostEstimate(flops=flops, bytes_accessed=1, transcendentals=0),
     )(*args)
 
 
@@ -624,8 +768,8 @@
     points = rows // FACES
     peers, segments = lax.axis_size("sub"), lax.axis_size("blk")
     blocks = peers // CORES
+    parents = group_sizes.shape[1]
     width, rims = sub_sends.shape[1], blk_sends.shape[1]
-    parents = group_sizes.shape[1]
     total = blocks * count
     limit = (4 << 20) if blocks <= 4 else (40 << 20)
     run = functools.partial(call, limit)
@@ -634,7 +778,7 @@
         return -(-size // to) * to
 
     rim_width = pad(blocks * rims, LANES)
-    head_width = pad(blocks * HEAD, LANES)
+    near_width = pad(blocks * HEAD, LANES) + blocks * LANES
     field = ((modes, total), f32)
     block = ((modes, count), f32)
     sends = [((rows, total), f32), ((points, blocks * width), f32), ((points, rim_width), f32)]
@@ -665,15 +809,18 @@
     def over_segments(rim):
         return lax.ppermute(rim, both, ones), lax.ppermute(rim, both, twos)
 
-    def shift(heads):
-        return lax.ppermute(heads, "sub", cores), lax.ppermute(heads, both, crossings)
-
     map_t = trace_map.T
     t3, tt3, k3 = run(
         prep_kernel,
         [((rows, 3 * modes), bf16), ((modes, 3 * rows), bf16), ((2 * modes, 3 * modes), bf16)],
         map_t, stiffness,
     )
+    down3, up3, c3 = run(
+        prep_coarse_kernel,
+        [((LANES // parents * modes, OCTANTS * parents // LANES * 3 * modes), bf16), ((modes, OCTANTS * 3 * modes), bf16), ((modes, 3 * modes), bf16)],
+        restriction, coarse_stiffness,
+    )
+
     height = pad(modes + 11 + pad(width, count) // count, 8)
     inputs = [
         right_side, conductivity.reshape(1, count), material.reshape(1, count), face_neighbour, sub_sends, blk_sends,
@@ -696,12 +843,18 @@
             ((1, blocks * width), i32), ((1, rim_width), i32), ((blocks, LANES), i32), ((blocks, LANES), f32),
             field, *sends,
         ],
-        *gathered, stiffness, map_t, t3,
+        *gathered, stiffness, map_t, t3, c3,
         scratch=[pltpu.VMEM((blocks, height, count), f32)],
     )
 
     edges, igs = run(
         functools.partial(rim_kernel, blocks, rims), [((8, rim_width), i32), ((modes, rim_width), f32)], rim, edge, inverse
+    )
+    gather, parent, octant = run(
+        functools.partial(layout_kernel, blocks, parents),
+        [((OCTANTS * parents // LANES, blocks * LANES), i32), ((1, total), i32), ((1, total), i32)],
+        sizes,
+        flops=3 * 10**10,
     )
     spot = jnp.arange(rim_width, dtype=i32)[None, :]
     rim_face = jnp.where(spot < blocks * rims, lax.div(rim, jnp.int32(count)), -1)
@@ -722,9 +875,13 @@
         args = [r, jump, own, swapped, far, tt3] + ([p] if kind == "step" else [])
         if not goes_on:
             (r,) = run(kernel, [part], *args)
-            outs = [block] if only_own else [field, ((modes, head_width), f32)]
-            kernel = functools.partial(finish_kernel, kind, None, blocks, width, rims)
-            return *run(kernel, outs, r, one, two, edge, tt3), x
+            finish = functools.partial(finish_kernel, kind, None, blocks, width, rims)
+            args = [r, one, two, edge, tt3]
+            if only_own:
+                return *run(finish, [block], *args), x
+            args += [sizes, coarse_cond]
+            (cross,) = run(functools.partial(cross_kernel, blocks, rims), [((modes + 8, LANES), f32)], *args)
+            return *run(finish, [field, ((modes + 8, near_width), f32)], *args, cross), cross, x
         r, p, p_edge = run(kernel, [field, field, ((modes, rim_width), f32)], *args, inverse, rim)
         rate = coefficients[1]
         (rim_out,) = run(
@@ -738,37 +895,35 @@
         )
         return r, p, traces, sub_out, rim_out, x
 
-    gather, parent, octant = run(
-        functools.partial(layout_kernel, blocks, parents),
-        [((OCTANTS * parents // LANES, blocks * LANES), i32), ((1, total), i32), ((1, total), i32)],
-        sizes,
-    )
-    down3, up3, c3 = run(
-        prep_coarse_kernel,
-        [((OCTANTS * modes, 3 * modes), bf16), ((OCTANTS * modes, 3 * modes), bf16), ((modes, 3 * modes), bf16)],
-        restriction, coarse_stiffness,
-    )
-
     x = None
     r = b
     pairs = steps(KF)
     for step in range(KF - 1):
         r, p, traces, sub_out, rim_out, x = apply("step", pairs[step], r, p, traces, sub_out, rim_out, x)
-    r, heads, x = apply("frame", None, r, p, traces, sub_out, rim_out, x)
-
-    correction, tails = run(
-        functools.partial(coarse_kernel, blocks, parents),
-        [field, ((modes, head_width), f32)],
-        r, *shift(heads), gather, parent, octant, coarse_cond, coarse_stiffness, down3, up3, c3,
+    r, near, cross, x = apply("frame", None, r, p, traces, sub_out, rim_out, x)
+
+    cross = lax.ppermute(cross, both, crossings)
+    near = lax.ppermute(near, "sub", cores)
+    coarse_width = blocks * parents + pad(blocks * LANES // OCTANTS, LANES)
+    front = ((blocks * LANES // OCTANTS // parents, 8, 2 * LANES), i32)
+    right, scale, leading = run(
+        functools.partial(restrict_kernel, blocks, parents),
+        [((modes, coarse_width), f32), ((1, coarse_width), f32), front],
+        r, near, gather, coarse_cond, down3,
+        flops=10**8,
+    )
+    p, rim_out = run(
+        functools.partial(coarse_kernel, blocks, parents, rims),
+        [field, sends[2]],
+        right, scale, leading, r, cross, gather, parent, octant, coarse_stiffness, down3, up3, c3, t3, rim, rim_face,
         scratch=[
-            pltpu.VMEM((modes, blocks * parents), f32),
-            pltpu.VMEM((8, LANES), f32),
-            pltpu.VMEM((OCTANTS * modes, blocks * parents), f32),
+            pltpu.VMEM((modes, coarse_width), f32),
+            pltpu.VMEM((1, coarse_width), f32),
+            pltpu.VMEM(*front),
+            pltpu.VMEM((modes, rim_width), f32),
         ],
     )
-    p, traces, sub_out, rim_out = run(
-        functools.partial(middle_kernel, blocks, width, rims), [field, *sends], correction, *shift(tails), t3, subs, rim
-    )
+    traces, sub_out = run(functools.partial(spread_kernel, blocks, width), sends[:2], p, t3, subs, rim_out)
     r, p, traces, sub_out, rim_out, x = apply("first", (0.0, 1.0 / CENTER), r, p, traces, sub_out, rim_out, x)
     for step in range(KF - 1):
         r, p, traces, sub_out, rim_out, x = apply("step", pairs[step], r, p, traces, sub_out, rim_out, x)

time: 66 us -> 60.5 us (0.917)
  waiting for transfers between devices: 10.4 us -> 6.5 us
  local copies, waits for them, and re-layouts: 3.02 us -> 0.8 us
  Pallas kernels: 28.2 us -> 30.2 us
  starting transfers between devices: 23 us -> 21.8 us
    ppermute x4 -> x2, waiting for transfers between devices: 5.41 us -> 0.98 us  [the longest x1 0.98 us: local(): near = lax.ppermute(near, 'sub', cores)]
    unnamed x24 -> x10, local copies, waits for them, and re-layouts: 3.02 us -> 0.8 us
    pallas_call x34 -> x36, Pallas kernels: 28.2 us -> 30.2 us  [call(): pl.pallas_call(kernel, out_shape=[jax.ShapeDtypeStruct(shape, kind) for s...]
    ppermute x4 -> x2, starting transfers between devices: 2.86 us -> 1.43 us  [the longest x1 1.16 us: local(): cross = lax.ppermute(cross, both, crossings)]
  transfers between devices with their start and end apart: 28 -> 26, of which waited for: 7 -> 7; matrix products, arithmetic and copies ran while one was open for 0% -> 0% of each run, Pallas kernels for 31% -> 37%
where the time goes in v4:
time: 60.5 us; the launch traced here: 60.3 us
  Pallas kernels  30.2 us (50%)
  starting transfers between devices  21.8 us (36%)
  waiting for transfers between devices  6.5 us (11%)
  between operations  1.03 us (2%)
  local copies, waits for them, and re-layouts  0.8 us (1%)
    pallas_call x36, Pallas kernels, call(): pl.pallas_call(kernel, out_shape=[jax.ShapeDtypeStruct(shape, kind) for s...  30.2 us
    ppermute x14, starting transfers between devices, over_segments(): return (lax.ppermute(rim, both, ones), lax.ppermute(rim, both, twos))  15.4 us
    ppermute x3, starting transfers between devices, local(): lax.ppermute(packed, 'sub', [(s, s ^ CORES * k) for s in range(peers)])  4.54 us
    ppermute x3, waiting for transfers between devices, local(): lax.ppermute(packed, 'sub', [(s, s ^ CORES * k) for s in range(peers)])  4.2 us
  transfers between devices with their start and end apart: 26, of which 7 were waited for; matrix products, arithmetic and copies ran while one was open for 0% of the time, Pallas kernels for 37%

profile of v4, /device:TPU:0, one launch (start us, length us, event | category | flops | bytes accessed | tf_op | source)
XLA Modules:
  0.0 60.3 jit_solution(6765529002605970640)
XLA Ops:
  0.7 1.6 %shard_map.131.refs_0_ = f32[80,256]{1,0:T(8,128)} custom-call(f32[64,256]{1,0:T(8,128)} %b_ref.1, f32[1,256]{1,0:T(1,128)} %bitcast.6, s32[1,256]{1,0:T(1,128)} %bitcast.7, s32[6,256]{1,0:T(8,128)} %face_ref.1, s32[1,128]{1,0:T(1,128)} %sub_ref.1, s32[1,16]{1,0:T(1,128)} %rim_ref.1, s32[1,64]{1,0:T(1,128)} %size_ref.1, f32[1,64]{1,0:T(1,128)} %bitcast.8), custom_call_target="tpu_custom_call" | custom-call | flops 3000000000 | bytes 1 | tf_op jit(solution)/shard_map/pallas_call | solution.py:740
  2.3 3.0 %collective-permute-start = (f32[80,256]{1,0:T(8,128)}, f32[80,256]{1,0:T(8,128)S(1)}, u32[]{:S(2)}, u32[]{:S(2)}) collective-permute-start(f32[80,256]{1,0:T(8,128)} %shard_map.131.refs_0_), channel_id=1, source_target_pairs={{0,2},{1,3},{2,0},{3,1},{4,6},{5,7},{6,4},{7,5},{8,10},{9,11},{10,... | collective-permute-start | bytes 245768 | tf_op jit(solution)/shard_map/ppermute | solution.py:837
  5.3 1.5 %collective-permute-start.1 = (f32[80,256]{1,0:T(8,128)}, f32[80,256]{1,0:T(8,128)S(1)}, u32[]{:S(2)}, u32[]{:S(2)}) collective-permute-start(f32[80,256]{1,0:T(8,128)} %shard_map.131.refs_0_), channel_id=1, source_target_pairs={{0,4},{1,5},{2,6},{3,7},{4,0},{5,1},{6,2},{7,3},{8,12},{9,13},{10,... | collective-permute-start | bytes 245768 | tf_op jit(solution)/shard_map/ppermute | solution.py:837
  7.0 0.8 %copy-done = f32[8,64,64]{2,1,0:T(8,128)S(1)} copy-done((f32[8,64,64]{2,1,0:T(8,128)S(1)}, f32[8,64,64]{2,1,0:T(8,128)}, u32[]{:S(2)}) %copy-start) | copy-done | bytes 131096
  8.3 2.5 %collective-permute-done.1.refs_2_ = f32[80,256]{1,0:T(8,128)S(1)} collective-permute-done((f32[80,256]{1,0:T(8,128)}, f32[80,256]{1,0:T(8,128)S(1)}, u32[]{:S(2)}, u32[]{:S(2)}) %collective-permute-start.1) | collective-permute-done | bytes 81952 | tf_op jit(solution)/shard_map/ppermute | solution.py:837
  10.8 1.5 %collective-permute-done.2.refs_3_ = f32[80,256]{1,0:T(8,128)S(1)} collective-permute-done((f32[80,256]{1,0:T(8,128)}, f32[80,256]{1,0:T(8,128)S(1)}, u32[]{:S(2)}, u32[]{:S(2)}) %collective-permute-start.2) | collective-permute-done | bytes 81952 | tf_op jit(solution)/shard_map/ppermute | solution.py:837
  12.3 0.8 %shard_map.134 = (f32[64,1024]{1,0:T(8,128)S(1)}, f32[64,1024]{1,0:T(8,128)S(1)}, f32[8,1024]{1,0:T(8,128)S(1)}, s32[8,1024]{1,0:T(8,128)S(1)}, s32[8,1024]{1,0:...) custom-call(f32[80,256]{1,0:T(8,128)S(1)} %copy-done.1, ...), custom_call_target="tpu_custom_call" | custom-call | flops 3000000000 | bytes 1 | tf_op jit(solution)/shard_map/pallas_call | solution.py:740
  13.2 1.6 %collective-permute-start.4 = (f32[16,128]{1,0:T(8,128)S(1)}, f32[16,128]{1,0:T(8,128)S(1)}, u32[]{:S(2)}, u32[]{:S(2)}) collective-permute-start(f32[16,128]{1,0:T(8,128)S(1)} %get-tuple-element.110), channel_id=1, source_target_pairs={{0,8},{1,9},{2,10},{3,11},{4,12},{5,13},{6,14},{7,15},{8,0},{9,1},... | collective-permute-start | bytes 24584 | tf_op jit(solution)/shard_map/ppermute | solution.py:810
  14.8 0.5 collective-permute-start.5
  15.5 1.7 %shard_map.135 = (f32[96,1024]{1,0:T(8,128)S(1)}, f32[64,1024]{1,0:T(8,128)S(1)}, f32[64,256]{1,0:T(8,128)S(1)}) custom-call(f32[64,1024]{1,0:T(8,128)S(1)} %get-tuple-element.96.refs_0_.refs_6_, f32[96,1024]{1,0:T(8,128)S(1)} %get-tuple-element.97.refs_1_, f32[16,512]{1,0:T(8,128)S(1)} %get-tuple-element.98.refs_2_, ...), custom_call_target="tpu_custom_call" | custom-call | flops 3000000000 | bytes 1 | tf_op jit(solution)/shard_map/pallas_call | solution.py:740
  17.2 0.7 %shard_map.136 = (f32[64,1024]{1,0:T(8,128)S(1)}, f32[64,1024]{1,0:T(8,128)S(1)}, f32[64,128]{1,0:T(8,128)S(1)}) custom-call(f32[64,1024]{1,0:T(8,128)S(1)} %get-tuple-element.95.refs_0_, f32[96,1024]{1,0:T(8,128)S(1)} %get-tuple-element.103.refs_1_, f32[64,1024]{1,0:T(8,128)S(1)} %get-tuple-element.104.refs_2_, ...), custom_call_target="tpu_custom_call" | custom-call | flops 3000000000 | bytes 1 | tf_op jit(solution)/shard_map/pallas_call | solution.py:740
  17.9 0.6 collective-permute-done.5.two_ref.refs_2_
  18.9 2.1 %collective-permute-start.7 = (f32[16,128]{1,0:T(8,128)S(1)}, f32[16,128]{1,0:T(8,128)S(1)}, u32[]{:S(2)}, u32[]{:S(2)}) collective-permute-start(f32[16,128]{1,0:T(8,128)S(1)} %shard_map.138.refs_9_), channel_id=1, source_target_pairs={{0,8},{1,9},{2,10},{3,11},{4,12},{5,13},{6,14},{7,15},{8,0},{9,1},... | collective-permute-start | bytes 24584 | tf_op jit(solution)/shard_map/ppermute | solution.py:810
  21.0 0.5 collective-permute-start.8
  21.5 0.8 %shard_map.139 = (f32[64,1024]{1,0:T(8,128)S(1)}, f32[64,1024]{1,0:T(8,128)S(1)}, f32[96,1024]{1,0:T(8,128)S(1)}, f32[16,512]{1,0:T(8,128)S(1)}) custom-call(f32[64,1024]{1,0:T(8,128)S(1)} %get-tuple-element.109.refs_0_, f32[16,128]{1,0:T(8,128)S(1)} %collective-permute-done.4.one_ref.refs_1_, f32[16,128]{1,0:T(8,128)S(1)} %collective-permute-done.5.two_ref.refs_2_, ...), custom_call_target="tpu_custom_call" | custom-call | flops 3000000000 | bytes 1 | tf_op jit(solution)/shard_map/pallas_call | solution.py:740
  22.4 1.6 %shard_map.140 = (f32[96,1024]{1,0:T(8,128)S(1)}, f32[64,1024]{1,0:T(8,128)S(1)}, f32[64,256]{1,0:T(8,128)S(1)}) custom-call(f32[64,1024]{1,0:T(8,128)S(1)} %get-tuple-element.118.refs_0_.refs_6_, f32[96,1024]{1,0:T(8,128)S(1)} %get-tuple-element.119.refs_1_, f32[16,512]{1,0:T(8,128)S(1)} %get-tuple-element.120.refs_2_, ...), custom_call_target="tpu_custom_call" | custom-call | flops 3000000000 | bytes 1 | tf_op jit(solution)/shard_map/pallas_call | solution.py:740
  24.1 0.7 %shard_map.141 = (f32[64,1024]{1,0:T(8,128)S(1)}, f32[64,1024]{1,0:T(8,128)S(1)}, f32[64,128]{1,0:T(8,128)S(1)}) custom-call(f32[64,1024]{1,0:T(8,128)S(1)} %get-tuple-element.117.refs_0_, f32[96,1024]{1,0:T(8,128)S(1)} %get-tuple-element.122.refs_1_, f32[64,1024]{1,0:T(8,128)S(1)} %get-tuple-element.123.refs_2_, ...), custom_call_target="tpu_custom_call" | custom-call | flops 3000000000 | bytes 1 | tf_op jit(solution)/shard_map/pallas_call | solution.py:740
  24.8 0.4 shard_map.142.refs_9_
  25.2 1.1 %collective-permute-start.10 = (f32[16,128]{1,0:T(8,128)S(1)}, f32[16,128]{1,0:T(8,128)S(1)}, u32[]{:S(2)}, u32[]{:S(2)}) collective-permute-start(f32[16,128]{1,0:T(8,128)S(1)} %shard_map.142.refs_9_), channel_id=1, source_target_pairs={{0,8},{1,9},{2,10},{3,11},{4,12},{5,13},{6,14},{7,15},{8,0},{9,1},... | collective-permute-start | bytes 24584 | tf_op jit(solution)/shard_map/ppermute | solution.py:810
  26.3 0.9 %collective-permute-start.11 = (f32[16,128]{1,0:T(8,128)S(1)}, f32[16,128]{1,0:T(8,128)S(1)}, u32[]{:S(2)}, u32[]{:S(2)}) collective-permute-start(f32[16,128]{1,0:T(8,128)S(1)} %shard_map.142.refs_9_), channel_id=1, source_target_pairs={{0,2},{1,3},{2,0},{3,1},{4,6},{5,7},{6,4},{7,5},{8,16},{9,17},{10,... | collective-permute-start | bytes 24584 | tf_op jit(solution)/shard_map/ppermute | solution.py:810
  27.2 0.8 %shard_map.143 = (f32[64,1024]{1,0:T(8,128)S(1)}, f32[64,1024]{1,0:T(8,128)S(1)}, f32[96,1024]{1,0:T(8,128)S(1)}, f32[16,512]{1,0:T(8,128)S(1)}) custom-call(f32[64,1024]{1,0:T(8,128)S(1)} %get-tuple-element.124.refs_0_, f32[16,128]{1,0:T(8,128)S(1)} %collective-permute-done.7.one_ref.refs_1_, f32[16,128]{1,0:T(8,128)S(1)} %collective-permute-done.8.two_ref.refs_2_, ...), custom_call_target="tpu_custom_call" | custom-call | flops 3000000000 | bytes 1 | tf_op jit(solution)/shard_map/pallas_call | solution.py:740
  28.1 1.6 %shard_map.144 = (f32[96,1024]{1,0:T(8,128)S(1)}, f32[64,1024]{1,0:T(8,128)S(1)}, f32[64,256]{1,0:T(8,128)S(1)}) custom-call(f32[64,1024]{1,0:T(8,128)S(1)} %get-tuple-element.128.refs_0_, f32[96,1024]{1,0:T(8,128)S(1)} %get-tuple-element.129.refs_1_, f32[16,512]{1,0:T(8,128)S(1)} %get-tuple-element.130.refs_2_, f32[8,1024]{1,0:T(8,128)S(1)} %get-tuple-element.99.refs_3_, ...), custom_call_target="tpu_custom_call" | custom-call | flops 3000000000 | bytes 1 | tf_op jit(solution)/shard_map/pallas_call | solution.py:740
  29.7 0.7 %shard_map.145.r_ref.refs_0_ = f32[64,1024]{1,0:T(8,128)S(1)} custom-call(f32[64,1024]{1,0:T(8,128)S(1)} %get-tuple-element.127.refs_0_, f32[96,1024]{1,0:T(8,128)S(1)} %get-tuple-element.132.refs_1_, f32[64,1024]{1,0:T(8,128)S(1)} %get-tuple-element.133.refs_2_, f32[16,512]{1,0:T(8,128)S(1)} %collective-permute-done.9.refs_3_, ...), custom_call_target="tpu_custom_call" | custom-call | flops 3000000000 | bytes 1 | tf_op jit(solution)/shard_map/pallas_call | solution.py:740
  30.7 1.2 %collective-permute-start.13 = (f32[72,128]{1,0:T(8,128)S(1)}, f32[72,128]{1,0:T(8,128)S(1)}, u32[]{:S(2)}, u32[]{:S(2)}) collective-permute-start(f32[72,128]{1,0:T(8,128)S(1)} %shard_map.146.refs_7_), channel_id=1, source_target_pairs={{0,2},{1,8},{2,0},{3,10},{4,6},{5,12},{6,4},{7,14},{8,1},{9,16},{1... | collective-permute-start | bytes 110600 | tf_op jit(solution)/shard_map/ppermute | solution.py:905
  31.9 0.6 shard_map.147
  32.9 1.0 %collective-permute-done.12.near_ref = f32[72,640]{1,0:T(8,128)S(1)} collective-permute-done((f32[72,640]{1,0:T(8,128)S(1)}, f32[72,640]{1,0:T(8,128)S(1)}, u32[]{:S(2)}, u32[]{:S(2)}) %collective-permute-start.12) | collective-permute-done | bytes 184352 | tf_op jit(solution)/shard_map/ppermute | solution.py:906
  33.9 1.2 %shard_map.149 = (f32[64,384]{1,0:T(8,128)S(1)}, f32[1,384]{1,0:T(1,128)S(1)}, s32[1,8,256]{2,1,0:T(8,128)S(1)}) custom-call(f32[64,1024]{1,0:T(8,128)S(1)} %get-tuple-element.136.r_ref.refs_0_, f32[72,640]{1,0:T(8,128)S(1)} %collective-permute-done.12.near_ref, s32[4,512]{1,0:T(4,128)S(1)} %get-tuple-element.138.gather_ref, ...), custom_call_target="tpu_custom_call" | custom-call | flops 100000000 | bytes 1 | tf_op jit(solution)/shard_map/pallas_call | solution.py:740
  35.1 2.1 %shard_map.150 = (f32[64,1024]{1,0:T(8,128)S(1)}, f32[16,128]{1,0:T(8,128)S(1)}) custom-call(f32[64,384]{1,0:T(8,128)S(1)} %get-tuple-element.140.right_ref, f32[1,384]{1,0:T(1,128)S(1)} %get-tuple-element.141.scale_ref, s32[1,8,256]{2,1,0:T(8,128)S(1)} %get-tuple-element.142.front_ref, f32[64,1024]{1,0:T(8,128)S(1)} %get-tuple-element.136.r_ref.refs_0_, ...), custom_call_target="tpu_custom_call" | custom-call | flops 3000000000 | bytes 1 | tf_op jit(solution)/shard_map/pallas_call | solution.py:740
  37.2 1.3 %collective-permute-start.15 = (f32[16,128]{1,0:T(8,128)S(1)}, f32[16,128]{1,0:T(8,128)S(1)}, u32[]{:S(2)}, u32[]{:S(2)}) collective-permute-start(f32[16,128]{1,0:T(8,128)S(1)} %get-tuple-element.147._), channel_id=1, source_target_pairs={{0,8},{1,9},{2,10},{3,11},{4,12},{5,13},{6,14},{7,15},{8,0},{9,1},... | collective-permute-start | bytes 24584 | tf_op jit(solution)/shard_map/ppermute | solution.py:810
  38.5 1.2 %collective-permute-start.16 = (f32[16,128]{1,0:T(8,128)S(1)}, f32[16,128]{1,0:T(8,128)S(1)}, u32[]{:S(2)}, u32[]{:S(2)}) collective-permute-start(f32[16,128]{1,0:T(8,128)S(1)} %get-tuple-element.147._), channel_id=1, source_target_pairs={{0,2},{1,3},{2,0},{3,1},{4,6},{5,7},{6,4},{7,5},{8,16},{9,17},{10,... | collective-permute-start | bytes 24584 | tf_op jit(solution)/shard_map/ppermute | solution.py:810
  40.2 1.6 %shard_map.152 = (f32[96,1024]{1,0:T(8,128)S(1)}, f32[64,1024]{1,0:T(8,128)S(1)}, f32[64,256]{1,0:T(8,128)S(1)}) custom-call(f32[64,1024]{1,0:T(8,128)S(1)} %get-tuple-element.146.p_ref.refs_0_, f32[96,1024]{1,0:T(8,128)S(1)} %get-tuple-element.148.refs_1_, f32[16,512]{1,0:T(8,128)S(1)} %get-tuple-element.149.refs_2_, ...), custom_call_target="tpu_custom_call" | custom-call | flops 3000000000 | bytes 1 | tf_op jit(solution)/shard_map/pallas_call | solution.py:740
  41.8 0.7 %shard_map.153 = (f32[64,1024]{1,0:T(8,128)S(1)}, f32[64,1024]{1,0:T(8,128)S(1)}, f32[64,128]{1,0:T(8,128)S(1)}) custom-call(f32[64,1024]{1,0:T(8,128)S(1)} %get-tuple-element.136.r_ref.refs_0_, f32[96,1024]{1,0:T(8,128)S(1)} %get-tuple-element.151.refs_1_, f32[64,1024]{1,0:T(8,128)S(1)} %get-tuple-element.152.refs_2_, ...), custom_call_target="tpu_custom_call" | custom-call | flops 3000000000 | bytes 1 | tf_op jit(solution)/shard_map/pallas_call | solution.py:740
  43.0 1.0 %collective-permute-start.18 = (f32[16,128]{1,0:T(8,128)S(1)}, f32[16,128]{1,0:T(8,128)S(1)}, u32[]{:S(2)}, u32[]{:S(2)}) collective-permute-start(f32[16,128]{1,0:T(8,128)S(1)} %shard_map.154.refs_9_), channel_id=1, source_target_pairs={{0,8},{1,9},{2,10},{3,11},{4,12},{5,13},{6,14},{7,15},{8,0},{9,1},... | collective-permute-start | bytes 24584 | tf_op jit(solution)/shard_map/ppermute | solution.py:810
  43.9 1.5 %collective-permute-start.19 = (f32[16,128]{1,0:T(8,128)S(1)}, f32[16,128]{1,0:T(8,128)S(1)}, u32[]{:S(2)}, u32[]{:S(2)}) collective-permute-start(f32[16,128]{1,0:T(8,128)S(1)} %shard_map.154.refs_9_), channel_id=1, source_target_pairs={{0,2},{1,3},{2,0},{3,1},{4,6},{5,7},{6,4},{7,5},{8,16},{9,17},{10,... | collective-permute-start | bytes 24584 | tf_op jit(solution)/shard_map/ppermute | solution.py:810
  45.4 0.8 %shard_map.155 = (f32[64,1024]{1,0:T(8,128)S(1)}, f32[64,1024]{1,0:T(8,128)S(1)}, f32[96,1024]{1,0:T(8,128)S(1)}, f32[16,512]{1,0:T(8,128)S(1)}) custom-call(f32[64,1024]{1,0:T(8,128)S(1)} %get-tuple-element.153.refs_0_, f32[16,128]{1,0:T(8,128)S(1)} %collective-permute-done.15.one_ref.refs_1_, f32[16,128]{1,0:T(8,128)S(1)} %collective-permute-done.16.two_ref.refs_2_, ...), custom_call_target="tpu_custom_call" | custom-call | flops 3000000000 | bytes 1 | tf_op jit(solution)/shard_map/pallas_call | solution.py:740
  46.3 1.6 %shard_map.156 = (f32[96,1024]{1,0:T(8,128)S(1)}, f32[64,1024]{1,0:T(8,128)S(1)}, f32[64,256]{1,0:T(8,128)S(1)}) custom-call(f32[64,1024]{1,0:T(8,128)S(1)} %get-tuple-element.157.refs_0_.refs_6_, f32[96,1024]{1,0:T(8,128)S(1)} %get-tuple-element.158.refs_1_, f32[16,512]{1,0:T(8,128)S(1)} %get-tuple-element.159.refs_2_, ...), custom_call_target="tpu_custom_call" | custom-call | flops 3000000000 | bytes 1 | tf_op jit(solution)/shard_map/pallas_call | solution.py:740
  47.9 0.7 %shard_map.157 = (f32[64,1024]{1,0:T(8,128)S(1)}, f32[64,1024]{1,0:T(8,128)S(1)}, f32[64,128]{1,0:T(8,128)S(1)}) custom-call(f32[64,1024]{1,0:T(8,128)S(1)} %get-tuple-element.156.refs_0_, f32[96,1024]{1,0:T(8,128)S(1)} %get-tuple-element.161.refs_1_, f32[64,1024]{1,0:T(8,128)S(1)} %get-tuple-element.162.refs_2_, ...), custom_call_target="tpu_custom_call" | custom-call | flops 3000000000 | bytes 1 | tf_op jit(solution)/shard_map/pallas_call | solution.py:740
  49.1 1.1 %collective-permute-start.21 = (f32[16,128]{1,0:T(8,128)S(1)}, f32[16,128]{1,0:T(8,128)S(1)}, u32[]{:S(2)}, u32[]{:S(2)}) collective-permute-start(f32[16,128]{1,0:T(8,128)S(1)} %shard_map.158.refs_9_), channel_id=1, source_target_pairs={{0,8},{1,9},{2,10},{3,11},{4,12},{5,13},{6,14},{7,15},{8,0},{9,1},... | collective-permute-start | bytes 24584 | tf_op jit(solution)/shard_map/ppermute | solution.py:810
  50.2 0.8 %collective-permute-start.22 = (f32[16,128]{1,0:T(8,128)S(1)}, f32[16,128]{1,0:T(8,128)S(1)}, u32[]{:S(2)}, u32[]{:S(2)}) collective-permute-start(f32[16,128]{1,0:T(8,128)S(1)} %shard_map.158.refs_9_), channel_id=1, source_target_pairs={{0,2},{1,3},{2,0},{3,1},{4,6},{5,7},{6,4},{7,5},{8,16},{9,17},{10,... | collective-permute-start | bytes 24584 | tf_op jit(solution)/shard_map/ppermute | solution.py:810
  51.1 0.8 %shard_map.159 = (f32[64,1024]{1,0:T(8,128)S(1)}, f32[64,1024]{1,0:T(8,128)S(1)}, f32[96,1024]{1,0:T(8,128)S(1)}, f32[16,512]{1,0:T(8,128)S(1)}) custom-call(f32[64,1024]{1,0:T(8,128)S(1)} %get-tuple-element.163.refs_0_, f32[16,128]{1,0:T(8,128)S(1)} %collective-permute-done.18.one_ref.refs_1_, f32[16,128]{1,0:T(8,128)S(1)} %collective-permute-done.19.two_ref.refs_2_, ...), custom_call_target="tpu_custom_call" | custom-call | flops 3000000000 | bytes 1 | tf_op jit(solution)/shard_map/pallas_call | solution.py:740
  52.0 1.6 %shard_map.160 = (f32[96,1024]{1,0:T(8,128)S(1)}, f32[64,1024]{1,0:T(8,128)S(1)}, f32[64,256]{1,0:T(8,128)S(1)}) custom-call(f32[64,1024]{1,0:T(8,128)S(1)} %get-tuple-element.167.refs_0_.refs_6_, f32[96,1024]{1,0:T(8,128)S(1)} %get-tuple-element.168.refs_1_, f32[16,512]{1,0:T(8,128)S(1)} %get-tuple-element.169.refs_2_, ...), custom_call_target="tpu_custom_call" | custom-call | flops 3000000000 | bytes 1 | tf_op jit(solution)/shard_map/pallas_call | solution.py:740
  53.6 0.7 %shard_map.161 = (f32[64,1024]{1,0:T(8,128)S(1)}, f32[64,1024]{1,0:T(8,128)S(1)}, f32[64,128]{1,0:T(8,128)S(1)}) custom-call(f32[64,1024]{1,0:T(8,128)S(1)} %get-tuple-element.166.refs_0_, f32[96,1024]{1,0:T(8,128)S(1)} %get-tuple-element.171.refs_1_, f32[64,1024]{1,0:T(8,128)S(1)} %get-tuple-element.172.refs_2_, ...), custom_call_target="tpu_custom_call" | custom-call | flops 3000000000 | bytes 1 | tf_op jit(solution)/shard_map/pallas_call | solution.py:740
  54.7 1.0 %collective-permute-start.24 = (f32[16,128]{1,0:T(8,128)S(1)}, f32[16,128]{1,0:T(8,128)S(1)}, u32[]{:S(2)}, u32[]{:S(2)}) collective-permute-start(f32[16,128]{1,0:T(8,128)S(1)} %shard_map.162.refs_9_), channel_id=1, source_target_pairs={{0,8},{1,9},{2,10},{3,11},{4,12},{5,13},{6,14},{7,15},{8,0},{9,1},... | collective-permute-start | bytes 24584 | tf_op jit(solution)/shard_map/ppermute | solution.py:810
  55.7 0.6 %collective-permute-start.25 = (f32[16,128]{1,0:T(8,128)S(1)}, f32[16,128]{1,0:T(8,128)S(1)}, u32[]{:S(2)}, u32[]{:S(2)}) collective-permute-start(f32[16,128]{1,0:T(8,128)S(1)} %shard_map.162.refs_9_), channel_id=1, source_target_pairs={{0,2},{1,3},{2,0},{3,1},{4,6},{5,7},{6,4},{7,5},{8,16},{9,17},{10,... | collective-permute-start | bytes 24584 | tf_op jit(solution)/shard_map/ppermute | solution.py:810
  56.4 0.8 %shard_map.163 = (f32[64,1024]{1,0:T(8,128)S(1)}, f32[64,1024]{1,0:T(8,128)S(1)}, f32[96,1024]{1,0:T(8,128)S(1)}, f32[16,512]{1,0:T(8,128)S(1)}) custom-call(f32[64,1024]{1,0:T(8,128)S(1)} %get-tuple-element.173.refs_0_, f32[16,128]{1,0:T(8,128)S(1)} %collective-permute-done.21.one_ref.refs_1_, f32[16,128]{1,0:T(8,128)S(1)} %collective-permute-done.22.two_ref.refs_2_, ...), custom_call_target="tpu_custom_call" | custom-call | flops 3000000000 | bytes 1 | tf_op jit(solution)/shard_map/pallas_call | solution.py:740
  57.3 1.1 %shard_map.164 = (f32[96,256]{1,0:T(8,128)S(1)}, f32[64,256]{1,0:T(8,128)S(1)}, f32[64,256]{1,0:T(8,128)}) custom-call(f32[64,1024]{1,0:T(8,128)S(1)} %get-tuple-element.176.refs_0_, f32[96,1024]{1,0:T(8,128)S(1)} %get-tuple-element.177.refs_1_, f32[16,512]{1,0:T(8,128)S(1)} %get-tuple-element.178.refs_2_, f32[8,1024]{1,0:T(8,128)S(1)} %get-tuple-element.99.refs_3_, ...), custom_call_target="tpu_custom_call" | custom-call | flops 3000000000 | bytes 1 | tf_op jit(solution)/shard_map/pallas_call | solution.py:740
  58.8 0.6 collective-permute-done.25.refs_2_
  59.4 0.9 %shard_map.166 = f32[64,256]{1,0:T(8,128)} custom-call(f32[64,256]{1,0:T(8,128)S(1)} %shard_map.165.refs_0_, f32[16,128]{1,0:T(8,128)S(1)} %collective-permute-done.24.refs_1_, f32[16,128]{1,0:T(8,128)S(1)} %collective-permute-done.25.refs_2_, s32[8,1024]{1,0:T(8,128)S(1)} %get-tuple-element.111.edge_ref.refs_3_, ...), custom_call_target="tpu_custom_call" | custom-call | flops 3000000000 | bytes 1 | tf_op jit(solution)/shard_map/pallas_call | solution.py:740
  (51 shorter events, 4.6 us)
Async XLA Ops:
  0.6 6.2 %copy-start.2 = (f32[2,64,64]{2,1,0:T(8,128)S(1)}, f32[2,64,64]{2,1,0:T(8,128)}, u32[]{:S(2)}) copy-start(f32[2,64,64]{2,1,0:T(8,128)} %refs_4_.1) | copy-start | bytes 98308
  0.6 6.2 %copy-start.3 = (f32[96,64]{0,1:T(8,128)S(1)}, f32[96,64]{0,1:T(8,128)}, u32[]{:S(2)}) copy-start(f32[96,64]{0,1:T(8,128)} %param.16) | copy-start | bytes 73732
  2.3 6.0 %collective-permute-start = (f32[80,256]{1,0:T(8,128)}, f32[80,256]{1,0:T(8,128)S(1)}, u32[]{:S(2)}, u32[]{:S(2)}) collective-permute-start(f32[80,256]{1,0:T(8,128)} %shard_map.131.refs_0_), channel_id=1, source_target_pairs={{0,2},{1,3},{2,0},{3,1},{4,6},{5,7},{6,4},{7,5},{8,10},{9,11},{10,... | collective-permute-start | bytes 245768 | tf_op jit(solution)/shard_map/ppermute | solution.py:837
  5.3 5.5 %collective-permute-start.1 = (f32[80,256]{1,0:T(8,128)}, f32[80,256]{1,0:T(8,128)S(1)}, u32[]{:S(2)}, u32[]{:S(2)}) collective-permute-start(f32[80,256]{1,0:T(8,128)} %shard_map.131.refs_0_), channel_id=1, source_target_pairs={{0,4},{1,5},{2,6},{3,7},{4,0},{5,1},{6,2},{7,3},{8,12},{9,13},{10,... | collective-permute-start | bytes 245768 | tf_op jit(solution)/shard_map/ppermute | solution.py:837
  6.8 5.6 %collective-permute-start.2 = (f32[80,256]{1,0:T(8,128)}, f32[80,256]{1,0:T(8,128)S(1)}, u32[]{:S(2)}, u32[]{:S(2)}) collective-permute-start(f32[80,256]{1,0:T(8,128)} %shard_map.131.refs_0_), channel_id=1, source_target_pairs={{0,6},{1,7},{2,4},{3,5},{4,2},{5,3},{6,0},{7,1},{8,14},{9,15},{10,... | collective-permute-start | bytes 245768 | tf_op jit(solution)/shard_map/ppermute | solution.py:837
  6.8 1.0 %copy-start = (f32[8,64,64]{2,1,0:T(8,128)S(1)}, f32[8,64,64]{2,1,0:T(8,128)}, u32[]{:S(2)}) copy-start(f32[8,64,64]{2,1,0:T(8,128)} %restriction_ref.1) | copy-start | bytes 393220
  6.8 1.0 %copy-start.4 = (f32[64,64]{1,0:T(8,128)S(1)}, f32[64,64]{1,0:T(8,128)}, u32[]{:S(2)}) copy-start(f32[64,64]{1,0:T(8,128)} %stiff_ref.5) | copy-start | bytes 49156
  7.8 4.6 %copy-start.1 = (f32[80,256]{1,0:T(8,128)S(1)}, f32[80,256]{1,0:T(8,128)}, u32[]{:S(2)}) copy-start(f32[80,256]{1,0:T(8,128)} %shard_map.131.refs_0_) | copy-start | bytes 245764
  13.2 4.7 %collective-permute-start.4 = (f32[16,128]{1,0:T(8,128)S(1)}, f32[16,128]{1,0:T(8,128)S(1)}, u32[]{:S(2)}, u32[]{:S(2)}) collective-permute-start(f32[16,128]{1,0:T(8,128)S(1)} %get-tuple-element.110), channel_id=1, source_target_pairs={{0,8},{1,9},{2,10},{3,11},{4,12},{5,13},{6,14},{7,15},{8,0},{9,1},... | collective-permute-start | bytes 24584 | tf_op jit(solution)/shard_map/ppermute | solution.py:810
  14.8 3.7 %collective-permute-start.5 = (f32[16,128]{1,0:T(8,128)S(1)}, f32[16,128]{1,0:T(8,128)S(1)}, u32[]{:S(2)}, u32[]{:S(2)}) collective-permute-start(f32[16,128]{1,0:T(8,128)S(1)} %get-tuple-element.110), channel_id=1, source_target_pairs={{0,2},{1,3},{2,0},{3,1},{4,6},{5,7},{6,4},{7,5},{8,16},{9,17},{10,... | collective-permute-start | bytes 24584 | tf_op jit(solution)/shard_map/ppermute | solution.py:810
  15.3 1.8 %collective-permute-start.3 = (f32[16,512]{1,0:T(8,128)S(1)}, f32[16,512]{1,0:T(8,128)S(1)}, u32[]{:S(2)}, u32[]{:S(2)}) collective-permute-start(f32[16,512]{1,0:T(8,128)S(1)} %get-tuple-element.98.refs_2_), channel_id=1, source_target_pairs={{0,1},{1,0},{2,3},{3,2},{4,5},{5,4},{6,7},{7,6},{8,9},{9,8},{10,11... | collective-permute-start | bytes 98312 | tf_op jit(solution)/shard_map/ppermute | solution.py:864
  18.9 5.9 %collective-permute-start.7 = (f32[16,128]{1,0:T(8,128)S(1)}, f32[16,128]{1,0:T(8,128)S(1)}, u32[]{:S(2)}, u32[]{:S(2)}) collective-permute-start(f32[16,128]{1,0:T(8,128)S(1)} %shard_map.138.refs_9_), channel_id=1, source_target_pairs={{0,8},{1,9},{2,10},{3,11},{4,12},{5,13},{6,14},{7,15},{8,0},{9,1},... | collective-permute-start | bytes 24584 | tf_op jit(solution)/shard_map/ppermute | solution.py:810
  21.0 3.8 %collective-permute-start.8 = (f32[16,128]{1,0:T(8,128)S(1)}, f32[16,128]{1,0:T(8,128)S(1)}, u32[]{:S(2)}, u32[]{:S(2)}) collective-permute-start(f32[16,128]{1,0:T(8,128)S(1)} %shard_map.138.refs_9_), channel_id=1, source_target_pairs={{0,2},{1,3},{2,0},{3,1},{4,6},{5,7},{6,4},{7,5},{8,16},{9,17},{10,... | collective-permute-start | bytes 24584 | tf_op jit(solution)/shard_map/ppermute | solution.py:810
  22.3 1.7 %collective-permute-start.6 = (f32[16,512]{1,0:T(8,128)S(1)}, f32[16,512]{1,0:T(8,128)S(1)}, u32[]{:S(2)}, u32[]{:S(2)}) collective-permute-start(f32[16,512]{1,0:T(8,128)S(1)} %get-tuple-element.120.refs_2_), channel_id=1, source_target_pairs={{0,1},{1,0},{2,3},{3,2},{4,5},{5,4},{6,7},{7,6},{8,9},{9,8},{10,11... | collective-permute-start | bytes 98312 | tf_op jit(solution)/shard_map/ppermute | solution.py:864
  25.2 5.2 %collective-permute-start.10 = (f32[16,128]{1,0:T(8,128)S(1)}, f32[16,128]{1,0:T(8,128)S(1)}, u32[]{:S(2)}, u32[]{:S(2)}) collective-permute-start(f32[16,128]{1,0:T(8,128)S(1)} %shard_map.142.refs_9_), channel_id=1, source_target_pairs={{0,8},{1,9},{2,10},{3,11},{4,12},{5,13},{6,14},{7,15},{8,0},{9,1},... | collective-permute-start | bytes 24584 | tf_op jit(solution)/shard_map/ppermute | solution.py:810
  26.3 4.2 %collective-permute-start.11 = (f32[16,128]{1,0:T(8,128)S(1)}, f32[16,128]{1,0:T(8,128)S(1)}, u32[]{:S(2)}, u32[]{:S(2)}) collective-permute-start(f32[16,128]{1,0:T(8,128)S(1)} %shard_map.142.refs_9_), channel_id=1, source_target_pairs={{0,2},{1,3},{2,0},{3,1},{4,6},{5,7},{6,4},{7,5},{8,16},{9,17},{10,... | collective-permute-start | bytes 24584 | tf_op jit(solution)/shard_map/ppermute | solution.py:810
  28.0 1.7 %collective-permute-start.9 = (f32[16,512]{1,0:T(8,128)S(1)}, f32[16,512]{1,0:T(8,128)S(1)}, u32[]{:S(2)}, u32[]{:S(2)}) collective-permute-start(f32[16,512]{1,0:T(8,128)S(1)} %get-tuple-element.130.refs_2_), channel_id=1, source_target_pairs={{0,1},{1,0},{2,3},{3,2},{4,5},{5,4},{6,7},{7,6},{8,9},{9,8},{10,11... | collective-permute-start | bytes 98312 | tf_op jit(solution)/shard_map/ppermute | solution.py:864
  30.7 4.4 %collective-permute-start.13 = (f32[72,128]{1,0:T(8,128)S(1)}, f32[72,128]{1,0:T(8,128)S(1)}, u32[]{:S(2)}, u32[]{:S(2)}) collective-permute-start(f32[72,128]{1,0:T(8,128)S(1)} %shard_map.146.refs_7_), channel_id=1, source_target_pairs={{0,2},{1,8},{2,0},{3,10},{4,6},{5,12},{6,4},{7,14},{8,1},{9,16},{1... | collective-permute-start | bytes 110600 | tf_op jit(solution)/shard_map/ppermute | solution.py:905
  32.4 1.5 %collective-permute-start.12 = (f32[72,640]{1,0:T(8,128)S(1)}, f32[72,640]{1,0:T(8,128)S(1)}, u32[]{:S(2)}, u32[]{:S(2)}) collective-permute-start(f32[72,640]{1,0:T(8,128)S(1)} %get-tuple-element.137), channel_id=1, source_target_pairs={{0,1},{1,0},{2,3},{3,2},{4,5},{5,4},{6,7},{7,6},{8,9},{9,8},{10,11... | collective-permute-start | bytes 552968 | tf_op jit(solution)/shard_map/ppermute | solution.py:906
  37.2 5.3 %collective-permute-start.15 = (f32[16,128]{1,0:T(8,128)S(1)}, f32[16,128]{1,0:T(8,128)S(1)}, u32[]{:S(2)}, u32[]{:S(2)}) collective-permute-start(f32[16,128]{1,0:T(8,128)S(1)} %get-tuple-element.147._), channel_id=1, source_target_pairs={{0,8},{1,9},{2,10},{3,11},{4,12},{5,13},{6,14},{7,15},{8,0},{9,1},... | collective-permute-start | bytes 24584 | tf_op jit(solution)/shard_map/ppermute | solution.py:810
  38.5 4.0 %collective-permute-start.16 = (f32[16,128]{1,0:T(8,128)S(1)}, f32[16,128]{1,0:T(8,128)S(1)}, u32[]{:S(2)}, u32[]{:S(2)}) collective-permute-start(f32[16,128]{1,0:T(8,128)S(1)} %get-tuple-element.147._), channel_id=1, source_target_pairs={{0,2},{1,3},{2,0},{3,1},{4,6},{5,7},{6,4},{7,5},{8,16},{9,17},{10,... | collective-permute-start | bytes 24584 | tf_op jit(solution)/shard_map/ppermute | solution.py:810
  40.1 1.7 %collective-permute-start.14 = (f32[16,512]{1,0:T(8,128)S(1)}, f32[16,512]{1,0:T(8,128)S(1)}, u32[]{:S(2)}, u32[]{:S(2)}) collective-permute-start(f32[16,512]{1,0:T(8,128)S(1)} %get-tuple-element.149.refs_2_), channel_id=1, source_target_pairs={{0,1},{1,0},{2,3},{3,2},{4,5},{5,4},{6,7},{7,6},{8,9},{9,8},{10,11... | collective-permute-start | bytes 98312 | tf_op jit(solution)/shard_map/ppermute | solution.py:864
  43.0 5.7 %collective-permute-start.18 = (f32[16,128]{1,0:T(8,128)S(1)}, f32[16,128]{1,0:T(8,128)S(1)}, u32[]{:S(2)}, u32[]{:S(2)}) collective-permute-start(f32[16,128]{1,0:T(8,128)S(1)} %shard_map.154.refs_9_), channel_id=1, source_target_pairs={{0,8},{1,9},{2,10},{3,11},{4,12},{5,13},{6,14},{7,15},{8,0},{9,1},... | collective-permute-start | bytes 24584 | tf_op jit(solution)/shard_map/ppermute | solution.py:810
  43.9 4.7 %collective-permute-start.19 = (f32[16,128]{1,0:T(8,128)S(1)}, f32[16,128]{1,0:T(8,128)S(1)}, u32[]{:S(2)}, u32[]{:S(2)}) collective-permute-start(f32[16,128]{1,0:T(8,128)S(1)} %shard_map.154.refs_9_), channel_id=1, source_target_pairs={{0,2},{1,3},{2,0},{3,1},{4,6},{5,7},{6,4},{7,5},{8,16},{9,17},{10,... | collective-permute-start | bytes 24584 | tf_op jit(solution)/shard_map/ppermute | solution.py:810
  46.2 1.7 %collective-permute-start.17 = (f32[16,512]{1,0:T(8,128)S(1)}, f32[16,512]{1,0:T(8,128)S(1)}, u32[]{:S(2)}, u32[]{:S(2)}) collective-permute-start(f32[16,512]{1,0:T(8,128)S(1)} %get-tuple-element.159.refs_2_), channel_id=1, source_target_pairs={{0,1},{1,0},{2,3},{3,2},{4,5},{5,4},{6,7},{7,6},{8,9},{9,8},{10,11... | collective-permute-start | bytes 98312 | tf_op jit(solution)/shard_map/ppermute | solution.py:864
  49.1 5.2 %collective-permute-start.21 = (f32[16,128]{1,0:T(8,128)S(1)}, f32[16,128]{1,0:T(8,128)S(1)}, u32[]{:S(2)}, u32[]{:S(2)}) collective-permute-start(f32[16,128]{1,0:T(8,128)S(1)} %shard_map.158.refs_9_), channel_id=1, source_target_pairs={{0,8},{1,9},{2,10},{3,11},{4,12},{5,13},{6,14},{7,15},{8,0},{9,1},... | collective-permute-start | bytes 24584 | tf_op jit(solution)/shard_map/ppermute | solution.py:810
  50.2 4.1 %collective-permute-start.22 = (f32[16,128]{1,0:T(8,128)S(1)}, f32[16,128]{1,0:T(8,128)S(1)}, u32[]{:S(2)}, u32[]{:S(2)}) collective-permute-start(f32[16,128]{1,0:T(8,128)S(1)} %shard_map.158.refs_9_), channel_id=1, source_target_pairs={{0,2},{1,3},{2,0},{3,1},{4,6},{5,7},{6,4},{7,5},{8,16},{9,17},{10,... | collective-permute-start | bytes 24584 | tf_op jit(solution)/shard_map/ppermute | solution.py:810
  51.9 1.7 %collective-permute-start.20 = (f32[16,512]{1,0:T(8,128)S(1)}, f32[16,512]{1,0:T(8,128)S(1)}, u32[]{:S(2)}, u32[]{:S(2)}) collective-permute-start(f32[16,512]{1,0:T(8,128)S(1)} %get-tuple-element.169.refs_2_), channel_id=1, source_target_pairs={{0,1},{1,0},{2,3},{3,2},{4,5},{5,4},{6,7},{7,6},{8,9},{9,8},{10,11... | collective-permute-start | bytes 98312 | tf_op jit(solution)/shard_map/ppermute | solution.py:864
  54.7 4.1 %collective-permute-start.24 = (f32[16,128]{1,0:T(8,128)S(1)}, f32[16,128]{1,0:T(8,128)S(1)}, u32[]{:S(2)}, u32[]{:S(2)}) collective-permute-start(f32[16,128]{1,0:T(8,128)S(1)} %shard_map.162.refs_9_), channel_id=1, source_target_pairs={{0,8},{1,9},{2,10},{3,11},{4,12},{5,13},{6,14},{7,15},{8,0},{9,1},... | collective-permute-start | bytes 24584 | tf_op jit(solution)/shard_map/ppermute | solution.py:810
  55.7 3.7 %collective-permute-start.25 = (f32[16,128]{1,0:T(8,128)S(1)}, f32[16,128]{1,0:T(8,128)S(1)}, u32[]{:S(2)}, u32[]{:S(2)}) collective-permute-start(f32[16,128]{1,0:T(8,128)S(1)} %shard_map.162.refs_9_), channel_id=1, source_target_pairs={{0,2},{1,3},{2,0},{3,1},{4,6},{5,7},{6,4},{7,5},{8,16},{9,17},{10,... | collective-permute-start | bytes 24584 | tf_op jit(solution)/shard_map/ppermute | solution.py:810
  57.2 1.3 %collective-permute-start.23 = (f32[16,512]{1,0:T(8,128)S(1)}, f32[16,512]{1,0:T(8,128)S(1)}, u32[]{:S(2)}, u32[]{:S(2)}) collective-permute-start(f32[16,512]{1,0:T(8,128)S(1)} %get-tuple-element.178.refs_2_), channel_id=1, source_target_pairs={{0,1},{1,0},{2,3},{3,2},{4,5},{5,4},{6,7},{7,6},{8,9},{9,8},{10,11... | collective-permute-start | bytes 98312 | tf_op jit(solution)/shard_map/ppermute | solution.py:864

commit v5 on v4

--- a/solution.py
+++ b/solution.py
@@ -182,7 +182,7 @@
     gathered, refs = refs[:blocks], refs[blocks:]
     stiff_ref, map_ref, t_ref, _ = refs[:4]
     b_out, ig_out, meta_out, lane_out, at_out, far_out, edge_out, sub_out, rim_out, size_out, coarse_out = refs[4:15]
-    p_out, tr_out, subs_out, rims_out, held = refs[15:]
+    face_out, p_out, rims_out, held, edge = refs[15:]
     modes, count = map_ref.shape[0], gathered[0].shape[1]
     chip, core = own_place()
     for k, ref in enumerate(gathered):
@@ -197,9 +197,6 @@
     own_tiles = FACES * count // LANES
     sub_tiles = width // LANES
     rim_out[...] = jnp.zeros(rim_out.shape, jnp.int32)
-    rims_out[...] = jnp.zeros(rims_out.shape, jnp.float32)
-    peers = blocks * CORES
-    slots = width // peers
     group = LANES // rims
 
     def body(j):
@@ -214,10 +211,9 @@
         at = jnp.right_shift(column, 7)
         lane_out[0:FACES, cols(j, count)] = lane
         at_out[0:FACES, cols(j, count)] = at
-        other = jnp.bitwise_and(lax.div(lane, jnp.int32(slots)), 1) != core
-        sub = jnp.logical_and(jnp.logical_and(at >= own_tiles, at < own_tiles + sub_tiles), other)
         rim = jnp.logical_and(at == own_tiles + sub_tiles, lane < rims)
-        far_out[0:FACES, cols(j, count)] = jnp.where(sub, column - own_tiles * LANES, slots * core)
+        sub = jnp.logical_and(at >= own_tiles, at < own_tiles + sub_tiles)
+        far_out[0:FACES, cols(j, count)] = jnp.where(sub, column - own_tiles * LANES, -1)
         edge_out[0:FACES, cols(j, count)] = jnp.where(
             rim, jnp.bitwise_xor(lane, rims // 2) + (j % group) * rims, -1
         )
@@ -235,20 +231,15 @@
         ig_out[:, cols(j, count)] = inverse
         p_out[:, cols(j, count)] = b * inverse * (1.0 / CENTER)
 
-    def first(js, g):
-        span = cols(g, len(js) * count)
-        traces = product(t_ref[...], p_out[:, span])
-        tr_out[:, span] = traces
-        for i, j in enumerate(js):
-            tiles = trace_tiles(of_block(traces, i, count))
-            send_sub(j, tiles, sub_out, subs_out, width)
-            send_rim(j, tiles, rim_out, rims_out, rims)
-
     over(blocks, body)
-    over_groups(blocks, first)
-
-
-def sub_tiles_of(j, sends_ref, core, width, blocks):
+    spot = lax.broadcasted_iota(jnp.int32, rim_out.shape, 1)
+    face_out[...] = jnp.where(spot < blocks * rims, lax.div(rim_out[...], jnp.int32(count)), -1)
+    edge[...] = jnp.zeros(edge.shape, jnp.float32)
+    over(blocks, lambda j: keep_edge(j, p_out[:, cols(j, count)], rim_out, edge, rims))
+    rims_out[...] = rim_traces(t_ref, edge[...], face_out[...])
+
+
+def sub_tiles_of(j, sends_refs, core, width, blocks):
     slots = width // (blocks * CORES)
     pairs = LANES // slots // CORES
     lane = lanes()
@@ -258,10 +249,9 @@
     for t in range(width // LANES):
         tile = None
         for i in range(pairs):
-            sent = sends_ref[:, cols(j // pairs, LANES, (pairs * t + i) * width)]
-            there = take(sent, source)
-            there = jnp.where(lane // slots == CORES * i + core, there, 0.0)
-            tile = there if tile is None else tile + there
+            for ref, sender in zip(sends_refs, (core, 1 - core)):
+                there = take(ref[:, cols(j // pairs, LANES, (pairs * t + i) * width)], source)
+                tile = there if tile is None else jnp.where(lane // slots == CORES * i + sender, there, tile)
         tiles.append(tile)
     return tiles
 
@@ -271,8 +261,8 @@
 
 
 def local_kernel(only_own, blocks, width, first, *refs):
-    p_ref, tr_ref, subs_ref, meta_ref, lane_ref, at_ref, k_ref = refs[:7]
-    refs = refs[7:]
+    p_ref, tr_ref, meta_ref, lane_ref, at_ref, k_ref = refs[:6]
+    refs = refs[6:]
     if not first:
         x_ref, refs = refs[0], refs[1:]
     jump_out, own_out, x_out = refs
@@ -283,19 +273,18 @@
     def body(js, span, out):
         traces = tr_ref[:, span]
         at_rows, lane_rows = at_ref[:, span], lane_ref[:, span]
+        tiles = [
+            trace_tiles(of_block(traces, i, count)) for i in range(len(js))
+        ]
+
+        def tile(i, f, h):
+            row, place = slice(f, f + 1), slice(i * count + h, i * count + h + LANES)
+            return pick(tiles[i], at_rows[row, place], lane_rows[row, place])
+
+        jump_out[:, out] = traces - faces(tile, range(len(js)), count)
         both = product(k_ref[...], p_ref[:, span])
         meta = meta_ref[:, span]
         own_out[:, out] = meta[0:1] * jnp.where(meta[1:2] == 1.0, both[modes:], both[:modes])
-        tiles = [
-            trace_tiles(of_block(traces, i, count)) + sub_tiles_of(j, subs_ref, core, width, blocks)
-            for i, j in enumerate(js)
-        ]
-
-        def tile(i, f, h):
-            row, place = slice(f, f + 1), slice(i * count + h, i * count + h + LANES)
-            return pick(tiles[i], at_rows[row, place], lane_rows[row, place])
-
-        jump_out[:, out] = traces - faces(tile, range(len(js)), count)
 
     if only_own:
         body([chip], cols(chip, count), slice(0, count))
@@ -306,8 +295,8 @@
 
 
 def ahead_kernel(kind, coefficients, blocks, width, rims, *refs):
-    r_ref, jump_ref, own_ref, swapped_ref, far_ref, tt_ref = refs[:6]
-    refs = list(refs[6:])
+    r_ref, jump_ref, own_ref, subs_ref, swapped_ref, far_ref, tt_ref = refs[:7]
+    refs = list(refs[7:])
     chip, core = own_place()
     count = own_ref.shape[1] // (1 if kind == "last" else blocks)
     group = LANES // rims
@@ -320,13 +309,11 @@
         r_out = refs[0]
 
     def body(js, span, here):
-        tiles = [sub_tiles_of(j, swapped_ref, 1 - core, width, blocks) for j in js]
+        tiles = [sub_tiles_of(j, (subs_ref, swapped_ref), core, width, blocks) for j in js]
         far = far_ref[:, span]
 
         def tile(i, f, h):
             column = far[f : f + 1, i * count + h : i * count + h + LANES]
-            if len(tiles[i]) == 1:
-                return take(tiles[i][0], column)
             return pick(tiles[i], jnp.right_shift(column, 7), jnp.bitwise_and(column, LANES - 1))
 
         jump = product(tt_ref[...], jump_ref[:, here] - faces(tile, range(len(js)), count))
@@ -794,7 +781,7 @@
     def above_or_below(first):
         def partner(b, s):
             other = b + 1 if b % 2 == first else b - 1
-            return (other, s) if 0 <= other < segments else (b, s ^ 2)
+            return (other, s) if 0 <= other < segments else (b, s ^ 1)
 
         return everywhere(partner)
 
@@ -836,16 +823,17 @@
     gathered = [packed] + [
         lax.ppermute(packed, "sub", [(s, s ^ (CORES * k)) for s in range(peers)]) for k in range(1, blocks)
     ]
-    b, inverse, meta, lane, at, far, edge, subs, rim, sizes, coarse_cond, p, traces, sub_out, rim_out = run(
+    b, inverse, meta, lane, at, far, edge, subs, rim, sizes, coarse_cond, rim_face, p, rim_out = run(
         functools.partial(start_kernel, blocks, width, rims),
         [
             field, field, ((8, total), f32), *[((8, total), i32)] * 4,
             ((1, blocks * width), i32), ((1, rim_width), i32), ((blocks, LANES), i32), ((blocks, LANES), f32),
-            field, *sends,
+            ((1, rim_width), i32), field, sends[2],
         ],
         *gathered, stiffness, map_t, t3, c3,
-        scratch=[pltpu.VMEM((blocks, height, count), f32)],
-    )
+        scratch=[pltpu.VMEM((blocks, height, count), f32), pltpu.VMEM((modes, rim_width), f32)],
+    )
+    traces, sub_out = run(functools.partial(spread_kernel, blocks, width), sends[:2], p, t3, subs, rim_out)
 
     edges, igs = run(
         functools.partial(rim_kernel, blocks, rims), [((8, rim_width), i32), ((modes, rim_width), f32)], rim, edge, inverse
@@ -856,9 +844,6 @@
         sizes,
         flops=3 * 10**10,
     )
-    spot = jnp.arange(rim_width, dtype=i32)[None, :]
-    rim_face = jnp.where(spot < blocks * rims, lax.div(rim, jnp.int32(count)), -1)
-
     def apply(kind, coefficients, r, p, traces, sub_out, rim_out, x):
         one, two = over_segments(rim_out)
         swapped = lax.ppermute(sub_out, "sub", cores)
@@ -868,11 +853,11 @@
         jump, own, x = run(
             functools.partial(local_kernel, only_own, blocks, width, x is None),
             [col, part, block],
-            p, traces, sub_out, meta, lane, at, k3, *([] if x is None else [x]),
+            p, traces, meta, lane, at, k3, *([] if x is None else [x]),
         )
         goes_on = kind in ("step", "first")
         kernel = functools.partial(ahead_kernel, kind, coefficients, blocks, width, rims)
-        args = [r, jump, own, swapped, far, tt3] + ([p] if kind == "step" else [])
+        args = [r, jump, own, sub_out, swapped, far, tt3] + ([p] if kind == "step" else [])
         if not goes_on:
             (r,) = run(kernel, [part], *args)
             finish = functools.partial(finish_kernel, kind, None, blocks, width, rims)

time: 60.5 us -> 57.9 us (0.957)
  waiting for transfers between devices: 6.5 us -> 5.07 us
  Pallas kernels: 30.2 us -> 29.5 us
    ppermute x14, starting transfers between devices: 15.4 us -> 11.9 us  [over_segments(): return (lax.ppermute(rim, both, ones), lax.ppermute(rim, both, twos))]
    ppermute x7, starting transfers between devices: 0.43 us -> 2.89 us  [apply(): swapped = lax.ppermute(sub_out, 'sub', cores)]
    ppermute x1, starting transfers between devices: 0.27 us -> 1.49 us  [local(): near = lax.ppermute(near, 'sub', cores)]
    ppermute x14, waiting for transfers between devices: 1.16 us -> 0.04 us  [over_segments(): return (lax.ppermute(rim, both, ones), lax.ppermute(rim, both, twos))]
    pallas_call x36 -> x37, Pallas kernels: 30.2 us -> 29.5 us  [call(): pl.pallas_call(kernel, out_shape=[jax.ShapeDtypeStruct(shape, kind) for s...]
  transfers between devices with their start and end apart: 26 -> 26, of which waited for: 7 -> 4; matrix products, arithmetic and copies ran while one was open for 0% -> 0% of each run, Pallas kernels for 37% -> 38%
where the time goes in v5:
time: 57.9 us; the launch traced here: 57.7 us
  Pallas kernels  29.5 us (51%)
  starting transfers between devices  21.4 us (37%)
  waiting for transfers between devices  5.07 us (9%)
  between operations  1 us (2%)
  local copies, waits for them, and re-layouts  0.8 us (1%)
    pallas_call x37, Pallas kernels, call(): pl.pallas_call(kernel, out_shape=[jax.ShapeDtypeStruct(shape, kind) for s...  29.5 us
    ppermute x14, starting transfers between devices, over_segments(): return (lax.ppermute(rim, both, ones), lax.ppermute(rim, both, twos))  11.9 us
    ppermute x3, starting transfers between devices, local(): lax.ppermute(packed, 'sub', [(s, s ^ CORES * k) for s in range(peers)])  4.54 us
    ppermute x3, waiting for transfers between devices, local(): lax.ppermute(packed, 'sub', [(s, s ^ CORES * k) for s in range(peers)])  4.2 us
    ppermute x7, starting transfers between devices, apply(): swapped = lax.ppermute(sub_out, 'sub', cores)  2.89 us
    ppermute x1, starting transfers between devices, local(): near = lax.ppermute(near, 'sub', cores)  1.49 us
  transfers between devices with their start and end apart: 26, of which 4 were waited for; matrix products, arithmetic and copies ran while one was open for 0% of the time, Pallas kernels for 38%

profile of v5, /device:TPU:0, one launch (start us, length us, event | category | flops | bytes accessed | tf_op | source)
XLA Modules:
  0.0 57.7 jit_solution(88612102869779939)
XLA Ops:
  0.7 1.6 %shard_map.131.refs_0_ = f32[80,256]{1,0:T(8,128)} custom-call(f32[64,256]{1,0:T(8,128)} %b_ref.1, f32[1,256]{1,0:T(1,128)} %bitcast.6, s32[1,256]{1,0:T(1,128)} %bitcast.7, s32[6,256]{1,0:T(8,128)} %face_ref.1, s32[1,128]{1,0:T(1,128)} %sub_ref.1, s32[1,16]{1,0:T(1,128)} %rim_ref.1, s32[1,64]{1,0:T(1,128)} %size_ref.1, f32[1,64]{1,0:T(1,128)} %bitcast.8), custom_call_target="tpu_custom_call" | custom-call | flops 3000000000 | bytes 1 | tf_op jit(solution)/shard_map/pallas_call | solution.py:727
  2.3 3.0 %collective-permute-start = (f32[80,256]{1,0:T(8,128)}, f32[80,256]{1,0:T(8,128)S(1)}, u32[]{:S(2)}, u32[]{:S(2)}) collective-permute-start(f32[80,256]{1,0:T(8,128)} %shard_map.131.refs_0_), channel_id=1, source_target_pairs={{0,2},{1,3},{2,0},{3,1},{4,6},{5,7},{6,4},{7,5},{8,10},{9,11},{10,... | collective-permute-start | bytes 245768 | tf_op jit(solution)/shard_map/ppermute | solution.py:824
  5.3 1.5 %collective-permute-start.1 = (f32[80,256]{1,0:T(8,128)}, f32[80,256]{1,0:T(8,128)S(1)}, u32[]{:S(2)}, u32[]{:S(2)}) collective-permute-start(f32[80,256]{1,0:T(8,128)} %shard_map.131.refs_0_), channel_id=1, source_target_pairs={{0,4},{1,5},{2,6},{3,7},{4,0},{5,1},{6,2},{7,3},{8,12},{9,13},{10,... | collective-permute-start | bytes 245768 | tf_op jit(solution)/shard_map/ppermute | solution.py:824
  7.0 0.8 %copy-done = f32[8,64,64]{2,1,0:T(8,128)S(1)} copy-done((f32[8,64,64]{2,1,0:T(8,128)S(1)}, f32[8,64,64]{2,1,0:T(8,128)}, u32[]{:S(2)}) %copy-start) | copy-done | bytes 131096
  8.3 2.5 %collective-permute-done.1.refs_2_ = f32[80,256]{1,0:T(8,128)S(1)} collective-permute-done((f32[80,256]{1,0:T(8,128)}, f32[80,256]{1,0:T(8,128)S(1)}, u32[]{:S(2)}, u32[]{:S(2)}) %collective-permute-start.1) | collective-permute-done | bytes 81952 | tf_op jit(solution)/shard_map/ppermute | solution.py:824
  10.8 1.5 %collective-permute-done.2.refs_3_ = f32[80,256]{1,0:T(8,128)S(1)} collective-permute-done((f32[80,256]{1,0:T(8,128)}, f32[80,256]{1,0:T(8,128)S(1)}, u32[]{:S(2)}, u32[]{:S(2)}) %collective-permute-start.2) | collective-permute-done | bytes 81952 | tf_op jit(solution)/shard_map/ppermute | solution.py:824
  12.3 0.5 shard_map.134
  12.8 1.6 %collective-permute-start.4 = (f32[16,128]{1,0:T(8,128)S(1)}, f32[16,128]{1,0:T(8,128)S(1)}, u32[]{:S(2)}, u32[]{:S(2)}) collective-permute-start(f32[16,128]{1,0:T(8,128)S(1)} %get-tuple-element.99._), channel_id=1, source_target_pairs={{0,8},{1,9},{2,10},{3,11},{4,12},{5,13},{6,14},{7,15},{8,0},{9,1},... | collective-permute-start | bytes 24584 | tf_op jit(solution)/shard_map/ppermute | solution.py:797
  14.4 0.4 shard_map.135
  14.8 0.6 collective-permute-start.3
  15.6 1.5 %shard_map.136 = (f32[96,1024]{1,0:T(8,128)S(1)}, f32[64,1024]{1,0:T(8,128)S(1)}, f32[64,256]{1,0:T(8,128)S(1)}) custom-call(f32[64,1024]{1,0:T(8,128)S(1)} %get-tuple-element.97.p_ref.refs_0_.refs_7_, f32[96,1024]{1,0:T(8,128)S(1)} %get-tuple-element.100.refs_1_, f32[8,1024]{1,0:T(8,128)S(1)} %get-tuple-element.101.refs_2_, ...), custom_call_target="tpu_custom_call" | custom-call | flops 3000000000 | bytes 1 | tf_op jit(solution)/shard_map/pallas_call | solution.py:727
  17.1 0.7 %shard_map.137 = (f32[64,1024]{1,0:T(8,128)S(1)}, f32[64,1024]{1,0:T(8,128)S(1)}, f32[64,128]{1,0:T(8,128)S(1)}) custom-call(f32[64,1024]{1,0:T(8,128)S(1)} %get-tuple-element.96.refs_0_, f32[96,1024]{1,0:T(8,128)S(1)} %get-tuple-element.105.refs_1_, f32[64,1024]{1,0:T(8,128)S(1)} %get-tuple-element.106.refs_2_, f32[16,512]{1,0:T(8,128)S(1)} %get-tuple-element.107.refs_3_, ...), custom_call_target="tpu_custom_call" | custom-call | flops 3000000000 | bytes 1 | tf_op jit(solution)/shard_map/pallas_call | solution.py:727
  17.8 0.4 shard_map.139.refs_9_
  18.2 2.7 %collective-permute-start.7 = (f32[16,128]{1,0:T(8,128)S(1)}, f32[16,128]{1,0:T(8,128)S(1)}, u32[]{:S(2)}, u32[]{:S(2)}) collective-permute-start(f32[16,128]{1,0:T(8,128)S(1)} %shard_map.139.refs_9_), channel_id=1, source_target_pairs={{0,8},{1,9},{2,10},{3,11},{4,12},{5,13},{6,14},{7,15},{8,0},{9,1},... | collective-permute-start | bytes 24584 | tf_op jit(solution)/shard_map/ppermute | solution.py:797
  21.2 0.8 %shard_map.140 = (f32[64,1024]{1,0:T(8,128)S(1)}, f32[64,1024]{1,0:T(8,128)S(1)}, f32[96,1024]{1,0:T(8,128)S(1)}, f32[16,512]{1,0:T(8,128)S(1)}) custom-call(f32[64,1024]{1,0:T(8,128)S(1)} %get-tuple-element.112.refs_0_, f32[16,128]{1,0:T(8,128)S(1)} %collective-permute-done.4.one_ref.refs_1_, f32[16,128]{1,0:T(8,128)S(1)} %collective-permute-done.5.two_ref.refs_2_, ...), custom_call_target="tpu_custom_call" | custom-call | flops 3000000000 | bytes 1 | tf_op jit(solution)/shard_map/pallas_call | solution.py:727
  22.4 1.5 %shard_map.141 = (f32[96,1024]{1,0:T(8,128)S(1)}, f32[64,1024]{1,0:T(8,128)S(1)}, f32[64,256]{1,0:T(8,128)S(1)}) custom-call(f32[64,1024]{1,0:T(8,128)S(1)} %get-tuple-element.120.refs_0_.refs_7_, f32[96,1024]{1,0:T(8,128)S(1)} %get-tuple-element.121.refs_1_, f32[8,1024]{1,0:T(8,128)S(1)} %get-tuple-element.101.refs_2_, ...), custom_call_target="tpu_custom_call" | custom-call | flops 3000000000 | bytes 1 | tf_op jit(solution)/shard_map/pallas_call | solution.py:727
  23.8 0.7 %shard_map.142 = (f32[64,1024]{1,0:T(8,128)S(1)}, f32[64,1024]{1,0:T(8,128)S(1)}, f32[64,128]{1,0:T(8,128)S(1)}) custom-call(f32[64,1024]{1,0:T(8,128)S(1)} %get-tuple-element.119.refs_0_, f32[96,1024]{1,0:T(8,128)S(1)} %get-tuple-element.123.refs_1_, f32[64,1024]{1,0:T(8,128)S(1)} %get-tuple-element.124.refs_2_, f32[16,512]{1,0:T(8,128)S(1)} %get-tuple-element.125.refs_3_, ...), custom_call_target="tpu_custom_call" | custom-call | flops 3000000000 | bytes 1 | tf_op jit(solution)/shard_map/pallas_call | solution.py:727
  24.6 0.4 shard_map.143.refs_9_
  25.0 0.5 collective-permute-start.10
  25.8 0.8 %shard_map.144 = (f32[64,1024]{1,0:T(8,128)S(1)}, f32[64,1024]{1,0:T(8,128)S(1)}, f32[96,1024]{1,0:T(8,128)S(1)}, f32[16,512]{1,0:T(8,128)S(1)}) custom-call(f32[64,1024]{1,0:T(8,128)S(1)} %get-tuple-element.126.refs_0_, f32[16,128]{1,0:T(8,128)S(1)} %collective-permute-done.7.one_ref.refs_1_, f32[16,128]{1,0:T(8,128)S(1)} %collective-permute-done.8.two_ref.refs_2_, ...), custom_call_target="tpu_custom_call" | custom-call | flops 3000000000 | bytes 1 | tf_op jit(solution)/shard_map/pallas_call | solution.py:727
  26.9 1.5 %shard_map.145 = (f32[96,1024]{1,0:T(8,128)S(1)}, f32[64,1024]{1,0:T(8,128)S(1)}, f32[64,256]{1,0:T(8,128)S(1)}) custom-call(f32[64,1024]{1,0:T(8,128)S(1)} %get-tuple-element.130.refs_0_, f32[96,1024]{1,0:T(8,128)S(1)} %get-tuple-element.131.refs_1_, f32[8,1024]{1,0:T(8,128)S(1)} %get-tuple-element.101.refs_2_, s32[8,1024]{1,0:T(8,128)S(1)} %get-tuple-element.102.refs_3_, ...), custom_call_target="tpu_custom_call" | custom-call | flops 3000000000 | bytes 1 | tf_op jit(solution)/shard_map/pallas_call | solution.py:727
  28.4 0.7 %shard_map.146.r_ref.refs_0_ = f32[64,1024]{1,0:T(8,128)S(1)} custom-call(f32[64,1024]{1,0:T(8,128)S(1)} %get-tuple-element.129.refs_0_, f32[96,1024]{1,0:T(8,128)S(1)} %get-tuple-element.133.refs_1_, f32[64,1024]{1,0:T(8,128)S(1)} %get-tuple-element.134.refs_2_, f32[16,512]{1,0:T(8,128)S(1)} %get-tuple-element.135.refs_3_, ...), custom_call_target="tpu_custom_call" | custom-call | flops 3000000000 | bytes 1 | tf_op jit(solution)/shard_map/pallas_call | solution.py:727
  29.4 0.6 %collective-permute-start.13 = (f32[72,128]{1,0:T(8,128)S(1)}, f32[72,128]{1,0:T(8,128)S(1)}, u32[]{:S(2)}, u32[]{:S(2)}) collective-permute-start(f32[72,128]{1,0:T(8,128)S(1)} %shard_map.147.refs_7_), channel_id=1, source_target_pairs={{0,2},{1,8},{2,0},{3,10},{4,6},{5,12},{6,4},{7,14},{8,1},{9,16},{1... | collective-permute-start | bytes 110600 | tf_op jit(solution)/shard_map/ppermute | solution.py:890
  30.0 0.6 shard_map.148
  30.6 1.5 %collective-permute-start.12 = (f32[72,640]{1,0:T(8,128)S(1)}, f32[72,640]{1,0:T(8,128)S(1)}, u32[]{:S(2)}, u32[]{:S(2)}) collective-permute-start(f32[72,640]{1,0:T(8,128)S(1)} %get-tuple-element.139), channel_id=1, source_target_pairs={{0,1},{1,0},{2,3},{3,2},{4,5},{5,4},{6,7},{7,6},{8,9},{9,8},{10,11... | collective-permute-start | bytes 552968 | tf_op jit(solution)/shard_map/ppermute | solution.py:891
  32.3 0.8 %collective-permute-done.12.near_ref = f32[72,640]{1,0:T(8,128)S(1)} collective-permute-done((f32[72,640]{1,0:T(8,128)S(1)}, f32[72,640]{1,0:T(8,128)S(1)}, u32[]{:S(2)}, u32[]{:S(2)}) %collective-permute-start.12) | collective-permute-done | bytes 184352 | tf_op jit(solution)/shard_map/ppermute | solution.py:891
  33.1 1.2 %shard_map.150 = (f32[64,384]{1,0:T(8,128)S(1)}, f32[1,384]{1,0:T(1,128)S(1)}, s32[1,8,256]{2,1,0:T(8,128)S(1)}) custom-call(f32[64,1024]{1,0:T(8,128)S(1)} %get-tuple-element.138.r_ref.refs_0_, f32[72,640]{1,0:T(8,128)S(1)} %collective-permute-done.12.near_ref, s32[4,512]{1,0:T(4,128)S(1)} %get-tuple-element.140.gather_ref, ...), custom_call_target="tpu_custom_call" | custom-call | flops 100000000 | bytes 1 | tf_op jit(solution)/shard_map/pallas_call | solution.py:727
  34.3 2.1 %shard_map.151 = (f32[64,1024]{1,0:T(8,128)S(1)}, f32[16,128]{1,0:T(8,128)S(1)}) custom-call(f32[64,384]{1,0:T(8,128)S(1)} %get-tuple-element.142.right_ref, f32[1,384]{1,0:T(1,128)S(1)} %get-tuple-element.143.scale_ref, s32[1,8,256]{2,1,0:T(8,128)S(1)} %get-tuple-element.144.front_ref, f32[64,1024]{1,0:T(8,128)S(1)} %get-tuple-element.138.r_ref.refs_0_, ...), custom_call_target="tpu_custom_call" | custom-call | flops 3000000000 | bytes 1 | tf_op jit(solution)/shard_map/pallas_call | solution.py:727
  36.4 1.3 %collective-permute-start.15 = (f32[16,128]{1,0:T(8,128)S(1)}, f32[16,128]{1,0:T(8,128)S(1)}, u32[]{:S(2)}, u32[]{:S(2)}) collective-permute-start(f32[16,128]{1,0:T(8,128)S(1)} %get-tuple-element.149._), channel_id=1, source_target_pairs={{0,8},{1,9},{2,10},{3,11},{4,12},{5,13},{6,14},{7,15},{8,0},{9,1},... | collective-permute-start | bytes 24584 | tf_op jit(solution)/shard_map/ppermute | solution.py:797
  37.9 0.4 shard_map.152
  38.2 0.5 collective-permute-start.14
  38.7 1.5 %shard_map.153 = (f32[96,1024]{1,0:T(8,128)S(1)}, f32[64,1024]{1,0:T(8,128)S(1)}, f32[64,256]{1,0:T(8,128)S(1)}) custom-call(f32[64,1024]{1,0:T(8,128)S(1)} %get-tuple-element.148.p_ref.refs_0_, f32[96,1024]{1,0:T(8,128)S(1)} %get-tuple-element.150.refs_1_, f32[8,1024]{1,0:T(8,128)S(1)} %get-tuple-element.101.refs_2_, ...), custom_call_target="tpu_custom_call" | custom-call | flops 3000000000 | bytes 1 | tf_op jit(solution)/shard_map/pallas_call | solution.py:727
  40.2 0.7 %shard_map.154 = (f32[64,1024]{1,0:T(8,128)S(1)}, f32[64,1024]{1,0:T(8,128)S(1)}, f32[64,128]{1,0:T(8,128)S(1)}) custom-call(f32[64,1024]{1,0:T(8,128)S(1)} %get-tuple-element.138.r_ref.refs_0_, f32[96,1024]{1,0:T(8,128)S(1)} %get-tuple-element.152.refs_1_, f32[64,1024]{1,0:T(8,128)S(1)} %get-tuple-element.153.refs_2_, ...), custom_call_target="tpu_custom_call" | custom-call | flops 3000000000 | bytes 1 | tf_op jit(solution)/shard_map/pallas_call | solution.py:727
  41.0 0.4 shard_map.155.refs_9_
  41.4 1.9 %collective-permute-start.18 = (f32[16,128]{1,0:T(8,128)S(1)}, f32[16,128]{1,0:T(8,128)S(1)}, u32[]{:S(2)}, u32[]{:S(2)}) collective-permute-start(f32[16,128]{1,0:T(8,128)S(1)} %shard_map.155.refs_9_), channel_id=1, source_target_pairs={{0,8},{1,9},{2,10},{3,11},{4,12},{5,13},{6,14},{7,15},{8,0},{9,1},... | collective-permute-start | bytes 24584 | tf_op jit(solution)/shard_map/ppermute | solution.py:797
  43.6 0.8 %shard_map.156 = (f32[64,1024]{1,0:T(8,128)S(1)}, f32[64,1024]{1,0:T(8,128)S(1)}, f32[96,1024]{1,0:T(8,128)S(1)}, f32[16,512]{1,0:T(8,128)S(1)}) custom-call(f32[64,1024]{1,0:T(8,128)S(1)} %get-tuple-element.155.refs_0_, f32[16,128]{1,0:T(8,128)S(1)} %collective-permute-done.15.one_ref.refs_1_, f32[16,128]{1,0:T(8,128)S(1)} %collective-permute-done.16.two_ref.refs_2_, ...), custom_call_target="tpu_custom_call" | custom-call | flops 3000000000 | bytes 1 | tf_op jit(solution)/shard_map/pallas_call | solution.py:727
  44.7 1.5 %shard_map.157 = (f32[96,1024]{1,0:T(8,128)S(1)}, f32[64,1024]{1,0:T(8,128)S(1)}, f32[64,256]{1,0:T(8,128)S(1)}) custom-call(f32[64,1024]{1,0:T(8,128)S(1)} %get-tuple-element.159.refs_0_.refs_7_, f32[96,1024]{1,0:T(8,128)S(1)} %get-tuple-element.160.refs_1_, f32[8,1024]{1,0:T(8,128)S(1)} %get-tuple-element.101.refs_2_, ...), custom_call_target="tpu_custom_call" | custom-call | flops 3000000000 | bytes 1 | tf_op jit(solution)/shard_map/pallas_call | solution.py:727
  46.2 0.7 %shard_map.158 = (f32[64,1024]{1,0:T(8,128)S(1)}, f32[64,1024]{1,0:T(8,128)S(1)}, f32[64,128]{1,0:T(8,128)S(1)}) custom-call(f32[64,1024]{1,0:T(8,128)S(1)} %get-tuple-element.158.refs_0_, f32[96,1024]{1,0:T(8,128)S(1)} %get-tuple-element.162.refs_1_, f32[64,1024]{1,0:T(8,128)S(1)} %get-tuple-element.163.refs_2_, f32[16,512]{1,0:T(8,128)S(1)} %get-tuple-element.164.refs_3_, ...), custom_call_target="tpu_custom_call" | custom-call | flops 3000000000 | bytes 1 | tf_op jit(solution)/shard_map/pallas_call | solution.py:727
  47.0 0.4 shard_map.159.refs_9_
  47.4 0.8 %collective-permute-start.21 = (f32[16,128]{1,0:T(8,128)S(1)}, f32[16,128]{1,0:T(8,128)S(1)}, u32[]{:S(2)}, u32[]{:S(2)}) collective-permute-start(f32[16,128]{1,0:T(8,128)S(1)} %shard_map.159.refs_9_), channel_id=1, source_target_pairs={{0,8},{1,9},{2,10},{3,11},{4,12},{5,13},{6,14},{7,15},{8,0},{9,1},... | collective-permute-start | bytes 24584 | tf_op jit(solution)/shard_map/ppermute | solution.py:797
  48.4 0.8 %shard_map.160 = (f32[64,1024]{1,0:T(8,128)S(1)}, f32[64,1024]{1,0:T(8,128)S(1)}, f32[96,1024]{1,0:T(8,128)S(1)}, f32[16,512]{1,0:T(8,128)S(1)}) custom-call(f32[64,1024]{1,0:T(8,128)S(1)} %get-tuple-element.165.refs_0_, f32[16,128]{1,0:T(8,128)S(1)} %collective-permute-done.18.one_ref.refs_1_, f32[16,128]{1,0:T(8,128)S(1)} %collective-permute-done.19.two_ref.refs_2_, ...), custom_call_target="tpu_custom_call" | custom-call | flops 3000000000 | bytes 1 | tf_op jit(solution)/shard_map/pallas_call | solution.py:727
  49.6 1.5 %shard_map.161 = (f32[96,1024]{1,0:T(8,128)S(1)}, f32[64,1024]{1,0:T(8,128)S(1)}, f32[64,256]{1,0:T(8,128)S(1)}) custom-call(f32[64,1024]{1,0:T(8,128)S(1)} %get-tuple-element.169.refs_0_.refs_7_, f32[96,1024]{1,0:T(8,128)S(1)} %get-tuple-element.170.refs_1_, f32[8,1024]{1,0:T(8,128)S(1)} %get-tuple-element.101.refs_2_, ...), custom_call_target="tpu_custom_call" | custom-call | flops 3000000000 | bytes 1 | tf_op jit(solution)/shard_map/pallas_call | solution.py:727
  51.1 0.7 %shard_map.162 = (f32[64,1024]{1,0:T(8,128)S(1)}, f32[64,1024]{1,0:T(8,128)S(1)}, f32[64,128]{1,0:T(8,128)S(1)}) custom-call(f32[64,1024]{1,0:T(8,128)S(1)} %get-tuple-element.168.refs_0_, f32[96,1024]{1,0:T(8,128)S(1)} %get-tuple-element.172.refs_1_, f32[64,1024]{1,0:T(8,128)S(1)} %get-tuple-element.173.refs_2_, f32[16,512]{1,0:T(8,128)S(1)} %get-tuple-element.174.refs_3_, ...), custom_call_target="tpu_custom_call" | custom-call | flops 3000000000 | bytes 1 | tf_op jit(solution)/shard_map/pallas_call | solution.py:727
  51.8 0.4 shard_map.163.refs_9_
  52.2 1.8 %collective-permute-start.24 = (f32[16,128]{1,0:T(8,128)S(1)}, f32[16,128]{1,0:T(8,128)S(1)}, u32[]{:S(2)}, u32[]{:S(2)}) collective-permute-start(f32[16,128]{1,0:T(8,128)S(1)} %shard_map.163.refs_9_), channel_id=1, source_target_pairs={{0,8},{1,9},{2,10},{3,11},{4,12},{5,13},{6,14},{7,15},{8,0},{9,1},... | collective-permute-start | bytes 24584 | tf_op jit(solution)/shard_map/ppermute | solution.py:797
  54.2 0.8 %shard_map.164 = (f32[64,1024]{1,0:T(8,128)S(1)}, f32[64,1024]{1,0:T(8,128)S(1)}, f32[96,1024]{1,0:T(8,128)S(1)}, f32[16,512]{1,0:T(8,128)S(1)}) custom-call(f32[64,1024]{1,0:T(8,128)S(1)} %get-tuple-element.175.refs_0_, f32[16,128]{1,0:T(8,128)S(1)} %collective-permute-done.21.one_ref.refs_1_, f32[16,128]{1,0:T(8,128)S(1)} %collective-permute-done.22.two_ref.refs_2_, ...), custom_call_target="tpu_custom_call" | custom-call | flops 3000000000 | bytes 1 | tf_op jit(solution)/shard_map/pallas_call | solution.py:727
  55.4 1.0 %shard_map.165 = (f32[96,256]{1,0:T(8,128)S(1)}, f32[64,256]{1,0:T(8,128)S(1)}, f32[64,256]{1,0:T(8,128)}) custom-call(f32[64,1024]{1,0:T(8,128)S(1)} %get-tuple-element.178.refs_0_, f32[96,1024]{1,0:T(8,128)S(1)} %get-tuple-element.179.refs_1_, f32[8,1024]{1,0:T(8,128)S(1)} %get-tuple-element.101.refs_2_, s32[8,1024]{1,0:T(8,128)S(1)} %get-tuple-element.102.refs_3_, ...), custom_call_target="tpu_custom_call" | custom-call | flops 3000000000 | bytes 1 | tf_op jit(solution)/shard_map/pallas_call | solution.py:727
  56.8 0.9 %shard_map.167 = f32[64,256]{1,0:T(8,128)} custom-call(f32[64,256]{1,0:T(8,128)S(1)} %shard_map.166.refs_0_, f32[16,128]{1,0:T(8,128)S(1)} %collective-permute-done.24.refs_1_, f32[16,128]{1,0:T(8,128)S(1)} %collective-permute-done.25.refs_2_, s32[8,1024]{1,0:T(8,128)S(1)} %get-tuple-element.113.edge_ref.refs_3_, ...), custom_call_target="tpu_custom_call" | custom-call | flops 3000000000 | bytes 1 | tf_op jit(solution)/shard_map/pallas_call | solution.py:727
  (51 shorter events, 4.7 us)
Async XLA Ops:
  0.6 6.2 %copy-start.2 = (f32[2,64,64]{2,1,0:T(8,128)S(1)}, f32[2,64,64]{2,1,0:T(8,128)}, u32[]{:S(2)}) copy-start(f32[2,64,64]{2,1,0:T(8,128)} %refs_4_.1) | copy-start | bytes 98308
  0.6 6.2 %copy-start.3 = (f32[96,64]{0,1:T(8,128)S(1)}, f32[96,64]{0,1:T(8,128)}, u32[]{:S(2)}) copy-start(f32[96,64]{0,1:T(8,128)} %param.16) | copy-start | bytes 73732
  2.3 6.0 %collective-permute-start = (f32[80,256]{1,0:T(8,128)}, f32[80,256]{1,0:T(8,128)S(1)}, u32[]{:S(2)}, u32[]{:S(2)}) collective-permute-start(f32[80,256]{1,0:T(8,128)} %shard_map.131.refs_0_), channel_id=1, source_target_pairs={{0,2},{1,3},{2,0},{3,1},{4,6},{5,7},{6,4},{7,5},{8,10},{9,11},{10,... | collective-permute-start | bytes 245768 | tf_op jit(solution)/shard_map/ppermute | solution.py:824
  5.3 5.5 %collective-permute-start.1 = (f32[80,256]{1,0:T(8,128)}, f32[80,256]{1,0:T(8,128)S(1)}, u32[]{:S(2)}, u32[]{:S(2)}) collective-permute-start(f32[80,256]{1,0:T(8,128)} %shard_map.131.refs_0_), channel_id=1, source_target_pairs={{0,4},{1,5},{2,6},{3,7},{4,0},{5,1},{6,2},{7,3},{8,12},{9,13},{10,... | collective-permute-start | bytes 245768 | tf_op jit(solution)/shard_map/ppermute | solution.py:824
  6.8 5.6 %collective-permute-start.2 = (f32[80,256]{1,0:T(8,128)}, f32[80,256]{1,0:T(8,128)S(1)}, u32[]{:S(2)}, u32[]{:S(2)}) collective-permute-start(f32[80,256]{1,0:T(8,128)} %shard_map.131.refs_0_), channel_id=1, source_target_pairs={{0,6},{1,7},{2,4},{3,5},{4,2},{5,3},{6,0},{7,1},{8,14},{9,15},{10,... | collective-permute-start | bytes 245768 | tf_op jit(solution)/shard_map/ppermute | solution.py:824
  6.8 1.0 %copy-start = (f32[8,64,64]{2,1,0:T(8,128)S(1)}, f32[8,64,64]{2,1,0:T(8,128)}, u32[]{:S(2)}) copy-start(f32[8,64,64]{2,1,0:T(8,128)} %restriction_ref.1) | copy-start | bytes 393220
  6.8 1.0 %copy-start.4 = (f32[64,64]{1,0:T(8,128)S(1)}, f32[64,64]{1,0:T(8,128)}, u32[]{:S(2)}) copy-start(f32[64,64]{1,0:T(8,128)} %stiff_ref.5) | copy-start | bytes 49156
  7.8 4.6 %copy-start.1 = (f32[80,256]{1,0:T(8,128)S(1)}, f32[80,256]{1,0:T(8,128)}, u32[]{:S(2)}) copy-start(f32[80,256]{1,0:T(8,128)} %shard_map.131.refs_0_) | copy-start | bytes 245764
  12.8 5.0 %collective-permute-start.4 = (f32[16,128]{1,0:T(8,128)S(1)}, f32[16,128]{1,0:T(8,128)S(1)}, u32[]{:S(2)}, u32[]{:S(2)}) collective-permute-start(f32[16,128]{1,0:T(8,128)S(1)} %get-tuple-element.99._), channel_id=1, source_target_pairs={{0,8},{1,9},{2,10},{3,11},{4,12},{5,13},{6,14},{7,15},{8,0},{9,1},... | collective-permute-start | bytes 24584 | tf_op jit(solution)/shard_map/ppermute | solution.py:797
  14.4 3.4 %collective-permute-start.5 = (f32[16,128]{1,0:T(8,128)S(1)}, f32[16,128]{1,0:T(8,128)S(1)}, u32[]{:S(2)}, u32[]{:S(2)}) collective-permute-start(f32[16,128]{1,0:T(8,128)S(1)} %get-tuple-element.99._), channel_id=1, source_target_pairs={{0,1},{1,0},{2,3},{3,2},{4,5},{5,4},{6,7},{7,6},{8,16},{9,17},{10,... | collective-permute-start | bytes 24584 | tf_op jit(solution)/shard_map/ppermute | solution.py:797
  14.8 2.2 %collective-permute-start.3 = (f32[16,512]{1,0:T(8,128)S(1)}, f32[16,512]{1,0:T(8,128)S(1)}, u32[]{:S(2)}, u32[]{:S(2)}) collective-permute-start(f32[16,512]{1,0:T(8,128)S(1)} %get-tuple-element.107.refs_3_), channel_id=1, source_target_pairs={{0,1},{1,0},{2,3},{3,2},{4,5},{5,4},{6,7},{7,6},{8,9},{9,8},{10,11... | collective-permute-start | bytes 98312 | tf_op jit(solution)/shard_map/ppermute | solution.py:849
  18.2 6.4 %collective-permute-start.7 = (f32[16,128]{1,0:T(8,128)S(1)}, f32[16,128]{1,0:T(8,128)S(1)}, u32[]{:S(2)}, u32[]{:S(2)}) collective-permute-start(f32[16,128]{1,0:T(8,128)S(1)} %shard_map.139.refs_9_), channel_id=1, source_target_pairs={{0,8},{1,9},{2,10},{3,11},{4,12},{5,13},{6,14},{7,15},{8,0},{9,1},... | collective-permute-start | bytes 24584 | tf_op jit(solution)/shard_map/ppermute | solution.py:797
  21.0 3.6 %collective-permute-start.8 = (f32[16,128]{1,0:T(8,128)S(1)}, f32[16,128]{1,0:T(8,128)S(1)}, u32[]{:S(2)}, u32[]{:S(2)}) collective-permute-start(f32[16,128]{1,0:T(8,128)S(1)} %shard_map.139.refs_9_), channel_id=1, source_target_pairs={{0,1},{1,0},{2,3},{3,2},{4,5},{5,4},{6,7},{7,6},{8,16},{9,17},{10,... | collective-permute-start | bytes 24584 | tf_op jit(solution)/shard_map/ppermute | solution.py:797
  22.0 1.9 %collective-permute-start.6 = (f32[16,512]{1,0:T(8,128)S(1)}, f32[16,512]{1,0:T(8,128)S(1)}, u32[]{:S(2)}, u32[]{:S(2)}) collective-permute-start(f32[16,512]{1,0:T(8,128)S(1)} %get-tuple-element.125.refs_3_), channel_id=1, source_target_pairs={{0,1},{1,0},{2,3},{3,2},{4,5},{5,4},{6,7},{7,6},{8,9},{9,8},{10,11... | collective-permute-start | bytes 98312 | tf_op jit(solution)/shard_map/ppermute | solution.py:849
  25.0 4.1 %collective-permute-start.10 = (f32[16,128]{1,0:T(8,128)S(1)}, f32[16,128]{1,0:T(8,128)S(1)}, u32[]{:S(2)}, u32[]{:S(2)}) collective-permute-start(f32[16,128]{1,0:T(8,128)S(1)} %shard_map.143.refs_9_), channel_id=1, source_target_pairs={{0,8},{1,9},{2,10},{3,11},{4,12},{5,13},{6,14},{7,15},{8,0},{9,1},... | collective-permute-start | bytes 24584 | tf_op jit(solution)/shard_map/ppermute | solution.py:797
  25.5 3.6 %collective-permute-start.11 = (f32[16,128]{1,0:T(8,128)S(1)}, f32[16,128]{1,0:T(8,128)S(1)}, u32[]{:S(2)}, u32[]{:S(2)}) collective-permute-start(f32[16,128]{1,0:T(8,128)S(1)} %shard_map.143.refs_9_), channel_id=1, source_target_pairs={{0,1},{1,0},{2,3},{3,2},{4,5},{5,4},{6,7},{7,6},{8,16},{9,17},{10,... | collective-permute-start | bytes 24584 | tf_op jit(solution)/shard_map/ppermute | solution.py:797
  26.6 1.9 %collective-permute-start.9 = (f32[16,512]{1,0:T(8,128)S(1)}, f32[16,512]{1,0:T(8,128)S(1)}, u32[]{:S(2)}, u32[]{:S(2)}) collective-permute-start(f32[16,512]{1,0:T(8,128)S(1)} %get-tuple-element.135.refs_3_), channel_id=1, source_target_pairs={{0,1},{1,0},{2,3},{3,2},{4,5},{5,4},{6,7},{7,6},{8,9},{9,8},{10,11... | collective-permute-start | bytes 98312 | tf_op jit(solution)/shard_map/ppermute | solution.py:849
  29.4 4.9 %collective-permute-start.13 = (f32[72,128]{1,0:T(8,128)S(1)}, f32[72,128]{1,0:T(8,128)S(1)}, u32[]{:S(2)}, u32[]{:S(2)}) collective-permute-start(f32[72,128]{1,0:T(8,128)S(1)} %shard_map.147.refs_7_), channel_id=1, source_target_pairs={{0,2},{1,8},{2,0},{3,10},{4,6},{5,12},{6,4},{7,14},{8,1},{9,16},{1... | collective-permute-start | bytes 110600 | tf_op jit(solution)/shard_map/ppermute | solution.py:890
  30.6 2.5 %collective-permute-start.12 = (f32[72,640]{1,0:T(8,128)S(1)}, f32[72,640]{1,0:T(8,128)S(1)}, u32[]{:S(2)}, u32[]{:S(2)}) collective-permute-start(f32[72,640]{1,0:T(8,128)S(1)} %get-tuple-element.139), channel_id=1, source_target_pairs={{0,1},{1,0},{2,3},{3,2},{4,5},{5,4},{6,7},{7,6},{8,9},{9,8},{10,11... | collective-permute-start | bytes 552968 | tf_op jit(solution)/shard_map/ppermute | solution.py:891
  36.4 4.5 %collective-permute-start.15 = (f32[16,128]{1,0:T(8,128)S(1)}, f32[16,128]{1,0:T(8,128)S(1)}, u32[]{:S(2)}, u32[]{:S(2)}) collective-permute-start(f32[16,128]{1,0:T(8,128)S(1)} %get-tuple-element.149._), channel_id=1, source_target_pairs={{0,8},{1,9},{2,10},{3,11},{4,12},{5,13},{6,14},{7,15},{8,0},{9,1},... | collective-permute-start | bytes 24584 | tf_op jit(solution)/shard_map/ppermute | solution.py:797
  37.8 3.2 %collective-permute-start.16 = (f32[16,128]{1,0:T(8,128)S(1)}, f32[16,128]{1,0:T(8,128)S(1)}, u32[]{:S(2)}, u32[]{:S(2)}) collective-permute-start(f32[16,128]{1,0:T(8,128)S(1)} %get-tuple-element.149._), channel_id=1, source_target_pairs={{0,1},{1,0},{2,3},{3,2},{4,5},{5,4},{6,7},{7,6},{8,16},{9,17},{10,... | collective-permute-start | bytes 24584 | tf_op jit(solution)/shard_map/ppermute | solution.py:797
  38.2 2.0 %collective-permute-start.14 = (f32[16,512]{1,0:T(8,128)S(1)}, f32[16,512]{1,0:T(8,128)S(1)}, u32[]{:S(2)}, u32[]{:S(2)}) collective-permute-start(f32[16,512]{1,0:T(8,128)S(1)} %get-tuple-element.154.refs_3_), channel_id=1, source_target_pairs={{0,1},{1,0},{2,3},{3,2},{4,5},{5,4},{6,7},{7,6},{8,9},{9,8},{10,11... | collective-permute-start | bytes 98312 | tf_op jit(solution)/shard_map/ppermute | solution.py:849
  41.4 5.5 %collective-permute-start.18 = (f32[16,128]{1,0:T(8,128)S(1)}, f32[16,128]{1,0:T(8,128)S(1)}, u32[]{:S(2)}, u32[]{:S(2)}) collective-permute-start(f32[16,128]{1,0:T(8,128)S(1)} %shard_map.155.refs_9_), channel_id=1, source_target_pairs={{0,8},{1,9},{2,10},{3,11},{4,12},{5,13},{6,14},{7,15},{8,0},{9,1},... | collective-permute-start | bytes 24584 | tf_op jit(solution)/shard_map/ppermute | solution.py:797
  43.3 3.6 %collective-permute-start.19 = (f32[16,128]{1,0:T(8,128)S(1)}, f32[16,128]{1,0:T(8,128)S(1)}, u32[]{:S(2)}, u32[]{:S(2)}) collective-permute-start(f32[16,128]{1,0:T(8,128)S(1)} %shard_map.155.refs_9_), channel_id=1, source_target_pairs={{0,1},{1,0},{2,3},{3,2},{4,5},{5,4},{6,7},{7,6},{8,16},{9,17},{10,... | collective-permute-start | bytes 24584 | tf_op jit(solution)/shard_map/ppermute | solution.py:797
  44.4 1.8 %collective-permute-start.17 = (f32[16,512]{1,0:T(8,128)S(1)}, f32[16,512]{1,0:T(8,128)S(1)}, u32[]{:S(2)}, u32[]{:S(2)}) collective-permute-start(f32[16,512]{1,0:T(8,128)S(1)} %get-tuple-element.164.refs_3_), channel_id=1, source_target_pairs={{0,1},{1,0},{2,3},{3,2},{4,5},{5,4},{6,7},{7,6},{8,9},{9,8},{10,11... | collective-permute-start | bytes 98312 | tf_op jit(solution)/shard_map/ppermute | solution.py:849
  47.4 4.4 %collective-permute-start.21 = (f32[16,128]{1,0:T(8,128)S(1)}, f32[16,128]{1,0:T(8,128)S(1)}, u32[]{:S(2)}, u32[]{:S(2)}) collective-permute-start(f32[16,128]{1,0:T(8,128)S(1)} %shard_map.159.refs_9_), channel_id=1, source_target_pairs={{0,8},{1,9},{2,10},{3,11},{4,12},{5,13},{6,14},{7,15},{8,0},{9,1},... | collective-permute-start | bytes 24584 | tf_op jit(solution)/shard_map/ppermute | solution.py:797
  48.2 3.6 %collective-permute-start.22 = (f32[16,128]{1,0:T(8,128)S(1)}, f32[16,128]{1,0:T(8,128)S(1)}, u32[]{:S(2)}, u32[]{:S(2)}) collective-permute-start(f32[16,128]{1,0:T(8,128)S(1)} %shard_map.159.refs_9_), channel_id=1, source_target_pairs={{0,1},{1,0},{2,3},{3,2},{4,5},{5,4},{6,7},{7,6},{8,16},{9,17},{10,... | collective-permute-start | bytes 24584 | tf_op jit(solution)/shard_map/ppermute | solution.py:797
  49.2 1.8 %collective-permute-start.20 = (f32[16,512]{1,0:T(8,128)S(1)}, f32[16,512]{1,0:T(8,128)S(1)}, u32[]{:S(2)}, u32[]{:S(2)}) collective-permute-start(f32[16,512]{1,0:T(8,128)S(1)} %get-tuple-element.174.refs_3_), channel_id=1, source_target_pairs={{0,1},{1,0},{2,3},{3,2},{4,5},{5,4},{6,7},{7,6},{8,9},{9,8},{10,11... | collective-permute-start | bytes 98312 | tf_op jit(solution)/shard_map/ppermute | solution.py:849
  52.2 4.5 %collective-permute-start.24 = (f32[16,128]{1,0:T(8,128)S(1)}, f32[16,128]{1,0:T(8,128)S(1)}, u32[]{:S(2)}, u32[]{:S(2)}) collective-permute-start(f32[16,128]{1,0:T(8,128)S(1)} %shard_map.163.refs_9_), channel_id=1, source_target_pairs={{0,8},{1,9},{2,10},{3,11},{4,12},{5,13},{6,14},{7,15},{8,0},{9,1},... | collective-permute-start | bytes 24584 | tf_op jit(solution)/shard_map/ppermute | solution.py:797
  54.0 2.8 %collective-permute-start.25 = (f32[16,128]{1,0:T(8,128)S(1)}, f32[16,128]{1,0:T(8,128)S(1)}, u32[]{:S(2)}, u32[]{:S(2)}) collective-permute-start(f32[16,128]{1,0:T(8,128)S(1)} %shard_map.163.refs_9_), channel_id=1, source_target_pairs={{0,1},{1,0},{2,3},{3,2},{4,5},{5,4},{6,7},{7,6},{8,16},{9,17},{10,... | collective-permute-start | bytes 24584 | tf_op jit(solution)/shard_map/ppermute | solution.py:797
  55.0 1.4 %collective-permute-start.23 = (f32[16,512]{1,0:T(8,128)S(1)}, f32[16,512]{1,0:T(8,128)S(1)}, u32[]{:S(2)}, u32[]{:S(2)}) collective-permute-start(f32[16,512]{1,0:T(8,128)S(1)} %get-tuple-element.185.refs_3_), channel_id=1, source_target_pairs={{0,1},{1,0},{2,3},{3,2},{4,5},{5,4},{6,7},{7,6},{8,9},{9,8},{10,11... | collective-permute-start | bytes 98312 | tf_op jit(solution)/shard_map/ppermute | solution.py:849

commit v6 on v5

--- a/solution.py
+++ b/solution.py
@@ -723,7 +723,7 @@
 
 
 def call(limit, kernel, outs, *args, scratch=(), hbm=False, flops=3 * 10**9):
-    limit = (60 << 20) if hbm else limit
+    args = [pltpu.with_memory_space_constraint(x, pltpu.HBM) for x in args] if hbm else args
     return pl.pallas_call(
         kernel,
         out_shape=[jax.ShapeDtypeStruct(shape, kind) for shape, kind in outs],

time: 57.9 us -> 57 us (0.984)
  Pallas kernels: 29.5 us -> 28.7 us
    pallas_call x37, Pallas kernels: 29.5 us -> 28.7 us  [call(): pl.pallas_call(kernel, out_shape=[jax.ShapeDtypeStruct(shape, kind) for s...]
  transfers between devices with their start and end apart: 26 -> 26, of which waited for: 4 -> 3; matrix products, arithmetic and copies ran while one was open for 0% -> 0% of each run, Pallas kernels for 38% -> 39%
where the time goes in v6:
time: 57 us; the launch traced here: 56.8 us
  Pallas kernels  28.7 us (50%)
  starting transfers between devices  21.4 us (38%)
  waiting for transfers between devices  4.86 us (9%)
  between operations  1.01 us (2%)
  local copies, waits for them, and re-layouts  0.79 us (1%)
    pallas_call x37, Pallas kernels, call(): pl.pallas_call(kernel, out_shape=[jax.ShapeDtypeStruct(shape, kind) for s...  28.7 us
    ppermute x14, starting transfers between devices, over_segments(): return (lax.ppermute(rim, both, ones), lax.ppermute(rim, both, twos))  11.9 us
    ppermute x3, starting transfers between devices, local(): lax.ppermute(packed, 'sub', [(s, s ^ CORES * k) for s in range(peers)])  4.54 us
    ppermute x3, waiting for transfers between devices, local(): lax.ppermute(packed, 'sub', [(s, s ^ CORES * k) for s in range(peers)])  3.99 us
    ppermute x7, starting transfers between devices, apply(): swapped = lax.ppermute(sub_out, 'sub', cores)  2.88 us
    ppermute x1, starting transfers between devices, local(): near = lax.ppermute(near, 'sub', cores)  1.53 us
  transfers between devices with their start and end apart: 26, of which 3 were waited for; matrix products, arithmetic and copies ran while one was open for 0% of the time, Pallas kernels for 39%

profile of v6, /device:TPU:0, one launch (start us, length us, event | category | flops | bytes accessed | tf_op | source)
XLA Modules:
  0.0 56.8 jit_solution(8768156225390351639)
XLA Ops:
  0.7 1.0 %shard_map.131.refs_0_ = f32[80,256]{1,0:T(8,128)S(1)} custom-call(f32[64,256]{1,0:T(8,128)} %b_ref.1, f32[1,256]{1,0:T(1,128)} %bitcast.6, s32[1,256]{1,0:T(1,128)} %bitcast.7, s32[6,256]{1,0:T(8,128)} %face_ref.1, s32[1,128]{1,0:T(1,128)} %sub_ref.1, s32[1,16]{1,0:T(1,128)} %rim_ref.1, s32[1,64]{1,0:T(1,128)} %size_ref.1, f32[1,64]{1,0:T(1,128)} %bitcast.8), custom_call_target="tpu_custom_call" | custom-call | flops 3000000000 | bytes 1 | tf_op jit(solution)/shard_map/pallas_call | solution.py:727
  1.6 3.0 %collective-permute-start = (f32[80,256]{1,0:T(8,128)S(1)}, f32[80,256]{1,0:T(8,128)S(1)}, u32[]{:S(2)}, u32[]{:S(2)}) collective-permute-start(f32[80,256]{1,0:T(8,128)S(1)} %shard_map.131.refs_0_), channel_id=1, source_target_pairs={{0,2},{1,3},{2,0},{3,1},{4,6},{5,7},{6,4},{7,5},{8,10},{9,11},{10,... | collective-permute-start | bytes 245768 | tf_op jit(solution)/shard_map/ppermute | solution.py:824
  4.6 1.5 %collective-permute-start.1 = (f32[80,256]{1,0:T(8,128)S(1)}, f32[80,256]{1,0:T(8,128)S(1)}, u32[]{:S(2)}, u32[]{:S(2)}) collective-permute-start(f32[80,256]{1,0:T(8,128)S(1)} %shard_map.131.refs_0_), channel_id=1, source_target_pairs={{0,4},{1,5},{2,6},{3,7},{4,0},{5,1},{6,2},{7,3},{8,12},{9,13},{10,... | collective-permute-start | bytes 245768 | tf_op jit(solution)/shard_map/ppermute | solution.py:824
  6.3 0.8 %copy-done = f32[8,64,64]{2,1,0:T(8,128)S(1)} copy-done((f32[8,64,64]{2,1,0:T(8,128)S(1)}, f32[8,64,64]{2,1,0:T(8,128)}, u32[]{:S(2)}) %copy-start) | copy-done | bytes 131096
  7.5 2.4 %collective-permute-done.1.refs_2_ = f32[80,256]{1,0:T(8,128)S(1)} collective-permute-done((f32[80,256]{1,0:T(8,128)S(1)}, f32[80,256]{1,0:T(8,128)S(1)}, u32[]{:S(2)}, u32[]{:S(2)}) %collective-permute-start.1) | collective-permute-done | bytes 81952 | tf_op jit(solution)/shard_map/ppermute | solution.py:824
  9.9 1.5 %collective-permute-done.2.refs_3_ = f32[80,256]{1,0:T(8,128)S(1)} collective-permute-done((f32[80,256]{1,0:T(8,128)S(1)}, f32[80,256]{1,0:T(8,128)S(1)}, u32[]{:S(2)}, u32[]{:S(2)}) %collective-permute-start.2) | collective-permute-done | bytes 81952 | tf_op jit(solution)/shard_map/ppermute | solution.py:824
  11.5 0.5 shard_map.134
  12.0 1.6 %collective-permute-start.4 = (f32[16,128]{1,0:T(8,128)S(1)}, f32[16,128]{1,0:T(8,128)S(1)}, u32[]{:S(2)}, u32[]{:S(2)}) collective-permute-start(f32[16,128]{1,0:T(8,128)S(1)} %get-tuple-element.99._), channel_id=1, source_target_pairs={{0,8},{1,9},{2,10},{3,11},{4,12},{5,13},{6,14},{7,15},{8,0},{9,1},... | collective-permute-start | bytes 24584 | tf_op jit(solution)/shard_map/ppermute | solution.py:797
  13.6 0.4 shard_map.135
  14.0 0.6 %collective-permute-start.3 = (f32[16,512]{1,0:T(8,128)S(1)}, f32[16,512]{1,0:T(8,128)S(1)}, u32[]{:S(2)}, u32[]{:S(2)}) collective-permute-start(f32[16,512]{1,0:T(8,128)S(1)} %get-tuple-element.107.refs_3_), channel_id=1, source_target_pairs={{0,1},{1,0},{2,3},{3,2},{4,5},{5,4},{6,7},{7,6},{8,9},{9,8},{10,11... | collective-permute-start | bytes 98312 | tf_op jit(solution)/shard_map/ppermute | solution.py:849
  14.7 1.5 %shard_map.136 = (f32[96,1024]{1,0:T(8,128)S(1)}, f32[64,1024]{1,0:T(8,128)S(1)}, f32[64,256]{1,0:T(8,128)S(1)}) custom-call(f32[64,1024]{1,0:T(8,128)S(1)} %get-tuple-element.97.p_ref.refs_0_.refs_7_, f32[96,1024]{1,0:T(8,128)S(1)} %get-tuple-element.100.refs_1_, f32[8,1024]{1,0:T(8,128)S(1)} %get-tuple-element.101.refs_2_, ...), custom_call_target="tpu_custom_call" | custom-call | flops 3000000000 | bytes 1 | tf_op jit(solution)/shard_map/pallas_call | solution.py:727
  16.2 0.7 %shard_map.137 = (f32[64,1024]{1,0:T(8,128)S(1)}, f32[64,1024]{1,0:T(8,128)S(1)}, f32[64,128]{1,0:T(8,128)S(1)}) custom-call(f32[64,1024]{1,0:T(8,128)S(1)} %get-tuple-element.96.refs_0_, f32[96,1024]{1,0:T(8,128)S(1)} %get-tuple-element.105.refs_1_, f32[64,1024]{1,0:T(8,128)S(1)} %get-tuple-element.106.refs_2_, f32[16,512]{1,0:T(8,128)S(1)} %get-tuple-element.107.refs_3_, ...), custom_call_target="tpu_custom_call" | custom-call | flops 3000000000 | bytes 1 | tf_op jit(solution)/shard_map/pallas_call | solution.py:727
  16.9 0.4 shard_map.139.refs_9_
  17.3 2.7 %collective-permute-start.7 = (f32[16,128]{1,0:T(8,128)S(1)}, f32[16,128]{1,0:T(8,128)S(1)}, u32[]{:S(2)}, u32[]{:S(2)}) collective-permute-start(f32[16,128]{1,0:T(8,128)S(1)} %shard_map.139.refs_9_), channel_id=1, source_target_pairs={{0,8},{1,9},{2,10},{3,11},{4,12},{5,13},{6,14},{7,15},{8,0},{9,1},... | collective-permute-start | bytes 24584 | tf_op jit(solution)/shard_map/ppermute | solution.py:797
  20.3 0.8 %shard_map.140 = (f32[64,1024]{1,0:T(8,128)S(1)}, f32[64,1024]{1,0:T(8,128)S(1)}, f32[96,1024]{1,0:T(8,128)S(1)}, f32[16,512]{1,0:T(8,128)S(1)}) custom-call(f32[64,1024]{1,0:T(8,128)S(1)} %get-tuple-element.112.refs_0_, f32[16,128]{1,0:T(8,128)S(1)} %collective-permute-done.4.one_ref.refs_1_, f32[16,128]{1,0:T(8,128)S(1)} %collective-permute-done.5.two_ref.refs_2_, ...), custom_call_target="tpu_custom_call" | custom-call | flops 3000000000 | bytes 1 | tf_op jit(solution)/shard_map/pallas_call | solution.py:727
  21.5 1.5 %shard_map.141 = (f32[96,1024]{1,0:T(8,128)S(1)}, f32[64,1024]{1,0:T(8,128)S(1)}, f32[64,256]{1,0:T(8,128)S(1)}) custom-call(f32[64,1024]{1,0:T(8,128)S(1)} %get-tuple-element.120.refs_0_.refs_7_, f32[96,1024]{1,0:T(8,128)S(1)} %get-tuple-element.121.refs_1_, f32[8,1024]{1,0:T(8,128)S(1)} %get-tuple-element.101.refs_2_, ...), custom_call_target="tpu_custom_call" | custom-call | flops 3000000000 | bytes 1 | tf_op jit(solution)/shard_map/pallas_call | solution.py:727
  22.9 0.7 %shard_map.142 = (f32[64,1024]{1,0:T(8,128)S(1)}, f32[64,1024]{1,0:T(8,128)S(1)}, f32[64,128]{1,0:T(8,128)S(1)}) custom-call(f32[64,1024]{1,0:T(8,128)S(1)} %get-tuple-element.119.refs_0_, f32[96,1024]{1,0:T(8,128)S(1)} %get-tuple-element.123.refs_1_, f32[64,1024]{1,0:T(8,128)S(1)} %get-tuple-element.124.refs_2_, f32[16,512]{1,0:T(8,128)S(1)} %get-tuple-element.125.refs_3_, ...), custom_call_target="tpu_custom_call" | custom-call | flops 3000000000 | bytes 1 | tf_op jit(solution)/shard_map/pallas_call | solution.py:727
  23.7 0.4 shard_map.143.refs_9_
  24.1 0.5 collective-permute-start.10
  24.8 0.8 %shard_map.144 = (f32[64,1024]{1,0:T(8,128)S(1)}, f32[64,1024]{1,0:T(8,128)S(1)}, f32[96,1024]{1,0:T(8,128)S(1)}, f32[16,512]{1,0:T(8,128)S(1)}) custom-call(f32[64,1024]{1,0:T(8,128)S(1)} %get-tuple-element.126.refs_0_, f32[16,128]{1,0:T(8,128)S(1)} %collective-permute-done.7.one_ref.refs_1_, f32[16,128]{1,0:T(8,128)S(1)} %collective-permute-done.8.two_ref.refs_2_, ...), custom_call_target="tpu_custom_call" | custom-call | flops 3000000000 | bytes 1 | tf_op jit(solution)/shard_map/pallas_call | solution.py:727
  26.0 1.5 %shard_map.145 = (f32[96,1024]{1,0:T(8,128)S(1)}, f32[64,1024]{1,0:T(8,128)S(1)}, f32[64,256]{1,0:T(8,128)S(1)}) custom-call(f32[64,1024]{1,0:T(8,128)S(1)} %get-tuple-element.130.refs_0_, f32[96,1024]{1,0:T(8,128)S(1)} %get-tuple-element.131.refs_1_, f32[8,1024]{1,0:T(8,128)S(1)} %get-tuple-element.101.refs_2_, s32[8,1024]{1,0:T(8,128)S(1)} %get-tuple-element.102.refs_3_, ...), custom_call_target="tpu_custom_call" | custom-call | flops 3000000000 | bytes 1 | tf_op jit(solution)/shard_map/pallas_call | solution.py:727
  27.5 0.7 %shard_map.146.r_ref.refs_0_ = f32[64,1024]{1,0:T(8,128)S(1)} custom-call(f32[64,1024]{1,0:T(8,128)S(1)} %get-tuple-element.129.refs_0_, f32[96,1024]{1,0:T(8,128)S(1)} %get-tuple-element.133.refs_1_, f32[64,1024]{1,0:T(8,128)S(1)} %get-tuple-element.134.refs_2_, f32[16,512]{1,0:T(8,128)S(1)} %get-tuple-element.135.refs_3_, ...), custom_call_target="tpu_custom_call" | custom-call | flops 3000000000 | bytes 1 | tf_op jit(solution)/shard_map/pallas_call | solution.py:727
  28.5 0.6 %collective-permute-start.13 = (f32[72,128]{1,0:T(8,128)S(1)}, f32[72,128]{1,0:T(8,128)S(1)}, u32[]{:S(2)}, u32[]{:S(2)}) collective-permute-start(f32[72,128]{1,0:T(8,128)S(1)} %shard_map.147.refs_7_), channel_id=1, source_target_pairs={{0,2},{1,8},{2,0},{3,10},{4,6},{5,12},{6,4},{7,14},{8,1},{9,16},{1... | collective-permute-start | bytes 110600 | tf_op jit(solution)/shard_map/ppermute | solution.py:890
  29.1 0.6 shard_map.148
  29.7 1.5 %collective-permute-start.12 = (f32[72,640]{1,0:T(8,128)S(1)}, f32[72,640]{1,0:T(8,128)S(1)}, u32[]{:S(2)}, u32[]{:S(2)}) collective-permute-start(f32[72,640]{1,0:T(8,128)S(1)} %get-tuple-element.139), channel_id=1, source_target_pairs={{0,1},{1,0},{2,3},{3,2},{4,5},{5,4},{6,7},{7,6},{8,9},{9,8},{10,11... | collective-permute-start | bytes 552968 | tf_op jit(solution)/shard_map/ppermute | solution.py:891
  31.4 0.8 %collective-permute-done.12.near_ref = f32[72,640]{1,0:T(8,128)S(1)} collective-permute-done((f32[72,640]{1,0:T(8,128)S(1)}, f32[72,640]{1,0:T(8,128)S(1)}, u32[]{:S(2)}, u32[]{:S(2)}) %collective-permute-start.12) | collective-permute-done | bytes 184352 | tf_op jit(solution)/shard_map/ppermute | solution.py:891
  32.2 1.2 %shard_map.150 = (f32[64,384]{1,0:T(8,128)S(1)}, f32[1,384]{1,0:T(1,128)S(1)}, s32[1,8,256]{2,1,0:T(8,128)S(1)}) custom-call(f32[64,1024]{1,0:T(8,128)S(1)} %get-tuple-element.138.r_ref.refs_0_, f32[72,640]{1,0:T(8,128)S(1)} %collective-permute-done.12.near_ref, s32[4,512]{1,0:T(4,128)S(1)} %get-tuple-element.140.gather_ref, ...), custom_call_target="tpu_custom_call" | custom-call | flops 100000000 | bytes 1 | tf_op jit(solution)/shard_map/pallas_call | solution.py:727
  33.4 2.1 %shard_map.151 = (f32[64,1024]{1,0:T(8,128)S(1)}, f32[16,128]{1,0:T(8,128)S(1)}) custom-call(f32[64,384]{1,0:T(8,128)S(1)} %get-tuple-element.142.right_ref, f32[1,384]{1,0:T(1,128)S(1)} %get-tuple-element.143.scale_ref, s32[1,8,256]{2,1,0:T(8,128)S(1)} %get-tuple-element.144.front_ref, f32[64,1024]{1,0:T(8,128)S(1)} %get-tuple-element.138.r_ref.refs_0_, ...), custom_call_target="tpu_custom_call" | custom-call | flops 3000000000 | bytes 1 | tf_op jit(solution)/shard_map/pallas_call | solution.py:727
  35.5 1.3 %collective-permute-start.15 = (f32[16,128]{1,0:T(8,128)S(1)}, f32[16,128]{1,0:T(8,128)S(1)}, u32[]{:S(2)}, u32[]{:S(2)}) collective-permute-start(f32[16,128]{1,0:T(8,128)S(1)} %get-tuple-element.149._), channel_id=1, source_target_pairs={{0,8},{1,9},{2,10},{3,11},{4,12},{5,13},{6,14},{7,15},{8,0},{9,1},... | collective-permute-start | bytes 24584 | tf_op jit(solution)/shard_map/ppermute | solution.py:797
  36.9 0.4 shard_map.152
  37.3 0.5 collective-permute-start.14
  37.8 1.5 %shard_map.153 = (f32[96,1024]{1,0:T(8,128)S(1)}, f32[64,1024]{1,0:T(8,128)S(1)}, f32[64,256]{1,0:T(8,128)S(1)}) custom-call(f32[64,1024]{1,0:T(8,128)S(1)} %get-tuple-element.148.p_ref.refs_0_, f32[96,1024]{1,0:T(8,128)S(1)} %get-tuple-element.150.refs_1_, f32[8,1024]{1,0:T(8,128)S(1)} %get-tuple-element.101.refs_2_, ...), custom_call_target="tpu_custom_call" | custom-call | flops 3000000000 | bytes 1 | tf_op jit(solution)/shard_map/pallas_call | solution.py:727
  39.3 0.7 %shard_map.154 = (f32[64,1024]{1,0:T(8,128)S(1)}, f32[64,1024]{1,0:T(8,128)S(1)}, f32[64,128]{1,0:T(8,128)S(1)}) custom-call(f32[64,1024]{1,0:T(8,128)S(1)} %get-tuple-element.138.r_ref.refs_0_, f32[96,1024]{1,0:T(8,128)S(1)} %get-tuple-element.152.refs_1_, f32[64,1024]{1,0:T(8,128)S(1)} %get-tuple-element.153.refs_2_, ...), custom_call_target="tpu_custom_call" | custom-call | flops 3000000000 | bytes 1 | tf_op jit(solution)/shard_map/pallas_call | solution.py:727
  40.0 0.4 shard_map.155.refs_9_
  40.4 1.9 %collective-permute-start.18 = (f32[16,128]{1,0:T(8,128)S(1)}, f32[16,128]{1,0:T(8,128)S(1)}, u32[]{:S(2)}, u32[]{:S(2)}) collective-permute-start(f32[16,128]{1,0:T(8,128)S(1)} %shard_map.155.refs_9_), channel_id=1, source_target_pairs={{0,8},{1,9},{2,10},{3,11},{4,12},{5,13},{6,14},{7,15},{8,0},{9,1},... | collective-permute-start | bytes 24584 | tf_op jit(solution)/shard_map/ppermute | solution.py:797
  42.6 0.8 %shard_map.156 = (f32[64,1024]{1,0:T(8,128)S(1)}, f32[64,1024]{1,0:T(8,128)S(1)}, f32[96,1024]{1,0:T(8,128)S(1)}, f32[16,512]{1,0:T(8,128)S(1)}) custom-call(f32[64,1024]{1,0:T(8,128)S(1)} %get-tuple-element.155.refs_0_, f32[16,128]{1,0:T(8,128)S(1)} %collective-permute-done.15.one_ref.refs_1_, f32[16,128]{1,0:T(8,128)S(1)} %collective-permute-done.16.two_ref.refs_2_, ...), custom_call_target="tpu_custom_call" | custom-call | flops 3000000000 | bytes 1 | tf_op jit(solution)/shard_map/pallas_call | solution.py:727
  43.8 1.5 %shard_map.157 = (f32[96,1024]{1,0:T(8,128)S(1)}, f32[64,1024]{1,0:T(8,128)S(1)}, f32[64,256]{1,0:T(8,128)S(1)}) custom-call(f32[64,1024]{1,0:T(8,128)S(1)} %get-tuple-element.159.refs_0_.refs_7_, f32[96,1024]{1,0:T(8,128)S(1)} %get-tuple-element.160.refs_1_, f32[8,1024]{1,0:T(8,128)S(1)} %get-tuple-element.101.refs_2_, ...), custom_call_target="tpu_custom_call" | custom-call | flops 3000000000 | bytes 1 | tf_op jit(solution)/shard_map/pallas_call | solution.py:727
  45.2 0.7 %shard_map.158 = (f32[64,1024]{1,0:T(8,128)S(1)}, f32[64,1024]{1,0:T(8,128)S(1)}, f32[64,128]{1,0:T(8,128)S(1)}) custom-call(f32[64,1024]{1,0:T(8,128)S(1)} %get-tuple-element.158.refs_0_, f32[96,1024]{1,0:T(8,128)S(1)} %get-tuple-element.162.refs_1_, f32[64,1024]{1,0:T(8,128)S(1)} %get-tuple-element.163.refs_2_, f32[16,512]{1,0:T(8,128)S(1)} %get-tuple-element.164.refs_3_, ...), custom_call_target="tpu_custom_call" | custom-call | flops 3000000000 | bytes 1 | tf_op jit(solution)/shard_map/pallas_call | solution.py:727
  46.0 0.4 shard_map.159.refs_9_
  46.4 0.9 %collective-permute-start.21 = (f32[16,128]{1,0:T(8,128)S(1)}, f32[16,128]{1,0:T(8,128)S(1)}, u32[]{:S(2)}, u32[]{:S(2)}) collective-permute-start(f32[16,128]{1,0:T(8,128)S(1)} %shard_map.159.refs_9_), channel_id=1, source_target_pairs={{0,8},{1,9},{2,10},{3,11},{4,12},{5,13},{6,14},{7,15},{8,0},{9,1},... | collective-permute-start | bytes 24584 | tf_op jit(solution)/shard_map/ppermute | solution.py:797
  47.5 0.8 %shard_map.160 = (f32[64,1024]{1,0:T(8,128)S(1)}, f32[64,1024]{1,0:T(8,128)S(1)}, f32[96,1024]{1,0:T(8,128)S(1)}, f32[16,512]{1,0:T(8,128)S(1)}) custom-call(f32[64,1024]{1,0:T(8,128)S(1)} %get-tuple-element.165.refs_0_, f32[16,128]{1,0:T(8,128)S(1)} %collective-permute-done.18.one_ref.refs_1_, f32[16,128]{1,0:T(8,128)S(1)} %collective-permute-done.19.two_ref.refs_2_, ...), custom_call_target="tpu_custom_call" | custom-call | flops 3000000000 | bytes 1 | tf_op jit(solution)/shard_map/pallas_call | solution.py:727
  48.7 1.5 %shard_map.161 = (f32[96,1024]{1,0:T(8,128)S(1)}, f32[64,1024]{1,0:T(8,128)S(1)}, f32[64,256]{1,0:T(8,128)S(1)}) custom-call(f32[64,1024]{1,0:T(8,128)S(1)} %get-tuple-element.169.refs_0_.refs_7_, f32[96,1024]{1,0:T(8,128)S(1)} %get-tuple-element.170.refs_1_, f32[8,1024]{1,0:T(8,128)S(1)} %get-tuple-element.101.refs_2_, ...), custom_call_target="tpu_custom_call" | custom-call | flops 3000000000 | bytes 1 | tf_op jit(solution)/shard_map/pallas_call | solution.py:727
  50.1 0.7 %shard_map.162 = (f32[64,1024]{1,0:T(8,128)S(1)}, f32[64,1024]{1,0:T(8,128)S(1)}, f32[64,128]{1,0:T(8,128)S(1)}) custom-call(f32[64,1024]{1,0:T(8,128)S(1)} %get-tuple-element.168.refs_0_, f32[96,1024]{1,0:T(8,128)S(1)} %get-tuple-element.172.refs_1_, f32[64,1024]{1,0:T(8,128)S(1)} %get-tuple-element.173.refs_2_, f32[16,512]{1,0:T(8,128)S(1)} %get-tuple-element.174.refs_3_, ...), custom_call_target="tpu_custom_call" | custom-call | flops 3000000000 | bytes 1 | tf_op jit(solution)/shard_map/pallas_call | solution.py:727
  50.9 0.4 shard_map.163.refs_9_
  51.3 1.8 %collective-permute-start.24 = (f32[16,128]{1,0:T(8,128)S(1)}, f32[16,128]{1,0:T(8,128)S(1)}, u32[]{:S(2)}, u32[]{:S(2)}) collective-permute-start(f32[16,128]{1,0:T(8,128)S(1)} %shard_map.163.refs_9_), channel_id=1, source_target_pairs={{0,8},{1,9},{2,10},{3,11},{4,12},{5,13},{6,14},{7,15},{8,0},{9,1},... | collective-permute-start | bytes 24584 | tf_op jit(solution)/shard_map/ppermute | solution.py:797
  53.3 0.8 %shard_map.164 = (f32[64,1024]{1,0:T(8,128)S(1)}, f32[64,1024]{1,0:T(8,128)S(1)}, f32[96,1024]{1,0:T(8,128)S(1)}, f32[16,512]{1,0:T(8,128)S(1)}) custom-call(f32[64,1024]{1,0:T(8,128)S(1)} %get-tuple-element.175.refs_0_, f32[16,128]{1,0:T(8,128)S(1)} %collective-permute-done.21.one_ref.refs_1_, f32[16,128]{1,0:T(8,128)S(1)} %collective-permute-done.22.two_ref.refs_2_, ...), custom_call_target="tpu_custom_call" | custom-call | flops 3000000000 | bytes 1 | tf_op jit(solution)/shard_map/pallas_call | solution.py:727
  54.5 1.0 %shard_map.165 = (f32[96,256]{1,0:T(8,128)S(1)}, f32[64,256]{1,0:T(8,128)S(1)}, f32[64,256]{1,0:T(8,128)}) custom-call(f32[64,1024]{1,0:T(8,128)S(1)} %get-tuple-element.178.refs_0_, f32[96,1024]{1,0:T(8,128)S(1)} %get-tuple-element.179.refs_1_, f32[8,1024]{1,0:T(8,128)S(1)} %get-tuple-element.101.refs_2_, s32[8,1024]{1,0:T(8,128)S(1)} %get-tuple-element.102.refs_3_, ...), custom_call_target="tpu_custom_call" | custom-call | flops 3000000000 | bytes 1 | tf_op jit(solution)/shard_map/pallas_call | solution.py:727
  55.9 0.9 %shard_map.167 = f32[64,256]{1,0:T(8,128)} custom-call(f32[64,256]{1,0:T(8,128)S(1)} %shard_map.166.refs_0_, f32[16,128]{1,0:T(8,128)S(1)} %collective-permute-done.24.refs_1_, f32[16,128]{1,0:T(8,128)S(1)} %collective-permute-done.25.refs_2_, s32[8,1024]{1,0:T(8,128)S(1)} %get-tuple-element.113.edge_ref.refs_3_, ...), custom_call_target="tpu_custom_call" | custom-call | flops 3000000000 | bytes 1 | tf_op jit(solution)/shard_map/pallas_call | solution.py:727
  (49 shorter events, 4.6 us)
Async XLA Ops:
  0.6 5.5 %copy-start.1 = (f32[2,64,64]{2,1,0:T(8,128)S(1)}, f32[2,64,64]{2,1,0:T(8,128)}, u32[]{:S(2)}) copy-start(f32[2,64,64]{2,1,0:T(8,128)} %refs_4_.1) | copy-start | bytes 98308
  0.6 5.5 %copy-start.2 = (f32[96,64]{0,1:T(8,128)S(1)}, f32[96,64]{0,1:T(8,128)}, u32[]{:S(2)}) copy-start(f32[96,64]{0,1:T(8,128)} %param.16) | copy-start | bytes 73732
  1.6 5.9 %collective-permute-start = (f32[80,256]{1,0:T(8,128)S(1)}, f32[80,256]{1,0:T(8,128)S(1)}, u32[]{:S(2)}, u32[]{:S(2)}) collective-permute-start(f32[80,256]{1,0:T(8,128)S(1)} %shard_map.131.refs_0_), channel_id=1, source_target_pairs={{0,2},{1,3},{2,0},{3,1},{4,6},{5,7},{6,4},{7,5},{8,10},{9,11},{10,... | collective-permute-start | bytes 245768 | tf_op jit(solution)/shard_map/ppermute | solution.py:824
  4.6 5.3 %collective-permute-start.1 = (f32[80,256]{1,0:T(8,128)S(1)}, f32[80,256]{1,0:T(8,128)S(1)}, u32[]{:S(2)}, u32[]{:S(2)}) collective-permute-start(f32[80,256]{1,0:T(8,128)S(1)} %shard_map.131.refs_0_), channel_id=1, source_target_pairs={{0,4},{1,5},{2,6},{3,7},{4,0},{5,1},{6,2},{7,3},{8,12},{9,13},{10,... | collective-permute-start | bytes 245768 | tf_op jit(solution)/shard_map/ppermute | solution.py:824
  6.1 5.3 %collective-permute-start.2 = (f32[80,256]{1,0:T(8,128)S(1)}, f32[80,256]{1,0:T(8,128)S(1)}, u32[]{:S(2)}, u32[]{:S(2)}) collective-permute-start(f32[80,256]{1,0:T(8,128)S(1)} %shard_map.131.refs_0_), channel_id=1, source_target_pairs={{0,6},{1,7},{2,4},{3,5},{4,2},{5,3},{6,0},{7,1},{8,14},{9,15},{10,... | collective-permute-start | bytes 245768 | tf_op jit(solution)/shard_map/ppermute | solution.py:824
  6.2 1.0 %copy-start = (f32[8,64,64]{2,1,0:T(8,128)S(1)}, f32[8,64,64]{2,1,0:T(8,128)}, u32[]{:S(2)}) copy-start(f32[8,64,64]{2,1,0:T(8,128)} %restriction_ref.1) | copy-start | bytes 393220
  6.2 1.0 %copy-start.3 = (f32[64,64]{1,0:T(8,128)S(1)}, f32[64,64]{1,0:T(8,128)}, u32[]{:S(2)}) copy-start(f32[64,64]{1,0:T(8,128)} %stiff_ref.5) | copy-start | bytes 49156
  12.0 4.9 %collective-permute-start.4 = (f32[16,128]{1,0:T(8,128)S(1)}, f32[16,128]{1,0:T(8,128)S(1)}, u32[]{:S(2)}, u32[]{:S(2)}) collective-permute-start(f32[16,128]{1,0:T(8,128)S(1)} %get-tuple-element.99._), channel_id=1, source_target_pairs={{0,8},{1,9},{2,10},{3,11},{4,12},{5,13},{6,14},{7,15},{8,0},{9,1},... | collective-permute-start | bytes 24584 | tf_op jit(solution)/shard_map/ppermute | solution.py:797
  13.6 3.3 %collective-permute-start.5 = (f32[16,128]{1,0:T(8,128)S(1)}, f32[16,128]{1,0:T(8,128)S(1)}, u32[]{:S(2)}, u32[]{:S(2)}) collective-permute-start(f32[16,128]{1,0:T(8,128)S(1)} %get-tuple-element.99._), channel_id=1, source_target_pairs={{0,1},{1,0},{2,3},{3,2},{4,5},{5,4},{6,7},{7,6},{8,16},{9,17},{10,... | collective-permute-start | bytes 24584 | tf_op jit(solution)/shard_map/ppermute | solution.py:797
  14.0 2.2 %collective-permute-start.3 = (f32[16,512]{1,0:T(8,128)S(1)}, f32[16,512]{1,0:T(8,128)S(1)}, u32[]{:S(2)}, u32[]{:S(2)}) collective-permute-start(f32[16,512]{1,0:T(8,128)S(1)} %get-tuple-element.107.refs_3_), channel_id=1, source_target_pairs={{0,1},{1,0},{2,3},{3,2},{4,5},{5,4},{6,7},{7,6},{8,9},{9,8},{10,11... | collective-permute-start | bytes 98312 | tf_op jit(solution)/shard_map/ppermute | solution.py:849
  17.3 6.3 %collective-permute-start.7 = (f32[16,128]{1,0:T(8,128)S(1)}, f32[16,128]{1,0:T(8,128)S(1)}, u32[]{:S(2)}, u32[]{:S(2)}) collective-permute-start(f32[16,128]{1,0:T(8,128)S(1)} %shard_map.139.refs_9_), channel_id=1, source_target_pairs={{0,8},{1,9},{2,10},{3,11},{4,12},{5,13},{6,14},{7,15},{8,0},{9,1},... | collective-permute-start | bytes 24584 | tf_op jit(solution)/shard_map/ppermute | solution.py:797
  20.1 3.6 %collective-permute-start.8 = (f32[16,128]{1,0:T(8,128)S(1)}, f32[16,128]{1,0:T(8,128)S(1)}, u32[]{:S(2)}, u32[]{:S(2)}) collective-permute-start(f32[16,128]{1,0:T(8,128)S(1)} %shard_map.139.refs_9_), channel_id=1, source_target_pairs={{0,1},{1,0},{2,3},{3,2},{4,5},{5,4},{6,7},{7,6},{8,16},{9,17},{10,... | collective-permute-start | bytes 24584 | tf_op jit(solution)/shard_map/ppermute | solution.py:797
  21.1 1.8 %collective-permute-start.6 = (f32[16,512]{1,0:T(8,128)S(1)}, f32[16,512]{1,0:T(8,128)S(1)}, u32[]{:S(2)}, u32[]{:S(2)}) collective-permute-start(f32[16,512]{1,0:T(8,128)S(1)} %get-tuple-element.125.refs_3_), channel_id=1, source_target_pairs={{0,1},{1,0},{2,3},{3,2},{4,5},{5,4},{6,7},{7,6},{8,9},{9,8},{10,11... | collective-permute-start | bytes 98312 | tf_op jit(solution)/shard_map/ppermute | solution.py:849
  24.1 4.1 %collective-permute-start.10 = (f32[16,128]{1,0:T(8,128)S(1)}, f32[16,128]{1,0:T(8,128)S(1)}, u32[]{:S(2)}, u32[]{:S(2)}) collective-permute-start(f32[16,128]{1,0:T(8,128)S(1)} %shard_map.143.refs_9_), channel_id=1, source_target_pairs={{0,8},{1,9},{2,10},{3,11},{4,12},{5,13},{6,14},{7,15},{8,0},{9,1},... | collective-permute-start | bytes 24584 | tf_op jit(solution)/shard_map/ppermute | solution.py:797
  24.6 3.6 %collective-permute-start.11 = (f32[16,128]{1,0:T(8,128)S(1)}, f32[16,128]{1,0:T(8,128)S(1)}, u32[]{:S(2)}, u32[]{:S(2)}) collective-permute-start(f32[16,128]{1,0:T(8,128)S(1)} %shard_map.143.refs_9_), channel_id=1, source_target_pairs={{0,1},{1,0},{2,3},{3,2},{4,5},{5,4},{6,7},{7,6},{8,16},{9,17},{10,... | collective-permute-start | bytes 24584 | tf_op jit(solution)/shard_map/ppermute | solution.py:797
  25.7 1.8 %collective-permute-start.9 = (f32[16,512]{1,0:T(8,128)S(1)}, f32[16,512]{1,0:T(8,128)S(1)}, u32[]{:S(2)}, u32[]{:S(2)}) collective-permute-start(f32[16,512]{1,0:T(8,128)S(1)} %get-tuple-element.135.refs_3_), channel_id=1, source_target_pairs={{0,1},{1,0},{2,3},{3,2},{4,5},{5,4},{6,7},{7,6},{8,9},{9,8},{10,11... | collective-permute-start | bytes 98312 | tf_op jit(solution)/shard_map/ppermute | solution.py:849
  28.5 4.9 %collective-permute-start.13 = (f32[72,128]{1,0:T(8,128)S(1)}, f32[72,128]{1,0:T(8,128)S(1)}, u32[]{:S(2)}, u32[]{:S(2)}) collective-permute-start(f32[72,128]{1,0:T(8,128)S(1)} %shard_map.147.refs_7_), channel_id=1, source_target_pairs={{0,2},{1,8},{2,0},{3,10},{4,6},{5,12},{6,4},{7,14},{8,1},{9,16},{1... | collective-permute-start | bytes 110600 | tf_op jit(solution)/shard_map/ppermute | solution.py:890
  29.7 2.6 %collective-permute-start.12 = (f32[72,640]{1,0:T(8,128)S(1)}, f32[72,640]{1,0:T(8,128)S(1)}, u32[]{:S(2)}, u32[]{:S(2)}) collective-permute-start(f32[72,640]{1,0:T(8,128)S(1)} %get-tuple-element.139), channel_id=1, source_target_pairs={{0,1},{1,0},{2,3},{3,2},{4,5},{5,4},{6,7},{7,6},{8,9},{9,8},{10,11... | collective-permute-start | bytes 552968 | tf_op jit(solution)/shard_map/ppermute | solution.py:891
  35.5 4.5 %collective-permute-start.15 = (f32[16,128]{1,0:T(8,128)S(1)}, f32[16,128]{1,0:T(8,128)S(1)}, u32[]{:S(2)}, u32[]{:S(2)}) collective-permute-start(f32[16,128]{1,0:T(8,128)S(1)} %get-tuple-element.149._), channel_id=1, source_target_pairs={{0,8},{1,9},{2,10},{3,11},{4,12},{5,13},{6,14},{7,15},{8,0},{9,1},... | collective-permute-start | bytes 24584 | tf_op jit(solution)/shard_map/ppermute | solution.py:797
  36.8 3.2 %collective-permute-start.16 = (f32[16,128]{1,0:T(8,128)S(1)}, f32[16,128]{1,0:T(8,128)S(1)}, u32[]{:S(2)}, u32[]{:S(2)}) collective-permute-start(f32[16,128]{1,0:T(8,128)S(1)} %get-tuple-element.149._), channel_id=1, source_target_pairs={{0,1},{1,0},{2,3},{3,2},{4,5},{5,4},{6,7},{7,6},{8,16},{9,17},{10,... | collective-permute-start | bytes 24584 | tf_op jit(solution)/shard_map/ppermute | solution.py:797
  37.3 2.0 %collective-permute-start.14 = (f32[16,512]{1,0:T(8,128)S(1)}, f32[16,512]{1,0:T(8,128)S(1)}, u32[]{:S(2)}, u32[]{:S(2)}) collective-permute-start(f32[16,512]{1,0:T(8,128)S(1)} %get-tuple-element.154.refs_3_), channel_id=1, source_target_pairs={{0,1},{1,0},{2,3},{3,2},{4,5},{5,4},{6,7},{7,6},{8,9},{9,8},{10,11... | collective-permute-start | bytes 98312 | tf_op jit(solution)/shard_map/ppermute | solution.py:849
  40.4 5.5 %collective-permute-start.18 = (f32[16,128]{1,0:T(8,128)S(1)}, f32[16,128]{1,0:T(8,128)S(1)}, u32[]{:S(2)}, u32[]{:S(2)}) collective-permute-start(f32[16,128]{1,0:T(8,128)S(1)} %shard_map.155.refs_9_), channel_id=1, source_target_pairs={{0,8},{1,9},{2,10},{3,11},{4,12},{5,13},{6,14},{7,15},{8,0},{9,1},... | collective-permute-start | bytes 24584 | tf_op jit(solution)/shard_map/ppermute | solution.py:797
  42.4 3.6 %collective-permute-start.19 = (f32[16,128]{1,0:T(8,128)S(1)}, f32[16,128]{1,0:T(8,128)S(1)}, u32[]{:S(2)}, u32[]{:S(2)}) collective-permute-start(f32[16,128]{1,0:T(8,128)S(1)} %shard_map.155.refs_9_), channel_id=1, source_target_pairs={{0,1},{1,0},{2,3},{3,2},{4,5},{5,4},{6,7},{7,6},{8,16},{9,17},{10,... | collective-permute-start | bytes 24584 | tf_op jit(solution)/shard_map/ppermute | solution.py:797
  43.4 1.8 %collective-permute-start.17 = (f32[16,512]{1,0:T(8,128)S(1)}, f32[16,512]{1,0:T(8,128)S(1)}, u32[]{:S(2)}, u32[]{:S(2)}) collective-permute-start(f32[16,512]{1,0:T(8,128)S(1)} %get-tuple-element.164.refs_3_), channel_id=1, source_target_pairs={{0,1},{1,0},{2,3},{3,2},{4,5},{5,4},{6,7},{7,6},{8,9},{9,8},{10,11... | collective-permute-start | bytes 98312 | tf_op jit(solution)/shard_map/ppermute | solution.py:849
  46.4 4.5 %collective-permute-start.21 = (f32[16,128]{1,0:T(8,128)S(1)}, f32[16,128]{1,0:T(8,128)S(1)}, u32[]{:S(2)}, u32[]{:S(2)}) collective-permute-start(f32[16,128]{1,0:T(8,128)S(1)} %shard_map.159.refs_9_), channel_id=1, source_target_pairs={{0,8},{1,9},{2,10},{3,11},{4,12},{5,13},{6,14},{7,15},{8,0},{9,1},... | collective-permute-start | bytes 24584 | tf_op jit(solution)/shard_map/ppermute | solution.py:797
  47.3 3.6 %collective-permute-start.22 = (f32[16,128]{1,0:T(8,128)S(1)}, f32[16,128]{1,0:T(8,128)S(1)}, u32[]{:S(2)}, u32[]{:S(2)}) collective-permute-start(f32[16,128]{1,0:T(8,128)S(1)} %shard_map.159.refs_9_), channel_id=1, source_target_pairs={{0,1},{1,0},{2,3},{3,2},{4,5},{5,4},{6,7},{7,6},{8,16},{9,17},{10,... | collective-permute-start | bytes 24584 | tf_op jit(solution)/shard_map/ppermute | solution.py:797
  48.3 1.8 %collective-permute-start.20 = (f32[16,512]{1,0:T(8,128)S(1)}, f32[16,512]{1,0:T(8,128)S(1)}, u32[]{:S(2)}, u32[]{:S(2)}) collective-permute-start(f32[16,512]{1,0:T(8,128)S(1)} %get-tuple-element.174.refs_3_), channel_id=1, source_target_pairs={{0,1},{1,0},{2,3},{3,2},{4,5},{5,4},{6,7},{7,6},{8,9},{9,8},{10,11... | collective-permute-start | bytes 98312 | tf_op jit(solution)/shard_map/ppermute | solution.py:849
  51.3 4.5 %collective-permute-start.24 = (f32[16,128]{1,0:T(8,128)S(1)}, f32[16,128]{1,0:T(8,128)S(1)}, u32[]{:S(2)}, u32[]{:S(2)}) collective-permute-start(f32[16,128]{1,0:T(8,128)S(1)} %shard_map.163.refs_9_), channel_id=1, source_target_pairs={{0,8},{1,9},{2,10},{3,11},{4,12},{5,13},{6,14},{7,15},{8,0},{9,1},... | collective-permute-start | bytes 24584 | tf_op jit(solution)/shard_map/ppermute | solution.py:797
  53.1 2.8 %collective-permute-start.25 = (f32[16,128]{1,0:T(8,128)S(1)}, f32[16,128]{1,0:T(8,128)S(1)}, u32[]{:S(2)}, u32[]{:S(2)}) collective-permute-start(f32[16,128]{1,0:T(8,128)S(1)} %shard_map.163.refs_9_), channel_id=1, source_target_pairs={{0,1},{1,0},{2,3},{3,2},{4,5},{5,4},{6,7},{7,6},{8,16},{9,17},{10,... | collective-permute-start | bytes 24584 | tf_op jit(solution)/shard_map/ppermute | solution.py:797
  54.1 1.4 %collective-permute-start.23 = (f32[16,512]{1,0:T(8,128)S(1)}, f32[16,512]{1,0:T(8,128)S(1)}, u32[]{:S(2)}, u32[]{:S(2)}) collective-permute-start(f32[16,512]{1,0:T(8,128)S(1)} %get-tuple-element.185.refs_3_), channel_id=1, source_target_pairs={{0,1},{1,0},{2,3},{3,2},{4,5},{5,4},{6,7},{7,6},{8,9},{9,8},{10,11... | collective-permute-start | bytes 98312 | tf_op jit(solution)/shard_map/ppermute | solution.py:849

commit v7 on v6

--- a/solution.py
+++ b/solution.py
@@ -44,6 +44,13 @@
     return jnp.dot(left, right, preferred_element_type=jnp.float32)
 
 
+def face_product(left, x):
+    high, low = halves(x)
+    both = jnp.dot(left, jnp.concatenate([high, low], axis=0), preferred_element_type=jnp.float32)
+    modes = both.shape[0] // 2
+    return both[:modes] + both[modes:]
+
+
 def store_left(out, rows, x, base=0):
     high, low = halves(x)
     width = x.shape[1]
@@ -133,7 +140,11 @@
 def prep_kernel(map_ref, stiff_ref, t_out, tt_out, k_out):
     modes, rows = map_ref.shape
     transposed = map_ref[...]
-    store_left(tt_out, slice(0, modes), transposed)
+    high, low = halves(PENALTY * transposed)
+    tt_out[:modes, :rows] = high
+    tt_out[:modes, rows:] = high
+    tt_out[modes:, :rows] = low
+    tt_out[modes:, rows:] = jnp.zeros((modes, rows), jnp.bfloat16)
     store_left(t_out, slice(0, rows), transposed.T)
     for k in range(2):
         store_left(k_out, slice(k * modes, (k + 1) * modes), stiff_ref[k])
@@ -316,8 +327,8 @@
             column = far[f : f + 1, i * count + h : i * count + h + LANES]
             return pick(tiles[i], jnp.right_shift(column, 7), jnp.bitwise_and(column, LANES - 1))
 
-        jump = product(tt_ref[...], jump_ref[:, here] - faces(tile, range(len(js)), count))
-        residual = r_ref[:, span] - own_ref[:, here] - PENALTY * jump
+        jump = face_product(tt_ref[...], jump_ref[:, here] - faces(tile, range(len(js)), count))
+        residual = r_ref[:, span] - own_ref[:, here] - jump
         r_out[:, here] = residual
         if kind in ("frame", "last"):
             return
@@ -372,8 +383,8 @@
         spot = slice(t * LANES, (t + 1) * LANES)
         rim = rim_tile(one_ref, two_ref, spot, rims)
         edge = edges_ref[:, spot]
-        added = product(tt_ref[...], faces(lambda _, f, h: rim_seen(rim, edge, f, h), [0], LANES))
-        p = p_ref[:, spot] + (rate * PENALTY) * (igs_ref[:, spot] * added)
+        added = face_product(tt_ref[...], faces(lambda _, f, h: rim_seen(rim, edge, f, h), [0], LANES))
+        p = p_ref[:, spot] + rate * (igs_ref[:, spot] * added)
         rims_out[:, spot] = rim_traces(t_ref, p, face_ref[:, spot])
 
 
@@ -393,7 +404,7 @@
     seen = faces(lambda _, f, h: rim_seen(rim, edge, f, h), [0], LANES)
     residual = jnp.where(core == 0, r_ref[:, first_tile], r_ref[:, last_tile])
     cross_out[modes:, :] = jnp.zeros((cross_out.shape[0] - modes, LANES), jnp.float32)
-    cross_out[:modes, :] = residual + PENALTY * product(tt_ref[...], seen)
+    cross_out[:modes, :] = residual + face_product(tt_ref[...], seen)
     cross_out[modes : modes + 1, :] = size_ref[last : last + 1, :].astype(jnp.float32)
     cross_out[modes + 1 : modes + 2, :] = cond_ref[last : last + 1, :]
 
@@ -421,7 +432,7 @@
         def tile(i, f, h):
             return rim_seen(rim[i], edge, f, i * count + h)
 
-        added = PENALTY * product(tt_ref[...], faces(tile, range(len(js)), count))
+        added = face_product(tt_ref[...], faces(tile, range(len(js)), count))
         residual = r_ref[:, here] + added
         r_out[:, here] = residual
         if kind == "frame":
@@ -799,7 +810,7 @@
     map_t = trace_map.T
     t3, tt3, k3 = run(
         prep_kernel,
-        [((rows, 3 * modes), bf16), ((modes, 3 * rows), bf16), ((2 * modes, 3 * modes), bf16)],
+        [((rows, 3 * modes), bf16), ((2 * modes, 2 * rows), bf16), ((2 * modes, 3 * modes), bf16)],
         map_t, stiffness,
     )
     down3, up3, c3 = run(

time: 57 us -> 56.8 us (level)
  no operation moved by 1% of the time
where the time goes in v7:
time: 56.8 us; the launch traced here: 56.6 us
  Pallas kernels  28.7 us (51%)
  starting transfers between devices  21.3 us (38%)
  waiting for transfers between devices  4.86 us (9%)
  between operations  1.01 us (2%)
  local copies, waits for them, and re-layouts  0.79 us (1%)
    pallas_call x37, Pallas kernels, call(): pl.pallas_call(kernel, out_shape=[jax.ShapeDtypeStruct(shape, kind) for s...  28.7 us
    ppermute x14, starting transfers between devices, over_segments(): return (lax.ppermute(rim, both, ones), lax.ppermute(rim, both, twos))  11.7 us
    ppermute x3, starting transfers between devices, local(): lax.ppermute(packed, 'sub', [(s, s ^ CORES * k) for s in range(peers)])  4.54 us
    ppermute x3, waiting for transfers between devices, local(): lax.ppermute(packed, 'sub', [(s, s ^ CORES * k) for s in range(peers)])  3.99 us
    ppermute x7, starting transfers between devices, apply(): swapped = lax.ppermute(sub_out, 'sub', cores)  2.89 us
    ppermute x1, starting transfers between devices, local(): near = lax.ppermute(near, 'sub', cores)  1.54 us
  transfers between devices with their start and end apart: 26, of which 3 were waited for; matrix products, arithmetic and copies ran while one was open for 0% of the time, Pallas kernels for 39%

profile of v7, /device:TPU:0, one launch (start us, length us, event | category | flops | bytes accessed | tf_op | source)
XLA Modules:
  0.0 56.6 jit_solution(1789126475843479973)
XLA Ops:
  0.7 1.0 %shard_map.131.refs_0_ = f32[80,256]{1,0:T(8,128)S(1)} custom-call(f32[64,256]{1,0:T(8,128)} %b_ref.1, f32[1,256]{1,0:T(1,128)} %bitcast.6, s32[1,256]{1,0:T(1,128)} %bitcast.7, s32[6,256]{1,0:T(8,128)} %face_ref.1, s32[1,128]{1,0:T(1,128)} %sub_ref.1, s32[1,16]{1,0:T(1,128)} %rim_ref.1, s32[1,64]{1,0:T(1,128)} %size_ref.1, f32[1,64]{1,0:T(1,128)} %bitcast.8), custom_call_target="tpu_custom_call" | custom-call | flops 3000000000 | bytes 1 | tf_op jit(solution)/shard_map/pallas_call | solution.py:738
  1.6 3.0 %collective-permute-start = (f32[80,256]{1,0:T(8,128)S(1)}, f32[80,256]{1,0:T(8,128)S(1)}, u32[]{:S(2)}, u32[]{:S(2)}) collective-permute-start(f32[80,256]{1,0:T(8,128)S(1)} %shard_map.131.refs_0_), channel_id=1, source_target_pairs={{0,2},{1,3},{2,0},{3,1},{4,6},{5,7},{6,4},{7,5},{8,10},{9,11},{10,... | collective-permute-start | bytes 245768 | tf_op jit(solution)/shard_map/ppermute | solution.py:835
  4.6 1.5 %collective-permute-start.1 = (f32[80,256]{1,0:T(8,128)S(1)}, f32[80,256]{1,0:T(8,128)S(1)}, u32[]{:S(2)}, u32[]{:S(2)}) collective-permute-start(f32[80,256]{1,0:T(8,128)S(1)} %shard_map.131.refs_0_), channel_id=1, source_target_pairs={{0,4},{1,5},{2,6},{3,7},{4,0},{5,1},{6,2},{7,3},{8,12},{9,13},{10,... | collective-permute-start | bytes 245768 | tf_op jit(solution)/shard_map/ppermute | solution.py:835
  6.3 0.8 %copy-done = f32[8,64,64]{2,1,0:T(8,128)S(1)} copy-done((f32[8,64,64]{2,1,0:T(8,128)S(1)}, f32[8,64,64]{2,1,0:T(8,128)}, u32[]{:S(2)}) %copy-start) | copy-done | bytes 131096
  7.5 2.4 %collective-permute-done.1.refs_2_ = f32[80,256]{1,0:T(8,128)S(1)} collective-permute-done((f32[80,256]{1,0:T(8,128)S(1)}, f32[80,256]{1,0:T(8,128)S(1)}, u32[]{:S(2)}, u32[]{:S(2)}) %collective-permute-start.1) | collective-permute-done | bytes 81952 | tf_op jit(solution)/shard_map/ppermute | solution.py:835
  9.9 1.5 %collective-permute-done.2.refs_3_ = f32[80,256]{1,0:T(8,128)S(1)} collective-permute-done((f32[80,256]{1,0:T(8,128)S(1)}, f32[80,256]{1,0:T(8,128)S(1)}, u32[]{:S(2)}, u32[]{:S(2)}) %collective-permute-start.2) | collective-permute-done | bytes 81952 | tf_op jit(solution)/shard_map/ppermute | solution.py:835
  11.5 0.5 shard_map.134
  12.0 1.6 %collective-permute-start.4 = (f32[16,128]{1,0:T(8,128)S(1)}, f32[16,128]{1,0:T(8,128)S(1)}, u32[]{:S(2)}, u32[]{:S(2)}) collective-permute-start(f32[16,128]{1,0:T(8,128)S(1)} %get-tuple-element.99._), channel_id=1, source_target_pairs={{0,8},{1,9},{2,10},{3,11},{4,12},{5,13},{6,14},{7,15},{8,0},{9,1},... | collective-permute-start | bytes 24584 | tf_op jit(solution)/shard_map/ppermute | solution.py:808
  13.6 0.4 shard_map.135
  14.0 0.6 %collective-permute-start.3 = (f32[16,512]{1,0:T(8,128)S(1)}, f32[16,512]{1,0:T(8,128)S(1)}, u32[]{:S(2)}, u32[]{:S(2)}) collective-permute-start(f32[16,512]{1,0:T(8,128)S(1)} %get-tuple-element.107.refs_3_), channel_id=1, source_target_pairs={{0,1},{1,0},{2,3},{3,2},{4,5},{5,4},{6,7},{7,6},{8,9},{9,8},{10,11... | collective-permute-start | bytes 98312 | tf_op jit(solution)/shard_map/ppermute | solution.py:860
  14.7 1.5 %shard_map.136 = (f32[96,1024]{1,0:T(8,128)S(1)}, f32[64,1024]{1,0:T(8,128)S(1)}, f32[64,256]{1,0:T(8,128)S(1)}) custom-call(f32[64,1024]{1,0:T(8,128)S(1)} %get-tuple-element.97.p_ref.refs_0_.refs_7_, f32[96,1024]{1,0:T(8,128)S(1)} %get-tuple-element.100.refs_1_, f32[8,1024]{1,0:T(8,128)S(1)} %get-tuple-element.101.refs_2_, ...), custom_call_target="tpu_custom_call" | custom-call | flops 3000000000 | bytes 1 | tf_op jit(solution)/shard_map/pallas_call | solution.py:738
  16.2 0.7 %shard_map.137 = (f32[64,1024]{1,0:T(8,128)S(1)}, f32[64,1024]{1,0:T(8,128)S(1)}, f32[64,128]{1,0:T(8,128)S(1)}) custom-call(f32[64,1024]{1,0:T(8,128)S(1)} %get-tuple-element.96.refs_0_, f32[96,1024]{1,0:T(8,128)S(1)} %get-tuple-element.105.refs_1_, f32[64,1024]{1,0:T(8,128)S(1)} %get-tuple-element.106.refs_2_, f32[16,512]{1,0:T(8,128)S(1)} %get-tuple-element.107.refs_3_, ...), custom_call_target="tpu_custom_call" | custom-call | flops 3000000000 | bytes 1 | tf_op jit(solution)/shard_map/pallas_call | solution.py:738
  16.9 0.4 shard_map.139.refs_9_
  17.3 2.7 %collective-permute-start.7 = (f32[16,128]{1,0:T(8,128)S(1)}, f32[16,128]{1,0:T(8,128)S(1)}, u32[]{:S(2)}, u32[]{:S(2)}) collective-permute-start(f32[16,128]{1,0:T(8,128)S(1)} %shard_map.139.refs_9_), channel_id=1, source_target_pairs={{0,8},{1,9},{2,10},{3,11},{4,12},{5,13},{6,14},{7,15},{8,0},{9,1},... | collective-permute-start | bytes 24584 | tf_op jit(solution)/shard_map/ppermute | solution.py:808
  20.3 0.8 %shard_map.140 = (f32[64,1024]{1,0:T(8,128)S(1)}, f32[64,1024]{1,0:T(8,128)S(1)}, f32[96,1024]{1,0:T(8,128)S(1)}, f32[16,512]{1,0:T(8,128)S(1)}) custom-call(f32[64,1024]{1,0:T(8,128)S(1)} %get-tuple-element.112.refs_0_, f32[16,128]{1,0:T(8,128)S(1)} %collective-permute-done.4.one_ref.refs_1_, f32[16,128]{1,0:T(8,128)S(1)} %collective-permute-done.5.two_ref.refs_2_, ...), custom_call_target="tpu_custom_call" | custom-call | flops 3000000000 | bytes 1 | tf_op jit(solution)/shard_map/pallas_call | solution.py:738
  21.5 1.5 %shard_map.141 = (f32[96,1024]{1,0:T(8,128)S(1)}, f32[64,1024]{1,0:T(8,128)S(1)}, f32[64,256]{1,0:T(8,128)S(1)}) custom-call(f32[64,1024]{1,0:T(8,128)S(1)} %get-tuple-element.120.refs_0_.refs_7_, f32[96,1024]{1,0:T(8,128)S(1)} %get-tuple-element.121.refs_1_, f32[8,1024]{1,0:T(8,128)S(1)} %get-tuple-element.101.refs_2_, ...), custom_call_target="tpu_custom_call" | custom-call | flops 3000000000 | bytes 1 | tf_op jit(solution)/shard_map/pallas_call | solution.py:738
  22.9 0.7 %shard_map.142 = (f32[64,1024]{1,0:T(8,128)S(1)}, f32[64,1024]{1,0:T(8,128)S(1)}, f32[64,128]{1,0:T(8,128)S(1)}) custom-call(f32[64,1024]{1,0:T(8,128)S(1)} %get-tuple-element.119.refs_0_, f32[96,1024]{1,0:T(8,128)S(1)} %get-tuple-element.123.refs_1_, f32[64,1024]{1,0:T(8,128)S(1)} %get-tuple-element.124.refs_2_, f32[16,512]{1,0:T(8,128)S(1)} %get-tuple-element.125.refs_3_, ...), custom_call_target="tpu_custom_call" | custom-call | flops 3000000000 | bytes 1 | tf_op jit(solution)/shard_map/pallas_call | solution.py:738
  23.7 0.4 shard_map.143.refs_9_
  24.1 0.5 collective-permute-start.10
  24.8 0.8 %shard_map.144 = (f32[64,1024]{1,0:T(8,128)S(1)}, f32[64,1024]{1,0:T(8,128)S(1)}, f32[96,1024]{1,0:T(8,128)S(1)}, f32[16,512]{1,0:T(8,128)S(1)}) custom-call(f32[64,1024]{1,0:T(8,128)S(1)} %get-tuple-element.126.refs_0_, f32[16,128]{1,0:T(8,128)S(1)} %collective-permute-done.7.one_ref.refs_1_, f32[16,128]{1,0:T(8,128)S(1)} %collective-permute-done.8.two_ref.refs_2_, ...), custom_call_target="tpu_custom_call" | custom-call | flops 3000000000 | bytes 1 | tf_op jit(solution)/shard_map/pallas_call | solution.py:738
  26.0 1.5 %shard_map.145 = (f32[96,1024]{1,0:T(8,128)S(1)}, f32[64,1024]{1,0:T(8,128)S(1)}, f32[64,256]{1,0:T(8,128)S(1)}) custom-call(f32[64,1024]{1,0:T(8,128)S(1)} %get-tuple-element.130.refs_0_, f32[96,1024]{1,0:T(8,128)S(1)} %get-tuple-element.131.refs_1_, f32[8,1024]{1,0:T(8,128)S(1)} %get-tuple-element.101.refs_2_, s32[8,1024]{1,0:T(8,128)S(1)} %get-tuple-element.102.refs_3_, ...), custom_call_target="tpu_custom_call" | custom-call | flops 3000000000 | bytes 1 | tf_op jit(solution)/shard_map/pallas_call | solution.py:738
  27.5 0.6 %shard_map.146.r_ref.refs_0_ = f32[64,1024]{1,0:T(8,128)S(1)} custom-call(f32[64,1024]{1,0:T(8,128)S(1)} %get-tuple-element.129.refs_0_, f32[96,1024]{1,0:T(8,128)S(1)} %get-tuple-element.133.refs_1_, f32[64,1024]{1,0:T(8,128)S(1)} %get-tuple-element.134.refs_2_, f32[16,512]{1,0:T(8,128)S(1)} %get-tuple-element.135.refs_3_, ...), custom_call_target="tpu_custom_call" | custom-call | flops 3000000000 | bytes 1 | tf_op jit(solution)/shard_map/pallas_call | solution.py:738
  28.3 0.6 %collective-permute-start.13 = (f32[72,128]{1,0:T(8,128)S(1)}, f32[72,128]{1,0:T(8,128)S(1)}, u32[]{:S(2)}, u32[]{:S(2)}) collective-permute-start(f32[72,128]{1,0:T(8,128)S(1)} %shard_map.147.refs_7_), channel_id=1, source_target_pairs={{0,2},{1,8},{2,0},{3,10},{4,6},{5,12},{6,4},{7,14},{8,1},{9,16},{1... | collective-permute-start | bytes 110600 | tf_op jit(solution)/shard_map/ppermute | solution.py:901
  28.9 0.5 shard_map.148
  29.5 1.5 %collective-permute-start.12 = (f32[72,640]{1,0:T(8,128)S(1)}, f32[72,640]{1,0:T(8,128)S(1)}, u32[]{:S(2)}, u32[]{:S(2)}) collective-permute-start(f32[72,640]{1,0:T(8,128)S(1)} %get-tuple-element.139), channel_id=1, source_target_pairs={{0,1},{1,0},{2,3},{3,2},{4,5},{5,4},{6,7},{7,6},{8,9},{9,8},{10,11... | collective-permute-start | bytes 552968 | tf_op jit(solution)/shard_map/ppermute | solution.py:902
  31.3 0.8 %collective-permute-done.12.near_ref = f32[72,640]{1,0:T(8,128)S(1)} collective-permute-done((f32[72,640]{1,0:T(8,128)S(1)}, f32[72,640]{1,0:T(8,128)S(1)}, u32[]{:S(2)}, u32[]{:S(2)}) %collective-permute-start.12) | collective-permute-done | bytes 184352 | tf_op jit(solution)/shard_map/ppermute | solution.py:902
  32.1 1.2 %shard_map.150 = (f32[64,384]{1,0:T(8,128)S(1)}, f32[1,384]{1,0:T(1,128)S(1)}, s32[1,8,256]{2,1,0:T(8,128)S(1)}) custom-call(f32[64,1024]{1,0:T(8,128)S(1)} %get-tuple-element.138.r_ref.refs_0_, f32[72,640]{1,0:T(8,128)S(1)} %collective-permute-done.12.near_ref, s32[4,512]{1,0:T(4,128)S(1)} %get-tuple-element.140.gather_ref, ...), custom_call_target="tpu_custom_call" | custom-call | flops 100000000 | bytes 1 | tf_op jit(solution)/shard_map/pallas_call | solution.py:738
  33.3 2.1 %shard_map.151 = (f32[64,1024]{1,0:T(8,128)S(1)}, f32[16,128]{1,0:T(8,128)S(1)}) custom-call(f32[64,384]{1,0:T(8,128)S(1)} %get-tuple-element.142.right_ref, f32[1,384]{1,0:T(1,128)S(1)} %get-tuple-element.143.scale_ref, s32[1,8,256]{2,1,0:T(8,128)S(1)} %get-tuple-element.144.front_ref, f32[64,1024]{1,0:T(8,128)S(1)} %get-tuple-element.138.r_ref.refs_0_, ...), custom_call_target="tpu_custom_call" | custom-call | flops 3000000000 | bytes 1 | tf_op jit(solution)/shard_map/pallas_call | solution.py:738
  35.4 1.3 %collective-permute-start.15 = (f32[16,128]{1,0:T(8,128)S(1)}, f32[16,128]{1,0:T(8,128)S(1)}, u32[]{:S(2)}, u32[]{:S(2)}) collective-permute-start(f32[16,128]{1,0:T(8,128)S(1)} %get-tuple-element.149._), channel_id=1, source_target_pairs={{0,8},{1,9},{2,10},{3,11},{4,12},{5,13},{6,14},{7,15},{8,0},{9,1},... | collective-permute-start | bytes 24584 | tf_op jit(solution)/shard_map/ppermute | solution.py:808
  36.8 0.6 shard_map.152
  37.3 0.5 collective-permute-start.14
  37.8 1.5 %shard_map.153 = (f32[96,1024]{1,0:T(8,128)S(1)}, f32[64,1024]{1,0:T(8,128)S(1)}, f32[64,256]{1,0:T(8,128)S(1)}) custom-call(f32[64,1024]{1,0:T(8,128)S(1)} %get-tuple-element.148.p_ref.refs_0_, f32[96,1024]{1,0:T(8,128)S(1)} %get-tuple-element.150.refs_1_, f32[8,1024]{1,0:T(8,128)S(1)} %get-tuple-element.101.refs_2_, ...), custom_call_target="tpu_custom_call" | custom-call | flops 3000000000 | bytes 1 | tf_op jit(solution)/shard_map/pallas_call | solution.py:738
  39.3 0.7 %shard_map.154 = (f32[64,1024]{1,0:T(8,128)S(1)}, f32[64,1024]{1,0:T(8,128)S(1)}, f32[64,128]{1,0:T(8,128)S(1)}) custom-call(f32[64,1024]{1,0:T(8,128)S(1)} %get-tuple-element.138.r_ref.refs_0_, f32[96,1024]{1,0:T(8,128)S(1)} %get-tuple-element.152.refs_1_, f32[64,1024]{1,0:T(8,128)S(1)} %get-tuple-element.153.refs_2_, ...), custom_call_target="tpu_custom_call" | custom-call | flops 3000000000 | bytes 1 | tf_op jit(solution)/shard_map/pallas_call | solution.py:738
  40.0 0.4 shard_map.155.refs_9_
  40.4 1.9 %collective-permute-start.18 = (f32[16,128]{1,0:T(8,128)S(1)}, f32[16,128]{1,0:T(8,128)S(1)}, u32[]{:S(2)}, u32[]{:S(2)}) collective-permute-start(f32[16,128]{1,0:T(8,128)S(1)} %shard_map.155.refs_9_), channel_id=1, source_target_pairs={{0,8},{1,9},{2,10},{3,11},{4,12},{5,13},{6,14},{7,15},{8,0},{9,1},... | collective-permute-start | bytes 24584 | tf_op jit(solution)/shard_map/ppermute | solution.py:808
  42.6 0.8 %shard_map.156 = (f32[64,1024]{1,0:T(8,128)S(1)}, f32[64,1024]{1,0:T(8,128)S(1)}, f32[96,1024]{1,0:T(8,128)S(1)}, f32[16,512]{1,0:T(8,128)S(1)}) custom-call(f32[64,1024]{1,0:T(8,128)S(1)} %get-tuple-element.155.refs_0_, f32[16,128]{1,0:T(8,128)S(1)} %collective-permute-done.15.one_ref.refs_1_, f32[16,128]{1,0:T(8,128)S(1)} %collective-permute-done.16.two_ref.refs_2_, ...), custom_call_target="tpu_custom_call" | custom-call | flops 3000000000 | bytes 1 | tf_op jit(solution)/shard_map/pallas_call | solution.py:738
  43.8 1.5 %shard_map.157 = (f32[96,1024]{1,0:T(8,128)S(1)}, f32[64,1024]{1,0:T(8,128)S(1)}, f32[64,256]{1,0:T(8,128)S(1)}) custom-call(f32[64,1024]{1,0:T(8,128)S(1)} %get-tuple-element.159.refs_0_.refs_7_, f32[96,1024]{1,0:T(8,128)S(1)} %get-tuple-element.160.refs_1_, f32[8,1024]{1,0:T(8,128)S(1)} %get-tuple-element.101.refs_2_, ...), custom_call_target="tpu_custom_call" | custom-call | flops 3000000000 | bytes 1 | tf_op jit(solution)/shard_map/pallas_call | solution.py:738
  45.2 0.7 %shard_map.158 = (f32[64,1024]{1,0:T(8,128)S(1)}, f32[64,1024]{1,0:T(8,128)S(1)}, f32[64,128]{1,0:T(8,128)S(1)}) custom-call(f32[64,1024]{1,0:T(8,128)S(1)} %get-tuple-element.158.refs_0_, f32[96,1024]{1,0:T(8,128)S(1)} %get-tuple-element.162.refs_1_, f32[64,1024]{1,0:T(8,128)S(1)} %get-tuple-element.163.refs_2_, f32[16,512]{1,0:T(8,128)S(1)} %get-tuple-element.164.refs_3_, ...), custom_call_target="tpu_custom_call" | custom-call | flops 3000000000 | bytes 1 | tf_op jit(solution)/shard_map/pallas_call | solution.py:738
  46.0 0.4 shard_map.159.refs_9_
  46.4 0.9 %collective-permute-start.21 = (f32[16,128]{1,0:T(8,128)S(1)}, f32[16,128]{1,0:T(8,128)S(1)}, u32[]{:S(2)}, u32[]{:S(2)}) collective-permute-start(f32[16,128]{1,0:T(8,128)S(1)} %shard_map.159.refs_9_), channel_id=1, source_target_pairs={{0,8},{1,9},{2,10},{3,11},{4,12},{5,13},{6,14},{7,15},{8,0},{9,1},... | collective-permute-start | bytes 24584 | tf_op jit(solution)/shard_map/ppermute | solution.py:808
  47.5 0.8 %shard_map.160 = (f32[64,1024]{1,0:T(8,128)S(1)}, f32[64,1024]{1,0:T(8,128)S(1)}, f32[96,1024]{1,0:T(8,128)S(1)}, f32[16,512]{1,0:T(8,128)S(1)}) custom-call(f32[64,1024]{1,0:T(8,128)S(1)} %get-tuple-element.165.refs_0_, f32[16,128]{1,0:T(8,128)S(1)} %collective-permute-done.18.one_ref.refs_1_, f32[16,128]{1,0:T(8,128)S(1)} %collective-permute-done.19.two_ref.refs_2_, ...), custom_call_target="tpu_custom_call" | custom-call | flops 3000000000 | bytes 1 | tf_op jit(solution)/shard_map/pallas_call | solution.py:738
  48.7 1.5 %shard_map.161 = (f32[96,1024]{1,0:T(8,128)S(1)}, f32[64,1024]{1,0:T(8,128)S(1)}, f32[64,256]{1,0:T(8,128)S(1)}) custom-call(f32[64,1024]{1,0:T(8,128)S(1)} %get-tuple-element.169.refs_0_.refs_7_, f32[96,1024]{1,0:T(8,128)S(1)} %get-tuple-element.170.refs_1_, f32[8,1024]{1,0:T(8,128)S(1)} %get-tuple-element.101.refs_2_, ...), custom_call_target="tpu_custom_call" | custom-call | flops 3000000000 | bytes 1 | tf_op jit(solution)/shard_map/pallas_call | solution.py:738
  50.1 0.7 %shard_map.162 = (f32[64,1024]{1,0:T(8,128)S(1)}, f32[64,1024]{1,0:T(8,128)S(1)}, f32[64,128]{1,0:T(8,128)S(1)}) custom-call(f32[64,1024]{1,0:T(8,128)S(1)} %get-tuple-element.168.refs_0_, f32[96,1024]{1,0:T(8,128)S(1)} %get-tuple-element.172.refs_1_, f32[64,1024]{1,0:T(8,128)S(1)} %get-tuple-element.173.refs_2_, f32[16,512]{1,0:T(8,128)S(1)} %get-tuple-element.174.refs_3_, ...), custom_call_target="tpu_custom_call" | custom-call | flops 3000000000 | bytes 1 | tf_op jit(solution)/shard_map/pallas_call | solution.py:738
  50.9 0.4 shard_map.163.refs_9_
  51.3 1.6 %collective-permute-start.24 = (f32[16,128]{1,0:T(8,128)S(1)}, f32[16,128]{1,0:T(8,128)S(1)}, u32[]{:S(2)}, u32[]{:S(2)}) collective-permute-start(f32[16,128]{1,0:T(8,128)S(1)} %shard_map.163.refs_9_), channel_id=1, source_target_pairs={{0,8},{1,9},{2,10},{3,11},{4,12},{5,13},{6,14},{7,15},{8,0},{9,1},... | collective-permute-start | bytes 24584 | tf_op jit(solution)/shard_map/ppermute | solution.py:808
  53.1 0.8 %shard_map.164 = (f32[64,1024]{1,0:T(8,128)S(1)}, f32[64,1024]{1,0:T(8,128)S(1)}, f32[96,1024]{1,0:T(8,128)S(1)}, f32[16,512]{1,0:T(8,128)S(1)}) custom-call(f32[64,1024]{1,0:T(8,128)S(1)} %get-tuple-element.175.refs_0_, f32[16,128]{1,0:T(8,128)S(1)} %collective-permute-done.21.one_ref.refs_1_, f32[16,128]{1,0:T(8,128)S(1)} %collective-permute-done.22.two_ref.refs_2_, ...), custom_call_target="tpu_custom_call" | custom-call | flops 3000000000 | bytes 1 | tf_op jit(solution)/shard_map/pallas_call | solution.py:738
  54.3 1.0 %shard_map.165 = (f32[96,256]{1,0:T(8,128)S(1)}, f32[64,256]{1,0:T(8,128)S(1)}, f32[64,256]{1,0:T(8,128)}) custom-call(f32[64,1024]{1,0:T(8,128)S(1)} %get-tuple-element.178.refs_0_, f32[96,1024]{1,0:T(8,128)S(1)} %get-tuple-element.179.refs_1_, f32[8,1024]{1,0:T(8,128)S(1)} %get-tuple-element.101.refs_2_, s32[8,1024]{1,0:T(8,128)S(1)} %get-tuple-element.102.refs_3_, ...), custom_call_target="tpu_custom_call" | custom-call | flops 3000000000 | bytes 1 | tf_op jit(solution)/shard_map/pallas_call | solution.py:738
  55.7 0.9 %shard_map.167 = f32[64,256]{1,0:T(8,128)} custom-call(f32[64,256]{1,0:T(8,128)S(1)} %shard_map.166.refs_0_, f32[16,128]{1,0:T(8,128)S(1)} %collective-permute-done.24.refs_1_, f32[16,128]{1,0:T(8,128)S(1)} %collective-permute-done.25.refs_2_, s32[8,1024]{1,0:T(8,128)S(1)} %get-tuple-element.113.edge_ref.refs_3_, ...), custom_call_target="tpu_custom_call" | custom-call | flops 3000000000 | bytes 1 | tf_op jit(solution)/shard_map/pallas_call | solution.py:738
  (49 shorter events, 4.6 us)
Async XLA Ops:
  0.6 5.5 %copy-start.1 = (f32[2,64,64]{2,1,0:T(8,128)S(1)}, f32[2,64,64]{2,1,0:T(8,128)}, u32[]{:S(2)}) copy-start(f32[2,64,64]{2,1,0:T(8,128)} %refs_4_.1) | copy-start | bytes 98308
  0.6 5.5 %copy-start.2 = (f32[96,64]{0,1:T(8,128)S(1)}, f32[96,64]{0,1:T(8,128)}, u32[]{:S(2)}) copy-start(f32[96,64]{0,1:T(8,128)} %param.16) | copy-start | bytes 73732
  1.6 5.9 %collective-permute-start = (f32[80,256]{1,0:T(8,128)S(1)}, f32[80,256]{1,0:T(8,128)S(1)}, u32[]{:S(2)}, u32[]{:S(2)}) collective-permute-start(f32[80,256]{1,0:T(8,128)S(1)} %shard_map.131.refs_0_), channel_id=1, source_target_pairs={{0,2},{1,3},{2,0},{3,1},{4,6},{5,7},{6,4},{7,5},{8,10},{9,11},{10,... | collective-permute-start | bytes 245768 | tf_op jit(solution)/shard_map/ppermute | solution.py:835
  4.6 5.3 %collective-permute-start.1 = (f32[80,256]{1,0:T(8,128)S(1)}, f32[80,256]{1,0:T(8,128)S(1)}, u32[]{:S(2)}, u32[]{:S(2)}) collective-permute-start(f32[80,256]{1,0:T(8,128)S(1)} %shard_map.131.refs_0_), channel_id=1, source_target_pairs={{0,4},{1,5},{2,6},{3,7},{4,0},{5,1},{6,2},{7,3},{8,12},{9,13},{10,... | collective-permute-start | bytes 245768 | tf_op jit(solution)/shard_map/ppermute | solution.py:835
  6.1 5.3 %collective-permute-start.2 = (f32[80,256]{1,0:T(8,128)S(1)}, f32[80,256]{1,0:T(8,128)S(1)}, u32[]{:S(2)}, u32[]{:S(2)}) collective-permute-start(f32[80,256]{1,0:T(8,128)S(1)} %shard_map.131.refs_0_), channel_id=1, source_target_pairs={{0,6},{1,7},{2,4},{3,5},{4,2},{5,3},{6,0},{7,1},{8,14},{9,15},{10,... | collective-permute-start | bytes 245768 | tf_op jit(solution)/shard_map/ppermute | solution.py:835
  6.2 1.0 %copy-start = (f32[8,64,64]{2,1,0:T(8,128)S(1)}, f32[8,64,64]{2,1,0:T(8,128)}, u32[]{:S(2)}) copy-start(f32[8,64,64]{2,1,0:T(8,128)} %restriction_ref.1) | copy-start | bytes 393220
  6.2 1.0 %copy-start.3 = (f32[64,64]{1,0:T(8,128)S(1)}, f32[64,64]{1,0:T(8,128)}, u32[]{:S(2)}) copy-start(f32[64,64]{1,0:T(8,128)} %stiff_ref.5) | copy-start | bytes 49156
  12.0 4.9 %collective-permute-start.4 = (f32[16,128]{1,0:T(8,128)S(1)}, f32[16,128]{1,0:T(8,128)S(1)}, u32[]{:S(2)}, u32[]{:S(2)}) collective-permute-start(f32[16,128]{1,0:T(8,128)S(1)} %get-tuple-element.99._), channel_id=1, source_target_pairs={{0,8},{1,9},{2,10},{3,11},{4,12},{5,13},{6,14},{7,15},{8,0},{9,1},... | collective-permute-start | bytes 24584 | tf_op jit(solution)/shard_map/ppermute | solution.py:808
  13.6 3.3 %collective-permute-start.5 = (f32[16,128]{1,0:T(8,128)S(1)}, f32[16,128]{1,0:T(8,128)S(1)}, u32[]{:S(2)}, u32[]{:S(2)}) collective-permute-start(f32[16,128]{1,0:T(8,128)S(1)} %get-tuple-element.99._), channel_id=1, source_target_pairs={{0,1},{1,0},{2,3},{3,2},{4,5},{5,4},{6,7},{7,6},{8,16},{9,17},{10,... | collective-permute-start | bytes 24584 | tf_op jit(solution)/shard_map/ppermute | solution.py:808
  14.0 2.2 %collective-permute-start.3 = (f32[16,512]{1,0:T(8,128)S(1)}, f32[16,512]{1,0:T(8,128)S(1)}, u32[]{:S(2)}, u32[]{:S(2)}) collective-permute-start(f32[16,512]{1,0:T(8,128)S(1)} %get-tuple-element.107.refs_3_), channel_id=1, source_target_pairs={{0,1},{1,0},{2,3},{3,2},{4,5},{5,4},{6,7},{7,6},{8,9},{9,8},{10,11... | collective-permute-start | bytes 98312 | tf_op jit(solution)/shard_map/ppermute | solution.py:860
  17.3 6.3 %collective-permute-start.7 = (f32[16,128]{1,0:T(8,128)S(1)}, f32[16,128]{1,0:T(8,128)S(1)}, u32[]{:S(2)}, u32[]{:S(2)}) collective-permute-start(f32[16,128]{1,0:T(8,128)S(1)} %shard_map.139.refs_9_), channel_id=1, source_target_pairs={{0,8},{1,9},{2,10},{3,11},{4,12},{5,13},{6,14},{7,15},{8,0},{9,1},... | collective-permute-start | bytes 24584 | tf_op jit(solution)/shard_map/ppermute | solution.py:808
  20.1 3.6 %collective-permute-start.8 = (f32[16,128]{1,0:T(8,128)S(1)}, f32[16,128]{1,0:T(8,128)S(1)}, u32[]{:S(2)}, u32[]{:S(2)}) collective-permute-start(f32[16,128]{1,0:T(8,128)S(1)} %shard_map.139.refs_9_), channel_id=1, source_target_pairs={{0,1},{1,0},{2,3},{3,2},{4,5},{5,4},{6,7},{7,6},{8,16},{9,17},{10,... | collective-permute-start | bytes 24584 | tf_op jit(solution)/shard_map/ppermute | solution.py:808
  21.1 1.8 %collective-permute-start.6 = (f32[16,512]{1,0:T(8,128)S(1)}, f32[16,512]{1,0:T(8,128)S(1)}, u32[]{:S(2)}, u32[]{:S(2)}) collective-permute-start(f32[16,512]{1,0:T(8,128)S(1)} %get-tuple-element.125.refs_3_), channel_id=1, source_target_pairs={{0,1},{1,0},{2,3},{3,2},{4,5},{5,4},{6,7},{7,6},{8,9},{9,8},{10,11... | collective-permute-start | bytes 98312 | tf_op jit(solution)/shard_map/ppermute | solution.py:860
  24.1 4.0 %collective-permute-start.10 = (f32[16,128]{1,0:T(8,128)S(1)}, f32[16,128]{1,0:T(8,128)S(1)}, u32[]{:S(2)}, u32[]{:S(2)}) collective-permute-start(f32[16,128]{1,0:T(8,128)S(1)} %shard_map.143.refs_9_), channel_id=1, source_target_pairs={{0,8},{1,9},{2,10},{3,11},{4,12},{5,13},{6,14},{7,15},{8,0},{9,1},... | collective-permute-start | bytes 24584 | tf_op jit(solution)/shard_map/ppermute | solution.py:808
  24.6 3.5 %collective-permute-start.11 = (f32[16,128]{1,0:T(8,128)S(1)}, f32[16,128]{1,0:T(8,128)S(1)}, u32[]{:S(2)}, u32[]{:S(2)}) collective-permute-start(f32[16,128]{1,0:T(8,128)S(1)} %shard_map.143.refs_9_), channel_id=1, source_target_pairs={{0,1},{1,0},{2,3},{3,2},{4,5},{5,4},{6,7},{7,6},{8,16},{9,17},{10,... | collective-permute-start | bytes 24584 | tf_op jit(solution)/shard_map/ppermute | solution.py:808
  25.6 1.8 %collective-permute-start.9 = (f32[16,512]{1,0:T(8,128)S(1)}, f32[16,512]{1,0:T(8,128)S(1)}, u32[]{:S(2)}, u32[]{:S(2)}) collective-permute-start(f32[16,512]{1,0:T(8,128)S(1)} %get-tuple-element.135.refs_3_), channel_id=1, source_target_pairs={{0,1},{1,0},{2,3},{3,2},{4,5},{5,4},{6,7},{7,6},{8,9},{9,8},{10,11... | collective-permute-start | bytes 98312 | tf_op jit(solution)/shard_map/ppermute | solution.py:860
  28.3 4.9 %collective-permute-start.13 = (f32[72,128]{1,0:T(8,128)S(1)}, f32[72,128]{1,0:T(8,128)S(1)}, u32[]{:S(2)}, u32[]{:S(2)}) collective-permute-start(f32[72,128]{1,0:T(8,128)S(1)} %shard_map.147.refs_7_), channel_id=1, source_target_pairs={{0,2},{1,8},{2,0},{3,10},{4,6},{5,12},{6,4},{7,14},{8,1},{9,16},{1... | collective-permute-start | bytes 110600 | tf_op jit(solution)/shard_map/ppermute | solution.py:901
  29.5 2.6 %collective-permute-start.12 = (f32[72,640]{1,0:T(8,128)S(1)}, f32[72,640]{1,0:T(8,128)S(1)}, u32[]{:S(2)}, u32[]{:S(2)}) collective-permute-start(f32[72,640]{1,0:T(8,128)S(1)} %get-tuple-element.139), channel_id=1, source_target_pairs={{0,1},{1,0},{2,3},{3,2},{4,5},{5,4},{6,7},{7,6},{8,9},{9,8},{10,11... | collective-permute-start | bytes 552968 | tf_op jit(solution)/shard_map/ppermute | solution.py:902
  35.4 4.6 %collective-permute-start.15 = (f32[16,128]{1,0:T(8,128)S(1)}, f32[16,128]{1,0:T(8,128)S(1)}, u32[]{:S(2)}, u32[]{:S(2)}) collective-permute-start(f32[16,128]{1,0:T(8,128)S(1)} %get-tuple-element.149._), channel_id=1, source_target_pairs={{0,8},{1,9},{2,10},{3,11},{4,12},{5,13},{6,14},{7,15},{8,0},{9,1},... | collective-permute-start | bytes 24584 | tf_op jit(solution)/shard_map/ppermute | solution.py:808
  36.7 3.3 %collective-permute-start.16 = (f32[16,128]{1,0:T(8,128)S(1)}, f32[16,128]{1,0:T(8,128)S(1)}, u32[]{:S(2)}, u32[]{:S(2)}) collective-permute-start(f32[16,128]{1,0:T(8,128)S(1)} %get-tuple-element.149._), channel_id=1, source_target_pairs={{0,1},{1,0},{2,3},{3,2},{4,5},{5,4},{6,7},{7,6},{8,16},{9,17},{10,... | collective-permute-start | bytes 24584 | tf_op jit(solution)/shard_map/ppermute | solution.py:808
  37.3 2.0 %collective-permute-start.14 = (f32[16,512]{1,0:T(8,128)S(1)}, f32[16,512]{1,0:T(8,128)S(1)}, u32[]{:S(2)}, u32[]{:S(2)}) collective-permute-start(f32[16,512]{1,0:T(8,128)S(1)} %get-tuple-element.154.refs_3_), channel_id=1, source_target_pairs={{0,1},{1,0},{2,3},{3,2},{4,5},{5,4},{6,7},{7,6},{8,9},{9,8},{10,11... | collective-permute-start | bytes 98312 | tf_op jit(solution)/shard_map/ppermute | solution.py:860
  40.4 5.5 %collective-permute-start.18 = (f32[16,128]{1,0:T(8,128)S(1)}, f32[16,128]{1,0:T(8,128)S(1)}, u32[]{:S(2)}, u32[]{:S(2)}) collective-permute-start(f32[16,128]{1,0:T(8,128)S(1)} %shard_map.155.refs_9_), channel_id=1, source_target_pairs={{0,8},{1,9},{2,10},{3,11},{4,12},{5,13},{6,14},{7,15},{8,0},{9,1},... | collective-permute-start | bytes 24584 | tf_op jit(solution)/shard_map/ppermute | solution.py:808
  42.4 3.6 %collective-permute-start.19 = (f32[16,128]{1,0:T(8,128)S(1)}, f32[16,128]{1,0:T(8,128)S(1)}, u32[]{:S(2)}, u32[]{:S(2)}) collective-permute-start(f32[16,128]{1,0:T(8,128)S(1)} %shard_map.155.refs_9_), channel_id=1, source_target_pairs={{0,1},{1,0},{2,3},{3,2},{4,5},{5,4},{6,7},{7,6},{8,16},{9,17},{10,... | collective-permute-start | bytes 24584 | tf_op jit(solution)/shard_map/ppermute | solution.py:808
  43.4 1.8 %collective-permute-start.17 = (f32[16,512]{1,0:T(8,128)S(1)}, f32[16,512]{1,0:T(8,128)S(1)}, u32[]{:S(2)}, u32[]{:S(2)}) collective-permute-start(f32[16,512]{1,0:T(8,128)S(1)} %get-tuple-element.164.refs_3_), channel_id=1, source_target_pairs={{0,1},{1,0},{2,3},{3,2},{4,5},{5,4},{6,7},{7,6},{8,9},{9,8},{10,11... | collective-permute-start | bytes 98312 | tf_op jit(solution)/shard_map/ppermute | solution.py:860
  46.4 4.4 %collective-permute-start.21 = (f32[16,128]{1,0:T(8,128)S(1)}, f32[16,128]{1,0:T(8,128)S(1)}, u32[]{:S(2)}, u32[]{:S(2)}) collective-permute-start(f32[16,128]{1,0:T(8,128)S(1)} %shard_map.159.refs_9_), channel_id=1, source_target_pairs={{0,8},{1,9},{2,10},{3,11},{4,12},{5,13},{6,14},{7,15},{8,0},{9,1},... | collective-permute-start | bytes 24584 | tf_op jit(solution)/shard_map/ppermute | solution.py:808
  47.3 3.6 %collective-permute-start.22 = (f32[16,128]{1,0:T(8,128)S(1)}, f32[16,128]{1,0:T(8,128)S(1)}, u32[]{:S(2)}, u32[]{:S(2)}) collective-permute-start(f32[16,128]{1,0:T(8,128)S(1)} %shard_map.159.refs_9_), channel_id=1, source_target_pairs={{0,1},{1,0},{2,3},{3,2},{4,5},{5,4},{6,7},{7,6},{8,16},{9,17},{10,... | collective-permute-start | bytes 24584 | tf_op jit(solution)/shard_map/ppermute | solution.py:808
  48.3 1.8 %collective-permute-start.20 = (f32[16,512]{1,0:T(8,128)S(1)}, f32[16,512]{1,0:T(8,128)S(1)}, u32[]{:S(2)}, u32[]{:S(2)}) collective-permute-start(f32[16,512]{1,0:T(8,128)S(1)} %get-tuple-element.174.refs_3_), channel_id=1, source_target_pairs={{0,1},{1,0},{2,3},{3,2},{4,5},{5,4},{6,7},{7,6},{8,9},{9,8},{10,11... | collective-permute-start | bytes 98312 | tf_op jit(solution)/shard_map/ppermute | solution.py:860
  51.3 4.3 %collective-permute-start.24 = (f32[16,128]{1,0:T(8,128)S(1)}, f32[16,128]{1,0:T(8,128)S(1)}, u32[]{:S(2)}, u32[]{:S(2)}) collective-permute-start(f32[16,128]{1,0:T(8,128)S(1)} %shard_map.163.refs_9_), channel_id=1, source_target_pairs={{0,8},{1,9},{2,10},{3,11},{4,12},{5,13},{6,14},{7,15},{8,0},{9,1},... | collective-permute-start | bytes 24584 | tf_op jit(solution)/shard_map/ppermute | solution.py:808
  52.9 2.8 %collective-permute-start.25 = (f32[16,128]{1,0:T(8,128)S(1)}, f32[16,128]{1,0:T(8,128)S(1)}, u32[]{:S(2)}, u32[]{:S(2)}) collective-permute-start(f32[16,128]{1,0:T(8,128)S(1)} %shard_map.163.refs_9_), channel_id=1, source_target_pairs={{0,1},{1,0},{2,3},{3,2},{4,5},{5,4},{6,7},{7,6},{8,16},{9,17},{10,... | collective-permute-start | bytes 24584 | tf_op jit(solution)/shard_map/ppermute | solution.py:808
  53.9 1.4 %collective-permute-start.23 = (f32[16,512]{1,0:T(8,128)S(1)}, f32[16,512]{1,0:T(8,128)S(1)}, u32[]{:S(2)}, u32[]{:S(2)}) collective-permute-start(f32[16,512]{1,0:T(8,128)S(1)} %get-tuple-element.185.refs_3_), channel_id=1, source_target_pairs={{0,1},{1,0},{2,3},{3,2},{4,5},{5,4},{6,7},{7,6},{8,9},{9,8},{10,11... | collective-permute-start | bytes 98312 | tf_op jit(solution)/shard_map/ppermute | solution.py:860

commit v8 on v7

--- a/solution.py
+++ b/solution.py
@@ -197,7 +197,7 @@
     modes, count = map_ref.shape[0], gathered[0].shape[1]
     chip, core = own_place()
     for k, ref in enumerate(gathered):
-        held[jnp.bitwise_xor(chip, k)] = ref[...]
+        held[jnp.bitwise_xor(chip, (blocks - k) % blocks)] = ref[...]
     eye = lax.broadcasted_iota(jnp.int32, (modes, modes), 0) == lax.broadcasted_iota(
         jnp.int32, (modes, modes), 1
     )
@@ -832,7 +832,7 @@
         hbm=True,
     )
     gathered = [packed] + [
-        lax.ppermute(packed, "sub", [(s, s ^ (CORES * k)) for s in range(peers)]) for k in range(1, blocks)
+        lax.ppermute(packed, "sub", [(s, s ^ (CORES * k)) for s in range(peers)]) for k in range(blocks - 1, 0, -1)
     ]
     b, inverse, meta, lane, at, far, edge, subs, rim, sizes, coarse_cond, rim_face, p, rim_out = run(
         functools.partial(start_kernel, blocks, width, rims),

time: 56.8 us -> 55.8 us (0.982)
  waiting for transfers between devices: 4.86 us -> 3.85 us
    ppermute x3, waiting for transfers between devices: 3.99 us -> 2.98 us  [local(): lax.ppermute(packed, 'sub', [(s, s ^ CORES * k) for s in range(peers)])]
  transfers between devices with their start and end apart: 26 -> 26, of which waited for: 3 -> 4; matrix products, arithmetic and copies ran while one was open for 0% -> 0% of each run, Pallas kernels for 39% -> 39%
where the time goes in v8:
time: 55.8 us; the launch traced here: 55.6 us
  Pallas kernels  28.7 us (51%)
  starting transfers between devices  21.3 us (38%)
  waiting for transfers between devices  3.85 us (7%)
  between operations  1.01 us (2%)
  local copies, waits for them, and re-layouts  0.79 us (1%)
    pallas_call x37, Pallas kernels, call(): pl.pallas_call(kernel, out_shape=[jax.ShapeDtypeStruct(shape, kind) for s...  28.7 us
    ppermute x14, starting transfers between devices, over_segments(): return (lax.ppermute(rim, both, ones), lax.ppermute(rim, both, twos))  11.7 us
    ppermute x3, starting transfers between devices, local(): lax.ppermute(packed, 'sub', [(s, s ^ CORES * k) for s in range(peers)])  4.6 us
    ppermute x3, waiting for transfers between devices, local(): lax.ppermute(packed, 'sub', [(s, s ^ CORES * k) for s in range(peers)])  2.98 us
    ppermute x7, starting transfers between devices, apply(): swapped = lax.ppermute(sub_out, 'sub', cores)  2.9 us
  transfers between devices with their start and end apart: 26, of which 4 were waited for; matrix products, arithmetic and copies ran while one was open for 0% of the time, Pallas kernels for 39%

profile of v8, /device:TPU:0, one launch (start us, length us, event | category | flops | bytes accessed | tf_op | source)
XLA Modules:
  0.0 55.6 jit_solution(18124587187481586842)
XLA Ops:
  0.7 1.0 %shard_map.131.refs_0_ = f32[80,256]{1,0:T(8,128)S(1)} custom-call(f32[64,256]{1,0:T(8,128)} %b_ref.1, f32[1,256]{1,0:T(1,128)} %bitcast.6, s32[1,256]{1,0:T(1,128)} %bitcast.7, s32[6,256]{1,0:T(8,128)} %face_ref.1, s32[1,128]{1,0:T(1,128)} %sub_ref.1, s32[1,16]{1,0:T(1,128)} %rim_ref.1, s32[1,64]{1,0:T(1,128)} %size_ref.1, f32[1,64]{1,0:T(1,128)} %bitcast.8), custom_call_target="tpu_custom_call" | custom-call | flops 3000000000 | bytes 1 | tf_op jit(solution)/shard_map/pallas_call | solution.py:738
  1.6 4.0 %collective-permute-start = (f32[80,256]{1,0:T(8,128)S(1)}, f32[80,256]{1,0:T(8,128)S(1)}, u32[]{:S(2)}, u32[]{:S(2)}) collective-permute-start(f32[80,256]{1,0:T(8,128)S(1)} %shard_map.131.refs_0_), channel_id=1, source_target_pairs={{0,6},{1,7},{2,4},{3,5},{4,2},{5,3},{6,0},{7,1},{8,14},{9,15},{10,... | collective-permute-start | bytes 245768 | tf_op jit(solution)/shard_map/ppermute | solution.py:835
  5.6 0.5 collective-permute-start.1
  6.4 0.8 %copy-done = f32[8,64,64]{2,1,0:T(8,128)S(1)} copy-done((f32[8,64,64]{2,1,0:T(8,128)S(1)}, f32[8,64,64]{2,1,0:T(8,128)}, u32[]{:S(2)}) %copy-start) | copy-done | bytes 131096
  7.5 0.6 %collective-permute-done.refs_1_ = f32[80,256]{1,0:T(8,128)S(1)} collective-permute-done((f32[80,256]{1,0:T(8,128)S(1)}, f32[80,256]{1,0:T(8,128)S(1)}, u32[]{:S(2)}, u32[]{:S(2)}) %collective-permute-start) | collective-permute-done | bytes 81952 | tf_op jit(solution)/shard_map/ppermute | solution.py:835
  8.2 1.9 %collective-permute-done.1.refs_2_ = f32[80,256]{1,0:T(8,128)S(1)} collective-permute-done((f32[80,256]{1,0:T(8,128)S(1)}, f32[80,256]{1,0:T(8,128)S(1)}, u32[]{:S(2)}, u32[]{:S(2)}) %collective-permute-start.1) | collective-permute-done | bytes 81952 | tf_op jit(solution)/shard_map/ppermute | solution.py:835
  10.0 0.5 collective-permute-done.2.refs_3_
  10.5 0.5 shard_map.134
  11.0 1.6 %collective-permute-start.4 = (f32[16,128]{1,0:T(8,128)S(1)}, f32[16,128]{1,0:T(8,128)S(1)}, u32[]{:S(2)}, u32[]{:S(2)}) collective-permute-start(f32[16,128]{1,0:T(8,128)S(1)} %get-tuple-element.99._), channel_id=1, source_target_pairs={{0,8},{1,9},{2,10},{3,11},{4,12},{5,13},{6,14},{7,15},{8,0},{9,1},... | collective-permute-start | bytes 24584 | tf_op jit(solution)/shard_map/ppermute | solution.py:808
  13.0 0.6 %collective-permute-start.3 = (f32[16,512]{1,0:T(8,128)S(1)}, f32[16,512]{1,0:T(8,128)S(1)}, u32[]{:S(2)}, u32[]{:S(2)}) collective-permute-start(f32[16,512]{1,0:T(8,128)S(1)} %get-tuple-element.107.refs_3_), channel_id=1, source_target_pairs={{0,1},{1,0},{2,3},{3,2},{4,5},{5,4},{6,7},{7,6},{8,9},{9,8},{10,11... | collective-permute-start | bytes 98312 | tf_op jit(solution)/shard_map/ppermute | solution.py:860
  13.8 1.5 %shard_map.136 = (f32[96,1024]{1,0:T(8,128)S(1)}, f32[64,1024]{1,0:T(8,128)S(1)}, f32[64,256]{1,0:T(8,128)S(1)}) custom-call(f32[64,1024]{1,0:T(8,128)S(1)} %get-tuple-element.97.p_ref.refs_0_.refs_7_, f32[96,1024]{1,0:T(8,128)S(1)} %get-tuple-element.100.refs_1_, f32[8,1024]{1,0:T(8,128)S(1)} %get-tuple-element.101.refs_2_, ...), custom_call_target="tpu_custom_call" | custom-call | flops 3000000000 | bytes 1 | tf_op jit(solution)/shard_map/pallas_call | solution.py:738
  15.2 0.7 %shard_map.137 = (f32[64,1024]{1,0:T(8,128)S(1)}, f32[64,1024]{1,0:T(8,128)S(1)}, f32[64,128]{1,0:T(8,128)S(1)}) custom-call(f32[64,1024]{1,0:T(8,128)S(1)} %get-tuple-element.96.refs_0_, f32[96,1024]{1,0:T(8,128)S(1)} %get-tuple-element.105.refs_1_, f32[64,1024]{1,0:T(8,128)S(1)} %get-tuple-element.106.refs_2_, f32[16,512]{1,0:T(8,128)S(1)} %get-tuple-element.107.refs_3_, ...), custom_call_target="tpu_custom_call" | custom-call | flops 3000000000 | bytes 1 | tf_op jit(solution)/shard_map/pallas_call | solution.py:738
  16.0 0.4 shard_map.139.refs_9_
  16.4 2.7 %collective-permute-start.7 = (f32[16,128]{1,0:T(8,128)S(1)}, f32[16,128]{1,0:T(8,128)S(1)}, u32[]{:S(2)}, u32[]{:S(2)}) collective-permute-start(f32[16,128]{1,0:T(8,128)S(1)} %shard_map.139.refs_9_), channel_id=1, source_target_pairs={{0,8},{1,9},{2,10},{3,11},{4,12},{5,13},{6,14},{7,15},{8,0},{9,1},... | collective-permute-start | bytes 24584 | tf_op jit(solution)/shard_map/ppermute | solution.py:808
  19.3 0.8 %shard_map.140 = (f32[64,1024]{1,0:T(8,128)S(1)}, f32[64,1024]{1,0:T(8,128)S(1)}, f32[96,1024]{1,0:T(8,128)S(1)}, f32[16,512]{1,0:T(8,128)S(1)}) custom-call(f32[64,1024]{1,0:T(8,128)S(1)} %get-tuple-element.112.refs_0_, f32[16,128]{1,0:T(8,128)S(1)} %collective-permute-done.4.one_ref.refs_1_, f32[16,128]{1,0:T(8,128)S(1)} %collective-permute-done.5.two_ref.refs_2_, ...), custom_call_target="tpu_custom_call" | custom-call | flops 3000000000 | bytes 1 | tf_op jit(solution)/shard_map/pallas_call | solution.py:738
  20.5 1.5 %shard_map.141 = (f32[96,1024]{1,0:T(8,128)S(1)}, f32[64,1024]{1,0:T(8,128)S(1)}, f32[64,256]{1,0:T(8,128)S(1)}) custom-call(f32[64,1024]{1,0:T(8,128)S(1)} %get-tuple-element.120.refs_0_.refs_7_, f32[96,1024]{1,0:T(8,128)S(1)} %get-tuple-element.121.refs_1_, f32[8,1024]{1,0:T(8,128)S(1)} %get-tuple-element.101.refs_2_, ...), custom_call_target="tpu_custom_call" | custom-call | flops 3000000000 | bytes 1 | tf_op jit(solution)/shard_map/pallas_call | solution.py:738
  22.0 0.7 %shard_map.142 = (f32[64,1024]{1,0:T(8,128)S(1)}, f32[64,1024]{1,0:T(8,128)S(1)}, f32[64,128]{1,0:T(8,128)S(1)}) custom-call(f32[64,1024]{1,0:T(8,128)S(1)} %get-tuple-element.119.refs_0_, f32[96,1024]{1,0:T(8,128)S(1)} %get-tuple-element.123.refs_1_, f32[64,1024]{1,0:T(8,128)S(1)} %get-tuple-element.124.refs_2_, f32[16,512]{1,0:T(8,128)S(1)} %get-tuple-element.125.refs_3_, ...), custom_call_target="tpu_custom_call" | custom-call | flops 3000000000 | bytes 1 | tf_op jit(solution)/shard_map/pallas_call | solution.py:738
  22.7 0.4 shard_map.143.refs_9_
  23.1 0.5 collective-permute-start.10
  23.9 0.8 %shard_map.144 = (f32[64,1024]{1,0:T(8,128)S(1)}, f32[64,1024]{1,0:T(8,128)S(1)}, f32[96,1024]{1,0:T(8,128)S(1)}, f32[16,512]{1,0:T(8,128)S(1)}) custom-call(f32[64,1024]{1,0:T(8,128)S(1)} %get-tuple-element.126.refs_0_, f32[16,128]{1,0:T(8,128)S(1)} %collective-permute-done.7.one_ref.refs_1_, f32[16,128]{1,0:T(8,128)S(1)} %collective-permute-done.8.two_ref.refs_2_, ...), custom_call_target="tpu_custom_call" | custom-call | flops 3000000000 | bytes 1 | tf_op jit(solution)/shard_map/pallas_call | solution.py:738
  25.0 1.5 %shard_map.145 = (f32[96,1024]{1,0:T(8,128)S(1)}, f32[64,1024]{1,0:T(8,128)S(1)}, f32[64,256]{1,0:T(8,128)S(1)}) custom-call(f32[64,1024]{1,0:T(8,128)S(1)} %get-tuple-element.130.refs_0_, f32[96,1024]{1,0:T(8,128)S(1)} %get-tuple-element.131.refs_1_, f32[8,1024]{1,0:T(8,128)S(1)} %get-tuple-element.101.refs_2_, s32[8,1024]{1,0:T(8,128)S(1)} %get-tuple-element.102.refs_3_, ...), custom_call_target="tpu_custom_call" | custom-call | flops 3000000000 | bytes 1 | tf_op jit(solution)/shard_map/pallas_call | solution.py:738
  26.5 0.6 %shard_map.146.r_ref.refs_0_ = f32[64,1024]{1,0:T(8,128)S(1)} custom-call(f32[64,1024]{1,0:T(8,128)S(1)} %get-tuple-element.129.refs_0_, f32[96,1024]{1,0:T(8,128)S(1)} %get-tuple-element.133.refs_1_, f32[64,1024]{1,0:T(8,128)S(1)} %get-tuple-element.134.refs_2_, f32[16,512]{1,0:T(8,128)S(1)} %get-tuple-element.135.refs_3_, ...), custom_call_target="tpu_custom_call" | custom-call | flops 3000000000 | bytes 1 | tf_op jit(solution)/shard_map/pallas_call | solution.py:738
  27.4 1.1 %collective-permute-start.13 = (f32[72,128]{1,0:T(8,128)S(1)}, f32[72,128]{1,0:T(8,128)S(1)}, u32[]{:S(2)}, u32[]{:S(2)}) collective-permute-start(f32[72,128]{1,0:T(8,128)S(1)} %shard_map.147.refs_7_), channel_id=1, source_target_pairs={{0,2},{1,8},{2,0},{3,10},{4,6},{5,12},{6,4},{7,14},{8,1},{9,16},{1... | collective-permute-start | bytes 110600 | tf_op jit(solution)/shard_map/ppermute | solution.py:901
  28.4 0.5 shard_map.148
  29.0 1.1 %collective-permute-start.12 = (f32[72,640]{1,0:T(8,128)S(1)}, f32[72,640]{1,0:T(8,128)S(1)}, u32[]{:S(2)}, u32[]{:S(2)}) collective-permute-start(f32[72,640]{1,0:T(8,128)S(1)} %get-tuple-element.139), channel_id=1, source_target_pairs={{0,1},{1,0},{2,3},{3,2},{4,5},{5,4},{6,7},{7,6},{8,9},{9,8},{10,11... | collective-permute-start | bytes 552968 | tf_op jit(solution)/shard_map/ppermute | solution.py:902
  30.3 0.8 %collective-permute-done.12.near_ref = f32[72,640]{1,0:T(8,128)S(1)} collective-permute-done((f32[72,640]{1,0:T(8,128)S(1)}, f32[72,640]{1,0:T(8,128)S(1)}, u32[]{:S(2)}, u32[]{:S(2)}) %collective-permute-start.12) | collective-permute-done | bytes 184352 | tf_op jit(solution)/shard_map/ppermute | solution.py:902
  31.1 1.2 %shard_map.150 = (f32[64,384]{1,0:T(8,128)S(1)}, f32[1,384]{1,0:T(1,128)S(1)}, s32[1,8,256]{2,1,0:T(8,128)S(1)}) custom-call(f32[64,1024]{1,0:T(8,128)S(1)} %get-tuple-element.138.r_ref.refs_0_, f32[72,640]{1,0:T(8,128)S(1)} %collective-permute-done.12.near_ref, s32[4,512]{1,0:T(4,128)S(1)} %get-tuple-element.140.gather_ref, ...), custom_call_target="tpu_custom_call" | custom-call | flops 100000000 | bytes 1 | tf_op jit(solution)/shard_map/pallas_call | solution.py:738
  32.3 2.1 %shard_map.151 = (f32[64,1024]{1,0:T(8,128)S(1)}, f32[16,128]{1,0:T(8,128)S(1)}) custom-call(f32[64,384]{1,0:T(8,128)S(1)} %get-tuple-element.142.right_ref, f32[1,384]{1,0:T(1,128)S(1)} %get-tuple-element.143.scale_ref, s32[1,8,256]{2,1,0:T(8,128)S(1)} %get-tuple-element.144.front_ref, f32[64,1024]{1,0:T(8,128)S(1)} %get-tuple-element.138.r_ref.refs_0_, ...), custom_call_target="tpu_custom_call" | custom-call | flops 3000000000 | bytes 1 | tf_op jit(solution)/shard_map/pallas_call | solution.py:738
  34.4 1.3 %collective-permute-start.15 = (f32[16,128]{1,0:T(8,128)S(1)}, f32[16,128]{1,0:T(8,128)S(1)}, u32[]{:S(2)}, u32[]{:S(2)}) collective-permute-start(f32[16,128]{1,0:T(8,128)S(1)} %get-tuple-element.149._), channel_id=1, source_target_pairs={{0,8},{1,9},{2,10},{3,11},{4,12},{5,13},{6,14},{7,15},{8,0},{9,1},... | collective-permute-start | bytes 24584 | tf_op jit(solution)/shard_map/ppermute | solution.py:808
  35.8 0.6 shard_map.152
  36.4 0.5 collective-permute-start.14
  36.9 1.5 %shard_map.153 = (f32[96,1024]{1,0:T(8,128)S(1)}, f32[64,1024]{1,0:T(8,128)S(1)}, f32[64,256]{1,0:T(8,128)S(1)}) custom-call(f32[64,1024]{1,0:T(8,128)S(1)} %get-tuple-element.148.p_ref.refs_0_, f32[96,1024]{1,0:T(8,128)S(1)} %get-tuple-element.150.refs_1_, f32[8,1024]{1,0:T(8,128)S(1)} %get-tuple-element.101.refs_2_, ...), custom_call_target="tpu_custom_call" | custom-call | flops 3000000000 | bytes 1 | tf_op jit(solution)/shard_map/pallas_call | solution.py:738
  38.3 0.7 %shard_map.154 = (f32[64,1024]{1,0:T(8,128)S(1)}, f32[64,1024]{1,0:T(8,128)S(1)}, f32[64,128]{1,0:T(8,128)S(1)}) custom-call(f32[64,1024]{1,0:T(8,128)S(1)} %get-tuple-element.138.r_ref.refs_0_, f32[96,1024]{1,0:T(8,128)S(1)} %get-tuple-element.152.refs_1_, f32[64,1024]{1,0:T(8,128)S(1)} %get-tuple-element.153.refs_2_, ...), custom_call_target="tpu_custom_call" | custom-call | flops 3000000000 | bytes 1 | tf_op jit(solution)/shard_map/pallas_call | solution.py:738
  39.1 0.4 shard_map.155.refs_9_
  39.5 1.9 %collective-permute-start.18 = (f32[16,128]{1,0:T(8,128)S(1)}, f32[16,128]{1,0:T(8,128)S(1)}, u32[]{:S(2)}, u32[]{:S(2)}) collective-permute-start(f32[16,128]{1,0:T(8,128)S(1)} %shard_map.155.refs_9_), channel_id=1, source_target_pairs={{0,8},{1,9},{2,10},{3,11},{4,12},{5,13},{6,14},{7,15},{8,0},{9,1},... | collective-permute-start | bytes 24584 | tf_op jit(solution)/shard_map/ppermute | solution.py:808
  41.6 0.8 %shard_map.156 = (f32[64,1024]{1,0:T(8,128)S(1)}, f32[64,1024]{1,0:T(8,128)S(1)}, f32[96,1024]{1,0:T(8,128)S(1)}, f32[16,512]{1,0:T(8,128)S(1)}) custom-call(f32[64,1024]{1,0:T(8,128)S(1)} %get-tuple-element.155.refs_0_, f32[16,128]{1,0:T(8,128)S(1)} %collective-permute-done.15.one_ref.refs_1_, f32[16,128]{1,0:T(8,128)S(1)} %collective-permute-done.16.two_ref.refs_2_, ...), custom_call_target="tpu_custom_call" | custom-call | flops 3000000000 | bytes 1 | tf_op jit(solution)/shard_map/pallas_call | solution.py:738
  42.8 1.5 %shard_map.157 = (f32[96,1024]{1,0:T(8,128)S(1)}, f32[64,1024]{1,0:T(8,128)S(1)}, f32[64,256]{1,0:T(8,128)S(1)}) custom-call(f32[64,1024]{1,0:T(8,128)S(1)} %get-tuple-element.159.refs_0_.refs_7_, f32[96,1024]{1,0:T(8,128)S(1)} %get-tuple-element.160.refs_1_, f32[8,1024]{1,0:T(8,128)S(1)} %get-tuple-element.101.refs_2_, ...), custom_call_target="tpu_custom_call" | custom-call | flops 3000000000 | bytes 1 | tf_op jit(solution)/shard_map/pallas_call | solution.py:738
  44.3 0.7 %shard_map.158 = (f32[64,1024]{1,0:T(8,128)S(1)}, f32[64,1024]{1,0:T(8,128)S(1)}, f32[64,128]{1,0:T(8,128)S(1)}) custom-call(f32[64,1024]{1,0:T(8,128)S(1)} %get-tuple-element.158.refs_0_, f32[96,1024]{1,0:T(8,128)S(1)} %get-tuple-element.162.refs_1_, f32[64,1024]{1,0:T(8,128)S(1)} %get-tuple-element.163.refs_2_, f32[16,512]{1,0:T(8,128)S(1)} %get-tuple-element.164.refs_3_, ...), custom_call_target="tpu_custom_call" | custom-call | flops 3000000000 | bytes 1 | tf_op jit(solution)/shard_map/pallas_call | solution.py:738
  45.0 0.4 shard_map.159.refs_9_
  45.4 0.9 %collective-permute-start.21 = (f32[16,128]{1,0:T(8,128)S(1)}, f32[16,128]{1,0:T(8,128)S(1)}, u32[]{:S(2)}, u32[]{:S(2)}) collective-permute-start(f32[16,128]{1,0:T(8,128)S(1)} %shard_map.159.refs_9_), channel_id=1, source_target_pairs={{0,8},{1,9},{2,10},{3,11},{4,12},{5,13},{6,14},{7,15},{8,0},{9,1},... | collective-permute-start | bytes 24584 | tf_op jit(solution)/shard_map/ppermute | solution.py:808
  46.5 0.8 %shard_map.160 = (f32[64,1024]{1,0:T(8,128)S(1)}, f32[64,1024]{1,0:T(8,128)S(1)}, f32[96,1024]{1,0:T(8,128)S(1)}, f32[16,512]{1,0:T(8,128)S(1)}) custom-call(f32[64,1024]{1,0:T(8,128)S(1)} %get-tuple-element.165.refs_0_, f32[16,128]{1,0:T(8,128)S(1)} %collective-permute-done.18.one_ref.refs_1_, f32[16,128]{1,0:T(8,128)S(1)} %collective-permute-done.19.two_ref.refs_2_, ...), custom_call_target="tpu_custom_call" | custom-call | flops 3000000000 | bytes 1 | tf_op jit(solution)/shard_map/pallas_call | solution.py:738
  47.7 1.5 %shard_map.161 = (f32[96,1024]{1,0:T(8,128)S(1)}, f32[64,1024]{1,0:T(8,128)S(1)}, f32[64,256]{1,0:T(8,128)S(1)}) custom-call(f32[64,1024]{1,0:T(8,128)S(1)} %get-tuple-element.169.refs_0_.refs_7_, f32[96,1024]{1,0:T(8,128)S(1)} %get-tuple-element.170.refs_1_, f32[8,1024]{1,0:T(8,128)S(1)} %get-tuple-element.101.refs_2_, ...), custom_call_target="tpu_custom_call" | custom-call | flops 3000000000 | bytes 1 | tf_op jit(solution)/shard_map/pallas_call | solution.py:738
  49.2 0.7 %shard_map.162 = (f32[64,1024]{1,0:T(8,128)S(1)}, f32[64,1024]{1,0:T(8,128)S(1)}, f32[64,128]{1,0:T(8,128)S(1)}) custom-call(f32[64,1024]{1,0:T(8,128)S(1)} %get-tuple-element.168.refs_0_, f32[96,1024]{1,0:T(8,128)S(1)} %get-tuple-element.172.refs_1_, f32[64,1024]{1,0:T(8,128)S(1)} %get-tuple-element.173.refs_2_, f32[16,512]{1,0:T(8,128)S(1)} %get-tuple-element.174.refs_3_, ...), custom_call_target="tpu_custom_call" | custom-call | flops 3000000000 | bytes 1 | tf_op jit(solution)/shard_map/pallas_call | solution.py:738
  49.9 0.4 shard_map.163.refs_9_
  50.3 1.6 %collective-permute-start.24 = (f32[16,128]{1,0:T(8,128)S(1)}, f32[16,128]{1,0:T(8,128)S(1)}, u32[]{:S(2)}, u32[]{:S(2)}) collective-permute-start(f32[16,128]{1,0:T(8,128)S(1)} %shard_map.163.refs_9_), channel_id=1, source_target_pairs={{0,8},{1,9},{2,10},{3,11},{4,12},{5,13},{6,14},{7,15},{8,0},{9,1},... | collective-permute-start | bytes 24584 | tf_op jit(solution)/shard_map/ppermute | solution.py:808
  52.1 0.8 %shard_map.164 = (f32[64,1024]{1,0:T(8,128)S(1)}, f32[64,1024]{1,0:T(8,128)S(1)}, f32[96,1024]{1,0:T(8,128)S(1)}, f32[16,512]{1,0:T(8,128)S(1)}) custom-call(f32[64,1024]{1,0:T(8,128)S(1)} %get-tuple-element.175.refs_0_, f32[16,128]{1,0:T(8,128)S(1)} %collective-permute-done.21.one_ref.refs_1_, f32[16,128]{1,0:T(8,128)S(1)} %collective-permute-done.22.two_ref.refs_2_, ...), custom_call_target="tpu_custom_call" | custom-call | flops 3000000000 | bytes 1 | tf_op jit(solution)/shard_map/pallas_call | solution.py:738
  53.3 1.0 %shard_map.165 = (f32[96,256]{1,0:T(8,128)S(1)}, f32[64,256]{1,0:T(8,128)S(1)}, f32[64,256]{1,0:T(8,128)}) custom-call(f32[64,1024]{1,0:T(8,128)S(1)} %get-tuple-element.178.refs_0_, f32[96,1024]{1,0:T(8,128)S(1)} %get-tuple-element.179.refs_1_, f32[8,1024]{1,0:T(8,128)S(1)} %get-tuple-element.101.refs_2_, s32[8,1024]{1,0:T(8,128)S(1)} %get-tuple-element.102.refs_3_, ...), custom_call_target="tpu_custom_call" | custom-call | flops 3000000000 | bytes 1 | tf_op jit(solution)/shard_map/pallas_call | solution.py:738
  54.7 0.9 %shard_map.167 = f32[64,256]{1,0:T(8,128)} custom-call(f32[64,256]{1,0:T(8,128)S(1)} %shard_map.166.refs_0_, f32[16,128]{1,0:T(8,128)S(1)} %collective-permute-done.24.refs_1_, f32[16,128]{1,0:T(8,128)S(1)} %collective-permute-done.25.refs_2_, s32[8,1024]{1,0:T(8,128)S(1)} %get-tuple-element.113.edge_ref.refs_3_, ...), custom_call_target="tpu_custom_call" | custom-call | flops 3000000000 | bytes 1 | tf_op jit(solution)/shard_map/pallas_call | solution.py:738
  (49 shorter events, 5.1 us)
Async XLA Ops:
  0.6 5.6 %copy-start.1 = (f32[2,64,64]{2,1,0:T(8,128)S(1)}, f32[2,64,64]{2,1,0:T(8,128)}, u32[]{:S(2)}) copy-start(f32[2,64,64]{2,1,0:T(8,128)} %refs_4_.1) | copy-start | bytes 98308
  0.6 5.6 %copy-start.2 = (f32[96,64]{0,1:T(8,128)S(1)}, f32[96,64]{0,1:T(8,128)}, u32[]{:S(2)}) copy-start(f32[96,64]{0,1:T(8,128)} %param.16) | copy-start | bytes 73732
  1.6 6.5 %collective-permute-start = (f32[80,256]{1,0:T(8,128)S(1)}, f32[80,256]{1,0:T(8,128)S(1)}, u32[]{:S(2)}, u32[]{:S(2)}) collective-permute-start(f32[80,256]{1,0:T(8,128)S(1)} %shard_map.131.refs_0_), channel_id=1, source_target_pairs={{0,6},{1,7},{2,4},{3,5},{4,2},{5,3},{6,0},{7,1},{8,14},{9,15},{10,... | collective-permute-start | bytes 245768 | tf_op jit(solution)/shard_map/ppermute | solution.py:835
  5.6 4.4 %collective-permute-start.1 = (f32[80,256]{1,0:T(8,128)S(1)}, f32[80,256]{1,0:T(8,128)S(1)}, u32[]{:S(2)}, u32[]{:S(2)}) collective-permute-start(f32[80,256]{1,0:T(8,128)S(1)} %shard_map.131.refs_0_), channel_id=1, source_target_pairs={{0,4},{1,5},{2,6},{3,7},{4,0},{5,1},{6,2},{7,3},{8,12},{9,13},{10,... | collective-permute-start | bytes 245768 | tf_op jit(solution)/shard_map/ppermute | solution.py:835
  6.1 4.4 %collective-permute-start.2 = (f32[80,256]{1,0:T(8,128)S(1)}, f32[80,256]{1,0:T(8,128)S(1)}, u32[]{:S(2)}, u32[]{:S(2)}) collective-permute-start(f32[80,256]{1,0:T(8,128)S(1)} %shard_map.131.refs_0_), channel_id=1, source_target_pairs={{0,2},{1,3},{2,0},{3,1},{4,6},{5,7},{6,4},{7,5},{8,10},{9,11},{10,... | collective-permute-start | bytes 245768 | tf_op jit(solution)/shard_map/ppermute | solution.py:835
  6.2 1.0 %copy-start = (f32[8,64,64]{2,1,0:T(8,128)S(1)}, f32[8,64,64]{2,1,0:T(8,128)}, u32[]{:S(2)}) copy-start(f32[8,64,64]{2,1,0:T(8,128)} %restriction_ref.1) | copy-start | bytes 393220
  6.2 1.0 %copy-start.3 = (f32[64,64]{1,0:T(8,128)S(1)}, f32[64,64]{1,0:T(8,128)}, u32[]{:S(2)}) copy-start(f32[64,64]{1,0:T(8,128)} %stiff_ref.5) | copy-start | bytes 49156
  11.0 4.9 %collective-permute-start.4 = (f32[16,128]{1,0:T(8,128)S(1)}, f32[16,128]{1,0:T(8,128)S(1)}, u32[]{:S(2)}, u32[]{:S(2)}) collective-permute-start(f32[16,128]{1,0:T(8,128)S(1)} %get-tuple-element.99._), channel_id=1, source_target_pairs={{0,8},{1,9},{2,10},{3,11},{4,12},{5,13},{6,14},{7,15},{8,0},{9,1},... | collective-permute-start | bytes 24584 | tf_op jit(solution)/shard_map/ppermute | solution.py:808
  12.6 3.3 %collective-permute-start.5 = (f32[16,128]{1,0:T(8,128)S(1)}, f32[16,128]{1,0:T(8,128)S(1)}, u32[]{:S(2)}, u32[]{:S(2)}) collective-permute-start(f32[16,128]{1,0:T(8,128)S(1)} %get-tuple-element.99._), channel_id=1, source_target_pairs={{0,1},{1,0},{2,3},{3,2},{4,5},{5,4},{6,7},{7,6},{8,16},{9,17},{10,... | collective-permute-start | bytes 24584 | tf_op jit(solution)/shard_map/ppermute | solution.py:808
  13.0 2.2 %collective-permute-start.3 = (f32[16,512]{1,0:T(8,128)S(1)}, f32[16,512]{1,0:T(8,128)S(1)}, u32[]{:S(2)}, u32[]{:S(2)}) collective-permute-start(f32[16,512]{1,0:T(8,128)S(1)} %get-tuple-element.107.refs_3_), channel_id=1, source_target_pairs={{0,1},{1,0},{2,3},{3,2},{4,5},{5,4},{6,7},{7,6},{8,9},{9,8},{10,11... | collective-permute-start | bytes 98312 | tf_op jit(solution)/shard_map/ppermute | solution.py:860
  16.4 6.3 %collective-permute-start.7 = (f32[16,128]{1,0:T(8,128)S(1)}, f32[16,128]{1,0:T(8,128)S(1)}, u32[]{:S(2)}, u32[]{:S(2)}) collective-permute-start(f32[16,128]{1,0:T(8,128)S(1)} %shard_map.139.refs_9_), channel_id=1, source_target_pairs={{0,8},{1,9},{2,10},{3,11},{4,12},{5,13},{6,14},{7,15},{8,0},{9,1},... | collective-permute-start | bytes 24584 | tf_op jit(solution)/shard_map/ppermute | solution.py:808
  19.1 3.6 %collective-permute-start.8 = (f32[16,128]{1,0:T(8,128)S(1)}, f32[16,128]{1,0:T(8,128)S(1)}, u32[]{:S(2)}, u32[]{:S(2)}) collective-permute-start(f32[16,128]{1,0:T(8,128)S(1)} %shard_map.139.refs_9_), channel_id=1, source_target_pairs={{0,1},{1,0},{2,3},{3,2},{4,5},{5,4},{6,7},{7,6},{8,16},{9,17},{10,... | collective-permute-start | bytes 24584 | tf_op jit(solution)/shard_map/ppermute | solution.py:808
  20.1 1.8 %collective-permute-start.6 = (f32[16,512]{1,0:T(8,128)S(1)}, f32[16,512]{1,0:T(8,128)S(1)}, u32[]{:S(2)}, u32[]{:S(2)}) collective-permute-start(f32[16,512]{1,0:T(8,128)S(1)} %get-tuple-element.125.refs_3_), channel_id=1, source_target_pairs={{0,1},{1,0},{2,3},{3,2},{4,5},{5,4},{6,7},{7,6},{8,9},{9,8},{10,11... | collective-permute-start | bytes 98312 | tf_op jit(solution)/shard_map/ppermute | solution.py:860
  23.1 4.0 %collective-permute-start.10 = (f32[16,128]{1,0:T(8,128)S(1)}, f32[16,128]{1,0:T(8,128)S(1)}, u32[]{:S(2)}, u32[]{:S(2)}) collective-permute-start(f32[16,128]{1,0:T(8,128)S(1)} %shard_map.143.refs_9_), channel_id=1, source_target_pairs={{0,8},{1,9},{2,10},{3,11},{4,12},{5,13},{6,14},{7,15},{8,0},{9,1},... | collective-permute-start | bytes 24584 | tf_op jit(solution)/shard_map/ppermute | solution.py:808
  23.6 3.5 %collective-permute-start.11 = (f32[16,128]{1,0:T(8,128)S(1)}, f32[16,128]{1,0:T(8,128)S(1)}, u32[]{:S(2)}, u32[]{:S(2)}) collective-permute-start(f32[16,128]{1,0:T(8,128)S(1)} %shard_map.143.refs_9_), channel_id=1, source_target_pairs={{0,1},{1,0},{2,3},{3,2},{4,5},{5,4},{6,7},{7,6},{8,16},{9,17},{10,... | collective-permute-start | bytes 24584 | tf_op jit(solution)/shard_map/ppermute | solution.py:808
  24.7 1.8 %collective-permute-start.9 = (f32[16,512]{1,0:T(8,128)S(1)}, f32[16,512]{1,0:T(8,128)S(1)}, u32[]{:S(2)}, u32[]{:S(2)}) collective-permute-start(f32[16,512]{1,0:T(8,128)S(1)} %get-tuple-element.135.refs_3_), channel_id=1, source_target_pairs={{0,1},{1,0},{2,3},{3,2},{4,5},{5,4},{6,7},{7,6},{8,9},{9,8},{10,11... | collective-permute-start | bytes 98312 | tf_op jit(solution)/shard_map/ppermute | solution.py:860
  27.4 4.9 %collective-permute-start.13 = (f32[72,128]{1,0:T(8,128)S(1)}, f32[72,128]{1,0:T(8,128)S(1)}, u32[]{:S(2)}, u32[]{:S(2)}) collective-permute-start(f32[72,128]{1,0:T(8,128)S(1)} %shard_map.147.refs_7_), channel_id=1, source_target_pairs={{0,2},{1,8},{2,0},{3,10},{4,6},{5,12},{6,4},{7,14},{8,1},{9,16},{1... | collective-permute-start | bytes 110600 | tf_op jit(solution)/shard_map/ppermute | solution.py:901
  29.0 2.1 %collective-permute-start.12 = (f32[72,640]{1,0:T(8,128)S(1)}, f32[72,640]{1,0:T(8,128)S(1)}, u32[]{:S(2)}, u32[]{:S(2)}) collective-permute-start(f32[72,640]{1,0:T(8,128)S(1)} %get-tuple-element.139), channel_id=1, source_target_pairs={{0,1},{1,0},{2,3},{3,2},{4,5},{5,4},{6,7},{7,6},{8,9},{9,8},{10,11... | collective-permute-start | bytes 552968 | tf_op jit(solution)/shard_map/ppermute | solution.py:902
  34.4 4.6 %collective-permute-start.15 = (f32[16,128]{1,0:T(8,128)S(1)}, f32[16,128]{1,0:T(8,128)S(1)}, u32[]{:S(2)}, u32[]{:S(2)}) collective-permute-start(f32[16,128]{1,0:T(8,128)S(1)} %get-tuple-element.149._), channel_id=1, source_target_pairs={{0,8},{1,9},{2,10},{3,11},{4,12},{5,13},{6,14},{7,15},{8,0},{9,1},... | collective-permute-start | bytes 24584 | tf_op jit(solution)/shard_map/ppermute | solution.py:808
  35.7 3.3 %collective-permute-start.16 = (f32[16,128]{1,0:T(8,128)S(1)}, f32[16,128]{1,0:T(8,128)S(1)}, u32[]{:S(2)}, u32[]{:S(2)}) collective-permute-start(f32[16,128]{1,0:T(8,128)S(1)} %get-tuple-element.149._), channel_id=1, source_target_pairs={{0,1},{1,0},{2,3},{3,2},{4,5},{5,4},{6,7},{7,6},{8,16},{9,17},{10,... | collective-permute-start | bytes 24584 | tf_op jit(solution)/shard_map/ppermute | solution.py:808
  36.4 2.0 %collective-permute-start.14 = (f32[16,512]{1,0:T(8,128)S(1)}, f32[16,512]{1,0:T(8,128)S(1)}, u32[]{:S(2)}, u32[]{:S(2)}) collective-permute-start(f32[16,512]{1,0:T(8,128)S(1)} %get-tuple-element.154.refs_3_), channel_id=1, source_target_pairs={{0,1},{1,0},{2,3},{3,2},{4,5},{5,4},{6,7},{7,6},{8,9},{9,8},{10,11... | collective-permute-start | bytes 98312 | tf_op jit(solution)/shard_map/ppermute | solution.py:860
  39.5 5.5 %collective-permute-start.18 = (f32[16,128]{1,0:T(8,128)S(1)}, f32[16,128]{1,0:T(8,128)S(1)}, u32[]{:S(2)}, u32[]{:S(2)}) collective-permute-start(f32[16,128]{1,0:T(8,128)S(1)} %shard_map.155.refs_9_), channel_id=1, source_target_pairs={{0,8},{1,9},{2,10},{3,11},{4,12},{5,13},{6,14},{7,15},{8,0},{9,1},... | collective-permute-start | bytes 24584 | tf_op jit(solution)/shard_map/ppermute | solution.py:808
  41.4 3.6 %collective-permute-start.19 = (f32[16,128]{1,0:T(8,128)S(1)}, f32[16,128]{1,0:T(8,128)S(1)}, u32[]{:S(2)}, u32[]{:S(2)}) collective-permute-start(f32[16,128]{1,0:T(8,128)S(1)} %shard_map.155.refs_9_), channel_id=1, source_target_pairs={{0,1},{1,0},{2,3},{3,2},{4,5},{5,4},{6,7},{7,6},{8,16},{9,17},{10,... | collective-permute-start | bytes 24584 | tf_op jit(solution)/shard_map/ppermute | solution.py:808
  42.4 1.8 %collective-permute-start.17 = (f32[16,512]{1,0:T(8,128)S(1)}, f32[16,512]{1,0:T(8,128)S(1)}, u32[]{:S(2)}, u32[]{:S(2)}) collective-permute-start(f32[16,512]{1,0:T(8,128)S(1)} %get-tuple-element.164.refs_3_), channel_id=1, source_target_pairs={{0,1},{1,0},{2,3},{3,2},{4,5},{5,4},{6,7},{7,6},{8,9},{9,8},{10,11... | collective-permute-start | bytes 98312 | tf_op jit(solution)/shard_map/ppermute | solution.py:860
  45.4 4.4 %collective-permute-start.21 = (f32[16,128]{1,0:T(8,128)S(1)}, f32[16,128]{1,0:T(8,128)S(1)}, u32[]{:S(2)}, u32[]{:S(2)}) collective-permute-start(f32[16,128]{1,0:T(8,128)S(1)} %shard_map.159.refs_9_), channel_id=1, source_target_pairs={{0,8},{1,9},{2,10},{3,11},{4,12},{5,13},{6,14},{7,15},{8,0},{9,1},... | collective-permute-start | bytes 24584 | tf_op jit(solution)/shard_map/ppermute | solution.py:808
  46.3 3.6 %collective-permute-start.22 = (f32[16,128]{1,0:T(8,128)S(1)}, f32[16,128]{1,0:T(8,128)S(1)}, u32[]{:S(2)}, u32[]{:S(2)}) collective-permute-start(f32[16,128]{1,0:T(8,128)S(1)} %shard_map.159.refs_9_), channel_id=1, source_target_pairs={{0,1},{1,0},{2,3},{3,2},{4,5},{5,4},{6,7},{7,6},{8,16},{9,17},{10,... | collective-permute-start | bytes 24584 | tf_op jit(solution)/shard_map/ppermute | solution.py:808
  47.3 1.8 %collective-permute-start.20 = (f32[16,512]{1,0:T(8,128)S(1)}, f32[16,512]{1,0:T(8,128)S(1)}, u32[]{:S(2)}, u32[]{:S(2)}) collective-permute-start(f32[16,512]{1,0:T(8,128)S(1)} %get-tuple-element.174.refs_3_), channel_id=1, source_target_pairs={{0,1},{1,0},{2,3},{3,2},{4,5},{5,4},{6,7},{7,6},{8,9},{9,8},{10,11... | collective-permute-start | bytes 98312 | tf_op jit(solution)/shard_map/ppermute | solution.py:860
  50.3 4.3 %collective-permute-start.24 = (f32[16,128]{1,0:T(8,128)S(1)}, f32[16,128]{1,0:T(8,128)S(1)}, u32[]{:S(2)}, u32[]{:S(2)}) collective-permute-start(f32[16,128]{1,0:T(8,128)S(1)} %shard_map.163.refs_9_), channel_id=1, source_target_pairs={{0,8},{1,9},{2,10},{3,11},{4,12},{5,13},{6,14},{7,15},{8,0},{9,1},... | collective-permute-start | bytes 24584 | tf_op jit(solution)/shard_map/ppermute | solution.py:808
  51.9 2.8 %collective-permute-start.25 = (f32[16,128]{1,0:T(8,128)S(1)}, f32[16,128]{1,0:T(8,128)S(1)}, u32[]{:S(2)}, u32[]{:S(2)}) collective-permute-start(f32[16,128]{1,0:T(8,128)S(1)} %shard_map.163.refs_9_), channel_id=1, source_target_pairs={{0,1},{1,0},{2,3},{3,2},{4,5},{5,4},{6,7},{7,6},{8,16},{9,17},{10,... | collective-permute-start | bytes 24584 | tf_op jit(solution)/shard_map/ppermute | solution.py:808
  53.0 1.4 %collective-permute-start.23 = (f32[16,512]{1,0:T(8,128)S(1)}, f32[16,512]{1,0:T(8,128)S(1)}, u32[]{:S(2)}, u32[]{:S(2)}) collective-permute-start(f32[16,512]{1,0:T(8,128)S(1)} %get-tuple-element.185.refs_3_), channel_id=1, source_target_pairs={{0,1},{1,0},{2,3},{3,2},{4,5},{5,4},{6,7},{7,6},{8,9},{9,8},{10,11... | collective-permute-start | bytes 98312 | tf_op jit(solution)/shard_map/ppermute | solution.py:860

commit v9 on v8

--- a/solution.py
+++ b/solution.py
@@ -157,7 +157,12 @@
     for o in range(OCTANTS):
         rows = slice(o % pairs * modes, (o % pairs + 1) * modes)
         store_left(down_out, rows, restriction_ref[o], o // pairs * 3 * modes)
-        store_left(up_out, slice(0, modes), restriction_ref[o].T, o * 3 * modes)
+        high, low = halves(restriction_ref[o].T)
+        base = o * 2 * modes
+        up_out[:modes, base : base + modes] = high
+        up_out[:modes, base + modes : base + 2 * modes] = high
+        up_out[modes:, base : base + modes] = low
+        up_out[modes:, base + modes : base + 2 * modes] = jnp.zeros((modes, modes), jnp.bfloat16)
 
 
 def pack_kernel(
@@ -708,8 +713,9 @@
         parts = []
         for o in range(OCTANTS):
             mine = (octant == o).astype(jnp.float32).astype(jnp.bfloat16)
-            parts += [high * mine, low * mine, high * mine]
-        p = jnp.dot(up_ref[...], jnp.concatenate(parts, axis=0), preferred_element_type=jnp.float32)
+            parts += [high * mine, low * mine]
+        both = jnp.dot(up_ref[...], jnp.concatenate(parts, axis=0), preferred_element_type=jnp.float32)
+        p = both[:modes] + both[modes:]
         p_out[:, span] = p
         for i, j in enumerate(js):
             keep_edge(j, of_block(p, i, count), rim_ref, edge, rims)
@@ -815,7 +821,7 @@
     )
     down3, up3, c3 = run(
         prep_coarse_kernel,
-        [((LANES // parents * modes, OCTANTS * parents // LANES * 3 * modes), bf16), ((modes, OCTANTS * 3 * modes), bf16), ((modes, 3 * modes), bf16)],
+        [((LANES // parents * modes, OCTANTS * parents // LANES * 3 * modes), bf16), ((2 * modes, OCTANTS * 2 * modes), bf16), ((modes, 3 * modes), bf16)],
         restriction, coarse_stiffness,
     )
 

time: 55.8 us -> 55.6 us (level)
  no operation moved by 1% of the time
where the time goes in v9:
time: 55.6 us; the launch traced here: 55.5 us
  Pallas kernels  28.5 us (51%)
  starting transfers between devices  21.3 us (38%)
  waiting for transfers between devices  3.86 us (7%)
  between operations  1 us (2%)
  local copies, waits for them, and re-layouts  0.79 us (1%)
    pallas_call x37, Pallas kernels, call(): pl.pallas_call(kernel, out_shape=[jax.ShapeDtypeStruct(shape, kind) for s...  28.5 us
    ppermute x14, starting transfers between devices, over_segments(): return (lax.ppermute(rim, both, ones), lax.ppermute(rim, both, twos))  11.7 us
    ppermute x3, starting transfers between devices, local(): lax.ppermute(packed, 'sub', [(s, s ^ CORES * k) for s in range(peers)])  4.6 us
    ppermute x3, waiting for transfers between devices, local(): lax.ppermute(packed, 'sub', [(s, s ^ CORES * k) for s in range(peers)])  2.99 us
    ppermute x7, starting transfers between devices, apply(): swapped = lax.ppermute(sub_out, 'sub', cores)  2.89 us
  transfers between devices with their start and end apart: 26, of which 4 were waited for; matrix products, arithmetic and copies ran while one was open for 0% of the time, Pallas kernels for 39%

profile of v9, /device:TPU:0, one launch (start us, length us, event | category | flops | bytes accessed | tf_op | source)
XLA Modules:
  0.0 55.5 jit_solution(5328241121667225444)
XLA Ops:
  0.7 1.0 %shard_map.131.refs_0_ = f32[80,256]{1,0:T(8,128)S(1)} custom-call(f32[64,256]{1,0:T(8,128)} %b_ref.1, f32[1,256]{1,0:T(1,128)} %bitcast.6, s32[1,256]{1,0:T(1,128)} %bitcast.7, s32[6,256]{1,0:T(8,128)} %face_ref.1, s32[1,128]{1,0:T(1,128)} %sub_ref.1, s32[1,16]{1,0:T(1,128)} %rim_ref.1, s32[1,64]{1,0:T(1,128)} %size_ref.1, f32[1,64]{1,0:T(1,128)} %bitcast.8), custom_call_target="tpu_custom_call" | custom-call | flops 3000000000 | bytes 1 | tf_op jit(solution)/shard_map/pallas_call | solution.py:744
  1.6 4.0 %collective-permute-start = (f32[80,256]{1,0:T(8,128)S(1)}, f32[80,256]{1,0:T(8,128)S(1)}, u32[]{:S(2)}, u32[]{:S(2)}) collective-permute-start(f32[80,256]{1,0:T(8,128)S(1)} %shard_map.131.refs_0_), channel_id=1, source_target_pairs={{0,6},{1,7},{2,4},{3,5},{4,2},{5,3},{6,0},{7,1},{8,14},{9,15},{10,... | collective-permute-start | bytes 245768 | tf_op jit(solution)/shard_map/ppermute | solution.py:841
  5.6 0.5 collective-permute-start.1
  6.4 0.8 %copy-done = f32[8,64,64]{2,1,0:T(8,128)S(1)} copy-done((f32[8,64,64]{2,1,0:T(8,128)S(1)}, f32[8,64,64]{2,1,0:T(8,128)}, u32[]{:S(2)}) %copy-start) | copy-done | bytes 131096
  7.5 0.6 %collective-permute-done.refs_1_ = f32[80,256]{1,0:T(8,128)S(1)} collective-permute-done((f32[80,256]{1,0:T(8,128)S(1)}, f32[80,256]{1,0:T(8,128)S(1)}, u32[]{:S(2)}, u32[]{:S(2)}) %collective-permute-start) | collective-permute-done | bytes 81952 | tf_op jit(solution)/shard_map/ppermute | solution.py:841
  8.2 1.9 %collective-permute-done.1.refs_2_ = f32[80,256]{1,0:T(8,128)S(1)} collective-permute-done((f32[80,256]{1,0:T(8,128)S(1)}, f32[80,256]{1,0:T(8,128)S(1)}, u32[]{:S(2)}, u32[]{:S(2)}) %collective-permute-start.1) | collective-permute-done | bytes 81952 | tf_op jit(solution)/shard_map/ppermute | solution.py:841
  10.0 0.5 collective-permute-done.2.refs_3_
  10.5 0.5 shard_map.134
  11.0 1.6 %collective-permute-start.4 = (f32[16,128]{1,0:T(8,128)S(1)}, f32[16,128]{1,0:T(8,128)S(1)}, u32[]{:S(2)}, u32[]{:S(2)}) collective-permute-start(f32[16,128]{1,0:T(8,128)S(1)} %get-tuple-element.99._), channel_id=1, source_target_pairs={{0,8},{1,9},{2,10},{3,11},{4,12},{5,13},{6,14},{7,15},{8,0},{9,1},... | collective-permute-start | bytes 24584 | tf_op jit(solution)/shard_map/ppermute | solution.py:814
  12.6 0.4 shard_map.135
  13.0 0.6 %collective-permute-start.3 = (f32[16,512]{1,0:T(8,128)S(1)}, f32[16,512]{1,0:T(8,128)S(1)}, u32[]{:S(2)}, u32[]{:S(2)}) collective-permute-start(f32[16,512]{1,0:T(8,128)S(1)} %get-tuple-element.107.refs_3_), channel_id=1, source_target_pairs={{0,1},{1,0},{2,3},{3,2},{4,5},{5,4},{6,7},{7,6},{8,9},{9,8},{10,11... | collective-permute-start | bytes 98312 | tf_op jit(solution)/shard_map/ppermute | solution.py:866
  13.8 1.5 %shard_map.136 = (f32[96,1024]{1,0:T(8,128)S(1)}, f32[64,1024]{1,0:T(8,128)S(1)}, f32[64,256]{1,0:T(8,128)S(1)}) custom-call(f32[64,1024]{1,0:T(8,128)S(1)} %get-tuple-element.97.p_ref.refs_0_.refs_7_, f32[96,1024]{1,0:T(8,128)S(1)} %get-tuple-element.100.refs_1_, f32[8,1024]{1,0:T(8,128)S(1)} %get-tuple-element.101.refs_2_, ...), custom_call_target="tpu_custom_call" | custom-call | flops 3000000000 | bytes 1 | tf_op jit(solution)/shard_map/pallas_call | solution.py:744
  15.2 0.7 %shard_map.137 = (f32[64,1024]{1,0:T(8,128)S(1)}, f32[64,1024]{1,0:T(8,128)S(1)}, f32[64,128]{1,0:T(8,128)S(1)}) custom-call(f32[64,1024]{1,0:T(8,128)S(1)} %get-tuple-element.96.refs_0_, f32[96,1024]{1,0:T(8,128)S(1)} %get-tuple-element.105.refs_1_, f32[64,1024]{1,0:T(8,128)S(1)} %get-tuple-element.106.refs_2_, f32[16,512]{1,0:T(8,128)S(1)} %get-tuple-element.107.refs_3_, ...), custom_call_target="tpu_custom_call" | custom-call | flops 3000000000 | bytes 1 | tf_op jit(solution)/shard_map/pallas_call | solution.py:744
  16.0 0.4 shard_map.139.refs_9_
  16.4 2.7 %collective-permute-start.7 = (f32[16,128]{1,0:T(8,128)S(1)}, f32[16,128]{1,0:T(8,128)S(1)}, u32[]{:S(2)}, u32[]{:S(2)}) collective-permute-start(f32[16,128]{1,0:T(8,128)S(1)} %shard_map.139.refs_9_), channel_id=1, source_target_pairs={{0,8},{1,9},{2,10},{3,11},{4,12},{5,13},{6,14},{7,15},{8,0},{9,1},... | collective-permute-start | bytes 24584 | tf_op jit(solution)/shard_map/ppermute | solution.py:814
  19.3 0.8 %shard_map.140 = (f32[64,1024]{1,0:T(8,128)S(1)}, f32[64,1024]{1,0:T(8,128)S(1)}, f32[96,1024]{1,0:T(8,128)S(1)}, f32[16,512]{1,0:T(8,128)S(1)}) custom-call(f32[64,1024]{1,0:T(8,128)S(1)} %get-tuple-element.112.refs_0_, f32[16,128]{1,0:T(8,128)S(1)} %collective-permute-done.4.one_ref.refs_1_, f32[16,128]{1,0:T(8,128)S(1)} %collective-permute-done.5.two_ref.refs_2_, ...), custom_call_target="tpu_custom_call" | custom-call | flops 3000000000 | bytes 1 | tf_op jit(solution)/shard_map/pallas_call | solution.py:744
  20.5 1.5 %shard_map.141 = (f32[96,1024]{1,0:T(8,128)S(1)}, f32[64,1024]{1,0:T(8,128)S(1)}, f32[64,256]{1,0:T(8,128)S(1)}) custom-call(f32[64,1024]{1,0:T(8,128)S(1)} %get-tuple-element.120.refs_0_.refs_7_, f32[96,1024]{1,0:T(8,128)S(1)} %get-tuple-element.121.refs_1_, f32[8,1024]{1,0:T(8,128)S(1)} %get-tuple-element.101.refs_2_, ...), custom_call_target="tpu_custom_call" | custom-call | flops 3000000000 | bytes 1 | tf_op jit(solution)/shard_map/pallas_call | solution.py:744
  22.0 0.7 %shard_map.142 = (f32[64,1024]{1,0:T(8,128)S(1)}, f32[64,1024]{1,0:T(8,128)S(1)}, f32[64,128]{1,0:T(8,128)S(1)}) custom-call(f32[64,1024]{1,0:T(8,128)S(1)} %get-tuple-element.119.refs_0_, f32[96,1024]{1,0:T(8,128)S(1)} %get-tuple-element.123.refs_1_, f32[64,1024]{1,0:T(8,128)S(1)} %get-tuple-element.124.refs_2_, f32[16,512]{1,0:T(8,128)S(1)} %get-tuple-element.125.refs_3_, ...), custom_call_target="tpu_custom_call" | custom-call | flops 3000000000 | bytes 1 | tf_op jit(solution)/shard_map/pallas_call | solution.py:744
  22.7 0.4 shard_map.143.refs_9_
  23.1 0.5 collective-permute-start.10
  23.9 0.8 %shard_map.144 = (f32[64,1024]{1,0:T(8,128)S(1)}, f32[64,1024]{1,0:T(8,128)S(1)}, f32[96,1024]{1,0:T(8,128)S(1)}, f32[16,512]{1,0:T(8,128)S(1)}) custom-call(f32[64,1024]{1,0:T(8,128)S(1)} %get-tuple-element.126.refs_0_, f32[16,128]{1,0:T(8,128)S(1)} %collective-permute-done.7.one_ref.refs_1_, f32[16,128]{1,0:T(8,128)S(1)} %collective-permute-done.8.two_ref.refs_2_, ...), custom_call_target="tpu_custom_call" | custom-call | flops 3000000000 | bytes 1 | tf_op jit(solution)/shard_map/pallas_call | solution.py:744
  25.0 1.5 %shard_map.145 = (f32[96,1024]{1,0:T(8,128)S(1)}, f32[64,1024]{1,0:T(8,128)S(1)}, f32[64,256]{1,0:T(8,128)S(1)}) custom-call(f32[64,1024]{1,0:T(8,128)S(1)} %get-tuple-element.130.refs_0_, f32[96,1024]{1,0:T(8,128)S(1)} %get-tuple-element.131.refs_1_, f32[8,1024]{1,0:T(8,128)S(1)} %get-tuple-element.101.refs_2_, s32[8,1024]{1,0:T(8,128)S(1)} %get-tuple-element.102.refs_3_, ...), custom_call_target="tpu_custom_call" | custom-call | flops 3000000000 | bytes 1 | tf_op jit(solution)/shard_map/pallas_call | solution.py:744
  26.5 0.6 %shard_map.146.r_ref.refs_0_ = f32[64,1024]{1,0:T(8,128)S(1)} custom-call(f32[64,1024]{1,0:T(8,128)S(1)} %get-tuple-element.129.refs_0_, f32[96,1024]{1,0:T(8,128)S(1)} %get-tuple-element.133.refs_1_, f32[64,1024]{1,0:T(8,128)S(1)} %get-tuple-element.134.refs_2_, f32[16,512]{1,0:T(8,128)S(1)} %get-tuple-element.135.refs_3_, ...), custom_call_target="tpu_custom_call" | custom-call | flops 3000000000 | bytes 1 | tf_op jit(solution)/shard_map/pallas_call | solution.py:744
  27.4 1.0 %collective-permute-start.13 = (f32[72,128]{1,0:T(8,128)S(1)}, f32[72,128]{1,0:T(8,128)S(1)}, u32[]{:S(2)}, u32[]{:S(2)}) collective-permute-start(f32[72,128]{1,0:T(8,128)S(1)} %shard_map.147.refs_7_), channel_id=1, source_target_pairs={{0,2},{1,8},{2,0},{3,10},{4,6},{5,12},{6,4},{7,14},{8,1},{9,16},{1... | collective-permute-start | bytes 110600 | tf_op jit(solution)/shard_map/ppermute | solution.py:907
  28.4 0.5 shard_map.148
  29.0 1.1 %collective-permute-start.12 = (f32[72,640]{1,0:T(8,128)S(1)}, f32[72,640]{1,0:T(8,128)S(1)}, u32[]{:S(2)}, u32[]{:S(2)}) collective-permute-start(f32[72,640]{1,0:T(8,128)S(1)} %get-tuple-element.139), channel_id=1, source_target_pairs={{0,1},{1,0},{2,3},{3,2},{4,5},{5,4},{6,7},{7,6},{8,9},{9,8},{10,11... | collective-permute-start | bytes 552968 | tf_op jit(solution)/shard_map/ppermute | solution.py:908
  30.3 0.8 %collective-permute-done.12.near_ref = f32[72,640]{1,0:T(8,128)S(1)} collective-permute-done((f32[72,640]{1,0:T(8,128)S(1)}, f32[72,640]{1,0:T(8,128)S(1)}, u32[]{:S(2)}, u32[]{:S(2)}) %collective-permute-start.12) | collective-permute-done | bytes 184352 | tf_op jit(solution)/shard_map/ppermute | solution.py:908
  31.1 1.2 %shard_map.150 = (f32[64,384]{1,0:T(8,128)S(1)}, f32[1,384]{1,0:T(1,128)S(1)}, s32[1,8,256]{2,1,0:T(8,128)S(1)}) custom-call(f32[64,1024]{1,0:T(8,128)S(1)} %get-tuple-element.138.r_ref.refs_0_, f32[72,640]{1,0:T(8,128)S(1)} %collective-permute-done.12.near_ref, s32[4,512]{1,0:T(4,128)S(1)} %get-tuple-element.140.gather_ref, ...), custom_call_target="tpu_custom_call" | custom-call | flops 100000000 | bytes 1 | tf_op jit(solution)/shard_map/pallas_call | solution.py:744
  32.3 1.9 %shard_map.151 = (f32[64,1024]{1,0:T(8,128)S(1)}, f32[16,128]{1,0:T(8,128)S(1)}) custom-call(f32[64,384]{1,0:T(8,128)S(1)} %get-tuple-element.142.right_ref, f32[1,384]{1,0:T(1,128)S(1)} %get-tuple-element.143.scale_ref, s32[1,8,256]{2,1,0:T(8,128)S(1)} %get-tuple-element.144.front_ref, f32[64,1024]{1,0:T(8,128)S(1)} %get-tuple-element.138.r_ref.refs_0_, ...), custom_call_target="tpu_custom_call" | custom-call | flops 3000000000 | bytes 1 | tf_op jit(solution)/shard_map/pallas_call | solution.py:744
  34.3 1.3 %collective-permute-start.15 = (f32[16,128]{1,0:T(8,128)S(1)}, f32[16,128]{1,0:T(8,128)S(1)}, u32[]{:S(2)}, u32[]{:S(2)}) collective-permute-start(f32[16,128]{1,0:T(8,128)S(1)} %get-tuple-element.149._), channel_id=1, source_target_pairs={{0,8},{1,9},{2,10},{3,11},{4,12},{5,13},{6,14},{7,15},{8,0},{9,1},... | collective-permute-start | bytes 24584 | tf_op jit(solution)/shard_map/ppermute | solution.py:814
  36.0 0.5 collective-permute-start.14
  36.5 1.6 %shard_map.153 = (f32[96,1024]{1,0:T(8,128)S(1)}, f32[64,1024]{1,0:T(8,128)S(1)}, f32[64,256]{1,0:T(8,128)S(1)}) custom-call(f32[64,1024]{1,0:T(8,128)S(1)} %get-tuple-element.148.p_ref.refs_0_, f32[96,1024]{1,0:T(8,128)S(1)} %get-tuple-element.150.refs_1_, f32[8,1024]{1,0:T(8,128)S(1)} %get-tuple-element.101.refs_2_, ...), custom_call_target="tpu_custom_call" | custom-call | flops 3000000000 | bytes 1 | tf_op jit(solution)/shard_map/pallas_call | solution.py:744
  38.2 0.7 %shard_map.154 = (f32[64,1024]{1,0:T(8,128)S(1)}, f32[64,1024]{1,0:T(8,128)S(1)}, f32[64,128]{1,0:T(8,128)S(1)}) custom-call(f32[64,1024]{1,0:T(8,128)S(1)} %get-tuple-element.138.r_ref.refs_0_, f32[96,1024]{1,0:T(8,128)S(1)} %get-tuple-element.152.refs_1_, f32[64,1024]{1,0:T(8,128)S(1)} %get-tuple-element.153.refs_2_, ...), custom_call_target="tpu_custom_call" | custom-call | flops 3000000000 | bytes 1 | tf_op jit(solution)/shard_map/pallas_call | solution.py:744
  38.9 0.4 shard_map.155.refs_9_
  39.3 1.9 %collective-permute-start.18 = (f32[16,128]{1,0:T(8,128)S(1)}, f32[16,128]{1,0:T(8,128)S(1)}, u32[]{:S(2)}, u32[]{:S(2)}) collective-permute-start(f32[16,128]{1,0:T(8,128)S(1)} %shard_map.155.refs_9_), channel_id=1, source_target_pairs={{0,8},{1,9},{2,10},{3,11},{4,12},{5,13},{6,14},{7,15},{8,0},{9,1},... | collective-permute-start | bytes 24584 | tf_op jit(solution)/shard_map/ppermute | solution.py:814
  41.5 0.8 %shard_map.156 = (f32[64,1024]{1,0:T(8,128)S(1)}, f32[64,1024]{1,0:T(8,128)S(1)}, f32[96,1024]{1,0:T(8,128)S(1)}, f32[16,512]{1,0:T(8,128)S(1)}) custom-call(f32[64,1024]{1,0:T(8,128)S(1)} %get-tuple-element.155.refs_0_, f32[16,128]{1,0:T(8,128)S(1)} %collective-permute-done.15.one_ref.refs_1_, f32[16,128]{1,0:T(8,128)S(1)} %collective-permute-done.16.two_ref.refs_2_, ...), custom_call_target="tpu_custom_call" | custom-call | flops 3000000000 | bytes 1 | tf_op jit(solution)/shard_map/pallas_call | solution.py:744
  42.6 1.5 %shard_map.157 = (f32[96,1024]{1,0:T(8,128)S(1)}, f32[64,1024]{1,0:T(8,128)S(1)}, f32[64,256]{1,0:T(8,128)S(1)}) custom-call(f32[64,1024]{1,0:T(8,128)S(1)} %get-tuple-element.159.refs_0_.refs_7_, f32[96,1024]{1,0:T(8,128)S(1)} %get-tuple-element.160.refs_1_, f32[8,1024]{1,0:T(8,128)S(1)} %get-tuple-element.101.refs_2_, ...), custom_call_target="tpu_custom_call" | custom-call | flops 3000000000 | bytes 1 | tf_op jit(solution)/shard_map/pallas_call | solution.py:744
  44.1 0.7 %shard_map.158 = (f32[64,1024]{1,0:T(8,128)S(1)}, f32[64,1024]{1,0:T(8,128)S(1)}, f32[64,128]{1,0:T(8,128)S(1)}) custom-call(f32[64,1024]{1,0:T(8,128)S(1)} %get-tuple-element.158.refs_0_, f32[96,1024]{1,0:T(8,128)S(1)} %get-tuple-element.162.refs_1_, f32[64,1024]{1,0:T(8,128)S(1)} %get-tuple-element.163.refs_2_, f32[16,512]{1,0:T(8,128)S(1)} %get-tuple-element.164.refs_3_, ...), custom_call_target="tpu_custom_call" | custom-call | flops 3000000000 | bytes 1 | tf_op jit(solution)/shard_map/pallas_call | solution.py:744
  44.8 0.4 shard_map.159.refs_9_
  45.3 0.9 %collective-permute-start.21 = (f32[16,128]{1,0:T(8,128)S(1)}, f32[16,128]{1,0:T(8,128)S(1)}, u32[]{:S(2)}, u32[]{:S(2)}) collective-permute-start(f32[16,128]{1,0:T(8,128)S(1)} %shard_map.159.refs_9_), channel_id=1, source_target_pairs={{0,8},{1,9},{2,10},{3,11},{4,12},{5,13},{6,14},{7,15},{8,0},{9,1},... | collective-permute-start | bytes 24584 | tf_op jit(solution)/shard_map/ppermute | solution.py:814
  46.4 0.8 %shard_map.160 = (f32[64,1024]{1,0:T(8,128)S(1)}, f32[64,1024]{1,0:T(8,128)S(1)}, f32[96,1024]{1,0:T(8,128)S(1)}, f32[16,512]{1,0:T(8,128)S(1)}) custom-call(f32[64,1024]{1,0:T(8,128)S(1)} %get-tuple-element.165.refs_0_, f32[16,128]{1,0:T(8,128)S(1)} %collective-permute-done.18.one_ref.refs_1_, f32[16,128]{1,0:T(8,128)S(1)} %collective-permute-done.19.two_ref.refs_2_, ...), custom_call_target="tpu_custom_call" | custom-call | flops 3000000000 | bytes 1 | tf_op jit(solution)/shard_map/pallas_call | solution.py:744
  47.5 1.5 %shard_map.161 = (f32[96,1024]{1,0:T(8,128)S(1)}, f32[64,1024]{1,0:T(8,128)S(1)}, f32[64,256]{1,0:T(8,128)S(1)}) custom-call(f32[64,1024]{1,0:T(8,128)S(1)} %get-tuple-element.169.refs_0_.refs_7_, f32[96,1024]{1,0:T(8,128)S(1)} %get-tuple-element.170.refs_1_, f32[8,1024]{1,0:T(8,128)S(1)} %get-tuple-element.101.refs_2_, ...), custom_call_target="tpu_custom_call" | custom-call | flops 3000000000 | bytes 1 | tf_op jit(solution)/shard_map/pallas_call | solution.py:744
  49.0 0.7 %shard_map.162 = (f32[64,1024]{1,0:T(8,128)S(1)}, f32[64,1024]{1,0:T(8,128)S(1)}, f32[64,128]{1,0:T(8,128)S(1)}) custom-call(f32[64,1024]{1,0:T(8,128)S(1)} %get-tuple-element.168.refs_0_, f32[96,1024]{1,0:T(8,128)S(1)} %get-tuple-element.172.refs_1_, f32[64,1024]{1,0:T(8,128)S(1)} %get-tuple-element.173.refs_2_, f32[16,512]{1,0:T(8,128)S(1)} %get-tuple-element.174.refs_3_, ...), custom_call_target="tpu_custom_call" | custom-call | flops 3000000000 | bytes 1 | tf_op jit(solution)/shard_map/pallas_call | solution.py:744
  49.7 0.4 shard_map.163.refs_9_
  50.2 1.6 %collective-permute-start.24 = (f32[16,128]{1,0:T(8,128)S(1)}, f32[16,128]{1,0:T(8,128)S(1)}, u32[]{:S(2)}, u32[]{:S(2)}) collective-permute-start(f32[16,128]{1,0:T(8,128)S(1)} %shard_map.163.refs_9_), channel_id=1, source_target_pairs={{0,8},{1,9},{2,10},{3,11},{4,12},{5,13},{6,14},{7,15},{8,0},{9,1},... | collective-permute-start | bytes 24584 | tf_op jit(solution)/shard_map/ppermute | solution.py:814
  52.0 0.8 %shard_map.164 = (f32[64,1024]{1,0:T(8,128)S(1)}, f32[64,1024]{1,0:T(8,128)S(1)}, f32[96,1024]{1,0:T(8,128)S(1)}, f32[16,512]{1,0:T(8,128)S(1)}) custom-call(f32[64,1024]{1,0:T(8,128)S(1)} %get-tuple-element.175.refs_0_, f32[16,128]{1,0:T(8,128)S(1)} %collective-permute-done.21.one_ref.refs_1_, f32[16,128]{1,0:T(8,128)S(1)} %collective-permute-done.22.two_ref.refs_2_, ...), custom_call_target="tpu_custom_call" | custom-call | flops 3000000000 | bytes 1 | tf_op jit(solution)/shard_map/pallas_call | solution.py:744
  53.2 1.0 %shard_map.165 = (f32[96,256]{1,0:T(8,128)S(1)}, f32[64,256]{1,0:T(8,128)S(1)}, f32[64,256]{1,0:T(8,128)}) custom-call(f32[64,1024]{1,0:T(8,128)S(1)} %get-tuple-element.178.refs_0_, f32[96,1024]{1,0:T(8,128)S(1)} %get-tuple-element.179.refs_1_, f32[8,1024]{1,0:T(8,128)S(1)} %get-tuple-element.101.refs_2_, s32[8,1024]{1,0:T(8,128)S(1)} %get-tuple-element.102.refs_3_, ...), custom_call_target="tpu_custom_call" | custom-call | flops 3000000000 | bytes 1 | tf_op jit(solution)/shard_map/pallas_call | solution.py:744
  54.5 0.9 %shard_map.167 = f32[64,256]{1,0:T(8,128)} custom-call(f32[64,256]{1,0:T(8,128)S(1)} %shard_map.166.refs_0_, f32[16,128]{1,0:T(8,128)S(1)} %collective-permute-done.24.refs_1_, f32[16,128]{1,0:T(8,128)S(1)} %collective-permute-done.25.refs_2_, s32[8,1024]{1,0:T(8,128)S(1)} %get-tuple-element.113.edge_ref.refs_3_, ...), custom_call_target="tpu_custom_call" | custom-call | flops 3000000000 | bytes 1 | tf_op jit(solution)/shard_map/pallas_call | solution.py:744
  (49 shorter events, 5.1 us)
Async XLA Ops:
  0.6 5.6 %copy-start.1 = (f32[2,64,64]{2,1,0:T(8,128)S(1)}, f32[2,64,64]{2,1,0:T(8,128)}, u32[]{:S(2)}) copy-start(f32[2,64,64]{2,1,0:T(8,128)} %refs_4_.1) | copy-start | bytes 98308
  0.6 5.6 %copy-start.2 = (f32[96,64]{0,1:T(8,128)S(1)}, f32[96,64]{0,1:T(8,128)}, u32[]{:S(2)}) copy-start(f32[96,64]{0,1:T(8,128)} %param.16) | copy-start | bytes 73732
  1.6 6.5 %collective-permute-start = (f32[80,256]{1,0:T(8,128)S(1)}, f32[80,256]{1,0:T(8,128)S(1)}, u32[]{:S(2)}, u32[]{:S(2)}) collective-permute-start(f32[80,256]{1,0:T(8,128)S(1)} %shard_map.131.refs_0_), channel_id=1, source_target_pairs={{0,6},{1,7},{2,4},{3,5},{4,2},{5,3},{6,0},{7,1},{8,14},{9,15},{10,... | collective-permute-start | bytes 245768 | tf_op jit(solution)/shard_map/ppermute | solution.py:841
  5.6 4.4 %collective-permute-start.1 = (f32[80,256]{1,0:T(8,128)S(1)}, f32[80,256]{1,0:T(8,128)S(1)}, u32[]{:S(2)}, u32[]{:S(2)}) collective-permute-start(f32[80,256]{1,0:T(8,128)S(1)} %shard_map.131.refs_0_), channel_id=1, source_target_pairs={{0,4},{1,5},{2,6},{3,7},{4,0},{5,1},{6,2},{7,3},{8,12},{9,13},{10,... | collective-permute-start | bytes 245768 | tf_op jit(solution)/shard_map/ppermute | solution.py:841
  6.1 4.4 %collective-permute-start.2 = (f32[80,256]{1,0:T(8,128)S(1)}, f32[80,256]{1,0:T(8,128)S(1)}, u32[]{:S(2)}, u32[]{:S(2)}) collective-permute-start(f32[80,256]{1,0:T(8,128)S(1)} %shard_map.131.refs_0_), channel_id=1, source_target_pairs={{0,2},{1,3},{2,0},{3,1},{4,6},{5,7},{6,4},{7,5},{8,10},{9,11},{10,... | collective-permute-start | bytes 245768 | tf_op jit(solution)/shard_map/ppermute | solution.py:841
  6.2 1.0 %copy-start = (f32[8,64,64]{2,1,0:T(8,128)S(1)}, f32[8,64,64]{2,1,0:T(8,128)}, u32[]{:S(2)}) copy-start(f32[8,64,64]{2,1,0:T(8,128)} %restriction_ref.1) | copy-start | bytes 393220
  6.2 1.0 %copy-start.3 = (f32[64,64]{1,0:T(8,128)S(1)}, f32[64,64]{1,0:T(8,128)}, u32[]{:S(2)}) copy-start(f32[64,64]{1,0:T(8,128)} %stiff_ref.5) | copy-start | bytes 49156
  11.0 4.9 %collective-permute-start.4 = (f32[16,128]{1,0:T(8,128)S(1)}, f32[16,128]{1,0:T(8,128)S(1)}, u32[]{:S(2)}, u32[]{:S(2)}) collective-permute-start(f32[16,128]{1,0:T(8,128)S(1)} %get-tuple-element.99._), channel_id=1, source_target_pairs={{0,8},{1,9},{2,10},{3,11},{4,12},{5,13},{6,14},{7,15},{8,0},{9,1},... | collective-permute-start | bytes 24584 | tf_op jit(solution)/shard_map/ppermute | solution.py:814
  12.6 3.3 %collective-permute-start.5 = (f32[16,128]{1,0:T(8,128)S(1)}, f32[16,128]{1,0:T(8,128)S(1)}, u32[]{:S(2)}, u32[]{:S(2)}) collective-permute-start(f32[16,128]{1,0:T(8,128)S(1)} %get-tuple-element.99._), channel_id=1, source_target_pairs={{0,1},{1,0},{2,3},{3,2},{4,5},{5,4},{6,7},{7,6},{8,16},{9,17},{10,... | collective-permute-start | bytes 24584 | tf_op jit(solution)/shard_map/ppermute | solution.py:814
  13.0 2.2 %collective-permute-start.3 = (f32[16,512]{1,0:T(8,128)S(1)}, f32[16,512]{1,0:T(8,128)S(1)}, u32[]{:S(2)}, u32[]{:S(2)}) collective-permute-start(f32[16,512]{1,0:T(8,128)S(1)} %get-tuple-element.107.refs_3_), channel_id=1, source_target_pairs={{0,1},{1,0},{2,3},{3,2},{4,5},{5,4},{6,7},{7,6},{8,9},{9,8},{10,11... | collective-permute-start | bytes 98312 | tf_op jit(solution)/shard_map/ppermute | solution.py:866
  16.4 6.3 %collective-permute-start.7 = (f32[16,128]{1,0:T(8,128)S(1)}, f32[16,128]{1,0:T(8,128)S(1)}, u32[]{:S(2)}, u32[]{:S(2)}) collective-permute-start(f32[16,128]{1,0:T(8,128)S(1)} %shard_map.139.refs_9_), channel_id=1, source_target_pairs={{0,8},{1,9},{2,10},{3,11},{4,12},{5,13},{6,14},{7,15},{8,0},{9,1},... | collective-permute-start | bytes 24584 | tf_op jit(solution)/shard_map/ppermute | solution.py:814
  19.1 3.6 %collective-permute-start.8 = (f32[16,128]{1,0:T(8,128)S(1)}, f32[16,128]{1,0:T(8,128)S(1)}, u32[]{:S(2)}, u32[]{:S(2)}) collective-permute-start(f32[16,128]{1,0:T(8,128)S(1)} %shard_map.139.refs_9_), channel_id=1, source_target_pairs={{0,1},{1,0},{2,3},{3,2},{4,5},{5,4},{6,7},{7,6},{8,16},{9,17},{10,... | collective-permute-start | bytes 24584 | tf_op jit(solution)/shard_map/ppermute | solution.py:814
  20.1 1.8 %collective-permute-start.6 = (f32[16,512]{1,0:T(8,128)S(1)}, f32[16,512]{1,0:T(8,128)S(1)}, u32[]{:S(2)}, u32[]{:S(2)}) collective-permute-start(f32[16,512]{1,0:T(8,128)S(1)} %get-tuple-element.125.refs_3_), channel_id=1, source_target_pairs={{0,1},{1,0},{2,3},{3,2},{4,5},{5,4},{6,7},{7,6},{8,9},{9,8},{10,11... | collective-permute-start | bytes 98312 | tf_op jit(solution)/shard_map/ppermute | solution.py:866
  23.1 4.0 %collective-permute-start.10 = (f32[16,128]{1,0:T(8,128)S(1)}, f32[16,128]{1,0:T(8,128)S(1)}, u32[]{:S(2)}, u32[]{:S(2)}) collective-permute-start(f32[16,128]{1,0:T(8,128)S(1)} %shard_map.143.refs_9_), channel_id=1, source_target_pairs={{0,8},{1,9},{2,10},{3,11},{4,12},{5,13},{6,14},{7,15},{8,0},{9,1},... | collective-permute-start | bytes 24584 | tf_op jit(solution)/shard_map/ppermute | solution.py:814
  23.7 3.5 %collective-permute-start.11 = (f32[16,128]{1,0:T(8,128)S(1)}, f32[16,128]{1,0:T(8,128)S(1)}, u32[]{:S(2)}, u32[]{:S(2)}) collective-permute-start(f32[16,128]{1,0:T(8,128)S(1)} %shard_map.143.refs_9_), channel_id=1, source_target_pairs={{0,1},{1,0},{2,3},{3,2},{4,5},{5,4},{6,7},{7,6},{8,16},{9,17},{10,... | collective-permute-start | bytes 24584 | tf_op jit(solution)/shard_map/ppermute | solution.py:814
  24.7 1.8 %collective-permute-start.9 = (f32[16,512]{1,0:T(8,128)S(1)}, f32[16,512]{1,0:T(8,128)S(1)}, u32[]{:S(2)}, u32[]{:S(2)}) collective-permute-start(f32[16,512]{1,0:T(8,128)S(1)} %get-tuple-element.135.refs_3_), channel_id=1, source_target_pairs={{0,1},{1,0},{2,3},{3,2},{4,5},{5,4},{6,7},{7,6},{8,9},{9,8},{10,11... | collective-permute-start | bytes 98312 | tf_op jit(solution)/shard_map/ppermute | solution.py:866
  27.4 4.9 %collective-permute-start.13 = (f32[72,128]{1,0:T(8,128)S(1)}, f32[72,128]{1,0:T(8,128)S(1)}, u32[]{:S(2)}, u32[]{:S(2)}) collective-permute-start(f32[72,128]{1,0:T(8,128)S(1)} %shard_map.147.refs_7_), channel_id=1, source_target_pairs={{0,2},{1,8},{2,0},{3,10},{4,6},{5,12},{6,4},{7,14},{8,1},{9,16},{1... | collective-permute-start | bytes 110600 | tf_op jit(solution)/shard_map/ppermute | solution.py:907
  29.0 2.1 %collective-permute-start.12 = (f32[72,640]{1,0:T(8,128)S(1)}, f32[72,640]{1,0:T(8,128)S(1)}, u32[]{:S(2)}, u32[]{:S(2)}) collective-permute-start(f32[72,640]{1,0:T(8,128)S(1)} %get-tuple-element.139), channel_id=1, source_target_pairs={{0,1},{1,0},{2,3},{3,2},{4,5},{5,4},{6,7},{7,6},{8,9},{9,8},{10,11... | collective-permute-start | bytes 552968 | tf_op jit(solution)/shard_map/ppermute | solution.py:908
  34.3 4.6 %collective-permute-start.15 = (f32[16,128]{1,0:T(8,128)S(1)}, f32[16,128]{1,0:T(8,128)S(1)}, u32[]{:S(2)}, u32[]{:S(2)}) collective-permute-start(f32[16,128]{1,0:T(8,128)S(1)} %get-tuple-element.149._), channel_id=1, source_target_pairs={{0,8},{1,9},{2,10},{3,11},{4,12},{5,13},{6,14},{7,15},{8,0},{9,1},... | collective-permute-start | bytes 24584 | tf_op jit(solution)/shard_map/ppermute | solution.py:814
  35.6 3.3 %collective-permute-start.16 = (f32[16,128]{1,0:T(8,128)S(1)}, f32[16,128]{1,0:T(8,128)S(1)}, u32[]{:S(2)}, u32[]{:S(2)}) collective-permute-start(f32[16,128]{1,0:T(8,128)S(1)} %get-tuple-element.149._), channel_id=1, source_target_pairs={{0,1},{1,0},{2,3},{3,2},{4,5},{5,4},{6,7},{7,6},{8,16},{9,17},{10,... | collective-permute-start | bytes 24584 | tf_op jit(solution)/shard_map/ppermute | solution.py:814
  36.0 2.1 %collective-permute-start.14 = (f32[16,512]{1,0:T(8,128)S(1)}, f32[16,512]{1,0:T(8,128)S(1)}, u32[]{:S(2)}, u32[]{:S(2)}) collective-permute-start(f32[16,512]{1,0:T(8,128)S(1)} %get-tuple-element.154.refs_3_), channel_id=1, source_target_pairs={{0,1},{1,0},{2,3},{3,2},{4,5},{5,4},{6,7},{7,6},{8,9},{9,8},{10,11... | collective-permute-start | bytes 98312 | tf_op jit(solution)/shard_map/ppermute | solution.py:866
  39.3 5.5 %collective-permute-start.18 = (f32[16,128]{1,0:T(8,128)S(1)}, f32[16,128]{1,0:T(8,128)S(1)}, u32[]{:S(2)}, u32[]{:S(2)}) collective-permute-start(f32[16,128]{1,0:T(8,128)S(1)} %shard_map.155.refs_9_), channel_id=1, source_target_pairs={{0,8},{1,9},{2,10},{3,11},{4,12},{5,13},{6,14},{7,15},{8,0},{9,1},... | collective-permute-start | bytes 24584 | tf_op jit(solution)/shard_map/ppermute | solution.py:814
  41.3 3.6 %collective-permute-start.19 = (f32[16,128]{1,0:T(8,128)S(1)}, f32[16,128]{1,0:T(8,128)S(1)}, u32[]{:S(2)}, u32[]{:S(2)}) collective-permute-start(f32[16,128]{1,0:T(8,128)S(1)} %shard_map.155.refs_9_), channel_id=1, source_target_pairs={{0,1},{1,0},{2,3},{3,2},{4,5},{5,4},{6,7},{7,6},{8,16},{9,17},{10,... | collective-permute-start | bytes 24584 | tf_op jit(solution)/shard_map/ppermute | solution.py:814
  42.3 1.8 %collective-permute-start.17 = (f32[16,512]{1,0:T(8,128)S(1)}, f32[16,512]{1,0:T(8,128)S(1)}, u32[]{:S(2)}, u32[]{:S(2)}) collective-permute-start(f32[16,512]{1,0:T(8,128)S(1)} %get-tuple-element.164.refs_3_), channel_id=1, source_target_pairs={{0,1},{1,0},{2,3},{3,2},{4,5},{5,4},{6,7},{7,6},{8,9},{9,8},{10,11... | collective-permute-start | bytes 98312 | tf_op jit(solution)/shard_map/ppermute | solution.py:866
  45.3 4.4 %collective-permute-start.21 = (f32[16,128]{1,0:T(8,128)S(1)}, f32[16,128]{1,0:T(8,128)S(1)}, u32[]{:S(2)}, u32[]{:S(2)}) collective-permute-start(f32[16,128]{1,0:T(8,128)S(1)} %shard_map.159.refs_9_), channel_id=1, source_target_pairs={{0,8},{1,9},{2,10},{3,11},{4,12},{5,13},{6,14},{7,15},{8,0},{9,1},... | collective-permute-start | bytes 24584 | tf_op jit(solution)/shard_map/ppermute | solution.py:814
  46.1 3.6 %collective-permute-start.22 = (f32[16,128]{1,0:T(8,128)S(1)}, f32[16,128]{1,0:T(8,128)S(1)}, u32[]{:S(2)}, u32[]{:S(2)}) collective-permute-start(f32[16,128]{1,0:T(8,128)S(1)} %shard_map.159.refs_9_), channel_id=1, source_target_pairs={{0,1},{1,0},{2,3},{3,2},{4,5},{5,4},{6,7},{7,6},{8,16},{9,17},{10,... | collective-permute-start | bytes 24584 | tf_op jit(solution)/shard_map/ppermute | solution.py:814
  47.2 1.8 %collective-permute-start.20 = (f32[16,512]{1,0:T(8,128)S(1)}, f32[16,512]{1,0:T(8,128)S(1)}, u32[]{:S(2)}, u32[]{:S(2)}) collective-permute-start(f32[16,512]{1,0:T(8,128)S(1)} %get-tuple-element.174.refs_3_), channel_id=1, source_target_pairs={{0,1},{1,0},{2,3},{3,2},{4,5},{5,4},{6,7},{7,6},{8,9},{9,8},{10,11... | collective-permute-start | bytes 98312 | tf_op jit(solution)/shard_map/ppermute | solution.py:866
  50.2 4.4 %collective-permute-start.24 = (f32[16,128]{1,0:T(8,128)S(1)}, f32[16,128]{1,0:T(8,128)S(1)}, u32[]{:S(2)}, u32[]{:S(2)}) collective-permute-start(f32[16,128]{1,0:T(8,128)S(1)} %shard_map.163.refs_9_), channel_id=1, source_target_pairs={{0,8},{1,9},{2,10},{3,11},{4,12},{5,13},{6,14},{7,15},{8,0},{9,1},... | collective-permute-start | bytes 24584 | tf_op jit(solution)/shard_map/ppermute | solution.py:814
  51.8 2.8 %collective-permute-start.25 = (f32[16,128]{1,0:T(8,128)S(1)}, f32[16,128]{1,0:T(8,128)S(1)}, u32[]{:S(2)}, u32[]{:S(2)}) collective-permute-start(f32[16,128]{1,0:T(8,128)S(1)} %shard_map.163.refs_9_), channel_id=1, source_target_pairs={{0,1},{1,0},{2,3},{3,2},{4,5},{5,4},{6,7},{7,6},{8,16},{9,17},{10,... | collective-permute-start | bytes 24584 | tf_op jit(solution)/shard_map/ppermute | solution.py:814
  52.8 1.4 %collective-permute-start.23 = (f32[16,512]{1,0:T(8,128)S(1)}, f32[16,512]{1,0:T(8,128)S(1)}, u32[]{:S(2)}, u32[]{:S(2)}) collective-permute-start(f32[16,512]{1,0:T(8,128)S(1)} %get-tuple-element.185.refs_3_), channel_id=1, source_target_pairs={{0,1},{1,0},{2,3},{3,2},{4,5},{5,4},{6,7},{7,6},{8,9},{9,8},{10,11... | collective-permute-start | bytes 98312 | tf_op jit(solution)/shard_map/ppermute | solution.py:866
